TPU v7x, 32 devices: a whole 2x2x4 slice. The times are simulated.
32 devices in a mesh: seq: 8 (over z, x), mp: 4 (over y, core).
Axes of the slice: x: 2, y: 2, z: 4, core: 2. Of those that a mesh axis runs over, the one named last changes fastest.
Arguments:
- scan_points: bfloat16 [16384, 512], P('seq'), may hold values from -6 to 6
- send_order: int32 [16384], P('seq'), may hold values from 0 to 2047, as said below
- arrive_order: int32 [16384], P('seq'), may hold values from 0 to 2047, as said below
- qkv_weight: bfloat16 [512, 3, 512], P(None, None, 'mp')
- out_weight: bfloat16 [512, 512], P(None, 'mp'), may hold values from -0.25 to 0.25
- voxel_grads: bfloat16 [16384, 512], P('seq'), may hold values from -6 to 6
- voxel_shard: int32 [16384, 1], P('seq'), may hold values from 0 to 7; in each aligned block of 2048 rows (0 to 2047, 2048 to 4095, ...) at most 512 rows name the same one
- voxel_point: int32 [16384], P('seq'), may hold values from 0 to 2047
Outputs:
- d_points: float32 [16384, 512], P('seq', 'mp')
- grad_qkv: float32 [512, 3, 512], P('seq', None, 'mp')
- grad_out: float32 [512, 512], P('seq', 'mp')
Inputs may be any that keep to these rules, and one draw needn't show every extreme that they name: `send_order`: each aligned block of 2048 entries is a permutation of the numbers 0 to 2047. `arrive_order`: each aligned block of 2048 entries is a permutation of the numbers 0 to 2047. `voxel_shard`: among the rows of one device, at most 512 name the same shard.
All inputs are finite; a program needn't handle non-finite values.
Results may differ from a plain program's by a relative error of at most 0.035.
The roundings to bfloat16 on the way count: a program that leaves them out, or rounds other values in their place, can miss the bound.
Values may be sent and summed in bfloat16 or wider, within the bound.
No kernel may reach another device: no remote copies, remote signals or barrier semaphores. Data moves between devices by JAX's collectives and lax.ppermute only.
A program may use at most 192 MiB of HBM per device.

v0:
```python
import jax
import jax.numpy as jnp
from jax import lax
from jax.sharding import PartitionSpec as P

HD = 16
PATCH = 1024


score_scale = 0.25
epsilon = 1e-05


def patch_pass(queries, key_rows, values, d_attended):
    row_count = queries.shape[0]
    head_count = queries.shape[1] // HD
    query_heads = queries.reshape(row_count, head_count, HD)
    key_heads = key_rows.reshape(row_count, head_count, HD)
    value_heads = values.reshape(row_count, head_count, HD)
    scores = (
        jnp.einsum("qhc,khc->hqk", query_heads, key_heads, preferred_element_type=jnp.float32)
        * score_scale
    )
    row_max = jnp.max(scores, axis=2, keepdims=True)
    weights_exp = jnp.exp(scores - row_max)
    probabilities = weights_exp / jnp.sum(weights_exp, axis=2, keepdims=True)
    prob_rounded = probabilities.astype(jnp.bfloat16)
    attended = jnp.einsum(
        "hqk,khc->qhc", prob_rounded, value_heads, preferred_element_type=jnp.float32
    ).astype(jnp.bfloat16)
    grad_heads = d_attended.reshape(row_count, head_count, HD)
    d_probabilities = jnp.einsum(
        "qhc,khc->hqk", grad_heads, value_heads, preferred_element_type=jnp.float32
    )
    d_values = jnp.einsum(
        "hqk,qhc->khc", prob_rounded, grad_heads, preferred_element_type=jnp.float32
    ).astype(jnp.bfloat16)
    row_delta = jnp.sum(grad_heads.astype(jnp.float32) * attended.astype(jnp.float32), axis=2)
    d_scores = (probabilities * (d_probabilities - row_delta.T[:, :, None]) * score_scale).astype(
        jnp.bfloat16
    )
    d_query = jnp.einsum(
        "hqk,khc->qhc", d_scores, key_heads, preferred_element_type=jnp.float32
    ).astype(jnp.bfloat16)
    d_keys = jnp.einsum(
        "hqk,qhc->khc", d_scores, query_heads, preferred_element_type=jnp.float32
    ).astype(jnp.bfloat16)
    stacked = jnp.stack([d_query, d_keys, d_values], axis=1).reshape(row_count, 3, head_count * HD)
    return (attended.reshape(row_count, head_count * HD), stacked)


def local(
    scan_points,
    send_order,
    arrive_order,
    qkv_weight,
    out_weight,
    voxel_grads,
    voxel_shard,
    voxel_point,
):
    shards = lax.axis_size("seq")
    local_rows = scan_points.shape[0]
    feature_count = scan_points.shape[1]
    local_cols = out_weight.shape[1]
    offset = lax.axis_index("mp") * local_cols
    outgoing = jnp.take(scan_points, send_order, axis=0)
    arrived = lax.all_to_all(outgoing, "seq", split_axis=0, concat_axis=0, tiled=True)
    points = jnp.take(arrived, arrive_order, axis=0)
    point_float = points.astype(jnp.float32)
    row_mean = jnp.mean(point_float, axis=1, keepdims=True)
    centered = point_float - row_mean
    row_var = jnp.mean(centered * centered, axis=1, keepdims=True)
    inv_scale = lax.rsqrt(row_var + epsilon)
    normed = centered * inv_scale
    hidden = normed.astype(jnp.bfloat16)
    projected = jnp.einsum(
        "pd,dtc->ptc", hidden, qkv_weight, preferred_element_type=jnp.float32
    ).astype(jnp.bfloat16)
    voxels = voxel_grads.shape[0]
    capacity = 2 * voxels // shards
    targets = voxel_shard[:, 0]
    onehot = (targets[:, None] == jnp.arange(shards, dtype=jnp.int32)[None, :]).astype(jnp.int32)
    before = jnp.cumsum(onehot, axis=0) - onehot
    places = targets * capacity + jnp.sum(before * onehot, axis=1)
    send_index = jnp.full((shards * capacity,), local_rows, jnp.int32).at[places].set(voxel_point)
    send_rows = (
        jnp.zeros((shards * capacity, feature_count), jnp.bfloat16).at[places].set(voxel_grads)
    )
    got_rows, got_index = (
        lax.all_to_all(send_rows, "seq", split_axis=0, concat_axis=0, tiled=True),
        lax.all_to_all(send_index, "seq", split_axis=0, concat_axis=0, tiled=True),
    )
    d_sum = jax.ops.segment_sum(
        got_rows.astype(jnp.float32), got_index, num_segments=local_rows + 1
    )[:local_rows]
    d_out = d_sum.astype(jnp.bfloat16)
    d_attended = jnp.dot(d_out, out_weight, preferred_element_type=jnp.float32).astype(jnp.bfloat16)
    patches = local_rows // PATCH

    def one_patch(operands):
        proj_patch, grad_patch = operands
        return patch_pass(proj_patch[:, 0], proj_patch[:, 1], proj_patch[:, 2], grad_patch)

    attended, d_projected = lax.map(
        one_patch,
        (
            projected.reshape(patches, PATCH, 3, local_cols),
            d_attended.reshape(patches, PATCH, local_cols),
        ),
    )
    attended = attended.reshape(local_rows, local_cols)
    d_projected = d_projected.reshape(local_rows, 3, local_cols)
    upper = jnp.einsum("pd,ptc->dtc", hidden, d_projected, preferred_element_type=jnp.float32)
    lower = jnp.dot(d_out.T, attended, preferred_element_type=jnp.float32)
    summed = lax.psum_scatter(
        jnp.concatenate([upper, lower[:, None, :]], axis=1).astype(jnp.bfloat16),
        "seq",
        scatter_dimension=0,
        tiled=True,
    ).astype(jnp.float32)
    grad_qkv = summed[:, :3, :]
    grad_out = summed[:, 3, :]
    d_partial = jnp.einsum(
        "ptc,dtc->pd", d_projected, qkv_weight, preferred_element_type=jnp.float32
    )
    d_hidden = lax.psum(d_partial.astype(jnp.bfloat16), "mp").astype(jnp.float32)
    mean_grad = jnp.mean(d_hidden, axis=1, keepdims=True)
    mean_cross = jnp.mean(d_hidden * normed, axis=1, keepdims=True)
    full_grad = d_out.astype(jnp.float32) + inv_scale * (d_hidden - mean_grad - normed * mean_cross)
    d_points = lax.dynamic_slice_in_dim(full_grad, offset, local_cols, 1)
    return (d_points, grad_qkv, grad_out)


def solution(mesh):
    in_specs = (
        P("seq", None),
        P("seq"),
        P("seq"),
        P(None, None, "mp"),
        P(None, "mp"),
        P("seq", None),
        P("seq", None),
        P("seq"),
    )
    out_specs = (P("seq", "mp"), P("seq", None, "mp"), P("seq", "mp"))
    return jax.shard_map(local, mesh=mesh, in_specs=in_specs, out_specs=out_specs, check_vma=False)
```

profile of v0, /device:TPU:0, one launch (start us, length us, event | category | flops | bytes accessed | tf_op | source)
XLA Modules:
  0.0 482.3 jit_solution(10939536025763135270)
XLA Ops:
  8.0 0.9 fusion.32
  8.9 2.3 reduce-window.6
  11.1 0.3 slice_reduce_fusion
  11.4 0.2 reduce-window.9
  11.7 0.7 fusion.31
  12.4 0.7 compare_select_fusion
  13.1 8.8 %scatter_custom_fusion = s32[4096]{0:T(1024)} fusion(s32[2048]{0:T(1024)S(1)} %bitcast.161, s32[2048]{0:T(1024)} %param.19, s32[]{:T(128)} %constant.31.clone.1), kind=kCustom, calls=%fused_computation.71 | custom fusion | bytes 16896 | tf_op jit(solution)/shard_map/scatter | solution.py:86
  21.9 7.3 %all-to-all-start = ((s32[8,512,1]{1,2,0:T(1,128)}), s32[8,512,1]{1,2,0:T(1,128)S(1)}, u32[]{:S(2)}, u32[]{:S(2)}) async-start(s32[8,512,1]{1,2,0:T(1,128)} %bitcast.19), calls=%async_computation | async-start | bytes 32768 | tf_op jit(solution)/shard_map/all_to_all | solution.py:92
  29.2 0.7 compare_and_fusion.1
  29.9 0.7 fusion.35
  30.6 9.2 %gather_fusion = bf16[2048,512]{1,0:T(8,128)(2,1)} fusion(bf16[2048,512]{1,0:T(8,128)(2,1)S(1)} %copy-done, s32[2048]{0:T(1024)S(1)} %fusion.35), kind=kCustom, calls=%fused_computation.clone | custom fusion | bytes 4202496 | tf_op jit(solution)/shard_map/jit(_take)/gather | solution.py:67
  39.8 2.8 broadcast_select_fusion.1
  42.5 6.0 %all-to-all-start.2 = ((bf16[8,256,512]{2,1,0:T(8,128)(2,1)}), bf16[8,256,512]{2,1,0:T(8,128)(2,1)S(1)}, u32[]{:S(2)}, u32[]{:S(2)}) async-start(bf16[8,256,512]{2,1,0:T(8,128)(2,1)} %bitcast.152), calls=%async_computation.2 | async-start | bytes 4194304 | tf_op jit(solution)/shard_map/all_to_all | solution.py:68
  48.5 12.6 %scatter_custom_fusion.1 = bf16[4096,512]{1,0:T(8,128)(2,1)} fusion(s32[2048]{0:T(1024)S(1)} %bitcast.162, bf16[2048,512]{1,0:T(8,128)(2,1)} %param.17, bf16[]{:T(256)} %constant.28.clone.1), kind=kCustom, calls=%fused_computation.42 | custom fusion | bytes 4194816 | tf_op jit(solution)/shard_map/scatter | solution.py:88
  61.1 35.1 %all-to-all-done.2 = bf16[8,256,512]{2,1,0:T(8,128)(2,1)S(1)} async-done(((bf16[8,256,512]{2,1,0:T(8,128)(2,1)}), bf16[8,256,512]{2,1,0:T(8,128)(2,1)S(1)}, u32[]{:S(2)}, u32[]{:S(2)}) %all-to-all-start.2) | async-done | bytes 2097184 | tf_op jit(solution)/shard_map/all_to_all | solution.py:68
  96.2 4.7 all-to-all-start.1
  101.0 9.2 %gather_fusion.1 = bf16[2048,512]{1,0:T(8,128)(2,1)} fusion(bf16[2048,512]{1,0:T(8,128)(2,1)S(1)} %bitcast.135, s32[2048]{0:T(1024)S(1)} %fusion.36), kind=kCustom, calls=%fused_computation.1.clone | custom fusion | bytes 4202496 | tf_op jit(solution)/shard_map/jit(_take)/gather | solution.py:69
  110.2 2.2 convert_reduce_fusion
  112.5 2.7 fusion.13
  115.3 0.6 copy-done.8
  115.8 3.3 convolution_convert_fusion.4
  119.2 74.3 %all-to-all-done.1 = bf16[8,512,512]{2,1,0:T(8,128)(2,1)} async-done(((bf16[8,512,512]{2,1,0:T(8,128)(2,1)}), bf16[8,512,512]{2,1,0:T(8,128)(2,1)}, u32[]{:S(2)}, u32[]{:S(2)}) %all-to-all-start.1) | async-done | bytes 4194336 | tf_op jit(solution)/shard_map/all_to_all | solution.py:91
  193.5 30.1 %scatter_custom_fusion.2 = f32[2049,512]{1,0:T(8,128)} fusion(s32[4096]{0:T(1024)S(1)} %bitcast.160, bf16[4096,512]{1,0:T(8,128)(2,1)} %bitcast.38, f32[]{:T(128)} %constant.30.clone.1), kind=kCustom, calls=%fused_computation.25 | custom fusion | flops 4194304 | bytes 8390660 | tf_op jit(solution)/shard_map/scatter-add | solution.py:94
  223.5 2.9 convolution_convert_fusion.5
  226.4 170.9 %while.12 = (s32[]{:T(128)}, bf16[2,1024,128]{2,1,0:T(8,128)(2,1)S(1)}, bf16[2,1024,3,128]{3,1,0,2:T(8,128)(2,1)}, bf16[2,1024,3,128]{3,1,0,2:T(8,128)(2,1)}, bf16[2,1024,128]{2,1,0:T(8,128)(2,1)S(1)}, /*index=5*/s32[]{:T(128)}) while((s32[]{:T(128)}, bf16[2,1024,128]{2,1,0:T(8,128)(2,1)S(1)}, bf16[2,1024,3,128]{3,1,0,2:T(8,128)(2,1)}, ...), condition=%wide.region_12.14_spmd, body=%wide.region_8.13_spmd.sunk | while | flops 1696326656 | bytes 283541632 | solution.py:105
  226.8 1.2 constant_dynamic-slice_fusion.5
  228.0 0.3 copy.60
  228.4 14.6 %fusion.91 = (f32[8,1024]{1,0:T(8,128)S(1)}, f32[8,1024,1024]{1,2,0:T(8,128)}) fusion(bf16[1024,8,16]{0,2,1:T(8,128)(2,1)S(1)} %bitcast.141, bf16[1024,8,16]{0,2,1:T(8,128)(2,1)S(1)} %bitcast.143), kind=kOutput, calls=%fused_computation.81.clone.1 | convolution fusion | flops 293602304 | bytes 34111488 | tf_op jit(solution)/shard_map/while/body/eval_jaxpr/sub | solution.py:25
  242.9 17.8 %fusion.92 = bf16[8,1024,1024]{1,2,0:T(8,128)(2,1)} fusion(f32[8,1024,1024]{1,2,0:T(8,128)} %get-tuple-element.112, f32[8,1024]{1,0:T(8,128)S(1)} %get-tuple-element.113), kind=kLoop, calls=%fused_computation.12.clone.1 | loop fusion | flops 16777216 | bytes 50364416 | tf_op jit(solution)/shard_map/while/body/eval_jaxpr/convert_element_type | solution.py:27
  260.7 10.2 %convolution_convert_fusion.10 = bf16[8,16,1024]{2,1,0:T(8,128)(2,1)S(1)} fusion(bf16[1024,8,16]{0,2,1:T(8,128)(2,1)S(1)} %bitcast.137, bf16[8,1024,1024]{1,2,0:T(8,128)(2,1)} %fusion.92), kind=kOutput, calls=%fused_computation.14.clone.1 | convolution fusion | flops 268566528 | bytes 17301504 | tf_op jit(solution)/shard_map/while/body/eval_jaxpr/hqk,qhc->khc/dot_general | solution.py:35
  270.9 8.1 %multiply_reduce_fusion.4 = (f32[1024,8]{0,1:T(8,128)S(1)}, bf16[8,16,1024]{2,1,0:T(8,128)(2,1)S(1)}) fusion(bf16[1024,8,16]{0,2,1:T(8,128)(2,1)S(1)} %bitcast.138, bf16[1024,8,16]{0,2,1:T(8,128)(2,1)S(1)} %bitcast.145, bf16[8,1024,1024]{1,2,0:T(8,128)(2,1)} %fusion.92), kind=kOutput, calls=%fused_computation.19.clone.1 | convolution fusion | flops 269082624 | bytes 17596416 | tf_op jit(solution)/shard_map/while/body/eval_jaxpr/hqk,khc->qhc/dot_general | solution.py:28
  279.0 0.2 copy.61
  279.2 13.0 %multiply_convert_fusion.2 = bf16[8,1024,1024]{1,2,0:T(8,128)(2,1)S(1)} fusion(f32[8,1024]{1,0:T(8,128)S(1)} %bitcast.154, f32[8,1024,1024]{1,2,0:T(8,128)} %get-tuple-element.112, f32[8,1024]{1,0:T(8,128)S(1)} %get-tuple-element.113, bf16[1024,8,16]{0,2,1:T(8,128)(2,1)S(1)} %bitcast.139, bf16[1024,8,16]{0,2,1:T(8,128)(2,1)S(1)} %bitcast.146), kind=kOutput, calls=%fused_computation.6.clone.1 | convolution fusion | flops 310378496 | bytes 50921472 | tf_op jit(solution)/shard_map/while/body/eval_jaxpr/qhc,khc->hqk/dot_general | solution.py:32
  292.2 5.7 %copy-done.2 = bf16[8,1024,1024]{1,2,0:T(8,128)(2,1)} copy-done((bf16[8,1024,1024]{1,2,0:T(8,128)(2,1)}, bf16[8,1024,1024]{1,2,0:T(8,128)(2,1)S(1)}, u32[]{:S(2)}) %copy-start.2) | copy-done | bytes 16777240 | tf_op jit(solution)/shard_map/while
  297.9 2.3 convolution_convert_fusion.12
  300.2 10.2 %convolution_convert_fusion.11 = bf16[8,16,1024]{2,1,0:T(8,128)(2,1)S(1)} fusion(bf16[1024,8,16]{0,2,1:T(8,128)(2,1)S(1)} %bitcast.142, bf16[8,1024,1024]{1,2,0:T(8,128)(2,1)} %copy-done.2), kind=kOutput, calls=%fused_computation.15.clone.1 | convolution fusion | flops 268566528 | bytes 17301504 | tf_op jit(solution)/shard_map/while/body/eval_jaxpr/hqk,qhc->khc/dot_general | solution.py:45
  310.5 0.4 copy.62
  310.9 1.1 constant_dynamic-update-slice_fusion.5
  312.2 1.2 constant_dynamic-slice_fusion.5
  313.4 0.3 copy.60
  313.7 14.5 %fusion.91 = (f32[8,1024]{1,0:T(8,128)S(1)}, f32[8,1024,1024]{1,2,0:T(8,128)}) fusion(bf16[1024,8,16]{0,2,1:T(8,128)(2,1)S(1)} %bitcast.141, bf16[1024,8,16]{0,2,1:T(8,128)(2,1)S(1)} %bitcast.143), kind=kOutput, calls=%fused_computation.81.clone.1 | convolution fusion | flops 293602304 | bytes 34111488 | tf_op jit(solution)/shard_map/while/body/eval_jaxpr/sub | solution.py:25
  328.3 17.8 %fusion.92 = bf16[8,1024,1024]{1,2,0:T(8,128)(2,1)} fusion(f32[8,1024,1024]{1,2,0:T(8,128)} %get-tuple-element.112, f32[8,1024]{1,0:T(8,128)S(1)} %get-tuple-element.113), kind=kLoop, calls=%fused_computation.12.clone.1 | loop fusion | flops 16777216 | bytes 50364416 | tf_op jit(solution)/shard_map/while/body/eval_jaxpr/convert_element_type | solution.py:27
  346.1 10.2 %convolution_convert_fusion.10 = bf16[8,16,1024]{2,1,0:T(8,128)(2,1)S(1)} fusion(bf16[1024,8,16]{0,2,1:T(8,128)(2,1)S(1)} %bitcast.137, bf16[8,1024,1024]{1,2,0:T(8,128)(2,1)} %fusion.92), kind=kOutput, calls=%fused_computation.14.clone.1 | convolution fusion | flops 268566528 | bytes 17301504 | tf_op jit(solution)/shard_map/while/body/eval_jaxpr/hqk,qhc->khc/dot_general | solution.py:35
  356.3 8.1 %multiply_reduce_fusion.4 = (f32[1024,8]{0,1:T(8,128)S(1)}, bf16[8,16,1024]{2,1,0:T(8,128)(2,1)S(1)}) fusion(bf16[1024,8,16]{0,2,1:T(8,128)(2,1)S(1)} %bitcast.138, bf16[1024,8,16]{0,2,1:T(8,128)(2,1)S(1)} %bitcast.145, bf16[8,1024,1024]{1,2,0:T(8,128)(2,1)} %fusion.92), kind=kOutput, calls=%fused_computation.19.clone.1 | convolution fusion | flops 269082624 | bytes 17596416 | tf_op jit(solution)/shard_map/while/body/eval_jaxpr/hqk,khc->qhc/dot_general | solution.py:28
  364.4 0.2 copy.61
  364.6 13.0 %multiply_convert_fusion.2 = bf16[8,1024,1024]{1,2,0:T(8,128)(2,1)S(1)} fusion(f32[8,1024]{1,0:T(8,128)S(1)} %bitcast.154, f32[8,1024,1024]{1,2,0:T(8,128)} %get-tuple-element.112, f32[8,1024]{1,0:T(8,128)S(1)} %get-tuple-element.113, bf16[1024,8,16]{0,2,1:T(8,128)(2,1)S(1)} %bitcast.139, bf16[1024,8,16]{0,2,1:T(8,128)(2,1)S(1)} %bitcast.146), kind=kOutput, calls=%fused_computation.6.clone.1 | convolution fusion | flops 310378496 | bytes 50921472 | tf_op jit(solution)/shard_map/while/body/eval_jaxpr/qhc,khc->hqk/dot_general | solution.py:32
  377.6 5.7 %copy-done.2 = bf16[8,1024,1024]{1,2,0:T(8,128)(2,1)} copy-done((bf16[8,1024,1024]{1,2,0:T(8,128)(2,1)}, bf16[8,1024,1024]{1,2,0:T(8,128)(2,1)S(1)}, u32[]{:S(2)}) %copy-start.2) | copy-done | bytes 16777240 | tf_op jit(solution)/shard_map/while
  383.3 2.3 convolution_convert_fusion.12
  385.6 10.2 %convolution_convert_fusion.11 = bf16[8,16,1024]{2,1,0:T(8,128)(2,1)S(1)} fusion(bf16[1024,8,16]{0,2,1:T(8,128)(2,1)S(1)} %bitcast.142, bf16[8,1024,1024]{1,2,0:T(8,128)(2,1)} %copy-done.2), kind=kOutput, calls=%fused_computation.15.clone.1 | convolution fusion | flops 268566528 | bytes 17301504 | tf_op jit(solution)/shard_map/while/body/eval_jaxpr/hqk,qhc->khc/dot_general | solution.py:45
  395.9 0.4 copy.62
  396.3 1.0 constant_dynamic-update-slice_fusion.5
  397.4 3.1 fusion.23
  400.5 0.2 copy-done.15
  400.7 2.2 fusion.20
  402.9 0.8 pad_maximum_fusion.1
  403.9 4.0 bitcast_convert_fusion
  407.9 3.8 slice.44
  411.8 53.3 %reduce-scatter.2.cloned.1.call-done = bf16[64,4,128]{2,0,1:T(8,128)(2,1)} async-done(((bf16[512,4,128]{2,0,1:T(8,128)(2,1)}), bf16[64,4,128]{2,0,1:T(8,128)(2,1)}) %reduce-scatter.2.cloned.1.call-update) | async-done | bytes 65552 | tf_op jit(solution)/shard_map/reduce_scatter | solution.py:116
  465.1 0.8 convert_element_type.86
  465.9 0.6 slice_bitcast_fusion
  466.6 4.2 convert_reduce_fusion.1
  470.9 0.6 convert_element_type.85
  471.5 2.7 fusion.26
  474.2 0.6 slice.39
  (58 shorter events, 1.0 us)
Async XLA Ops:
  8.0 22.6 %copy-start = (bf16[2048,512]{1,0:T(8,128)(2,1)S(1)}, bf16[2048,512]{1,0:T(8,128)(2,1)}, u32[]{:S(2)}) copy-start(bf16[2048,512]{1,0:T(8,128)(2,1)} %param.12) | copy-start | bytes 6291460
  21.9 20.6 %all-to-all-start = ((s32[8,512,1]{1,2,0:T(1,128)}), s32[8,512,1]{1,2,0:T(1,128)S(1)}, u32[]{:S(2)}, u32[]{:S(2)}) async-start(s32[8,512,1]{1,2,0:T(1,128)} %bitcast.19), calls=%async_computation | async-start | bytes 32768 | tf_op jit(solution)/shard_map/all_to_all | solution.py:92
  42.5 53.7 %all-to-all-start.2 = ((bf16[8,256,512]{2,1,0:T(8,128)(2,1)}), bf16[8,256,512]{2,1,0:T(8,128)(2,1)S(1)}, u32[]{:S(2)}, u32[]{:S(2)}) async-start(bf16[8,256,512]{2,1,0:T(8,128)(2,1)} %bitcast.152), calls=%async_computation.2 | async-start | bytes 4194304 | tf_op jit(solution)/shard_map/all_to_all | solution.py:68
  96.2 4.8 copy-start.14
  96.2 97.2 %all-to-all-start.1 = ((bf16[8,512,512]{2,1,0:T(8,128)(2,1)}), bf16[8,512,512]{2,1,0:T(8,128)(2,1)}, u32[]{:S(2)}, u32[]{:S(2)}) async-start(bf16[8,512,512]{2,1,0:T(8,128)(2,1)} %bitcast.150), calls=%async_computation.1 | async-start | bytes 8388608 | tf_op jit(solution)/shard_map/all_to_all | solution.py:91
  100.9 364.2 %reduce-scatter.2.cloned.1.call-start = ((), (), s32[]{:S(2)}) async-start(), calls=%async_computation.5 | async-start | bytes 589824 | tf_op jit(solution)/shard_map/reduce_scatter | solution.py:116
  101.0 14.2 %copy-start.12 = (pred[2048]{0:T(1024)(128)(4,1)}, pred[2048]{0:T(1024)(128)(4,1)S(1)}, u32[]{:S(2)}) copy-start(pred[2048]{0:T(1024)(128)(4,1)S(1)} %compare_and_fusion) | copy-start | bytes 6148
  110.2 5.6 %copy-start.3 = (bf16[2048,512]{1,0:T(8,128)(2,1)S(1)}, bf16[2048,512]{1,0:T(8,128)(2,1)}, u32[]{:S(2)}) copy-start(bf16[2048,512]{1,0:T(8,128)(2,1)} %gather_fusion.1) | copy-start | bytes 6291460
  110.2 5.6 %copy-start.16 = (bf16[512,3,128]{2,0,1:T(8,128)(2,1)S(1)}, bf16[512,3,128]{2,0,1:T(8,128)(2,1)}, u32[]{:S(2)}) copy-start(bf16[512,3,128]{2,0,1:T(8,128)(2,1)} %param.15) | copy-start | bytes 1179652
  112.5 2.8 copy-start.10
  115.2 0.6 copy-start.8
  193.5 30.1 %copy-start.7 = (bf16[512,128]{1,0:T(8,128)(2,1)S(1)}, bf16[512,128]{1,0:T(8,128)(2,1)}, u32[]{:S(2)}) copy-start(bf16[512,128]{1,0:T(8,128)(2,1)} %param.16) | copy-start | bytes 393220
  292.2 5.7 %copy-start.2 = (bf16[8,1024,1024]{1,2,0:T(8,128)(2,1)}, bf16[8,1024,1024]{1,2,0:T(8,128)(2,1)S(1)}, u32[]{:S(2)}) copy-start(bf16[8,1024,1024]{1,2,0:T(8,128)(2,1)S(1)} %multiply_convert_fusion.2) | copy-start | bytes 50331652 | tf_op jit(solution)/shard_map/while
  377.5 5.7 %copy-start.2 = (bf16[8,1024,1024]{1,2,0:T(8,128)(2,1)}, bf16[8,1024,1024]{1,2,0:T(8,128)(2,1)S(1)}, u32[]{:S(2)}) copy-start(bf16[8,1024,1024]{1,2,0:T(8,128)(2,1)S(1)} %multiply_convert_fusion.2) | copy-start | bytes 50331652 | tf_op jit(solution)/shard_map/while
  397.4 3.1 copy-start.4
  397.4 3.1 copy-start.9
  397.4 3.1 copy-start.11
  397.4 3.2 copy-start.13
  397.4 3.3 copy-start.15
  400.7 3.1 copy-start.17
  403.8 62.8 %all-reduce.2.cloned.1.call-start = ((), (), s32[]{:S(2)}) async-start(), calls=%async_computation.4 | async-start | bytes 4194304 | tf_op jit(solution)/shard_map/psum | solution.py:127
  466.6 4.3 copy-start.5
  470.8 4.0 copy-start.1
  470.9 3.3 copy-start.6
Sparse Core Ops, SparseCore 0:
  403.9 61.1 reduce-scatter.1
Sparse Core Ops, SparseCore 1:
  408.0 49.9 all-reduce.1
where the time goes:
time: 484 us; the launch traced here: 482 us
  waiting for transfers between devices  163 us (34%)
  matrix products  132 us (27%)
  other arithmetic  89.1 us (18%)
  local copies, waits for them, and re-layouts  64.1 us (13%)
  starting transfers between devices  18 us (4%)
  between operations  15.8 us (3%)
    all_to_all x1, waiting for transfers between devices, local(): lax.all_to_all(send_rows, 'seq', split_axis=0, concat_axis=0, tiled=True)  74.3 us
    reduce_scatter x1, waiting for transfers between devices, local(): lax.psum_scatter(jnp.concatenate([upper, lower[:, None, :]], axis=1).asty...  53.3 us
    convert_element_type x2, other arithmetic, patch_pass(): prob_rounded = probabilities.astype(jnp.bfloat16)  35.6 us
    all_to_all x1, waiting for transfers between devices, local(): lax.all_to_all(outgoing, 'seq', split_axis=0, concat_axis=0, tiled=True)  35.1 us
    scatter-add x1, other arithmetic, local(): jax.ops.segment_sum(got_rows.astype(jnp.float32), got_index, num_segments...  30.1 us
    sub x2, matrix products, patch_pass(): weights_exp = jnp.exp(scores - row_max)  29.1 us
    dot_general x2, matrix products, patch_pass(): jnp.einsum('qhc,khc->hqk', grad_heads, value_heads, preferred_element_typ...  26 us
    dot_general x2, matrix products, patch_pass(): jnp.einsum('hqk,qhc->khc', d_scores, query_heads, preferred_element_type=...  20.4 us
  transfers between devices with their start and end apart: 5, of which 3 were waited for; matrix products, arithmetic and copies ran while one was open for 11% of the time, Pallas kernels for 0%

commit v1 on v0

v1 whole, which is shorter than its diff:
```python
import functools

import jax
import jax.numpy as jnp
from jax import lax
from jax.experimental import pallas as pl
from jax.experimental.pallas import tpu as pltpu
from jax.sharding import PartitionSpec as P

HD = 16
PATCH = 1024
LANES = 128
INDEX_ROWS = 16
INDEX_BASE = 64

score_scale = 0.25
epsilon = 1e-05
log2_e = 1.4426950408889634

f32 = jnp.float32
bf16 = jnp.bfloat16
i32 = jnp.int32

ROWS_BY_ROWS = (((1,), (1,)), ((), ()))


def params(mib):
    return pltpu.CompilerParams(vmem_limit_bytes=mib << 20)


def cost(flops, bytes_accessed, transcendentals=0):
    return pl.CostEstimate(
        flops=int(flops), bytes_accessed=int(bytes_accessed), transcendentals=int(transcendentals)
    )


def dot(a, b):
    return jnp.dot(a, b, preferred_element_type=f32)


def dot_rows(a, b):
    return lax.dot_general(a, b, ROWS_BY_ROWS, preferred_element_type=f32)


def ones_where(mask):
    return jnp.where(mask, 1.0, 0.0).astype(bf16)


def permute_body(column_ref, order_ref, block_ref, out_ref):
    step = pl.program_id(0)
    source_rows = block_ref.shape[0]
    chunks = out_ref.shape[0] // LANES
    lane = lax.broadcasted_iota(i32, (LANES, LANES), 1)
    block = block_ref[...]
    for j in range(chunks):
        wanted = order_ref[pl.ds(step * chunks + j, 1), :].astype(f32)
        wanted = jnp.broadcast_to(wanted, (LANES, LANES)).T.astype(i32)
        onehot = jnp.concatenate(
            [ones_where(wanted == lane + k * LANES) for k in range(source_rows // LANES)], axis=1
        )
        out_ref[j * LANES : (j + 1) * LANES, :] = dot(onehot, block).astype(bf16)


def permute_rows(rows, order, column):
    row_count = order.shape[0]
    step_rows = min(512, row_count)
    return pl.pallas_call(
        permute_body,
        grid_spec=pltpu.PrefetchScalarGridSpec(
            num_scalar_prefetch=1,
            grid=(row_count // step_rows,),
            in_specs=[
                pl.BlockSpec((row_count // LANES, LANES), lambda i, c: (0, 0)),
                pl.BlockSpec((rows.shape[0], LANES), lambda i, c: (0, c[0])),
            ],
            out_specs=pl.BlockSpec((step_rows, LANES), lambda i, c: (i, 0)),
        ),
        out_shape=jax.ShapeDtypeStruct((row_count, LANES), bf16),
        compiler_params=params(32),
        cost_estimate=cost(2 * row_count * row_count * LANES * 4, 3 * row_count * LANES * 2),
        name="permute_rows",
    )(column, order.reshape(row_count // LANES, LANES), rows)


def bucket_body(shards, capacity, column_ref, shard_ref, point_ref, grads_ref, out_ref, place_ref):
    step = pl.program_id(0)
    row_count = grads_ref.shape[0]
    groups = row_count // LANES

    @pl.when(step == 0)
    def _():
        targets = shard_ref[...]
        masks = [ones_where(targets == t) for t in range(shards)]
        stacked = jnp.concatenate(masks, axis=0)
        above = ones_where(
            lax.broadcasted_iota(i32, (LANES, LANES), 0)
            < lax.broadcasted_iota(i32, (LANES, LANES), 1)
        )
        earlier = ones_where(
            lax.broadcasted_iota(i32, (groups, groups), 1)
            < lax.broadcasted_iota(i32, (groups, groups), 0)
        )
        in_row = dot(stacked, above)
        places = jnp.zeros((groups, LANES), f32)
        for t in range(shards):
            rows_before = jnp.sum(dot(earlier, masks[t]), axis=1, keepdims=True)
            place = in_row[t * groups : (t + 1) * groups] + rows_before + float(t * capacity)
            places = jnp.where(targets == t, place, places)
        place_ref[...] = places.astype(i32)

    slot = lax.broadcasted_iota(i32, (capacity, LANES), 0) + step * capacity
    onehot = jnp.concatenate(
        [ones_where(place_ref[j : j + 1, :] == slot) for j in range(groups)], axis=1
    )
    out_ref[0, :capacity, :] = dot(onehot, grads_ref[...]).astype(bf16)
    points = jnp.concatenate([point_ref[j : j + 1, :] for j in range(groups)], axis=1)
    high = points // INDEX_BASE
    low = points - high * INDEX_BASE
    digits = jnp.concatenate(
        [high.astype(f32), low.astype(f32), jnp.zeros((INDEX_ROWS - 2, row_count), f32)], axis=0
    )
    sent = dot_rows(digits.astype(bf16), onehot)
    chunks = capacity // LANES
    rows = [sent[d : d + 1, j * LANES : (j + 1) * LANES] for d in range(2) for j in range(chunks)]
    rows.append(jnp.zeros((INDEX_ROWS - 2 * chunks, LANES), f32))
    out_ref[0, capacity:, :] = jnp.concatenate(rows, axis=0).astype(bf16)


def bucket_rows(grads, targets, points, column, shards, capacity):
    row_count = grads.shape[0]
    groups = row_count // LANES
    return pl.pallas_call(
        functools.partial(bucket_body, shards, capacity),
        grid_spec=pltpu.PrefetchScalarGridSpec(
            num_scalar_prefetch=1,
            grid=(shards,),
            in_specs=[
                pl.BlockSpec((groups, LANES), lambda i, c: (0, 0)),
                pl.BlockSpec((groups, LANES), lambda i, c: (0, 0)),
                pl.BlockSpec((row_count, LANES), lambda i, c: (0, c[0])),
            ],
            out_specs=pl.BlockSpec((1, capacity + INDEX_ROWS, LANES), lambda i, c: (i, 0, 0)),
            scratch_shapes=[pltpu.VMEM((groups, LANES), i32)],
        ),
        out_shape=jax.ShapeDtypeStruct((shards, capacity + INDEX_ROWS, LANES), bf16),
        compiler_params=params(32),
        cost_estimate=cost(
            8 * shards * capacity * row_count * LANES, 3 * shards * capacity * LANES * 2
        ),
        name="bucket_rows",
    )(column, targets.reshape(groups, LANES), points.reshape(groups, LANES), grads)


def segment_body(got_ref, out_ref, total_ref):
    step = pl.program_id(0)
    capacity = got_ref.shape[1] - INDEX_ROWS
    chunks = capacity // LANES
    row_count = out_ref.shape[0]
    digits = got_ref[0, capacity:, :].astype(f32)
    index = (digits[:chunks] * float(INDEX_BASE) + digits[chunks : 2 * chunks]).astype(i32)
    row = lax.broadcasted_iota(i32, (row_count, LANES), 0)
    onehot = jnp.concatenate([ones_where(index[j : j + 1] == row) for j in range(chunks)], axis=1)
    part = dot(onehot, got_ref[0, :capacity, :])

    @pl.when(step == 0)
    def _():
        total_ref[...] = part

    @pl.when(step > 0)
    def _():
        total_ref[...] += part

    @pl.when(step == pl.num_programs(0) - 1)
    def _():
        out_ref[...] = total_ref[...].astype(bf16)


def segment_rows(got, row_count):
    shards, message, _ = got.shape
    return pl.pallas_call(
        segment_body,
        grid=(shards,),
        in_specs=[pl.BlockSpec((1, message, LANES), lambda i: (i, 0, 0))],
        out_specs=pl.BlockSpec((row_count, LANES), lambda i: (0, 0)),
        out_shape=jax.ShapeDtypeStruct((row_count, LANES), bf16),
        scratch_shapes=[pltpu.VMEM((row_count, LANES), f32)],
        compiler_params=params(32),
        cost_estimate=cost(
            8 * shards * message * row_count * LANES, 3 * shards * message * LANES * 2
        ),
        name="segment_rows",
    )(got)


def project_body(
    column_ref,
    x0_ref,
    x1_ref,
    x2_ref,
    x3_ref,
    weight_ref,
    hidden_ref,
    normed_ref,
    inv_ref,
    key_ref,
    value_ref,
    query_t_ref,
    key_t_ref,
    value_t_ref,
):
    me = column_ref[0]
    blocks = [r[...].astype(f32) for r in (x0_ref, x1_ref, x2_ref, x3_ref)]
    features = float(LANES * len(blocks))
    mean = jnp.sum(blocks[0] + blocks[1] + (blocks[2] + blocks[3]), axis=1, keepdims=True) / features
    centered = [b - mean for b in blocks]
    squares = [c * c for c in centered]
    var = jnp.sum(squares[0] + squares[1] + (squares[2] + squares[3]), axis=1, keepdims=True) / features
    inv = lax.rsqrt(var + epsilon)
    normed_ref[...] = centered[0] * inv
    inv_ref[...] = jnp.broadcast_to(inv, inv_ref.shape)
    for block, mask in zip(centered, (0, 2, 1, 3)):
        at = pl.multiple_of((me ^ mask) * LANES, LANES)
        hidden_ref[:, pl.ds(at, LANES)] = (block * inv).astype(bf16)
    projected = dot(hidden_ref[...], weight_ref[...])
    key_ref[...] = projected[:, LANES : 2 * LANES].astype(bf16)
    value_ref[...] = projected[:, 2 * LANES :].astype(bf16)
    query_t_ref[...] = (projected[:, :LANES] * score_scale).T.astype(bf16)
    key_t_ref[...] = projected[:, LANES : 2 * LANES].T.astype(bf16)
    value_t_ref[...] = projected[:, 2 * LANES :].T.astype(bf16)


def project(blocks, weight, column):
    row_count = blocks[0].shape[0]
    step_rows = 512
    features = weight.shape[0]
    width = pl.BlockSpec((step_rows, LANES), lambda i, c: (i, 0))
    tall = pl.BlockSpec((LANES, step_rows), lambda i, c: (0, i))
    normal = lambda t: jax.ShapeDtypeStruct((row_count, LANES), t)
    turned = jax.ShapeDtypeStruct((LANES, row_count), bf16)
    return pl.pallas_call(
        project_body,
        grid_spec=pltpu.PrefetchScalarGridSpec(
            num_scalar_prefetch=1,
            grid=(row_count // step_rows,),
            in_specs=[width] * 4 + [pl.BlockSpec(weight.shape, lambda i, c: (0, 0))],
            out_specs=[
                pl.BlockSpec((step_rows, features), lambda i, c: (i, 0)),
                width,
                width,
                width,
                width,
                tall,
                tall,
                tall,
            ],
        ),
        out_shape=[
            jax.ShapeDtypeStruct((row_count, features), bf16),
            normal(f32),
            normal(f32),
            normal(bf16),
            normal(bf16),
            turned,
            turned,
            turned,
        ],
        compiler_params=params(32),
        cost_estimate=cost(4 * row_count * features * 3 * LANES, row_count * LANES * 40),
        name="project",
    )(column, *blocks, weight)


def forward_body(key_ref, query_t_ref, value_t_ref, exp_ref, attended_ref, inverse_ref):
    head = pl.program_id(1)
    at = pl.multiple_of(head * HD, HD)
    in_head = lax.broadcasted_iota(i32, (LANES, 1), 0) // HD == head
    query = jnp.where(in_head, query_t_ref[...], jnp.zeros((), bf16))
    scores = dot(key_ref[...], query)
    top = jnp.max(scores, axis=0, keepdims=True)
    weights = jnp.exp2((scores - top) * log2_e).astype(bf16)
    exp_ref[0] = weights
    extended = jnp.concatenate([value_t_ref[pl.ds(at, HD), :], jnp.ones((HD, PATCH), bf16)], axis=0)
    sums = dot(extended, weights)
    inverse = 1.0 / sums[HD : HD + 1]
    inverse_ref[0] = inverse
    attended_ref[pl.ds(at, HD), :] = (sums[:HD] * inverse).astype(bf16)


def attention_forward(keys, query_t, value_t):
    row_count = keys.shape[0]
    patches, heads = row_count // PATCH, LANES // HD
    tall = pl.BlockSpec((LANES, PATCH), lambda p, h: (0, p))
    per_head = lambda p, h: (p * heads + h, 0, 0)
    elements = patches * heads * PATCH * PATCH
    return pl.pallas_call(
        forward_body,
        grid=(patches, heads),
        in_specs=[pl.BlockSpec((PATCH, LANES), lambda p, h: (p, 0)), tall, tall],
        out_specs=[
            pl.BlockSpec((1, PATCH, PATCH), per_head),
            tall,
            pl.BlockSpec((1, 1, PATCH), per_head),
        ],
        out_shape=[
            jax.ShapeDtypeStruct((patches * heads, PATCH, PATCH), bf16),
            jax.ShapeDtypeStruct((LANES, row_count), bf16),
            jax.ShapeDtypeStruct((patches * heads, 1, PATCH), f32),
        ],
        compiler_params=params(48),
        cost_estimate=cost(1024 * elements, 2 * elements, elements),
        name="attention_forward",
    )(keys, query_t, value_t)


def backward_body(
    column_ref,
    exp_ref,
    inverse_ref,
    value_ref,
    query_t_ref,
    key_t_ref,
    attended_ref,
    g0_ref,
    g1_ref,
    g2_ref,
    g3_ref,
    weight_ref,
    d_out_ref,
    d_query_ref,
    d_key_ref,
    d_value_ref,
    d_attended_ref,
    key_sum_ref,
    value_sum_ref,
):
    head = pl.program_id(1)
    at = pl.multiple_of(head * HD, HD)
    in_head = lax.broadcasted_iota(i32, (LANES, 1), 0) // HD == head

    @pl.when(head == 0)
    def _():
        me = column_ref[0]
        for block, mask in zip((g0_ref, g1_ref, g2_ref, g3_ref), (0, 2, 1, 3)):
            start = pl.multiple_of((me ^ mask) * LANES, LANES)
            d_out_ref[:, pl.ds(start, LANES)] = block[...]
        d_attended_ref[...] = dot(d_out_ref[...], weight_ref[...]).T.astype(bf16)
        key_sum_ref[...] = jnp.zeros_like(key_sum_ref)
        value_sum_ref[...] = jnp.zeros_like(value_sum_ref)

    weights = exp_ref[0]
    scaled = jnp.where(in_head, d_attended_ref[...].astype(f32) * inverse_ref[0], 0.0).astype(bf16)
    delta = jnp.sum(
        scaled.astype(f32) * attended_ref[...].astype(f32), axis=0, keepdims=True
    )
    delta_high = delta.astype(bf16)
    delta_low = (delta - delta_high.astype(f32)).astype(bf16)
    left = jnp.concatenate([value_ref[...], jnp.full((PATCH, HD), -1.0, bf16)], axis=1)
    right = jnp.concatenate(
        [scaled, delta_high, delta_low, jnp.zeros((HD - 2, PATCH), bf16)], axis=0
    )
    d_scores = (weights.astype(f32) * dot(left, right)).astype(bf16)
    d_query = dot(key_t_ref[pl.ds(at, HD), :], d_scores)
    d_query_ref[pl.ds(at, HD), :] = (d_query * score_scale).astype(bf16)
    query = jnp.where(in_head, query_t_ref[...], jnp.zeros((), bf16))
    value_sum_ref[...] += dot_rows(weights, scaled)
    key_sum_ref[...] += dot_rows(d_scores, query)

    @pl.when(head == pl.num_programs(1) - 1)
    def _():
        d_key_ref[...] = key_sum_ref[...].astype(bf16)
        d_value_ref[...] = value_sum_ref[...].astype(bf16)


def attention_backward(weights, inverse, values, query_t, key_t, attended, grads, out_weight, column):
    row_count = values.shape[0]
    features = out_weight.shape[0]
    patches, heads = row_count // PATCH, LANES // HD
    tall = pl.BlockSpec((LANES, PATCH), lambda p, h, c: (0, p))
    wide = pl.BlockSpec((PATCH, LANES), lambda p, h, c: (p, 0))
    per_head = lambda p, h, c: (p * heads + h, 0, 0)
    elements = patches * heads * PATCH * PATCH
    return pl.pallas_call(
        backward_body,
        grid_spec=pltpu.PrefetchScalarGridSpec(
            num_scalar_prefetch=1,
            grid=(patches, heads),
            in_specs=[
                pl.BlockSpec((1, PATCH, PATCH), per_head),
                pl.BlockSpec((1, 1, PATCH), per_head),
                wide,
                tall,
                tall,
                tall,
                wide,
                wide,
                wide,
                wide,
                pl.BlockSpec(out_weight.shape, lambda p, h, c: (0, 0)),
            ],
            out_specs=[
                pl.BlockSpec((PATCH, features), lambda p, h, c: (p, 0)),
                tall,
                wide,
                wide,
            ],
            scratch_shapes=[
                pltpu.VMEM((LANES, PATCH), bf16),
                pltpu.VMEM((PATCH, LANES), f32),
                pltpu.VMEM((PATCH, LANES), f32),
            ],
        ),
        out_shape=[
            jax.ShapeDtypeStruct((row_count, features), bf16),
            jax.ShapeDtypeStruct((LANES, row_count), bf16),
            jax.ShapeDtypeStruct((row_count, LANES), bf16),
            jax.ShapeDtypeStruct((row_count, LANES), bf16),
        ],
        compiler_params=params(52),
        cost_estimate=cost(2048 * elements, 2 * elements),
        name="attention_backward",
    )(column, weights, inverse, values, query_t, key_t, attended, *grads, out_weight)


def weight_grad_body(d_query_ref, d_key_ref, d_value_ref, attended_ref, hidden_ref, d_out_ref, out_ref):
    hidden = hidden_ref[...]
    out_ref[:, :LANES] = dot(d_query_ref[...], hidden).T.astype(bf16)
    out_ref[:, LANES : 2 * LANES] = dot(d_key_ref[...].T, hidden).T.astype(bf16)
    out_ref[:, 2 * LANES : 3 * LANES] = dot(d_value_ref[...].T, hidden).T.astype(bf16)
    out_ref[:, 3 * LANES :] = dot(attended_ref[...], d_out_ref[...]).T.astype(bf16)


def weight_grads(d_query_t, d_keys, d_values, attended, hidden, d_out):
    row_count, features = hidden.shape
    return pl.pallas_call(
        weight_grad_body,
        out_shape=jax.ShapeDtypeStruct((features, 4 * LANES), bf16),
        compiler_params=params(48),
        cost_estimate=cost(8 * row_count * features * LANES, 8 * row_count * features),
        name="weight_grads",
    )(d_query_t, d_keys, d_values, attended, hidden, d_out)


def partial_body(column_ref, d_query_ref, d_key_ref, d_value_ref, weight_ref, hidden_ref, mine_ref, other_ref, sums_ref):
    me = column_ref[0]
    d_projected = jnp.concatenate([d_query_ref[...].T, d_key_ref[...], d_value_ref[...]], axis=1)
    part = dot_rows(d_projected, weight_ref[...]).astype(bf16)
    crossed = part.astype(f32) * hidden_ref[...].astype(f32)
    high = crossed.astype(bf16)
    low = (crossed - high.astype(f32)).astype(bf16)
    ones = jnp.ones((8, part.shape[1]), bf16)
    sums_ref[0:1, :] = dot_rows(ones, part)[0:1]
    sums_ref[1:2, :] = (dot_rows(ones, high) + dot_rows(ones, low))[0:1]
    odd = me % 2
    for j in range(4):
        block = part[:, j * LANES : (j + 1) * LANES]

        @pl.when(odd == j % 2)
        def _():
            mine_ref[:, (j // 2) * LANES : (j // 2 + 1) * LANES] = block

        @pl.when(odd != j % 2)
        def _():
            other_ref[:, (j // 2) * LANES : (j // 2 + 1) * LANES] = block


def hidden_part(d_query_t, d_keys, d_values, weight, hidden, column):
    row_count, features = hidden.shape
    step_rows = 512
    wide = pl.BlockSpec((step_rows, LANES), lambda i, c: (i, 0))
    half = pl.BlockSpec((step_rows, 2 * LANES), lambda i, c: (i, 0))
    halves = jax.ShapeDtypeStruct((row_count, 2 * LANES), bf16)
    return pl.pallas_call(
        partial_body,
        grid_spec=pltpu.PrefetchScalarGridSpec(
            num_scalar_prefetch=1,
            grid=(row_count // step_rows,),
            in_specs=[
                pl.BlockSpec((LANES, step_rows), lambda i, c: (0, i)),
                wide,
                wide,
                pl.BlockSpec(weight.shape, lambda i, c: (0, 0)),
                pl.BlockSpec((step_rows, features), lambda i, c: (i, 0)),
            ],
            out_specs=[half, half, pl.BlockSpec((2, step_rows), lambda i, c: (0, i))],
        ),
        out_shape=[halves, halves, jax.ShapeDtypeStruct((2, row_count), f32)],
        compiler_params=params(32),
        cost_estimate=cost(8 * row_count * features * LANES, 8 * row_count * features),
        name="hidden_part",
    )(column, d_query_t, d_keys, d_values, weight, hidden)


def local(
    scan_points,
    send_order,
    arrive_order,
    qkv_weight,
    out_weight,
    voxel_grads,
    voxel_shard,
    voxel_point,
):
    shards = lax.axis_size("seq")
    members = lax.axis_size("mp")
    local_rows, features = scan_points.shape
    voxels = voxel_grads.shape[0]
    capacity = 2 * voxels // shards
    me = lax.axis_index("mp")
    column = me.astype(i32).reshape(1)
    zero = jnp.zeros((1,), i32)
    weight = qkv_weight.reshape(features, 3 * LANES)

    def swap(rows, mask):
        return lax.ppermute(rows, "mp", [(i, i ^ mask) for i in range(members)])

    def exchange(rows):
        return lax.all_to_all(rows, "seq", split_axis=0, concat_axis=0, tiled=True)

    def all_columns(rows):
        across = swap(rows, 2)
        return (rows, across, swap(rows, 1), swap(across, 1))

    arrived = exchange(permute_rows(scan_points, send_order, column))
    buckets = bucket_rows(voxel_grads, voxel_shard, voxel_point, column, shards, capacity)
    got = exchange(buckets.reshape(shards * (capacity + INDEX_ROWS), LANES))
    got = got.reshape(shards, capacity + INDEX_ROWS, LANES)
    points = all_columns(permute_rows(arrived, arrive_order, zero))
    hidden, normed, inv_scale, keys, values, query_t, key_t, value_t = project(points, weight, column)
    weights, attended, inverse = attention_forward(keys, query_t, value_t)
    grads = all_columns(segment_rows(got, local_rows))
    d_out, d_query_t, d_keys, d_values = attention_backward(
        weights, inverse, values, query_t, key_t, attended, grads, out_weight, column
    )
    mine, other, sums = hidden_part(d_query_t, d_keys, d_values, weight, hidden, column)
    weight_parts = weight_grads(d_query_t, d_keys, d_values, attended, hidden, d_out)
    summed = jnp.sum(
        exchange(weight_parts).reshape(shards, features // shards, 4 * LANES).astype(f32), axis=0
    )
    grad_qkv = summed[:, : 3 * LANES].reshape(features // shards, 3, LANES)
    grad_out = summed[:, 3 * LANES :]

    pair = mine.astype(f32) + swap(other, 1).astype(f32)
    sums = sums + swap(sums, 1)
    top = me // 2 == 1
    low_half, high_half = pair[:, :LANES], pair[:, LANES:]
    kept = jnp.where(top, high_half, low_half)
    sent = jnp.where(top, low_half, high_half).astype(bf16)
    d_hidden = kept + swap(sent, 2).astype(f32)
    sums = (sums + swap(sums, 2)) / float(features)
    d_points = grads[0].astype(f32) + inv_scale * (
        d_hidden - sums[0][:, None] - normed * sums[1][:, None]
    )
    return (d_points, grad_qkv, grad_out)


def solution(mesh):
    in_specs = (
        P("seq", None),
        P("seq"),
        P("seq"),
        P(None, None, "mp"),
        P(None, "mp"),
        P("seq", None),
        P("seq", None),
        P("seq"),
    )
    out_specs = (P("seq", "mp"), P("seq", None, "mp"), P("seq", "mp"))
    return jax.shard_map(local, mesh=mesh, in_specs=in_specs, out_specs=out_specs, check_vma=False)
```

time: 484 us -> 197 us (0.41)
  matrix products: 132 us -> 0 us
  waiting for transfers between devices: 163 us -> 36.4 us
  Pallas kernels: 0 us -> 111 us
  other arithmetic: 89.1 us -> 5.59 us
  local copies, waits for them, and re-layouts: 64.1 us -> 20.9 us
  between operations: 15.8 us -> 0.85 us
    pallas_call x0 -> x9, Pallas kernels: none -> 111 us  [the longest x1 40.2 us: attention_backward(): pl.pallas_call(backward_body, grid_spec=pltpu.PrefetchScalarGridSpec(num_...]
    dot_general x15 -> x0, matrix products: 103 us -> none  [the longest x2 26 us: patch_pass(): jnp.einsum('qhc,khc->hqk', grad_heads, value_heads, preferred_element_typ...]
    all_to_all x3, waiting for transfers between devices: 109 us -> 21.2 us  [exchange(): return lax.all_to_all(rows, 'seq', split_axis=0, concat_axis=0, tiled=True)]
    reduce_scatter x1 -> x0, waiting for transfers between devices: 53.3 us -> none  [local(): lax.psum_scatter(jnp.concatenate([upper, lower[:, None, :]], axis=1).asty...]
    convert_element_type x5 -> x1, other arithmetic: 37.9 us -> 0.9 us  [local(): sent = jnp.where(top, low_half, high_half).astype(bf16)]
    scatter-add x1 -> x0, other arithmetic: 30.1 us -> none  [local(): jax.ops.segment_sum(got_rows.astype(jnp.float32), got_index, num_segments...]
    sub x2 -> x0, matrix products: 29.1 us -> none  [patch_pass(): weights_exp = jnp.exp(scores - row_max)]
    scatter x2 -> x0, local copies, waits for them, and re-layouts: 21.4 us -> none  [the longest x1 12.6 us: local(): jnp.zeros((shards * capacity, feature_count), jnp.bfloat16).at[places]]
  transfers between devices with their start and end apart: 5 -> 13, of which waited for: 3 -> 6; matrix products, arithmetic and copies ran while one was open for 11% -> 2% of each run, Pallas kernels for 0% -> 31%
where the time goes in v1:
time: 197 us; the launch traced here: 196 us
  Pallas kernels  111 us (56%)
  waiting for transfers between devices  36.4 us (18%)
  starting transfers between devices  21.3 us (11%)
  local copies, waits for them, and re-layouts  20.9 us (11%)
  other arithmetic  5.59 us (3%)
    pallas_call x1, Pallas kernels, attention_backward(): pl.pallas_call(backward_body, grid_spec=pltpu.PrefetchScalarGridSpec(num_...  40.2 us
    pallas_call x1, Pallas kernels, attention_forward(): pl.pallas_call(forward_body, grid=(patches, heads), in_specs=[pl.BlockSpe...  32.4 us
    all_to_all x3, waiting for transfers between devices, exchange(): return lax.all_to_all(rows, 'seq', split_axis=0, concat_axis=0, tiled=True)  21.2 us
    unnamed x62, local copies, waits for them, and re-layouts  20 us
    all_to_all x3, starting transfers between devices, exchange(): return lax.all_to_all(rows, 'seq', split_axis=0, concat_axis=0, tiled=True)  15.5 us
    ppermute x10, waiting for transfers between devices, swap(): return lax.ppermute(rows, 'mp', [(i, i ^ mask) for i in range(members)])  15.2 us
    pallas_call x1, Pallas kernels, bucket_rows(): pl.pallas_call(functools.partial(bucket_body, shards, capacity), grid_spe...  11 us
    pallas_call x1, Pallas kernels, segment_rows(): pl.pallas_call(segment_body, grid=(shards,), in_specs=[pl.BlockSpec((1, m...  7.35 us
  transfers between devices with their start and end apart: 13, of which 6 were waited for; matrix products, arithmetic and copies ran while one was open for 2% of the time, Pallas kernels for 31%

profile of v1, /device:TPU:0, one launch (start us, length us, event | category | flops | bytes accessed | tf_op | source)
XLA Modules:
  0.0 195.9 jit_solution(13693181867527016403)
XLA Ops:
  0.6 1.6 copy-done.10
  2.2 0.7 copy-done.19
  2.9 4.1 %permute_rows.2 = bf16[2048,128]{1,0:T(8,128)(2,1)} custom-call(s32[1]{0:T(128)} %bitcast.column_ref, s32[16,128]{1,0:T(8,128)S(1)} %bitcast.18, bf16[2048,512]{1,0:T(8,128)(2,1)S(1)} %copy-done.10), custom_call_target="tpu_custom_call" | custom-call | flops 4294967296 | bytes 1572864 | tf_op jit(solution)/shard_map/permute_rows/pallas_call | solution.py:67
  7.0 7.3 %all-to-all-start.1 = ((bf16[8,256,128]{2,1,0:T(8,128)(2,1)}), bf16[8,256,128]{2,1,0:T(8,128)(2,1)S(1)}, u32[]{:S(2)}, u32[]{:S(2)}) async-start(bf16[8,256,128]{2,1,0:T(8,128)(2,1)} %bitcast.5), calls=%async_computation.1 | async-start | bytes 1048576 | tf_op jit(solution)/shard_map/all_to_all | solution.py:517
  14.3 0.0 copy-start.11
  14.3 1.6 copy-done.11
  15.9 11.0 %bucket_rows.1 = bf16[8,528,128]{2,1,0:T(8,128)(2,1)} custom-call(s32[1]{0:T(128)} %bitcast.column_ref, s32[16,128]{1,0:T(8,128)S(1)} %bitcast.19, s32[16,128]{1,0:T(8,128)S(1)} %bitcast.20, bf16[2048,512]{1,0:T(8,128)(2,1)S(1)} %copy-done.11), custom_call_target="tpu_custom_call" | custom-call | flops 8589934592 | bytes 3145728 | tf_op jit(solution)/shard_map/bucket_rows/pallas_call | solution.py:132
  26.9 1.8 all-to-all-done.1
  28.7 4.3 %all-to-all-start = ((bf16[8,528,128]{2,1,0:T(8,128)(2,1)}), bf16[8,528,128]{2,1,0:T(8,128)(2,1)S(1)}, u32[]{:S(2)}, u32[]{:S(2)}) async-start(bf16[8,528,128]{2,1,0:T(8,128)(2,1)} %bucket_rows.1), calls=%async_computation | async-start | bytes 2162688 | tf_op jit(solution)/shard_map/all_to_all | solution.py:517
  33.0 3.3 %permute_rows.3.x0_ref = bf16[2048,128]{1,0:T(8,128)(2,1)S(1)} custom-call(s32[1]{0:T(128)} %constant.20.clone.1.column_ref, s32[16,128]{1,0:T(8,128)S(1)} %bitcast.21, bf16[2048,128]{1,0:T(8,128)(2,1)S(1)} %bitcast.17), custom_call_target="tpu_custom_call" | custom-call | flops 4294967296 | bytes 1572864 | tf_op jit(solution)/shard_map/permute_rows/pallas_call | solution.py:67
  36.3 0.0 copy-start.12
  36.3 0.0 copy-start.27
  36.3 1.6 collective-permute-start
  37.9 0.0 collective-permute-start.1
  37.9 11.4 %collective-permute-done.x1_ref = bf16[2048,128]{1,0:T(8,128)(2,1)S(1)} collective-permute-done((bf16[2048,128]{1,0:T(8,128)(2,1)S(1)}, bf16[2048,128]{1,0:T(8,128)(2,1)S(1)}, u32[]{:S(2)}, u32[]{:S(2)}) %collective-permute-start) | collective-permute-done | bytes 524320 | tf_op jit(solution)/shard_map/ppermute | solution.py:514
  49.3 0.0 collective-permute-start.2
  49.3 9.9 %all-to-all-done.got_ref = bf16[8,528,128]{2,1,0:T(8,128)(2,1)S(1)} async-done(((bf16[8,528,128]{2,1,0:T(8,128)(2,1)}), bf16[8,528,128]{2,1,0:T(8,128)(2,1)S(1)}, u32[]{:S(2)}, u32[]{:S(2)}) %all-to-all-start) | async-done | bytes 1081376 | tf_op jit(solution)/shard_map/all_to_all | solution.py:517
  59.2 7.4 %segment_rows.1.g0_ref = bf16[2048,128]{1,0:T(8,128)(2,1)} custom-call(bf16[8,528,128]{2,1,0:T(8,128)(2,1)S(1)} %all-to-all-done.got_ref), custom_call_target="tpu_custom_call" | custom-call | flops 8858370048 | bytes 3244032 | tf_op jit(solution)/shard_map/segment_rows/pallas_call | solution.py:180
  66.6 1.5 collective-permute-start.3
  68.1 0.2 copy.12
  68.3 0.2 copy.13.weight_ref
  68.5 0.1 collective-permute-start.4
  68.6 0.0 collective-permute-done.1.x2_ref
  68.6 0.8 copy-done.16
  69.4 0.0 collective-permute-done.2.x3_ref
  69.4 1.0 copy-done.13
  70.5 1.0 copy-done.15
  71.5 1.0 copy-done.17
  72.5 4.8 %project.1 = (bf16[2048,512]{1,0:T(8,128)(2,1)S(1)}, f32[2048,128]{1,0:T(8,128)S(1)}, f32[2048,128]{1,0:T(8,128)S(1)}, bf16[2048,128]{1,0:T(8,128)(2,1)S(1)}, bf...) custom-call(s32[1]{0:T(128)} %bitcast.column_ref, ...), custom_call_target="tpu_custom_call" | custom-call | flops 1610612736 | bytes 10485760 | tf_op jit(solution)/shard_map/project/pallas_call | solution.py:240
  77.4 1.0 copy-done.3
  78.3 1.0 copy-done.5
  79.3 0.8 copy-done.23
  80.1 0.9 copy-done.25
  81.0 0.0 collective-permute-done.3.g1_ref
  81.0 0.5 collective-permute-start.5
  81.5 32.4 %attention_forward.1 = (bf16[16,1024,1024]{2,1,0:T(8,128)(2,1)}, bf16[128,2048]{1,0:T(8,128)(2,1)S(1)}, f32[16,1,1024]{2,1,0:T(1,128)S(1)}) custom-call(bf16[2048,128]{1,0:T(8,128)(2,1)S(1)} %get-tuple-element.22.key_ref, bf16[128,2048]{1,0:T(8,128)(2,1)S(1)} %get-tuple-element.23.query_t_ref, bf16[128,2048]{1,0:T(8,128)(2,1)S(1)} %get-tuple-element.24.value_t_ref), custom_call_target="tpu_custom_call" | custom-call | flops 17179869184 | bytes 33554432 | tf_op jit(solution)/shard_map/attention_forward/pallas_call | solution.py:295
  113.8 0.8 copy-done.8
  114.6 0.0 collective-permute-done.4.g2_ref
  114.6 0.8 copy-done.28
  115.4 0.2 copy-done.29
  115.6 40.2 %attention_backward.1 = (bf16[2048,512]{1,0:T(8,128)(2,1)}, bf16[128,2048]{1,0:T(8,128)(2,1)S(1)}, bf16[2048,128]{1,0:T(8,128)(2,1)S(1)}, bf16[2048,128]{1,0:T(8,128)(2,1)S(1)}) custom-call(s32[1]{0:T(128)} %bitcast.column_ref, bf16[16,1024,1024]{2,1,0:T(8,128)(2,1)} %get-tuple-element.25.exp_ref, f32[16,1,1024]{2,1,0:T(1,128)S(1)} %get-tuple-element.26.inverse_ref, ...), custom_call_target="tpu_custom_call" | custom-call | flops 34359738368 | bytes 33554432 | tf_op jit(solution)/shard_map/attention_backward/pallas_call | solution.py:382
  155.8 4.9 %hidden_part.1 = (bf16[2048,256]{1,0:T(8,128)(2,1)S(1)}, bf16[2048,256]{1,0:T(8,128)(2,1)}, f32[2,2048]{1,0:T(2,128)S(1)}) custom-call(s32[1]{0:T(128)} %bitcast.column_ref, bf16[128,2048]{1,0:T(8,128)(2,1)S(1)} %get-tuple-element.30.d_query_ref, bf16[2048,128]{1,0:T(8,128)(2,1)S(1)} %get-tuple-element.31.d_key_ref, ...), custom_call_target="tpu_custom_call" | custom-call | flops 1073741824 | bytes 8388608 | tf_op jit(solution)/shard_map/hidden_part/pallas_call | solution.py:472
  160.7 0.8 copy-done
  161.5 1.0 copy-done.7
  162.5 0.1 collective-permute-start.6
  162.6 0.4 collective-permute-start.8
  163.0 1.9 collective-permute-done.8
  164.9 0.6 collective-permute-start.9
  165.5 1.0 copy-done.1
  166.6 1.0 copy-done.9
  167.6 2.9 %weight_grads.1 = bf16[512,512]{1,0:T(8,128)(2,1)S(1)} custom-call(bf16[128,2048]{1,0:T(8,128)(2,1)S(1)} %get-tuple-element.30.d_query_ref, bf16[2048,128]{1,0:T(8,128)(2,1)S(1)} %get-tuple-element.31.d_key_ref, bf16[2048,128]{1,0:T(8,128)(2,1)S(1)} %copy-done.1, bf16[128,2048]{1,0:T(8,128)(2,1)S(1)} %copy-done.9, ...), custom_call_target="tpu_custom_call" | custom-call | flops 1073741824 | bytes 8388608 | tf_op jit(solution)/shard_map/weight_grads/pallas_call | solution.py:434
  170.6 0.8 copy-done.2
  171.4 4.0 %all-to-all-start.2 = ((bf16[8,64,512]{2,1,0:T(8,128)(2,1)}), bf16[8,64,512]{2,1,0:T(8,128)(2,1)S(1)}, u32[]{:S(2)}, u32[]{:S(2)}) async-start(bf16[8,64,512]{2,1,0:T(8,128)(2,1)} %bitcast.16), calls=%async_computation.2 | async-start | bytes 1048576 | tf_op jit(solution)/shard_map/all_to_all | solution.py:517
  175.4 0.0 collective-permute-done.9
  175.4 1.8 convert_add_fusion
  177.2 1.3 copy-done.26
  178.5 0.9 select_convert_fusion
  179.4 1.0 collective-permute-start.7
  180.4 9.4 %all-to-all-done.2 = bf16[8,64,512]{2,1,0:T(8,128)(2,1)S(1)} async-done(((bf16[8,64,512]{2,1,0:T(8,128)(2,1)}), bf16[8,64,512]{2,1,0:T(8,128)(2,1)S(1)}, u32[]{:S(2)}, u32[]{:S(2)}) %all-to-all-start.2) | async-done | bytes 524320 | tf_op jit(solution)/shard_map/all_to_all | solution.py:517
  189.9 0.1 convert_reduce_fusion
  189.9 0.6 slice.29
  190.6 0.6 copy_bitcast_fusion
  191.2 1.8 collective-permute-done.7
  193.0 2.8 %multiply_add_fusion = f32[2048,128]{1,0:T(8,128)} fusion(f32[2048,128]{1,0:T(8,128)S(1)} %copy-done.6, f32[2048,128]{1,0:T(8,128)S(1)} %copy-done.4, bf16[2048,128]{1,0:T(8,128)(2,1)S(1)} %collective-permute-done.7, bf16[2048,128]{1,0:T(8,128)(2,1)} %segment_rows.1.g0_ref, f32[2048,256]{1,0:T(8,128)} %copy-done.26, f32[2048]{0:T(1024)S(1)} %bitcast.24, ...), kind=kLoop, calls=%fused_computation.2 | loop fusion | flops 2359296 | bytes 6307841 | tf_op jit(solution)/shard_map/add | solution.py:550
  (42 shorter events, 0.1 us)
Async XLA Ops:
  0.6 1.6 copy-start.10
  2.2 0.7 copy-start.19
  2.9 11.3 %copy-start.20 = (s32[2048,1]{0,1:T(1,128)S(1)}, s32[2048,1]{0,1:T(1,128)}, u32[]{:S(2)}) copy-start(s32[2048,1]{0,1:T(1,128)} %param.14) | copy-start | bytes 24580
  2.9 11.3 %copy-start.21 = (s32[2048]{0:T(1024)S(1)}, s32[2048]{0:T(1024)}, u32[]{:S(2)}) copy-start(s32[2048]{0:T(1024)} %param.15) | copy-start | bytes 24580
  7.0 21.7 %all-to-all-start.1 = ((bf16[8,256,128]{2,1,0:T(8,128)(2,1)}), bf16[8,256,128]{2,1,0:T(8,128)(2,1)S(1)}, u32[]{:S(2)}, u32[]{:S(2)}) async-start(bf16[8,256,128]{2,1,0:T(8,128)(2,1)} %bitcast.5), calls=%async_computation.1 | async-start | bytes 1048576 | tf_op jit(solution)/shard_map/all_to_all | solution.py:517
  14.3 1.6 copy-start.11
  26.9 6.1 %copy-start.22 = (s32[2048]{0:T(1024)S(1)}, s32[2048]{0:T(1024)}, u32[]{:S(2)}) copy-start(s32[2048]{0:T(1024)} %param.10) | copy-start | bytes 24580
  28.7 30.5 %all-to-all-start = ((bf16[8,528,128]{2,1,0:T(8,128)(2,1)}), bf16[8,528,128]{2,1,0:T(8,128)(2,1)S(1)}, u32[]{:S(2)}, u32[]{:S(2)}) async-start(bf16[8,528,128]{2,1,0:T(8,128)(2,1)} %bucket_rows.1), calls=%async_computation | async-start | bytes 2162688 | tf_op jit(solution)/shard_map/all_to_all | solution.py:517
  36.3 30.3 %copy-start.12 = (bf16[2048,128]{1,0:T(8,128)(2,1)}, bf16[2048,128]{1,0:T(8,128)(2,1)S(1)}, u32[]{:S(2)}) copy-start(bf16[2048,128]{1,0:T(8,128)(2,1)S(1)} %permute_rows.3.x0_ref) | copy-start | bytes 1572868
  36.3 31.8 %copy-start.27 = (bf16[512,3,128]{2,0,1:T(8,128)(2,1)S(1)}, bf16[512,3,128]{2,0,1:T(8,128)(2,1)}, u32[]{:S(2)}) copy-start(bf16[512,3,128]{2,0,1:T(8,128)(2,1)} %param.11) | copy-start | bytes 1179652
  36.3 13.0 %collective-permute-start = (bf16[2048,128]{1,0:T(8,128)(2,1)S(1)}, bf16[2048,128]{1,0:T(8,128)(2,1)S(1)}, u32[]{:S(2)}, u32[]{:S(2)}) collective-permute-start(bf16[2048,128]{1,0:T(8,128)(2,1)S(1)} %permute_rows.3.x0_ref), channel_id=1, source_target_pairs={{0,2},{1,3},{2,0},{3,1},{4,6},{5,7},{6,4},{7,5},{8,10},{9,11},{10,... | collective-permute-start | bytes 1572872 | tf_op jit(solution)/shard_map/ppermute | solution.py:514
  37.9 30.7 %collective-permute-start.1 = (bf16[2048,128]{1,0:T(8,128)(2,1)S(1)}, bf16[2048,128]{1,0:T(8,128)(2,1)S(1)}, u32[]{:S(2)}, u32[]{:S(2)}) collective-permute-start(bf16[2048,128]{1,0:T(8,128)(2,1)S(1)} %permute_rows.3.x0_ref), channel_id=1, source_target_pairs={{0,1},{1,0},{2,3},{3,2},{4,5},{5,4},{6,7},{7,6},{8,9},{9,8},{10,11... | collective-permute-start | bytes 1572872 | tf_op jit(solution)/shard_map/ppermute | solution.py:514
  49.3 17.3 %copy-start.14 = (bf16[2048,128]{1,0:T(8,128)(2,1)}, bf16[2048,128]{1,0:T(8,128)(2,1)S(1)}, u32[]{:S(2)}) copy-start(bf16[2048,128]{1,0:T(8,128)(2,1)S(1)} %collective-permute-done.x1_ref) | copy-start | bytes 1572868
  49.3 20.1 %collective-permute-start.2 = (bf16[2048,128]{1,0:T(8,128)(2,1)S(1)}, bf16[2048,128]{1,0:T(8,128)(2,1)}, u32[]{:S(2)}, u32[]{:S(2)}) collective-permute-start(bf16[2048,128]{1,0:T(8,128)(2,1)S(1)} %collective-permute-done.x1_ref), channel_id=1, source_target_pairs={{0,1},{1,0},{2,3},{3,2},{4,5},{5,4},{6,7},{7,6},{8,9},{9,8},{10,11... | collective-permute-start | bytes 1572872 | tf_op jit(solution)/shard_map/ppermute | solution.py:514
  66.6 14.4 %collective-permute-start.3 = (bf16[2048,128]{1,0:T(8,128)(2,1)}, bf16[2048,128]{1,0:T(8,128)(2,1)}, u32[]{:S(2)}, u32[]{:S(2)}) collective-permute-start(bf16[2048,128]{1,0:T(8,128)(2,1)} %segment_rows.1.g0_ref), channel_id=1, source_target_pairs={{0,2},{1,3},{2,0},{3,1},{4,6},{5,7},{6,4},{7,5},{8,10},{9,11},{10,... | collective-permute-start | bytes 1572872 | tf_op jit(solution)/shard_map/ppermute | solution.py:514
  68.5 46.1 %collective-permute-start.4 = (bf16[2048,128]{1,0:T(8,128)(2,1)}, bf16[2048,128]{1,0:T(8,128)(2,1)S(1)}, u32[]{:S(2)}, u32[]{:S(2)}) collective-permute-start(bf16[2048,128]{1,0:T(8,128)(2,1)} %segment_rows.1.g0_ref), channel_id=1, source_target_pairs={{0,1},{1,0},{2,3},{3,2},{4,5},{5,4},{6,7},{7,6},{8,9},{9,8},{10,11... | collective-permute-start | bytes 1572872 | tf_op jit(solution)/shard_map/ppermute | solution.py:514
  68.6 0.8 copy-start.16
  69.4 1.0 copy-start.13
  70.5 1.0 copy-start.15
  71.5 1.0 copy-start.17
  77.3 1.0 copy-start.3
  78.3 1.0 copy-start.5
  79.3 0.8 copy-start.23
  80.1 0.9 copy-start.25
  81.0 32.9 %copy-start.24 = (bf16[128,2048]{1,0:T(8,128)(2,1)}, bf16[128,2048]{1,0:T(8,128)(2,1)S(1)}, u32[]{:S(2)}) copy-start(bf16[128,2048]{1,0:T(8,128)(2,1)S(1)} %get-tuple-element.23.query_t_ref) | copy-start | bytes 1572868
  81.0 33.7 %collective-permute-start.5 = (bf16[2048,128]{1,0:T(8,128)(2,1)}, bf16[2048,128]{1,0:T(8,128)(2,1)S(1)}, u32[]{:S(2)}, u32[]{:S(2)}) collective-permute-start(bf16[2048,128]{1,0:T(8,128)(2,1)} %collective-permute-done.3.g1_ref), channel_id=1, source_target_pairs={{0,1},{1,0},{2,3},{3,2},{4,5},{5,4},{6,7},{7,6},{8,9},{9,8},{10,11... | collective-permute-start | bytes 1572872 | tf_op jit(solution)/shard_map/ppermute | solution.py:514
  81.4 34.1 %copy-start.18 = (bf16[512,128]{1,0:T(8,128)(2,1)S(1)}, bf16[512,128]{1,0:T(8,128)(2,1)}, u32[]{:S(2)}) copy-start(bf16[512,128]{1,0:T(8,128)(2,1)} %weight_ref.1) | copy-start | bytes 393220
  113.8 0.8 copy-start.8
  114.6 0.8 copy-start.28
  114.6 1.0 copy-start.29
  160.7 0.8 copy-start
  161.5 1.0 copy-start.7
  162.5 12.9 %collective-permute-start.6 = (bf16[2048,256]{1,0:T(8,128)(2,1)}, bf16[2048,256]{1,0:T(8,128)(2,1)}, u32[]{:S(2)}, u32[]{:S(2)}) collective-permute-start(bf16[2048,256]{1,0:T(8,128)(2,1)} %get-tuple-element.35), channel_id=1, source_target_pairs={{0,1},{1,0},{2,3},{3,2},{4,5},{5,4},{6,7},{7,6},{8,9},{9,8},{10,11... | collective-permute-start | bytes 3145736 | tf_op jit(solution)/shard_map/ppermute | solution.py:514
  162.6 2.3 %collective-permute-start.8 = (f32[2,2048]{1,0:T(2,128)S(1)}, f32[2,2048]{1,0:T(2,128)S(1)}, u32[]{:S(2)}, u32[]{:S(2)}) collective-permute-start(f32[2,2048]{1,0:T(2,128)S(1)} %get-tuple-element.36), channel_id=1, source_target_pairs={{0,1},{1,0},{2,3},{3,2},{4,5},{5,4},{6,7},{7,6},{8,9},{9,8},{10,11... | collective-permute-start | bytes 49160 | tf_op jit(solution)/shard_map/ppermute | solution.py:514
  164.9 10.5 %collective-permute-start.9 = (f32[2,2048]{1,0:T(2,128)S(1)}, f32[2,2048]{1,0:T(2,128)S(1)}, u32[]{:S(2)}, u32[]{:S(2)}) collective-permute-start(f32[2,2048]{1,0:T(2,128)S(1)} %add.18), channel_id=1, source_target_pairs={{0,2},{1,3},{2,0},{3,1},{4,6},{5,7},{6,4},{7,5},{8,10},{9,11},{10,... | collective-permute-start | bytes 49160 | tf_op jit(solution)/shard_map/ppermute | solution.py:514
  165.5 1.0 copy-start.1
  166.6 1.0 copy-start.9
  170.6 0.8 copy-start.2
  171.4 18.5 %all-to-all-start.2 = ((bf16[8,64,512]{2,1,0:T(8,128)(2,1)}), bf16[8,64,512]{2,1,0:T(8,128)(2,1)S(1)}, u32[]{:S(2)}, u32[]{:S(2)}) async-start(bf16[8,64,512]{2,1,0:T(8,128)(2,1)} %bitcast.16), calls=%async_computation.2 | async-start | bytes 1048576 | tf_op jit(solution)/shard_map/all_to_all | solution.py:517
  177.2 1.3 copy-start.26
  178.5 14.5 %copy-start.4 = (f32[2048,128]{1,0:T(8,128)S(1)}, f32[2048,128]{1,0:T(8,128)}, u32[]{:S(2)}) copy-start(f32[2048,128]{1,0:T(8,128)} %copy-done.3) | copy-start | bytes 3145732
  178.5 14.5 %copy-start.6 = (f32[2048,128]{1,0:T(8,128)S(1)}, f32[2048,128]{1,0:T(8,128)}, u32[]{:S(2)}) copy-start(f32[2048,128]{1,0:T(8,128)} %copy-done.5) | copy-start | bytes 3145732
  179.4 13.6 %collective-permute-start.7 = (bf16[2048,128]{1,0:T(8,128)(2,1)}, bf16[2048,128]{1,0:T(8,128)(2,1)S(1)}, u32[]{:S(2)}, u32[]{:S(2)}) collective-permute-start(bf16[2048,128]{1,0:T(8,128)(2,1)} %select_convert_fusion), channel_id=1, source_target_pairs={{0,2},{1,3},{2,0},{3,1},{4,6},{5,7},{6,4},{7,5},{8,10},{9,11},{10,... | collective-permute-start | bytes 1572872 | tf_op jit(solution)/shard_map/ppermute | solution.py:514

commit v2 on v1

v2 whole, which is shorter than its diff:
```python
import functools

import jax
import jax.numpy as jnp
from jax import lax
from jax.experimental import pallas as pl
from jax.experimental.pallas import tpu as pltpu
from jax.sharding import PartitionSpec as P

HD = 16
PATCH = 1024
LANES = 128
INDEX_ROWS = 16
INDEX_BASE = 64
BLOCK_MASKS = (0, 2, 1, 3)
SAFE_SCORE = 60.0

score_scale = 0.25
epsilon = 1e-05
log2_e = 1.4426950408889634

f32 = jnp.float32
bf16 = jnp.bfloat16
i32 = jnp.int32

ROWS_BY_ROWS = (((1,), (1,)), ((), ()))


def params(mib):
    return pltpu.CompilerParams(vmem_limit_bytes=mib << 20)


def cost(flops, bytes_accessed, transcendentals=0):
    return pl.CostEstimate(
        flops=int(flops), bytes_accessed=int(bytes_accessed), transcendentals=int(transcendentals)
    )


def dot(a, b):
    return jnp.dot(a, b, preferred_element_type=f32)


def dot_rows(a, b):
    return lax.dot_general(a, b, ROWS_BY_ROWS, preferred_element_type=f32)


def ones_where(mask):
    return jnp.where(mask, 1.0, 0.0).astype(bf16)


def permute_body(column_ref, order_ref, block_ref, out_ref):
    step = pl.program_id(0)
    source_rows = block_ref.shape[0]
    chunks = out_ref.shape[0] // LANES
    lane = lax.broadcasted_iota(i32, (LANES, LANES), 1)
    block = block_ref[...]
    for j in range(chunks):
        wanted = order_ref[pl.ds(step * chunks + j, 1), :].astype(f32)
        wanted = jnp.broadcast_to(wanted, (LANES, LANES)).T.astype(i32)
        onehot = jnp.concatenate(
            [ones_where(wanted == lane + k * LANES) for k in range(source_rows // LANES)], axis=1
        )
        out_ref[j * LANES : (j + 1) * LANES, :] = dot(onehot, block).astype(bf16)


def permute_rows(rows, order, column):
    row_count = order.shape[0]
    step_rows = min(512, row_count)
    return pl.pallas_call(
        permute_body,
        grid_spec=pltpu.PrefetchScalarGridSpec(
            num_scalar_prefetch=1,
            grid=(row_count // step_rows,),
            in_specs=[
                pl.BlockSpec((row_count // LANES, LANES), lambda i, c: (0, 0)),
                pl.BlockSpec((rows.shape[0], LANES), lambda i, c: (0, c[0])),
            ],
            out_specs=pl.BlockSpec((step_rows, LANES), lambda i, c: (i, 0)),
        ),
        out_shape=jax.ShapeDtypeStruct((row_count, LANES), bf16),
        compiler_params=params(32),
        cost_estimate=cost(2 * row_count * row_count * LANES * 4, 3 * row_count * LANES * 2),
        name="permute_rows",
    )(column, order.reshape(row_count // LANES, LANES), rows)


def bucket_body(shards, capacity, column_ref, shard_ref, point_ref, grads_ref, out_ref, place_ref):
    step = pl.program_id(0)
    row_count = grads_ref.shape[0]
    groups = row_count // LANES

    @pl.when(step == 0)
    def _():
        targets = shard_ref[...]
        masks = [ones_where(targets == t) for t in range(shards)]
        stacked = jnp.concatenate(masks, axis=0)
        above = ones_where(
            lax.broadcasted_iota(i32, (LANES, LANES), 0)
            < lax.broadcasted_iota(i32, (LANES, LANES), 1)
        )
        earlier = ones_where(
            lax.broadcasted_iota(i32, (groups, groups), 1)
            < lax.broadcasted_iota(i32, (groups, groups), 0)
        )
        in_row = dot(stacked, above)
        places = jnp.zeros((groups, LANES), f32)
        for t in range(shards):
            rows_before = jnp.sum(dot(earlier, masks[t]), axis=1, keepdims=True)
            place = in_row[t * groups : (t + 1) * groups] + rows_before + float(t * capacity)
            places = jnp.where(targets == t, place, places)
        place_ref[...] = places.astype(i32)

    slot = lax.broadcasted_iota(i32, (capacity, LANES), 0) + step * capacity
    onehot = jnp.concatenate(
        [ones_where(place_ref[j : j + 1, :] == slot) for j in range(groups)], axis=1
    )
    out_ref[0, :capacity, :] = dot(onehot, grads_ref[...]).astype(bf16)
    points = jnp.concatenate([point_ref[j : j + 1, :] for j in range(groups)], axis=1)
    high = points // INDEX_BASE
    low = points - high * INDEX_BASE
    digits = jnp.concatenate(
        [high.astype(f32), low.astype(f32), jnp.zeros((INDEX_ROWS - 2, row_count), f32)], axis=0
    )
    sent = dot_rows(digits.astype(bf16), onehot)
    chunks = capacity // LANES
    rows = [sent[d : d + 1, j * LANES : (j + 1) * LANES] for d in range(2) for j in range(chunks)]
    rows.append(jnp.zeros((INDEX_ROWS - 2 * chunks, LANES), f32))
    out_ref[0, capacity:, :] = jnp.concatenate(rows, axis=0).astype(bf16)


def bucket_rows(grads, targets, points, column, shards, capacity):
    row_count = grads.shape[0]
    groups = row_count // LANES
    return pl.pallas_call(
        functools.partial(bucket_body, shards, capacity),
        grid_spec=pltpu.PrefetchScalarGridSpec(
            num_scalar_prefetch=1,
            grid=(shards,),
            in_specs=[
                pl.BlockSpec((groups, LANES), lambda i, c: (0, 0)),
                pl.BlockSpec((groups, LANES), lambda i, c: (0, 0)),
                pl.BlockSpec((row_count, LANES), lambda i, c: (0, c[0])),
            ],
            out_specs=pl.BlockSpec((1, capacity + INDEX_ROWS, LANES), lambda i, c: (i, 0, 0)),
            scratch_shapes=[pltpu.VMEM((groups, LANES), i32)],
        ),
        out_shape=jax.ShapeDtypeStruct((shards, capacity + INDEX_ROWS, LANES), bf16),
        compiler_params=params(32),
        cost_estimate=cost(
            8 * shards * capacity * row_count * LANES, 3 * shards * capacity * LANES * 2
        ),
        name="bucket_rows",
    )(column, targets.reshape(groups, LANES), points.reshape(groups, LANES), grads)


def segment_body(got_ref, out_ref, total_ref):
    step = pl.program_id(0)
    capacity = got_ref.shape[1] - INDEX_ROWS
    chunks = capacity // LANES
    row_count = total_ref.shape[0]
    digits = got_ref[0, capacity:, :].astype(f32)
    index = (digits[:chunks] * float(INDEX_BASE) + digits[chunks : 2 * chunks]).astype(i32)
    row = lax.broadcasted_iota(i32, (row_count, LANES), 0)
    onehot = jnp.concatenate([ones_where(index[j : j + 1] == row) for j in range(chunks)], axis=1)
    part = dot(onehot, got_ref[0, :capacity, :])

    @pl.when(step == 0)
    def _():
        total_ref[...] = part

    @pl.when(step > 0)
    def _():
        total_ref[...] += part

    @pl.when(step == pl.num_programs(0) - 1)
    def _():
        out_ref[...] = total_ref[...].T.astype(bf16)


def segment_rows(got, row_count):
    shards, message, _ = got.shape
    return pl.pallas_call(
        segment_body,
        grid=(shards,),
        in_specs=[pl.BlockSpec((1, message, LANES), lambda i: (i, 0, 0))],
        out_specs=pl.BlockSpec((LANES, row_count), lambda i: (0, 0)),
        out_shape=jax.ShapeDtypeStruct((LANES, row_count), bf16),
        scratch_shapes=[pltpu.VMEM((row_count, LANES), f32)],
        compiler_params=params(32),
        cost_estimate=cost(
            8 * shards * message * row_count * LANES, 3 * shards * message * LANES * 2
        ),
        name="segment_rows",
    )(got)


def project_body(
    column_ref,
    x0_ref,
    x1_ref,
    x2_ref,
    x3_ref,
    weight_ref,
    hidden_ref,
    normed_ref,
    inv_ref,
    key_ref,
    base2_t_ref,
    query_t_ref,
    key_t_ref,
    value_t_ref,
):
    me = column_ref[0]
    blocks = [r[...].astype(f32) for r in (x0_ref, x1_ref, x2_ref, x3_ref)]
    features = float(LANES * len(blocks))
    mean = jnp.sum(blocks[0] + blocks[1] + (blocks[2] + blocks[3]), axis=1, keepdims=True) / features
    centered = [b - mean for b in blocks]
    squares = [c * c for c in centered]
    var = jnp.sum(squares[0] + squares[1] + (squares[2] + squares[3]), axis=1, keepdims=True) / features
    inv = lax.rsqrt(var + epsilon)
    normed_ref[...] = centered[0] * inv
    inv_ref[...] = jnp.broadcast_to(inv, inv_ref.shape)
    for block, mask in zip(centered, BLOCK_MASKS):
        at = pl.multiple_of((me ^ mask) * LANES, LANES)
        hidden_ref[:, pl.ds(at, LANES)] = (block * inv).astype(bf16)
    projected = dot(hidden_ref[...], weight_ref[...]).astype(bf16)
    key_ref[...] = projected[:, LANES : 2 * LANES]
    query = projected[:, :LANES].astype(f32).T * score_scale
    query_t_ref[...] = query.astype(bf16)
    base2_t_ref[...] = (query * log2_e).astype(bf16)
    key_t_ref[...] = projected[:, LANES : 2 * LANES].astype(f32).T.astype(bf16)
    value_t_ref[...] = projected[:, 2 * LANES :].astype(f32).T.astype(bf16)


def project(blocks, weight, column):
    row_count = blocks[0].shape[0]
    step_rows = 512
    features = weight.shape[0]
    width = pl.BlockSpec((step_rows, LANES), lambda i, c: (i, 0))
    tall = pl.BlockSpec((LANES, step_rows), lambda i, c: (0, i))
    normal = lambda t: jax.ShapeDtypeStruct((row_count, LANES), t)
    turned = jax.ShapeDtypeStruct((LANES, row_count), bf16)
    return pl.pallas_call(
        project_body,
        grid_spec=pltpu.PrefetchScalarGridSpec(
            num_scalar_prefetch=1,
            grid=(row_count // step_rows,),
            in_specs=[width] * 4 + [pl.BlockSpec(weight.shape, lambda i, c: (0, 0))],
            out_specs=[pl.BlockSpec((step_rows, features), lambda i, c: (i, 0))]
            + [width] * 3
            + [tall] * 4,
        ),
        out_shape=[jax.ShapeDtypeStruct((row_count, features), bf16)]
        + [normal(f32), normal(f32), normal(bf16)]
        + [turned] * 4,
        compiler_params=params(32),
        cost_estimate=cost(4 * row_count * features * 3 * LANES, row_count * LANES * 40),
        name="project",
    )(column, *blocks, weight)


def forward_body(
    key_ref,
    base2_t_ref,
    key_t_ref,
    value_t_ref,
    exp_ref,
    attended_ref,
    inverse_ref,
    covariance_ref,
    safe_ref,
):
    head = pl.program_id(0)
    at = pl.multiple_of(head * HD, HD)

    @pl.when(head == 0)
    def _():
        def largest(ref):
            squares = jnp.square(ref[...].astype(f32)).reshape(LANES // HD, HD, PATCH)
            return jnp.max(jnp.sum(squares, axis=1), axis=1, keepdims=True)

        bound = jnp.max(largest(base2_t_ref) * largest(key_t_ref))
        safe_ref[0] = (bound <= SAFE_SCORE * SAFE_SCORE).astype(i32)

    def attend(shifted):
        in_head = lax.broadcasted_iota(i32, (LANES, 1), 0) // HD == head
        query = jnp.where(in_head, base2_t_ref[...], jnp.zeros((), bf16))
        scores = dot(key_ref[...], query)
        if shifted:
            scores = scores - jnp.max(scores, axis=0, keepdims=True)
        weights = jnp.exp2(scores).astype(bf16)
        exp_ref[0] = weights
        keys = key_t_ref[pl.ds(at, HD), :].astype(f32)
        values = value_t_ref[pl.ds(at, HD), :].astype(f32)
        middle = jnp.mean(values, axis=1, keepdims=True)
        centered = values - middle
        features = [centered[j : j + 1] * keys for j in range(HD)]
        features += [keys, values, jnp.ones((HD, PATCH), f32)]
        sums = dot(jnp.concatenate([f.astype(bf16) for f in features], axis=0), weights)
        inverse = 1.0 / sums[(HD + 2) * HD : (HD + 2) * HD + 1]
        inverse_ref[0] = inverse
        mean_key = sums[HD * HD : (HD + 1) * HD] * inverse
        mean_value = sums[(HD + 1) * HD : (HD + 2) * HD] * inverse
        attended_ref[pl.ds(at, HD), :] = mean_value.astype(bf16)
        offset = mean_value - middle
        for j in range(HD):
            crossed = sums[j * HD : (j + 1) * HD] * inverse - offset[j : j + 1] * mean_key
            covariance_ref[0, j * HD : (j + 1) * HD, :] = crossed.astype(bf16)

    @pl.when(safe_ref[0] == 1)
    def _():
        attend(False)

    @pl.when(safe_ref[0] == 0)
    def _():
        attend(True)


def attention_forward(keys, base2_t, key_t, value_t):
    heads = LANES // HD
    tall = pl.BlockSpec((LANES, PATCH), lambda h: (0, 0))
    per_head = lambda h: (h, 0, 0)
    elements = heads * PATCH * PATCH
    return pl.pallas_call(
        forward_body,
        grid=(heads,),
        in_specs=[pl.BlockSpec((PATCH, LANES), lambda h: (0, 0)), tall, tall, tall],
        out_specs=[
            pl.BlockSpec((1, PATCH, PATCH), per_head),
            tall,
            pl.BlockSpec((1, 1, PATCH), per_head),
            pl.BlockSpec((1, HD * HD, PATCH), per_head),
        ],
        out_shape=[
            jax.ShapeDtypeStruct((heads, PATCH, PATCH), bf16),
            jax.ShapeDtypeStruct((LANES, PATCH), bf16),
            jax.ShapeDtypeStruct((heads, 1, PATCH), f32),
            jax.ShapeDtypeStruct((heads, HD * HD, PATCH), bf16),
        ],
        scratch_shapes=[pltpu.SMEM((1,), i32)],
        compiler_params=params(48),
        cost_estimate=cost(1600 * elements, 2 * elements, elements),
        name="attention_forward",
    )(keys, base2_t, key_t, value_t)


def backward_body(
    column_ref,
    exp_ref,
    inverse_ref,
    covariance_ref,
    query_t_ref,
    value_t_ref,
    attended_ref,
    g0_ref,
    g1_ref,
    g2_ref,
    g3_ref,
    weight_t_ref,
    d_out_ref,
    d_query_ref,
    d_key_ref,
    d_value_ref,
    d_attended_ref,
):
    head = pl.program_id(0)
    at = pl.multiple_of(head * HD, HD)

    @pl.when(head == 0)
    def _():
        me = column_ref[0]
        for block, mask in zip((g0_ref, g1_ref, g2_ref, g3_ref), BLOCK_MASKS):
            start = pl.multiple_of((me ^ mask) * LANES, LANES)
            d_out_ref[pl.ds(start, LANES), :] = block[...]
        d_attended_ref[...] = dot(weight_t_ref[...], d_out_ref[...]).astype(bf16)

    grads = d_attended_ref[pl.ds(at, HD), :].astype(f32)
    query = query_t_ref[pl.ds(at, HD), :].astype(f32)
    values = value_t_ref[pl.ds(at, HD), :].astype(f32)
    inverse = inverse_ref[0]
    middle = jnp.mean(values, axis=1, keepdims=True)
    centered = values - middle
    offset = attended_ref[pl.ds(at, HD), :].astype(f32) - middle
    scaled = grads * inverse
    delta = jnp.sum(scaled * offset, axis=0, keepdims=True)
    features = [scaled[j : j + 1] * query for j in range(HD)] + [delta * query, scaled]
    sums = dot_rows(jnp.concatenate([f.astype(bf16) for f in features], axis=0), exp_ref[0])
    d_value_ref[pl.ds(at, HD), :] = sums[(HD + 1) * HD :].astype(bf16)
    d_key = centered[0:1] * sums[:HD]
    d_query = grads[0:1] * covariance_ref[0, :HD, :].astype(f32)
    for j in range(1, HD):
        rows = slice(j * HD, (j + 1) * HD)
        d_key += centered[j : j + 1] * sums[rows]
        d_query += grads[j : j + 1] * covariance_ref[0, rows, :].astype(f32)
    d_key_ref[pl.ds(at, HD), :] = (d_key - sums[HD * HD : (HD + 1) * HD]).astype(bf16)
    d_query_ref[pl.ds(at, HD), :] = (d_query * score_scale).astype(bf16)


def attention_backward(patch, weights, inverse, covariance, query_t, value_t, attended, grads, weight_t, column):
    features = weight_t.shape[1]
    heads = LANES // HD
    tall = pl.BlockSpec((LANES, PATCH), lambda h, c: (0, 0))
    part = pl.BlockSpec((LANES, PATCH), lambda h, c: (0, patch))
    per_head = lambda h, c: (h, 0, 0)
    elements = heads * PATCH * PATCH
    turned = jax.ShapeDtypeStruct((LANES, PATCH), bf16)
    return pl.pallas_call(
        backward_body,
        grid_spec=pltpu.PrefetchScalarGridSpec(
            num_scalar_prefetch=1,
            grid=(heads,),
            in_specs=[
                pl.BlockSpec((1, PATCH, PATCH), per_head),
                pl.BlockSpec((1, 1, PATCH), per_head),
                pl.BlockSpec((1, HD * HD, PATCH), per_head),
                tall,
                tall,
                tall,
                part,
                part,
                part,
                part,
                pl.BlockSpec(weight_t.shape, lambda h, c: (0, 0)),
            ],
            out_specs=[pl.BlockSpec((features, PATCH), lambda h, c: (0, 0)), tall, tall, tall],
            scratch_shapes=[pltpu.VMEM((LANES, PATCH), bf16)],
        ),
        out_shape=[jax.ShapeDtypeStruct((features, PATCH), bf16), turned, turned, turned],
        compiler_params=params(48),
        cost_estimate=cost(1100 * elements, 2 * elements),
        name="attention_backward",
    )(column, weights, inverse, covariance, query_t, value_t, attended, *grads, weight_t)


def whole(shape, dtype):
    return jax.ShapeDtypeStruct(shape, dtype)


def weight_grad_body(*refs):
    *ins, out_ref = refs
    patches = [ins[:6], ins[6:]]
    for t in range(3):
        total = dot(patches[0][t][...], patches[0][4][...]) + dot(patches[1][t][...], patches[1][4][...])
        out_ref[:, t * LANES : (t + 1) * LANES] = total.T.astype(bf16)
    total = dot_rows(patches[0][3][...], patches[0][5][...]) + dot_rows(
        patches[1][3][...], patches[1][5][...]
    )
    out_ref[:, 3 * LANES :] = total.T.astype(bf16)


def weight_grads(patches):
    features = patches[0][4].shape[1]
    work = 2 * PATCH * features * LANES
    return pl.pallas_call(
        weight_grad_body,
        out_shape=whole((features, 4 * LANES), bf16),
        compiler_params=params(48),
        cost_estimate=cost(8 * work, 12 * PATCH * features),
        name="weight_grads",
    )(*patches[0], *patches[1])


def split_sums(sums):
    high = sums.astype(bf16)
    low = (sums - high.astype(f32)).astype(bf16)
    pad = jnp.zeros((INDEX_ROWS - 2 * sums.shape[0], sums.shape[1]), f32)
    return jnp.concatenate([high.astype(f32), low.astype(f32), pad], axis=0).astype(bf16)


def join_sums(rows):
    rows = rows.astype(f32)
    return rows[0:2] + rows[2:4]


def partial_body(
    column_ref,
    d_query_ref,
    d_key_ref,
    d_value_ref,
    query_ref,
    key_ref,
    value_ref,
    weight_ref,
    mine_ref,
    other_ref,
    sums_ref,
):
    me = column_ref[0]
    d_projected = jnp.concatenate([d_query_ref[...], d_key_ref[...], d_value_ref[...]], axis=0)
    plain = jnp.zeros((1, PATCH), f32)
    for j, mask in enumerate(BLOCK_MASKS):
        start = pl.multiple_of((me ^ mask) * LANES, LANES)
        block = dot(weight_ref[pl.ds(start, LANES), :], d_projected).astype(bf16)
        plain += jnp.sum(block.astype(f32), axis=0, keepdims=True)
        to = mine_ref if j < 2 else other_ref
        to[(j % 2) * LANES : (j % 2 + 1) * LANES, :] = block
    crossed = (
        d_query_ref[...].astype(f32) * (query_ref[...].astype(f32) / score_scale)
        + d_key_ref[...].astype(f32) * key_ref[...].astype(f32)
        + d_value_ref[...].astype(f32) * value_ref[...].astype(f32)
    )
    sums = jnp.concatenate([plain, jnp.sum(crossed, axis=0, keepdims=True)], axis=0)
    sums_ref[...] = sums
    other_ref[2 * LANES :, :] = split_sums(sums)


def hidden_part(d_query, d_key, d_value, query, key, value, weight, column):
    features = weight.shape[0]
    return pl.pallas_call(
        partial_body,
        in_specs=[pl.BlockSpec(memory_space=pltpu.SMEM)] + [pl.BlockSpec(memory_space=pltpu.VMEM)] * 7,
        out_shape=[
            whole((2 * LANES, PATCH), bf16),
            whole((2 * LANES + INDEX_ROWS, PATCH), bf16),
            whole((2, PATCH), f32),
        ],
        compiler_params=params(32),
        cost_estimate=cost(6 * PATCH * features * LANES, 4 * PATCH * features),
        name="hidden_part",
    )(column, d_query, d_key, d_value, query, key, value, weight)


def pair_body(mine_ref, sums_ref, got_ref, kept_ref, sums_out_ref, sent_ref):
    pair = mine_ref[...].astype(f32) + got_ref[: 2 * LANES, :].astype(f32)
    sums = sums_ref[...] + join_sums(got_ref[2 * LANES :, :])
    kept_ref[...] = pair[:LANES]
    sums_out_ref[...] = sums
    sent_ref[:LANES, :] = pair[LANES:].astype(bf16)
    sent_ref[LANES:, :] = split_sums(sums)


def pair_sum(mine, sums, got):
    return pl.pallas_call(
        pair_body,
        out_shape=[
            whole((LANES, PATCH), f32),
            whole((2, PATCH), f32),
            whole((LANES + INDEX_ROWS, PATCH), bf16),
        ],
        compiler_params=params(32),
        cost_estimate=cost(4 * LANES * PATCH, 16 * LANES * PATCH),
        name="pair_sum",
    )(mine, sums, got)


def points_body(kept_ref, sums_ref, got_ref, d_out_ref, normed_ref, inv_ref, *rest):
    out_ref = rest[-1]
    features = 4.0 * LANES
    means = (sums_ref[...] + join_sums(got_ref[LANES:, :])) / features
    d_hidden = kept_ref[...] + got_ref[:LANES, :].astype(f32) - means[0:1]
    cross = jnp.broadcast_to(means[1:2], (LANES, PATCH)).T
    inner = d_hidden.T - normed_ref[...] * cross
    out_ref[...] = d_out_ref[...].astype(f32).T + inv_ref[...] * inner


def points_grad(patch, patches, kept, sums, got, d_out, normed, inv_scale, before):
    full = lambda a: pl.BlockSpec(a.shape, lambda i: (0, 0))
    in_specs = [full(kept), full(sums), full(got), pl.BlockSpec((LANES, PATCH), lambda i: (0, patch))]
    in_specs += [full(normed), full(inv_scale)]
    operands = [kept, sums, got, d_out, normed, inv_scale]
    if before is not None:
        in_specs.append(pl.BlockSpec(memory_space=pl.ANY))
        operands.append(before)
    return pl.pallas_call(
        points_body,
        grid=(1,),
        in_specs=in_specs,
        out_specs=pl.BlockSpec((PATCH, LANES), lambda i: (patch, 0)),
        out_shape=whole((patches * PATCH, LANES), f32),
        input_output_aliases={} if before is None else {len(operands) - 1: 0},
        compiler_params=params(32),
        cost_estimate=cost(8 * LANES * PATCH, 24 * LANES * PATCH),
        name="points_grad",
    )(*operands)


def local(
    scan_points,
    send_order,
    arrive_order,
    qkv_weight,
    out_weight,
    voxel_grads,
    voxel_shard,
    voxel_point,
):
    shards = lax.axis_size("seq")
    members = lax.axis_size("mp")
    local_rows, features = scan_points.shape
    voxels = voxel_grads.shape[0]
    capacity = 2 * voxels // shards
    patches = local_rows // PATCH
    column = lax.axis_index("mp").astype(i32).reshape(1)
    zero = jnp.zeros((1,), i32)
    weight = qkv_weight.reshape(features, 3 * LANES)
    weight_t = out_weight.T

    def swap(rows, mask):
        return lax.ppermute(rows, "mp", [(i, i ^ mask) for i in range(members)])

    def exchange(rows):
        return lax.all_to_all(rows, "seq", split_axis=0, concat_axis=0, tiled=True)

    def all_columns(rows):
        across = swap(rows, 2)
        return (rows, across, swap(rows, 1), swap(across, 1))

    arrived = exchange(permute_rows(scan_points, send_order, column))
    buckets = bucket_rows(voxel_grads, voxel_shard, voxel_point, column, shards, capacity)
    got = exchange(buckets.reshape(shards * (capacity + INDEX_ROWS), LANES))
    projected, forwards = [], []
    for p in range(patches):
        own = permute_rows(arrived, arrive_order[p * PATCH : (p + 1) * PATCH], zero)
        projected.append(project(all_columns(own), weight, column))
    forwards.append(attention_forward(projected[0][3], projected[0][4], *projected[0][6:]))
    got, forwards[0] = lax.optimization_barrier((got, forwards[0]))
    summed_rows = segment_rows(got.reshape(shards, capacity + INDEX_ROWS, LANES), local_rows)
    projected[1], summed_rows = lax.optimization_barrier((projected[1], summed_rows))
    grads = all_columns(summed_rows)
    forwards.append(attention_forward(projected[1][3], projected[1][4], *projected[1][6:]))

    d_points = None
    grad_parts = []
    for p in range(patches):
        hidden, normed, inv_scale, _, _, query_t, key_t, value_t = projected[p]
        weights, attended, inverse, covariance = forwards[p]
        d_out, d_query, d_key, d_value = attention_backward(
            p, weights, inverse, covariance, query_t, value_t, attended, grads, weight_t, column
        )
        grad_parts.append((d_query, d_key, d_value, attended, hidden, d_out))
        mine, other, sums = hidden_part(d_query, d_key, d_value, query_t, key_t, value_t, weight, column)
        kept, sums, sent = pair_sum(mine, sums, swap(other, 1))
        d_points = points_grad(
            p, patches, kept, sums, swap(sent, 2), grads[0], normed, inv_scale, d_points
        )
    parts = exchange(weight_grads(grad_parts)).reshape(shards, features // shards, 4 * LANES)
    summed = jnp.sum(parts.astype(f32), axis=0)
    grad_qkv = summed[:, : 3 * LANES].reshape(features // shards, 3, LANES)
    grad_out = summed[:, 3 * LANES :]
    return (d_points, grad_qkv, grad_out)


def solution(mesh):
    in_specs = (
        P("seq", None),
        P("seq"),
        P("seq"),
        P(None, None, "mp"),
        P(None, "mp"),
        P("seq", None),
        P("seq", None),
        P("seq"),
    )
    out_specs = (P("seq", "mp"), P("seq", None, "mp"), P("seq", "mp"))
    return jax.shard_map(local, mesh=mesh, in_specs=in_specs, out_specs=out_specs, check_vma=False)
```

time: 197 us -> 205 us (1.041)
  local copies, waits for them, and re-layouts: 20.9 us -> 39.6 us
  Pallas kernels: 111 us -> 104 us
  other arithmetic: 5.59 us -> 1.13 us
  waiting for transfers between devices: 36.4 us -> 32.6 us
  starting transfers between devices: 21.3 us -> 24.7 us
    unnamed x62 -> x129, local copies, waits for them, and re-layouts: 20 us -> 38.8 us
    all_to_all x3, waiting for transfers between devices: 21.2 us -> 3.39 us  [exchange(): return lax.all_to_all(rows, 'seq', split_axis=0, concat_axis=0, tiled=True)]
    ppermute x10 -> x13, waiting for transfers between devices: 15.2 us -> 29.2 us  [swap(): return lax.ppermute(rows, 'mp', [(i, i ^ mask) for i in range(members)])]
    pallas_call x1 -> x2, Pallas kernels: 40.2 us -> 26.5 us  [attention_backward(): pl.pallas_call(backward_body, grid_spec=pltpu.PrefetchScalarGridSpec(num_...]
    pallas_call x3 -> x9, Pallas kernels: 40.2 us -> 46.3 us  [the longest x2 37.5 us: attention_forward(): pl.pallas_call(forward_body, grid=(heads,), in_specs=[pl.BlockSpec((PATCH...]
    add x3 -> x0, other arithmetic: 4.6 us -> none  [the longest x1 2.82 us: local(): grads[0].astype(f32)]
    ppermute x10 -> x13, starting transfers between devices: 5.78 us -> 8.12 us  [swap(): return lax.ppermute(rows, 'mp', [(i, i ^ mask) for i in range(members)])]
    pallas_call x2 -> x3, Pallas kernels: 7.32 us -> 8 us  [permute_rows(): pl.pallas_call(permute_body, grid_spec=pltpu.PrefetchScalarGridSpec(num_s...]
  transfers between devices with their start and end apart: 13 -> 16, of which waited for: 6 -> 6; matrix products, arithmetic and copies ran while one was open for 2% -> 1% of each run, Pallas kernels for 31% -> 31%
where the time goes in v2:
time: 205 us; the launch traced here: 203 us
  Pallas kernels  104 us (51%)
  local copies, waits for them, and re-layouts  39.6 us (19%)
  waiting for transfers between devices  32.6 us (16%)
  starting transfers between devices  24.7 us (12%)
    unnamed x129, local copies, waits for them, and re-layouts  38.8 us
    pallas_call x2, Pallas kernels, attention_forward(): pl.pallas_call(forward_body, grid=(heads,), in_specs=[pl.BlockSpec((PATCH...  37.5 us
    ppermute x13, waiting for transfers between devices, swap(): return lax.ppermute(rows, 'mp', [(i, i ^ mask) for i in range(members)])  29.2 us
    pallas_call x2, Pallas kernels, attention_backward(): pl.pallas_call(backward_body, grid_spec=pltpu.PrefetchScalarGridSpec(num_...  26.5 us
    all_to_all x3, starting transfers between devices, exchange(): return lax.all_to_all(rows, 'seq', split_axis=0, concat_axis=0, tiled=True)  16.6 us
    pallas_call x1, Pallas kernels, bucket_rows(): pl.pallas_call(functools.partial(bucket_body, shards, capacity), grid_spe...  11.1 us
    ppermute x13, starting transfers between devices, swap(): return lax.ppermute(rows, 'mp', [(i, i ^ mask) for i in range(members)])  8.12 us
    pallas_call x3, Pallas kernels, permute_rows(): pl.pallas_call(permute_body, grid_spec=pltpu.PrefetchScalarGridSpec(num_s...  8 us
  transfers between devices with their start and end apart: 16, of which 6 were waited for; matrix products, arithmetic and copies ran while one was open for 1% of the time, Pallas kernels for 31%

profile of v2, /device:TPU:0, one launch (start us, length us, event | category | flops | bytes accessed | tf_op | source)
XLA Modules:
  0.0 203.0 jit_solution(8987202545302510824)
XLA Ops:
  0.6 1.6 copy-done.41
  2.9 4.1 %permute_rows.3 = bf16[2048,128]{1,0:T(8,128)(2,1)} custom-call(s32[1]{0:T(128)} %bitcast.column_ref, s32[16,128]{1,0:T(8,128)S(1)} %bitcast.24, bf16[2048,512]{1,0:T(8,128)(2,1)S(1)} %copy-done.41), custom_call_target="tpu_custom_call" | custom-call | flops 4294967296 | bytes 1572864 | tf_op jit(solution)/shard_map/permute_rows/pallas_call | solution.py:69
  7.0 7.3 %all-to-all-start = ((bf16[8,256,128]{2,1,0:T(8,128)(2,1)}), bf16[8,256,128]{2,1,0:T(8,128)(2,1)S(1)}, u32[]{:S(2)}, u32[]{:S(2)}) async-start(bf16[8,256,128]{2,1,0:T(8,128)(2,1)} %bitcast.3), calls=%async_computation | async-start | bytes 1048576 | tf_op jit(solution)/shard_map/all_to_all | solution.py:602
  14.3 11.1 %bucket_rows.1 = bf16[8,528,128]{2,1,0:T(8,128)(2,1)} custom-call(s32[1]{0:T(128)} %bitcast.column_ref, s32[16,128]{1,0:T(8,128)S(1)} %bitcast.25, s32[16,128]{1,0:T(8,128)S(1)} %bitcast.26, bf16[2048,512]{1,0:T(8,128)(2,1)S(1)} %copy-done.42), custom_call_target="tpu_custom_call" | custom-call | flops 8589934592 | bytes 3145728 | tf_op jit(solution)/shard_map/bucket_rows/pallas_call | solution.py:134
  25.4 3.4 %all-to-all-done = bf16[8,256,128]{2,1,0:T(8,128)(2,1)S(1)} async-done(((bf16[8,256,128]{2,1,0:T(8,128)(2,1)}), bf16[8,256,128]{2,1,0:T(8,128)(2,1)S(1)}, u32[]{:S(2)}, u32[]{:S(2)}) %all-to-all-start) | async-done | bytes 524320 | tf_op jit(solution)/shard_map/all_to_all | solution.py:602
  28.8 3.6 %all-to-all-start.1 = ((bf16[8,528,128]{2,1,0:T(8,128)(2,1)}), bf16[8,528,128]{2,1,0:T(8,128)(2,1)S(1)}, u32[]{:S(2)}, u32[]{:S(2)}) async-start(bf16[8,528,128]{2,1,0:T(8,128)(2,1)} %bucket_rows.1), calls=%async_computation.1 | async-start | bytes 2162688 | tf_op jit(solution)/shard_map/all_to_all | solution.py:602
  32.4 1.6 permute_rows.5.x0_ref
  34.1 1.6 collective-permute-start.3
  35.6 2.3 %permute_rows.4.x0_ref = bf16[1024,128]{1,0:T(8,128)(2,1)} custom-call(s32[1]{0:T(128)} %constant.1.clone.1.column_ref, s32[8,128]{1,0:T(8,128)S(1)} %get-tuple-element.123.order_ref, bf16[2048,128]{1,0:T(8,128)(2,1)S(1)} %bitcast.21), custom_call_target="tpu_custom_call" | custom-call | flops 1073741824 | bytes 786432 | tf_op jit(solution)/shard_map/permute_rows/pallas_call | solution.py:69
  38.4 4.9 %collective-permute-done.3.x1_ref = bf16[1024,128]{1,0:T(8,128)(2,1)S(1)} collective-permute-done((bf16[1024,128]{1,0:T(8,128)(2,1)S(1)}, bf16[1024,128]{1,0:T(8,128)(2,1)S(1)}, u32[]{:S(2)}, u32[]{:S(2)}) %collective-permute-start.3) | collective-permute-done | bytes 262176 | tf_op jit(solution)/shard_map/ppermute | solution.py:599
  43.8 4.0 %collective-permute-done.x1_ref = bf16[1024,128]{1,0:T(8,128)(2,1)} collective-permute-done((bf16[1024,128]{1,0:T(8,128)(2,1)}, bf16[1024,128]{1,0:T(8,128)(2,1)}, u32[]{:S(2)}, u32[]{:S(2)}) %collective-permute-start) | collective-permute-done | bytes 262176 | tf_op jit(solution)/shard_map/ppermute | solution.py:599
  47.8 1.2 copy.14
  49.2 0.7 copy-done.49
  50.7 0.9 copy-done.46
  51.6 0.9 copy-done.48
  52.6 0.9 copy-done.50
  53.5 0.9 copy-done.52
  54.5 1.9 project.3
  56.4 0.8 copy-done.17
  57.2 0.8 copy-done.19
  58.1 3.4 %project.2 = (bf16[1024,512]{1,0:T(8,128)(2,1)S(1)}, f32[1024,128]{1,0:T(8,128)S(1)}, f32[1024,128]{1,0:T(8,128)S(1)}, bf16[1024,128]{1,0:T(8,128)(2,1)S(1)}, bf...) custom-call(s32[1]{0:T(128)} %bitcast.column_ref, ...), custom_call_target="tpu_custom_call" | custom-call | flops 805306368 | bytes 5242880 | tf_op jit(solution)/shard_map/project/pallas_call | solution.py:243
  61.5 1.0 copy-done
  62.4 0.8 copy-done.15
  64.6 0.7 copy-done.34
  66.8 18.8 %attention_forward.2 = (bf16[8,1024,1024]{2,1,0:T(8,128)(2,1)}, bf16[128,1024]{1,0:T(8,128)(2,1)S(1)}, f32[8,1,1024]{2,1,0:T(1,128)S(1)}, bf16[8,256,1024]{2,1,0:T(8,128)(2,1)S(1)}) custom-call(bf16[1024,128]{1,0:T(8,128)(2,1)S(1)} %get-tuple-element.69.key_ref, bf16[128,1024]{1,0:T(8,128)(2,1)S(1)} %get-tuple-element.70.base2_t_ref, ...), custom_call_target="tpu_custom_call" | custom-call | flops 13421772800 | bytes 16777216 | tf_op jit(solution)/shard_map/attention_forward/pallas_call | solution.py:324
  85.6 0.7 copy-done.38
  86.3 2.0 copy-done.60
  88.3 6.7 %segment_rows.1.g0_ref.d_out_ref = bf16[128,2048]{1,0:T(8,128)(2,1)S(1)} custom-call(bf16[8,528,128]{2,1,0:T(8,128)(2,1)S(1)} %all-to-all-done.1), custom_call_target="tpu_custom_call" | custom-call | flops 8858370048 | bytes 3244032 | tf_op jit(solution)/shard_map/segment_rows/pallas_call | solution.py:182
  95.0 1.6 collective-permute-start.6
  96.5 1.0 copy.17
  97.8 11.5 %collective-permute-done.6.g1_ref = bf16[128,2048]{1,0:T(8,128)(2,1)S(1)} collective-permute-done((bf16[128,2048]{1,0:T(8,128)(2,1)S(1)}, bf16[128,2048]{1,0:T(8,128)(2,1)S(1)}, u32[]{:S(2)}, u32[]{:S(2)}) %collective-permute-start.6) | collective-permute-done | bytes 524320 | tf_op jit(solution)/shard_map/ppermute | solution.py:599
  109.3 1.1 copy-done.32
  110.4 0.9 copy-done.35
  111.4 0.9 copy-done.57
  112.3 0.9 copy-done.59
  113.3 18.7 %attention_forward.3 = (bf16[8,1024,1024]{2,1,0:T(8,128)(2,1)}, bf16[128,1024]{1,0:T(8,128)(2,1)S(1)}, f32[8,1,1024]{2,1,0:T(1,128)S(1)}, bf16[8,256,1024]{2,1,0:T(8,128)(2,1)S(1)}) custom-call(bf16[1024,128]{1,0:T(8,128)(2,1)S(1)} %copy-done.57, bf16[128,1024]{1,0:T(8,128)(2,1)S(1)} %copy-done.59, bf16[128,1024]{1,0:T(8,128)(2,1)S(1)} %copy-done.32, ...), custom_call_target="tpu_custom_call" | custom-call | flops 13421772800 | bytes 16777216 | tf_op jit(solution)/shard_map/attention_forward/pallas_call | solution.py:324
  132.1 14.0 %attention_backward.3 = (bf16[512,1024]{1,0:T(8,128)(2,1)S(1)}, bf16[128,1024]{1,0:T(8,128)(2,1)S(1)}, bf16[128,1024]{1,0:T(8,128)(2,1)S(1)}, bf16[128,1024]{1,0:T(8,128)(2,1)S(1)}) custom-call(s32[1]{0:T(128)} %bitcast.column_ref, bf16[8,1024,1024]{2,1,0:T(8,128)(2,1)} %get-tuple-element.99.exp_ref, f32[8,1,1024]{2,1,0:T(1,128)S(1)} %get-tuple-element.100.inverse_ref, ...), custom_call_target="tpu_custom_call" | custom-call | flops 9227468800 | bytes 16777216 | tf_op jit(solution)/shard_map/attention_backward/pallas_call | solution.py:407
  146.1 1.3 copy-done.44
  147.4 12.6 %attention_backward.2 = (bf16[512,1024]{1,0:T(8,128)(2,1)S(1)}, bf16[128,1024]{1,0:T(8,128)(2,1)S(1)}, bf16[128,1024]{1,0:T(8,128)(2,1)S(1)}, bf16[128,1024]{1,0:T(8,128)(2,1)S(1)}) custom-call(s32[1]{0:T(128)} %bitcast.column_ref, bf16[8,1024,1024]{2,1,0:T(8,128)(2,1)} %get-tuple-element.82.exp_ref, f32[8,1,1024]{2,1,0:T(1,128)S(1)} %get-tuple-element.83.inverse_ref, ...), custom_call_target="tpu_custom_call" | custom-call | flops 9227468800 | bytes 16777216 | tf_op jit(solution)/shard_map/attention_backward/pallas_call | solution.py:407
  159.9 1.0 copy-done.2
  160.9 4.0 %weight_grads.1 = bf16[512,512]{1,0:T(8,128)(2,1)} custom-call(bf16[128,1024]{1,0:T(8,128)(2,1)S(1)} %get-tuple-element.104.d_query_ref.refs_0_, bf16[128,1024]{1,0:T(8,128)(2,1)S(1)} %get-tuple-element.105.d_key_ref.refs_1_, bf16[128,1024]{1,0:T(8,128)(2,1)S(1)} %get-tuple-element.106.d_value_ref.refs_2_, bf16[128,1024]{1,0:T(8,128)(2,1)S(1)} %copy-done.40, ...), custom_call_target="tpu_custom_call" | custom-call | flops 1073741824 | bytes 6291456 | tf_op jit(solution)/shard_map/weight_grads/pallas_call | solution.py:454
  164.9 5.7 %all-to-all-start.2 = ((bf16[8,64,512]{2,1,0:T(8,128)(2,1)}), bf16[8,64,512]{2,1,0:T(8,128)(2,1)}, u32[]{:S(2)}, u32[]{:S(2)}) async-start(bf16[8,64,512]{2,1,0:T(8,128)(2,1)} %bitcast.12), calls=%async_computation.2 | async-start | bytes 1048576 | tf_op jit(solution)/shard_map/all_to_all | solution.py:602
  170.6 0.9 copy-done.8
  171.6 0.9 copy-done.10
  172.5 0.9 copy-done.12
  173.5 0.9 copy-done.22
  174.4 0.9 copy-done.24
  175.4 0.9 copy-done.27
  176.4 1.0 hidden_part.3
  177.5 0.9 copy-done.4
  178.5 0.9 copy-done.6
  179.4 0.9 copy-done.30
  180.4 0.9 copy-done.33
  181.3 0.9 copy-done.37
  182.3 1.0 hidden_part.2
  184.0 1.6 collective-permute-start.12
  185.8 1.4 collective-permute-start.10
  187.2 6.7 %collective-permute-done.12.got_ref = bf16[144,1024]{1,0:T(8,128)(2,1)S(1)} collective-permute-done((bf16[144,1024]{1,0:T(8,128)(2,1)S(1)}, bf16[144,1024]{1,0:T(8,128)(2,1)S(1)}, u32[]{:S(2)}, u32[]{:S(2)}) %collective-permute-start.12) | collective-permute-done | bytes 294944 | tf_op jit(solution)/shard_map/ppermute | solution.py:599
  193.9 1.0 copy-done.18
  195.0 1.0 copy-done.20
  196.0 1.2 points_grad.2.rest_0_
  197.2 2.1 %collective-permute-done.10.got_ref = bf16[144,1024]{1,0:T(8,128)(2,1)S(1)} collective-permute-done((bf16[144,1024]{1,0:T(8,128)(2,1)S(1)}, bf16[144,1024]{1,0:T(8,128)(2,1)S(1)}, u32[]{:S(2)}, u32[]{:S(2)}) %collective-permute-start.10) | collective-permute-done | bytes 294944 | tf_op jit(solution)/shard_map/ppermute | solution.py:599
  199.4 1.2 points_grad.3
  200.6 1.1 convert_reduce_fusion
  (119 shorter events, 8.1 us)
Async XLA Ops:
  0.6 1.6 copy-start.41
  2.9 11.4 %copy-start.62 = (s32[2048]{0:T(1024)S(1)}, s32[2048]{0:T(1024)}, u32[]{:S(2)}) copy-start(s32[2048]{0:T(1024)} %param.10) | copy-start | bytes 24580
  2.9 11.4 %copy-start.42 = (bf16[2048,512]{1,0:T(8,128)(2,1)S(1)}, bf16[2048,512]{1,0:T(8,128)(2,1)}, u32[]{:S(2)}) copy-start(bf16[2048,512]{1,0:T(8,128)(2,1)} %grads_ref.1) | copy-start | bytes 6291460
  2.9 11.4 %copy-start.54 = (s32[2048,1]{0,1:T(1,128)S(1)}, s32[2048,1]{0,1:T(1,128)}, u32[]{:S(2)}) copy-start(s32[2048,1]{0,1:T(1,128)} %param.14) | copy-start | bytes 24580
  2.9 11.4 %copy-start.55 = (s32[2048]{0:T(1024)S(1)}, s32[2048]{0:T(1024)}, u32[]{:S(2)}) copy-start(s32[2048]{0:T(1024)} %param.15) | copy-start | bytes 24580
  7.0 21.7 %all-to-all-start = ((bf16[8,256,128]{2,1,0:T(8,128)(2,1)}), bf16[8,256,128]{2,1,0:T(8,128)(2,1)S(1)}, u32[]{:S(2)}, u32[]{:S(2)}) async-start(bf16[8,256,128]{2,1,0:T(8,128)(2,1)} %bitcast.3), calls=%async_computation | async-start | bytes 1048576 | tf_op jit(solution)/shard_map/all_to_all | solution.py:602
  28.8 59.5 %all-to-all-start.1 = ((bf16[8,528,128]{2,1,0:T(8,128)(2,1)}), bf16[8,528,128]{2,1,0:T(8,128)(2,1)S(1)}, u32[]{:S(2)}, u32[]{:S(2)}) async-start(bf16[8,528,128]{2,1,0:T(8,128)(2,1)} %bucket_rows.1), calls=%async_computation.1 | async-start | bytes 2162688 | tf_op jit(solution)/shard_map/all_to_all | solution.py:602
  34.1 15.2 %copy-start.45 = (bf16[1024,128]{1,0:T(8,128)(2,1)}, bf16[1024,128]{1,0:T(8,128)(2,1)S(1)}, u32[]{:S(2)}) copy-start(bf16[1024,128]{1,0:T(8,128)(2,1)S(1)} %permute_rows.5.x0_ref) | copy-start | bytes 786436
  34.1 9.3 %collective-permute-start.3 = (bf16[1024,128]{1,0:T(8,128)(2,1)S(1)}, bf16[1024,128]{1,0:T(8,128)(2,1)S(1)}, u32[]{:S(2)}, u32[]{:S(2)}) collective-permute-start(bf16[1024,128]{1,0:T(8,128)(2,1)S(1)} %permute_rows.5.x0_ref), channel_id=1, source_target_pairs={{0,2},{1,3},{2,0},{3,1},{4,6},{5,7},{6,4},{7,5},{8,10},{9,11},{10,... | collective-permute-start | bytes 786440 | tf_op jit(solution)/shard_map/ppermute | solution.py:599
  37.9 9.9 %collective-permute-start = (bf16[1024,128]{1,0:T(8,128)(2,1)}, bf16[1024,128]{1,0:T(8,128)(2,1)}, u32[]{:S(2)}, u32[]{:S(2)}) collective-permute-start(bf16[1024,128]{1,0:T(8,128)(2,1)} %permute_rows.4.x0_ref), channel_id=1, source_target_pairs={{0,2},{1,3},{2,0},{3,1},{4,6},{5,7},{6,4},{7,5},{8,10},{9,11},{10,... | collective-permute-start | bytes 786440 | tf_op jit(solution)/shard_map/ppermute | solution.py:599
  38.4 10.8 %collective-permute-start.4 = (bf16[1024,128]{1,0:T(8,128)(2,1)S(1)}, bf16[1024,128]{1,0:T(8,128)(2,1)S(1)}, u32[]{:S(2)}, u32[]{:S(2)}) collective-permute-start(bf16[1024,128]{1,0:T(8,128)(2,1)S(1)} %permute_rows.5.x0_ref), channel_id=1, source_target_pairs={{0,1},{1,0},{2,3},{3,2},{4,5},{5,4},{6,7},{7,6},{8,9},{9,8},{10,11... | collective-permute-start | bytes 786440 | tf_op jit(solution)/shard_map/ppermute | solution.py:599
  43.3 5.9 %copy-start.47 = (bf16[1024,128]{1,0:T(8,128)(2,1)}, bf16[1024,128]{1,0:T(8,128)(2,1)S(1)}, u32[]{:S(2)}) copy-start(bf16[1024,128]{1,0:T(8,128)(2,1)S(1)} %collective-permute-done.3.x1_ref) | copy-start | bytes 786436
  43.3 6.6 %collective-permute-start.5 = (bf16[1024,128]{1,0:T(8,128)(2,1)S(1)}, bf16[1024,128]{1,0:T(8,128)(2,1)S(1)}, u32[]{:S(2)}, u32[]{:S(2)}) collective-permute-start(bf16[1024,128]{1,0:T(8,128)(2,1)S(1)} %collective-permute-done.3.x1_ref), channel_id=1, source_target_pairs={{0,1},{1,0},{2,3},{3,2},{4,5},{5,4},{6,7},{7,6},{8,9},{9,8},{10,11... | collective-permute-start | bytes 786440 | tf_op jit(solution)/shard_map/ppermute | solution.py:599
  43.3 14.7 %collective-permute-start.1 = (bf16[1024,128]{1,0:T(8,128)(2,1)}, bf16[1024,128]{1,0:T(8,128)(2,1)}, u32[]{:S(2)}, u32[]{:S(2)}) collective-permute-start(bf16[1024,128]{1,0:T(8,128)(2,1)} %permute_rows.4.x0_ref), channel_id=1, source_target_pairs={{0,1},{1,0},{2,3},{3,2},{4,5},{5,4},{6,7},{7,6},{8,9},{9,8},{10,11... | collective-permute-start | bytes 786440 | tf_op jit(solution)/shard_map/ppermute | solution.py:599
  47.8 10.3 %collective-permute-start.2 = (bf16[1024,128]{1,0:T(8,128)(2,1)}, bf16[1024,128]{1,0:T(8,128)(2,1)}, u32[]{:S(2)}, u32[]{:S(2)}) collective-permute-start(bf16[1024,128]{1,0:T(8,128)(2,1)} %collective-permute-done.x1_ref), channel_id=1, source_target_pairs={{0,1},{1,0},{2,3},{3,2},{4,5},{5,4},{6,7},{7,6},{8,9},{9,8},{10,11... | collective-permute-start | bytes 786440 | tf_op jit(solution)/shard_map/ppermute | solution.py:599
  50.7 0.9 copy-start.46
  51.6 0.9 copy-start.48
  52.6 0.9 copy-start.50
  53.5 0.9 copy-start.52
  58.0 8.7 %copy-start.23 = (bf16[128,1024]{1,0:T(8,128)(2,1)}, bf16[128,1024]{1,0:T(8,128)(2,1)S(1)}, u32[]{:S(2)}) copy-start(bf16[128,1024]{1,0:T(8,128)(2,1)S(1)} %get-tuple-element.71.key_t_ref.key_ref) | copy-start | bytes 786436
  58.1 8.7 %copy-start.25 = (bf16[128,1024]{1,0:T(8,128)(2,1)}, bf16[128,1024]{1,0:T(8,128)(2,1)S(1)}, u32[]{:S(2)}) copy-start(bf16[128,1024]{1,0:T(8,128)(2,1)S(1)} %get-tuple-element.72.value_t_ref.value_ref) | copy-start | bytes 786436
  58.1 73.9 %copy-start.21 = (bf16[128,1024]{1,0:T(8,128)(2,1)}, bf16[128,1024]{1,0:T(8,128)(2,1)S(1)}, u32[]{:S(2)}) copy-start(bf16[128,1024]{1,0:T(8,128)(2,1)S(1)} %get-tuple-element.102.query_t_ref.query_ref) | copy-start | bytes 786436
  61.5 1.0 copy-start
  66.8 18.8 %copy-start.13 = (f32[1024,128]{1,0:T(8,128)}, f32[1024,128]{1,0:T(8,128)S(1)}, u32[]{:S(2)}) copy-start(f32[1024,128]{1,0:T(8,128)S(1)} %get-tuple-element.97.normed_ref) | copy-start | bytes 1572868
  86.3 2.0 copy-start.60
  95.0 14.3 %collective-permute-start.6 = (bf16[128,2048]{1,0:T(8,128)(2,1)S(1)}, bf16[128,2048]{1,0:T(8,128)(2,1)S(1)}, u32[]{:S(2)}, u32[]{:S(2)}) collective-permute-start(bf16[128,2048]{1,0:T(8,128)(2,1)S(1)} %segment_rows.1.g0_ref.d_out_ref), channel_id=1, source_target_pairs={{0,2},{1,3},{2,0},{3,1},{4,6},{5,7},{6,4},{7,5},{8,10},{9,11},{10,... | collective-permute-start | bytes 1572872 | tf_op jit(solution)/shard_map/ppermute | solution.py:599
  96.5 35.5 %copy-start.39 = (bf16[128,1024]{1,0:T(8,128)(2,1)S(1)}, bf16[128,1024]{1,0:T(8,128)(2,1)}, u32[]{:S(2)}) copy-start(bf16[128,1024]{1,0:T(8,128)(2,1)} %copy-done.38) | copy-start | bytes 786436
  97.6 34.4 %copy-start.26 = (bf16[128,1024]{1,0:T(8,128)(2,1)S(1)}, bf16[128,1024]{1,0:T(8,128)(2,1)}, u32[]{:S(2)}) copy-start(bf16[128,1024]{1,0:T(8,128)(2,1)} %copy-done.25) | copy-start | bytes 786436
  97.6 34.4 %collective-permute-start.7 = (bf16[128,2048]{1,0:T(8,128)(2,1)S(1)}, bf16[128,2048]{1,0:T(8,128)(2,1)S(1)}, u32[]{:S(2)}, u32[]{:S(2)}) collective-permute-start(bf16[128,2048]{1,0:T(8,128)(2,1)S(1)} %segment_rows.1.g0_ref.d_out_ref), channel_id=1, source_target_pairs={{0,1},{1,0},{2,3},{3,2},{4,5},{5,4},{6,7},{7,6},{8,9},{9,8},{10,11... | collective-permute-start | bytes 1572872 | tf_op jit(solution)/shard_map/ppermute | solution.py:599
  109.3 22.7 %copy-start.43 = (bf16[128,2048]{1,0:T(8,128)(2,1)}, bf16[128,2048]{1,0:T(8,128)(2,1)S(1)}, u32[]{:S(2)}) copy-start(bf16[128,2048]{1,0:T(8,128)(2,1)S(1)} %collective-permute-done.6.g1_ref) | copy-start | bytes 1572868
  109.3 22.7 %collective-permute-start.8 = (bf16[128,2048]{1,0:T(8,128)(2,1)S(1)}, bf16[128,2048]{1,0:T(8,128)(2,1)S(1)}, u32[]{:S(2)}, u32[]{:S(2)}) collective-permute-start(bf16[128,2048]{1,0:T(8,128)(2,1)S(1)} %collective-permute-done.6.g1_ref), channel_id=1, source_target_pairs={{0,1},{1,0},{2,3},{3,2},{4,5},{5,4},{6,7},{7,6},{8,9},{9,8},{10,11... | collective-permute-start | bytes 1572872 | tf_op jit(solution)/shard_map/ppermute | solution.py:599
  109.3 1.1 copy-start.32
  110.4 0.9 copy-start.35
  111.4 0.9 copy-start.57
  112.3 0.9 copy-start.59
  132.0 14.0 %copy-start.61 = (bf16[8,256,1024]{2,1,0:T(8,128)(2,1)}, bf16[8,256,1024]{2,1,0:T(8,128)(2,1)S(1)}, u32[]{:S(2)}) copy-start(bf16[8,256,1024]{2,1,0:T(8,128)(2,1)S(1)} %get-tuple-element.84.covariance_ref) | copy-start | bytes 12582916
  132.0 14.0 %copy-start.29 = (bf16[128,1024]{1,0:T(8,128)(2,1)S(1)}, bf16[128,1024]{1,0:T(8,128)(2,1)}, u32[]{:S(2)}) copy-start(bf16[128,1024]{1,0:T(8,128)(2,1)} %copy-done.28) | copy-start | bytes 786436
  132.0 14.0 %copy-start.36 = (bf16[128,1024]{1,0:T(8,128)(2,1)S(1)}, bf16[128,1024]{1,0:T(8,128)(2,1)}, u32[]{:S(2)}) copy-start(bf16[128,1024]{1,0:T(8,128)(2,1)} %copy-done.34) | copy-start | bytes 786436
  146.0 14.9 %copy-start.7 = (bf16[128,1024]{1,0:T(8,128)(2,1)}, bf16[128,1024]{1,0:T(8,128)(2,1)S(1)}, u32[]{:S(2)}) copy-start(bf16[128,1024]{1,0:T(8,128)(2,1)S(1)} %get-tuple-element.104.d_query_ref.refs_0_) | copy-start | bytes 786436
  146.0 14.9 %copy-start.9 = (bf16[128,1024]{1,0:T(8,128)(2,1)}, bf16[128,1024]{1,0:T(8,128)(2,1)S(1)}, u32[]{:S(2)}) copy-start(bf16[128,1024]{1,0:T(8,128)(2,1)S(1)} %get-tuple-element.105.d_key_ref.refs_1_) | copy-start | bytes 786436
  146.0 14.9 %copy-start.11 = (bf16[128,1024]{1,0:T(8,128)(2,1)}, bf16[128,1024]{1,0:T(8,128)(2,1)S(1)}, u32[]{:S(2)}) copy-start(bf16[128,1024]{1,0:T(8,128)(2,1)S(1)} %get-tuple-element.106.d_value_ref.refs_2_) | copy-start | bytes 786436
  146.1 1.3 copy-start.44
  147.4 13.6 %copy-start.1 = (bf16[1024,512]{1,0:T(8,128)(2,1)S(1)}, bf16[1024,512]{1,0:T(8,128)(2,1)}, u32[]{:S(2)}) copy-start(bf16[1024,512]{1,0:T(8,128)(2,1)} %copy-done) | copy-start | bytes 3145732
  147.4 13.6 %copy-start.40 = (bf16[128,1024]{1,0:T(8,128)(2,1)S(1)}, bf16[128,1024]{1,0:T(8,128)(2,1)}, u32[]{:S(2)}) copy-start(bf16[128,1024]{1,0:T(8,128)(2,1)} %copy-done.38) | copy-start | bytes 786436
  159.9 1.0 copy-start.2
  160.9 4.0 %copy-start.3 = (bf16[128,1024]{1,0:T(8,128)(2,1)}, bf16[128,1024]{1,0:T(8,128)(2,1)S(1)}, u32[]{:S(2)}) copy-start(bf16[128,1024]{1,0:T(8,128)(2,1)S(1)} %get-tuple-element.89.d_key_ref.refs_7_) | copy-start | bytes 786436
  160.9 4.0 %copy-start.5 = (bf16[128,1024]{1,0:T(8,128)(2,1)}, bf16[128,1024]{1,0:T(8,128)(2,1)S(1)}, u32[]{:S(2)}) copy-start(bf16[128,1024]{1,0:T(8,128)(2,1)S(1)} %get-tuple-element.90.d_value_ref.refs_8_) | copy-start | bytes 786436
  164.9 35.6 %all-to-all-start.2 = ((bf16[8,64,512]{2,1,0:T(8,128)(2,1)}), bf16[8,64,512]{2,1,0:T(8,128)(2,1)}, u32[]{:S(2)}, u32[]{:S(2)}) async-start(bf16[8,64,512]{2,1,0:T(8,128)(2,1)} %bitcast.12), calls=%async_computation.2 | async-start | bytes 1048576 | tf_op jit(solution)/shard_map/all_to_all | solution.py:602
  170.6 0.9 copy-start.8
  171.6 0.9 copy-start.10
  172.5 0.9 copy-start.12
  173.5 0.9 copy-start.22
  174.4 0.9 copy-start.24
  175.4 0.9 copy-start.27
  176.3 23.0 %copy-start.14 = (f32[1024,128]{1,0:T(8,128)S(1)}, f32[1024,128]{1,0:T(8,128)}, u32[]{:S(2)}) copy-start(f32[1024,128]{1,0:T(8,128)} %copy-done.13) | copy-start | bytes 1572868
  176.3 23.0 %copy-start.16 = (f32[1024,128]{1,0:T(8,128)S(1)}, f32[1024,128]{1,0:T(8,128)}, u32[]{:S(2)}) copy-start(f32[1024,128]{1,0:T(8,128)} %copy-done.15) | copy-start | bytes 1572868
  177.4 6.4 %collective-permute-start.11 = (bf16[272,1024]{1,0:T(8,128)(2,1)S(1)}, bf16[272,1024]{1,0:T(8,128)(2,1)S(1)}, u32[]{:S(2)}, u32[]{:S(2)}) collective-permute-start(bf16[272,1024]{1,0:T(8,128)(2,1)S(1)} %get-tuple-element.109), channel_id=1, source_target_pairs={{0,1},{1,0},{2,3},{3,2},{4,5},{5,4},{6,7},{7,6},{8,9},{9,8},{10,11... | collective-permute-start | bytes 1671176 | tf_op jit(solution)/shard_map/ppermute | solution.py:599
  177.5 0.9 copy-start.4
  178.5 0.9 copy-start.6
  183.3 2.3 %collective-permute-start.9 = (bf16[272,1024]{1,0:T(8,128)(2,1)S(1)}, bf16[272,1024]{1,0:T(8,128)(2,1)S(1)}, u32[]{:S(2)}, u32[]{:S(2)}) collective-permute-start(bf16[272,1024]{1,0:T(8,128)(2,1)S(1)} %get-tuple-element.93), channel_id=1, source_target_pairs={{0,1},{1,0},{2,3},{3,2},{4,5},{5,4},{6,7},{7,6},{8,9},{9,8},{10,11... | collective-permute-start | bytes 1671176 | tf_op jit(solution)/shard_map/ppermute | solution.py:599
  184.0 9.9 %collective-permute-start.12 = (bf16[144,1024]{1,0:T(8,128)(2,1)S(1)}, bf16[144,1024]{1,0:T(8,128)(2,1)S(1)}, u32[]{:S(2)}, u32[]{:S(2)}) collective-permute-start(bf16[144,1024]{1,0:T(8,128)(2,1)S(1)} %get-tuple-element.112), channel_id=1, source_target_pairs={{0,2},{1,3},{2,0},{3,1},{4,6},{5,7},{6,4},{7,5},{8,10},{9,11},{10,... | collective-permute-start | bytes 884744 | tf_op jit(solution)/shard_map/ppermute | solution.py:599
  185.8 13.6 %collective-permute-start.10 = (bf16[144,1024]{1,0:T(8,128)(2,1)S(1)}, bf16[144,1024]{1,0:T(8,128)(2,1)S(1)}, u32[]{:S(2)}, u32[]{:S(2)}) collective-permute-start(bf16[144,1024]{1,0:T(8,128)(2,1)S(1)} %get-tuple-element.96), channel_id=1, source_target_pairs={{0,2},{1,3},{2,0},{3,1},{4,6},{5,7},{6,4},{7,5},{8,10},{9,11},{10,... | collective-permute-start | bytes 884744 | tf_op jit(solution)/shard_map/ppermute | solution.py:599
  193.9 1.0 copy-start.18
  195.0 1.0 copy-start.20
  (15 other events, 11.6 us)

commit v3 on v2

--- a/solution.py
+++ b/solution.py
@@ -63,7 +63,7 @@
         out_ref[j * LANES : (j + 1) * LANES, :] = dot(onehot, block).astype(bf16)
 
 
-def permute_rows(rows, order, column):
+def permute_rows(rows, order, column, out, mib):
     row_count = order.shape[0]
     step_rows = min(512, row_count)
     return pl.pallas_call(
@@ -77,8 +77,8 @@
             ],
             out_specs=pl.BlockSpec((step_rows, LANES), lambda i, c: (i, 0)),
         ),
-        out_shape=jax.ShapeDtypeStruct((row_count, LANES), bf16),
-        compiler_params=params(32),
+        out_shape=out((row_count, LANES), bf16),
+        compiler_params=params(mib),
         cost_estimate=cost(2 * row_count * row_count * LANES * 4, 3 * row_count * LANES * 2),
         name="permute_rows",
     )(column, order.reshape(row_count // LANES, LANES), rows)
@@ -145,7 +145,7 @@
             scratch_shapes=[pltpu.VMEM((groups, LANES), i32)],
         ),
         out_shape=jax.ShapeDtypeStruct((shards, capacity + INDEX_ROWS, LANES), bf16),
-        compiler_params=params(32),
+        compiler_params=params(60),
         cost_estimate=cost(
             8 * shards * capacity * row_count * LANES, 3 * shards * capacity * LANES * 2
         ),
@@ -184,9 +184,9 @@
         grid=(shards,),
         in_specs=[pl.BlockSpec((1, message, LANES), lambda i: (i, 0, 0))],
         out_specs=pl.BlockSpec((LANES, row_count), lambda i: (0, 0)),
-        out_shape=jax.ShapeDtypeStruct((LANES, row_count), bf16),
+        out_shape=pltpu.VMEM((LANES, row_count), bf16),
         scratch_shapes=[pltpu.VMEM((row_count, LANES), f32)],
-        compiler_params=params(32),
+        compiler_params=params(16),
         cost_estimate=cost(
             8 * shards * message * row_count * LANES, 3 * shards * message * LANES * 2
         ),
@@ -238,8 +238,8 @@
     features = weight.shape[0]
     width = pl.BlockSpec((step_rows, LANES), lambda i, c: (i, 0))
     tall = pl.BlockSpec((LANES, step_rows), lambda i, c: (0, i))
-    normal = lambda t: jax.ShapeDtypeStruct((row_count, LANES), t)
-    turned = jax.ShapeDtypeStruct((LANES, row_count), bf16)
+    normal = lambda t: pltpu.VMEM((row_count, LANES), t)
+    turned = pltpu.VMEM((LANES, row_count), bf16)
     return pl.pallas_call(
         project_body,
         grid_spec=pltpu.PrefetchScalarGridSpec(
@@ -250,10 +250,11 @@
             + [width] * 3
             + [tall] * 4,
         ),
-        out_shape=[jax.ShapeDtypeStruct((row_count, features), bf16)]
-        + [normal(f32), normal(f32), normal(bf16)]
+        out_shape=[pltpu.VMEM((row_count, features), bf16)]
+        + [pltpu.HBM((row_count, LANES), f32)] * 2
+        + [normal(bf16)]
         + [turned] * 4,
-        compiler_params=params(32),
+        compiler_params=params(12),
         cost_estimate=cost(4 * row_count * features * 3 * LANES, row_count * LANES * 40),
         name="project",
     )(column, *blocks, weight)
@@ -332,13 +333,13 @@
             pl.BlockSpec((1, HD * HD, PATCH), per_head),
         ],
         out_shape=[
-            jax.ShapeDtypeStruct((heads, PATCH, PATCH), bf16),
-            jax.ShapeDtypeStruct((LANES, PATCH), bf16),
-            jax.ShapeDtypeStruct((heads, 1, PATCH), f32),
-            jax.ShapeDtypeStruct((heads, HD * HD, PATCH), bf16),
+            pltpu.HBM((heads, PATCH, PATCH), bf16),
+            pltpu.VMEM((LANES, PATCH), bf16),
+            pltpu.VMEM((heads, 1, PATCH), f32),
+            pltpu.HBM((heads, HD * HD, PATCH), bf16),
         ],
         scratch_shapes=[pltpu.SMEM((1,), i32)],
-        compiler_params=params(48),
+        compiler_params=params(28),
         cost_estimate=cost(1600 * elements, 2 * elements, elements),
         name="attention_forward",
     )(keys, base2_t, key_t, value_t)
@@ -362,12 +363,27 @@
     d_key_ref,
     d_value_ref,
     d_attended_ref,
+    exp_all_ref,
+    covariance_all_ref,
+    exp_sems,
+    covariance_sems,
 ):
     head = pl.program_id(0)
     at = pl.multiple_of(head * HD, HD)
 
+    def copies(h):
+        return (
+            pltpu.make_async_copy(exp_ref.at[h], exp_all_ref.at[h], exp_sems.at[h]),
+            pltpu.make_async_copy(
+                covariance_ref.at[h], covariance_all_ref.at[h], covariance_sems.at[h]
+            ),
+        )
+
     @pl.when(head == 0)
     def _():
+        for h in range(LANES // HD):
+            for copy in copies(h):
+                copy.start()
         me = column_ref[0]
         for block, mask in zip((g0_ref, g1_ref, g2_ref, g3_ref), BLOCK_MASKS):
             start = pl.multiple_of((me ^ mask) * LANES, LANES)
@@ -384,14 +400,16 @@
     scaled = grads * inverse
     delta = jnp.sum(scaled * offset, axis=0, keepdims=True)
     features = [scaled[j : j + 1] * query for j in range(HD)] + [delta * query, scaled]
-    sums = dot_rows(jnp.concatenate([f.astype(bf16) for f in features], axis=0), exp_ref[0])
+    for copy in copies(head):
+        copy.wait()
+    sums = dot_rows(jnp.concatenate([f.astype(bf16) for f in features], axis=0), exp_all_ref[head])
     d_value_ref[pl.ds(at, HD), :] = sums[(HD + 1) * HD :].astype(bf16)
     d_key = centered[0:1] * sums[:HD]
-    d_query = grads[0:1] * covariance_ref[0, :HD, :].astype(f32)
+    d_query = grads[0:1] * covariance_all_ref[head, :HD, :].astype(f32)
     for j in range(1, HD):
         rows = slice(j * HD, (j + 1) * HD)
         d_key += centered[j : j + 1] * sums[rows]
-        d_query += grads[j : j + 1] * covariance_ref[0, rows, :].astype(f32)
+        d_query += grads[j : j + 1] * covariance_all_ref[head, rows, :].astype(f32)
     d_key_ref[pl.ds(at, HD), :] = (d_key - sums[HD * HD : (HD + 1) * HD]).astype(bf16)
     d_query_ref[pl.ds(at, HD), :] = (d_query * score_scale).astype(bf16)
 
@@ -403,16 +421,16 @@
     part = pl.BlockSpec((LANES, PATCH), lambda h, c: (0, patch))
     per_head = lambda h, c: (h, 0, 0)
     elements = heads * PATCH * PATCH
-    turned = jax.ShapeDtypeStruct((LANES, PATCH), bf16)
+    turned = pltpu.VMEM((LANES, PATCH), bf16)
     return pl.pallas_call(
         backward_body,
         grid_spec=pltpu.PrefetchScalarGridSpec(
             num_scalar_prefetch=1,
             grid=(heads,),
             in_specs=[
-                pl.BlockSpec((1, PATCH, PATCH), per_head),
+                pl.BlockSpec(memory_space=pltpu.HBM),
                 pl.BlockSpec((1, 1, PATCH), per_head),
-                pl.BlockSpec((1, HD * HD, PATCH), per_head),
+                pl.BlockSpec(memory_space=pltpu.HBM),
                 tall,
                 tall,
                 tall,
@@ -423,10 +441,16 @@
                 pl.BlockSpec(weight_t.shape, lambda h, c: (0, 0)),
             ],
             out_specs=[pl.BlockSpec((features, PATCH), lambda h, c: (0, 0)), tall, tall, tall],
-            scratch_shapes=[pltpu.VMEM((LANES, PATCH), bf16)],
+            scratch_shapes=[
+                pltpu.VMEM((LANES, PATCH), bf16),
+                pltpu.VMEM((heads, PATCH, PATCH), bf16),
+                pltpu.VMEM((heads, HD * HD, PATCH), bf16),
+                pltpu.SemaphoreType.DMA((heads,)),
+                pltpu.SemaphoreType.DMA((heads,)),
+            ],
         ),
-        out_shape=[jax.ShapeDtypeStruct((features, PATCH), bf16), turned, turned, turned],
-        compiler_params=params(48),
+        out_shape=[pltpu.VMEM((features, PATCH), bf16), turned, turned, turned],
+        compiler_params=params(30),
         cost_estimate=cost(1100 * elements, 2 * elements),
         name="attention_backward",
     )(column, weights, inverse, covariance, query_t, value_t, attended, *grads, weight_t)
@@ -454,7 +478,7 @@
     return pl.pallas_call(
         weight_grad_body,
         out_shape=whole((features, 4 * LANES), bf16),
-        compiler_params=params(48),
+        compiler_params=params(12),
         cost_estimate=cost(8 * work, 12 * PATCH * features),
         name="weight_grads",
     )(*patches[0], *patches[1])
@@ -510,11 +534,11 @@
         partial_body,
         in_specs=[pl.BlockSpec(memory_space=pltpu.SMEM)] + [pl.BlockSpec(memory_space=pltpu.VMEM)] * 7,
         out_shape=[
-            whole((2 * LANES, PATCH), bf16),
-            whole((2 * LANES + INDEX_ROWS, PATCH), bf16),
-            whole((2, PATCH), f32),
+            pltpu.VMEM((2 * LANES, PATCH), bf16),
+            pltpu.VMEM((2 * LANES + INDEX_ROWS, PATCH), bf16),
+            pltpu.VMEM((2, PATCH), f32),
         ],
-        compiler_params=params(32),
+        compiler_params=params(12),
         cost_estimate=cost(6 * PATCH * features * LANES, 4 * PATCH * features),
         name="hidden_part",
     )(column, d_query, d_key, d_value, query, key, value, weight)
@@ -533,11 +557,11 @@
     return pl.pallas_call(
         pair_body,
         out_shape=[
-            whole((LANES, PATCH), f32),
-            whole((2, PATCH), f32),
-            whole((LANES + INDEX_ROWS, PATCH), bf16),
+            pltpu.VMEM((LANES, PATCH), f32),
+            pltpu.VMEM((2, PATCH), f32),
+            pltpu.VMEM((LANES + INDEX_ROWS, PATCH), bf16),
         ],
-        compiler_params=params(32),
+        compiler_params=params(6),
         cost_estimate=cost(4 * LANES * PATCH, 16 * LANES * PATCH),
         name="pair_sum",
     )(mine, sums, got)
@@ -568,7 +592,7 @@
         out_specs=pl.BlockSpec((PATCH, LANES), lambda i: (patch, 0)),
         out_shape=whole((patches * PATCH, LANES), f32),
         input_output_aliases={} if before is None else {len(operands) - 1: 0},
-        compiler_params=params(32),
+        compiler_params=params(8),
         cost_estimate=cost(8 * LANES * PATCH, 24 * LANES * PATCH),
         name="points_grad",
     )(*operands)
@@ -601,37 +625,61 @@
     def exchange(rows):
         return lax.all_to_all(rows, "seq", split_axis=0, concat_axis=0, tiled=True)
 
-    def all_columns(rows):
-        across = swap(rows, 2)
-        return (rows, across, swap(rows, 1), swap(across, 1))
-
-    arrived = exchange(permute_rows(scan_points, send_order, column))
+    def after(value, first):
+        return lax.optimization_barrier((value, first))
+
+    def in_hbm(value):
+        return pltpu.with_memory_space_constraint(value, pltpu.HBM)
+
+    arrived = exchange(permute_rows(scan_points, send_order, column, whole, 60))
     buckets = bucket_rows(voxel_grads, voxel_shard, voxel_point, column, shards, capacity)
     got = exchange(buckets.reshape(shards * (capacity + INDEX_ROWS), LANES))
-    projected, forwards = [], []
+    (weight, weight_t), arrived = after((weight, weight_t), arrived)
+    owns = [
+        permute_rows(arrived, arrive_order[p * PATCH : (p + 1) * PATCH], zero, pltpu.VMEM, 8)
+        for p in range(patches)
+    ]
+    across = [swap(own, 2) for own in owns]
+
+    def forward(p):
+        columns = (owns[p], across[p], swap(owns[p], 1), swap(across[p], 1))
+        projected = project(columns, weight, column)
+        return projected, attention_forward(projected[3], projected[4], *projected[6:])
+
+    projected0, forward0 = forward(0)
+    (got, across[1]), forward0 = after((got, across[1]), forward0)
+    summed_rows = segment_rows(got.reshape(shards, capacity + INDEX_ROWS, LANES), local_rows)
+    summed_across = swap(summed_rows, 2)
+    across[1], summed_rows = after(across[1], summed_rows)
+    projected1, forward1 = forward(1)
+    summed_across, forward1 = after(summed_across, forward1)
+    grads = (summed_rows, summed_across, swap(summed_rows, 1), swap(summed_across, 1))
+    forwards = [(projected0, forward0), (projected1, forward1)]
+
+    kept, sums, received, grad_parts = [], [], [], []
     for p in range(patches):
-        own = permute_rows(arrived, arrive_order[p * PATCH : (p + 1) * PATCH], zero)
-        projected.append(project(all_columns(own), weight, column))
-    forwards.append(attention_forward(projected[0][3], projected[0][4], *projected[0][6:]))
-    got, forwards[0] = lax.optimization_barrier((got, forwards[0]))
-    summed_rows = segment_rows(got.reshape(shards, capacity + INDEX_ROWS, LANES), local_rows)
-    projected[1], summed_rows = lax.optimization_barrier((projected[1], summed_rows))
-    grads = all_columns(summed_rows)
-    forwards.append(attention_forward(projected[1][3], projected[1][4], *projected[1][6:]))
-
-    d_points = None
-    grad_parts = []
-    for p in range(patches):
-        hidden, normed, inv_scale, _, _, query_t, key_t, value_t = projected[p]
-        weights, attended, inverse, covariance = forwards[p]
+        (hidden, _, _, _, _, query_t, key_t, value_t), (weights, attended, inverse, covariance) = forwards[p]
+        if p > 0:
+            weights, sent = after(weights, sent)
+            received.append(swap(sent, 2))
         d_out, d_query, d_key, d_value = attention_backward(
             p, weights, inverse, covariance, query_t, value_t, attended, grads, weight_t, column
         )
+        if p > 0:
+            received[p - 1], d_query = after(received[p - 1], d_query)
         grad_parts.append((d_query, d_key, d_value, attended, hidden, d_out))
-        mine, other, sums = hidden_part(d_query, d_key, d_value, query_t, key_t, value_t, weight, column)
-        kept, sums, sent = pair_sum(mine, sums, swap(other, 1))
+        mine, other, own_sums = hidden_part(d_query, d_key, d_value, query_t, key_t, value_t, weight, column)
+        if p == patches - 1:
+            grad_parts, other = after(grad_parts, other)
+        keep, pair_sums, sent = pair_sum(mine, own_sums, swap(other, 1))
+        kept.append(keep)
+        sums.append(pair_sums)
+    received.append(swap(sent, 2))
+    d_points = None
+    for p in range(patches):
+        normed, inv_scale = map(in_hbm, forwards[p][0][1:3])
         d_points = points_grad(
-            p, patches, kept, sums, swap(sent, 2), grads[0], normed, inv_scale, d_points
+            p, patches, kept[p], sums[p], received[p], grads[0], normed, inv_scale, d_points
         )
     parts = exchange(weight_grads(grad_parts)).reshape(shards, features // shards, 4 * LANES)
     summed = jnp.sum(parts.astype(f32), axis=0)

time: 205 us -> 158 us (0.77)
  local copies, waits for them, and re-layouts: 39.6 us -> 11.2 us
  waiting for transfers between devices: 32.6 us -> 19.1 us
    unnamed x129 -> x51, local copies, waits for them, and re-layouts: 38.8 us -> 10.3 us
    ppermute x13, waiting for transfers between devices: 29.2 us -> 17 us  [swap(): return lax.ppermute(rows, 'mp', [(i, i ^ mask) for i in range(members)])]
    pallas_call x2, Pallas kernels: 26.5 us -> 21.2 us  [attention_backward(): pl.pallas_call(backward_body, grid_spec=pltpu.PrefetchScalarGridSpec(num_...]
    pallas_call x2, Pallas kernels: 2.42 us -> 4.86 us  [points_grad(): pl.pallas_call(points_body, grid=(1,), in_specs=in_specs, out_specs=pl.Bl...]
  transfers between devices with their start and end apart: 16 -> 16, of which waited for: 6 -> 7; matrix products, arithmetic and copies ran while one was open for 1% -> 0% of each run, Pallas kernels for 31% -> 52%
where the time goes in v3:
time: 158 us
  Pallas kernels  103 us (65%)
  starting transfers between devices  23.8 us (15%)
  waiting for transfers between devices  19.1 us (12%)
  local copies, waits for them, and re-layouts  11.2 us (7%)
    pallas_call x2, Pallas kernels, attention_forward(): pl.pallas_call(forward_body, grid=(heads,), in_specs=[pl.BlockSpec((PATCH...  37.9 us
    pallas_call x2, Pallas kernels, attention_backward(): pl.pallas_call(backward_body, grid_spec=pltpu.PrefetchScalarGridSpec(num_...  21.2 us
    ppermute x13, waiting for transfers between devices, swap(): return lax.ppermute(rows, 'mp', [(i, i ^ mask) for i in range(members)])  17 us
    all_to_all x3, starting transfers between devices, exchange(): return lax.all_to_all(rows, 'seq', split_axis=0, concat_axis=0, tiled=True)  16.9 us
    pallas_call x1, Pallas kernels, bucket_rows(): pl.pallas_call(functools.partial(bucket_body, shards, capacity), grid_spe...  12.1 us
    unnamed x51, local copies, waits for them, and re-layouts  10.3 us
    pallas_call x3, Pallas kernels, permute_rows(): pl.pallas_call(permute_body, grid_spec=pltpu.PrefetchScalarGridSpec(num_s...  9.02 us
    ppermute x13, starting transfers between devices, swap(): return lax.ppermute(rows, 'mp', [(i, i ^ mask) for i in range(members)])  6.85 us
  transfers between devices with their start and end apart: 16, of which 7 were waited for; matrix products, arithmetic and copies ran while one was open for 0% of the time, Pallas kernels for 52%

profile of v3, /device:TPU:0, one launch (start us, length us, event | category | flops | bytes accessed | tf_op | source)
XLA Modules:
  0.0 157.7 jit_solution(5043999206010407353)
XLA Ops:
  0.7 5.1 %permute_rows.3 = bf16[2048,128]{1,0:T(8,128)(2,1)} custom-call(s32[1]{0:T(128)} %bitcast.column_ref, s32[16,128]{1,0:T(8,128)} %bitcast.26, bf16[2048,512]{1,0:T(8,128)(2,1)} %block_ref.1), custom_call_target="tpu_custom_call" | custom-call | flops 4294967296 | bytes 1572864 | tf_op jit(solution)/shard_map/permute_rows/pallas_call | solution.py:69
  5.8 7.3 %all-to-all-start.1 = ((bf16[8,256,128]{2,1,0:T(8,128)(2,1)}), bf16[8,256,128]{2,1,0:T(8,128)(2,1)S(1)}, u32[]{:S(2)}, u32[]{:S(2)}) async-start(bf16[8,256,128]{2,1,0:T(8,128)(2,1)} %bitcast.25), calls=%async_computation.1 | async-start | bytes 1048576 | tf_op jit(solution)/shard_map/all_to_all | solution.py:626
  13.1 0.1 copy.15
  13.2 0.2 copy.14
  13.4 12.1 %bucket_rows.1 = bf16[8,528,128]{2,1,0:T(8,128)(2,1)} custom-call(s32[1]{0:T(128)} %bitcast.column_ref, s32[16,128]{1,0:T(8,128)} %bitcast.27, s32[16,128]{1,0:T(8,128)} %bitcast.28, bf16[2048,512]{1,0:T(8,128)(2,1)} %grads_ref.1), custom_call_target="tpu_custom_call" | custom-call | flops 8589934592 | bytes 3145728 | tf_op jit(solution)/shard_map/bucket_rows/pallas_call | solution.py:134
  25.5 2.1 %all-to-all-done.1 = bf16[8,256,128]{2,1,0:T(8,128)(2,1)S(1)} async-done(((bf16[8,256,128]{2,1,0:T(8,128)(2,1)}), bf16[8,256,128]{2,1,0:T(8,128)(2,1)S(1)}, u32[]{:S(2)}, u32[]{:S(2)}) %all-to-all-start.1) | async-done | bytes 524320 | tf_op jit(solution)/shard_map/all_to_all | solution.py:626
  27.5 3.9 %all-to-all-start = ((bf16[8,528,128]{2,1,0:T(8,128)(2,1)}), bf16[8,528,128]{2,1,0:T(8,128)(2,1)S(1)}, u32[]{:S(2)}, u32[]{:S(2)}) async-start(bf16[8,528,128]{2,1,0:T(8,128)(2,1)} %bucket_rows.1), calls=%async_computation | async-start | bytes 2162688 | tf_op jit(solution)/shard_map/all_to_all | solution.py:626
  31.5 1.6 %permute_rows.5.x0_ref = bf16[1024,128]{1,0:T(8,128)(2,1)S(1)} custom-call(s32[1]{0:T(128)} %constant.1.clone.1.column_ref, s32[8,128]{1,0:T(8,128)S(1)} %get-tuple-element.160.order_ref, bf16[2048,128]{1,0:T(8,128)(2,1)S(1)} %bitcast.20), custom_call_target="tpu_custom_call" | custom-call | flops 1073741824 | bytes 786432 | tf_op jit(solution)/shard_map/permute_rows/pallas_call | solution.py:69
  33.1 1.6 collective-permute-start.1
  34.7 0.0 collective-permute-start.2
  34.7 6.1 %collective-permute-done.1.x1_ref = bf16[1024,128]{1,0:T(8,128)(2,1)S(1)} collective-permute-done((bf16[1024,128]{1,0:T(8,128)(2,1)S(1)}, bf16[1024,128]{1,0:T(8,128)(2,1)S(1)}, u32[]{:S(2)}, u32[]{:S(2)}) %collective-permute-start.1) | collective-permute-done | bytes 262176 | tf_op jit(solution)/shard_map/ppermute | solution.py:623
  40.8 2.3 %permute_rows.4.x0_ref = bf16[1024,128]{1,0:T(8,128)(2,1)} custom-call(s32[1]{0:T(128)} %constant.1.clone.1.column_ref, s32[8,128]{1,0:T(8,128)S(1)} %get-tuple-element.161.order_ref, bf16[2048,128]{1,0:T(8,128)(2,1)S(1)} %bitcast.21), custom_call_target="tpu_custom_call" | custom-call | flops 1073741824 | bytes 786432 | tf_op jit(solution)/shard_map/permute_rows/pallas_call | solution.py:69
  43.1 0.5 collective-permute-start.5
  43.6 1.5 collective-permute-start
  45.1 0.2 copy.16.weight_ref
  45.4 0.7 copy-done.15
  46.1 0.0 collective-permute-done.3.x3_ref
  46.1 0.7 copy-done.17
  46.8 0.9 copy-done.14
  47.7 0.9 copy-done.16
  48.7 0.9 copy-done.18
  49.6 2.6 %project.2 = (bf16[1024,512]{1,0:T(8,128)(2,1)S(1)}, f32[1024,128]{1,0:T(8,128)}, f32[1024,128]{1,0:T(8,128)}, bf16[1024,128]{1,0:T(8,128)(2,1)S(1)}, bf16[128,1...) custom-call(s32[1]{0:T(128)} %bitcast.column_ref, ...), custom_call_target="tpu_custom_call" | custom-call | flops 805306368 | bytes 5242880 | tf_op jit(solution)/shard_map/project/pallas_call | solution.py:243
  52.2 18.9 %attention_forward.2 = (bf16[8,1024,1024]{2,1,0:T(8,128)(2,1)}, bf16[128,1024]{1,0:T(8,128)(2,1)S(1)}, f32[8,1,1024]{2,1,0:T(1,128)S(1)}, bf16[8,256,1024]{2,1,0:T(8,128)(2,1)}) custom-call(bf16[1024,128]{1,0:T(8,128)(2,1)S(1)} %get-tuple-element.82.key_ref, bf16[128,1024]{1,0:T(8,128)(2,1)S(1)} %get-tuple-element.83.base2_t_ref, ...), custom_call_target="tpu_custom_call" | custom-call | flops 13421772800 | bytes 16777216 | tf_op jit(solution)/shard_map/attention_forward/pallas_call | solution.py:325
  71.1 0.7 copy-done.8
  71.8 0.0 collective-permute-done.x1_ref
  71.8 0.0 all-to-all-done
  71.9 0.7 copy-done.11
  72.6 6.7 %segment_rows.1.g0_ref.d_out_ref = bf16[128,2048]{1,0:T(8,128)(2,1)S(1)} custom-call(bf16[8,528,128]{2,1,0:T(8,128)(2,1)S(1)} %all-to-all-done), custom_call_target="tpu_custom_call" | custom-call | flops 8858370048 | bytes 3244032 | tf_op jit(solution)/shard_map/segment_rows/pallas_call | solution.py:182
  79.3 0.1 collective-permute-start.6
  79.3 0.6 collective-permute-start.4
  79.9 0.2 collective-permute-start.7
  80.1 0.0 collective-permute-done.5.x2_ref
  80.1 0.8 collective-permute-done.6.x3_ref
  80.9 3.5 %project.3 = (bf16[1024,512]{1,0:T(8,128)(2,1)S(1)}, f32[1024,128]{1,0:T(8,128)}, f32[1024,128]{1,0:T(8,128)}, bf16[1024,128]{1,0:T(8,128)(2,1)S(1)}, bf16[128,1...) custom-call(s32[1]{0:T(128)} %bitcast.column_ref, ...), custom_call_target="tpu_custom_call" | custom-call | flops 805306368 | bytes 5242880 | tf_op jit(solution)/shard_map/project/pallas_call | solution.py:243
  84.4 19.0 %attention_forward.3 = (bf16[8,1024,1024]{2,1,0:T(8,128)(2,1)}, bf16[128,1024]{1,0:T(8,128)(2,1)S(1)}, f32[8,1,1024]{2,1,0:T(1,128)S(1)}, bf16[8,256,1024]{2,1,0:T(8,128)(2,1)}) custom-call(bf16[1024,128]{1,0:T(8,128)(2,1)S(1)} %get-tuple-element.93.key_ref, bf16[128,1024]{1,0:T(8,128)(2,1)S(1)} %get-tuple-element.94.base2_t_ref, ...), custom_call_target="tpu_custom_call" | custom-call | flops 13421772800 | bytes 16777216 | tf_op jit(solution)/shard_map/attention_forward/pallas_call | solution.py:325
  103.4 0.0 collective-permute-done.4.g1_ref
  103.4 0.1 collective-permute-start.8
  103.5 0.0 collective-permute-done.7.g2_ref
  103.5 1.8 %collective-permute-done.8.g3_ref = bf16[128,2048]{1,0:T(8,128)(2,1)S(1)} collective-permute-done((bf16[128,2048]{1,0:T(8,128)(2,1)S(1)}, bf16[128,2048]{1,0:T(8,128)(2,1)S(1)}, u32[]{:S(2)}, u32[]{:S(2)}) %collective-permute-start.8) | collective-permute-done | bytes 524320 | tf_op jit(solution)/shard_map/ppermute | solution.py:623
  105.3 10.8 %attention_backward.2 = (bf16[512,1024]{1,0:T(8,128)(2,1)S(1)}, bf16[128,1024]{1,0:T(8,128)(2,1)S(1)}, bf16[128,1024]{1,0:T(8,128)(2,1)S(1)}, bf16[128,1024]{1,0:T(8,128)(2,1)S(1)}) custom-call(s32[1]{0:T(128)} %bitcast.column_ref, bf16[8,1024,1024]{2,1,0:T(8,128)(2,1)} %get-tuple-element.102.exp_ref, f32[8,1,1024]{2,1,0:T(1,128)S(1)} %get-tuple-element.103.inverse_ref, ...), custom_call_target="tpu_custom_call" | custom-call | flops 9227468800 | bytes 16777216 | tf_op jit(solution)/shard_map/attention_backward/pallas_call | solution.py:425
  116.1 1.0 hidden_part.2
  117.1 0.2 collective-permute-start.9
  117.4 1.8 %collective-permute-done.9.got_ref = bf16[272,1024]{1,0:T(8,128)(2,1)S(1)} collective-permute-done((bf16[272,1024]{1,0:T(8,128)(2,1)S(1)}, bf16[272,1024]{1,0:T(8,128)(2,1)S(1)}, u32[]{:S(2)}, u32[]{:S(2)}) %collective-permute-start.9) | collective-permute-done | bytes 557088 | tf_op jit(solution)/shard_map/ppermute | solution.py:623
  119.2 0.1 pair_sum.2
  119.3 0.8 copy-done.2
  120.1 0.8 collective-permute-start.10
  120.9 10.4 %attention_backward.3 = (bf16[512,1024]{1,0:T(8,128)(2,1)S(1)}, bf16[128,1024]{1,0:T(8,128)(2,1)S(1)}, bf16[128,1024]{1,0:T(8,128)(2,1)S(1)}, bf16[128,1024]{1,0:T(8,128)(2,1)S(1)}) custom-call(s32[1]{0:T(128)} %bitcast.column_ref, bf16[8,1024,1024]{2,1,0:T(8,128)(2,1)} %get-tuple-element.118.exp_ref, f32[8,1,1024]{2,1,0:T(1,128)S(1)} %get-tuple-element.119.inverse_ref, ...), custom_call_target="tpu_custom_call" | custom-call | flops 9227468800 | bytes 16777216 | tf_op jit(solution)/shard_map/attention_backward/pallas_call | solution.py:425
  131.3 0.0 collective-permute-done.10.got_ref
  131.3 1.0 hidden_part.3
  132.3 0.8 copy-done
  133.1 2.6 %weight_grads.1 = bf16[512,512]{1,0:T(8,128)(2,1)} custom-call(bf16[128,1024]{1,0:T(8,128)(2,1)S(1)} %get-tuple-element.145.d_query_ref.refs_0_, bf16[128,1024]{1,0:T(8,128)(2,1)S(1)} %get-tuple-element.146.d_key_ref.refs_1_, bf16[128,1024]{1,0:T(8,128)(2,1)S(1)} %get-tuple-element.147.d_value_ref.refs_2_, bf16[128,1024]{1,0:T(8,128)(2,1)S(1)} %copy-done.9, ...), custom_call_target="tpu_custom_call" | custom-call | flops 1073741824 | bytes 6291456 | tf_op jit(solution)/shard_map/weight_grads/pallas_call | solution.py:478
  135.7 5.7 %all-to-all-start.2 = ((bf16[8,64,512]{2,1,0:T(8,128)(2,1)}), bf16[8,64,512]{2,1,0:T(8,128)(2,1)S(1)}, u32[]{:S(2)}, u32[]{:S(2)}) async-start(bf16[8,64,512]{2,1,0:T(8,128)(2,1)} %bitcast.12), calls=%async_computation.2 | async-start | bytes 1048576 | tf_op jit(solution)/shard_map/all_to_all | solution.py:626
  141.5 0.0 collective-permute-start.11
  141.5 2.2 %collective-permute-done.11.got_ref = bf16[272,1024]{1,0:T(8,128)(2,1)S(1)} collective-permute-done((bf16[272,1024]{1,0:T(8,128)(2,1)}, bf16[272,1024]{1,0:T(8,128)(2,1)S(1)}, u32[]{:S(2)}, u32[]{:S(2)}) %collective-permute-start.11) | collective-permute-done | bytes 557088 | tf_op jit(solution)/shard_map/ppermute | solution.py:623
  143.6 1.0 copy-done.1
  144.7 0.1 pair_sum.3
  144.8 1.3 collective-permute-start.12
  146.1 1.0 copy-done.3
  147.2 2.4 %points_grad.2.rest_0_ = f32[2048,128]{1,0:T(8,128)} custom-call(f32[128,1024]{1,0:T(8,128)S(1)} %copy-done.3, f32[2,1024]{1,0:T(2,128)S(1)} %get-tuple-element.141.sums_ref, bf16[144,1024]{1,0:T(8,128)(2,1)S(1)} %collective-permute-done.10.got_ref, bf16[128,2048]{1,0:T(8,128)(2,1)S(1)} %segment_rows.1.g0_ref.d_out_ref, ...), custom_call_target="tpu_custom_call" | custom-call | flops 1048576 | bytes 3145728 | tf_op jit(solution)/shard_map/points_grad/pallas_call | solution.py:588
  149.6 4.3 %collective-permute-done.12.got_ref = bf16[144,1024]{1,0:T(8,128)(2,1)S(1)} collective-permute-done((bf16[144,1024]{1,0:T(8,128)(2,1)S(1)}, bf16[144,1024]{1,0:T(8,128)(2,1)S(1)}, u32[]{:S(2)}, u32[]{:S(2)}) %collective-permute-start.12) | collective-permute-done | bytes 294944 | tf_op jit(solution)/shard_map/ppermute | solution.py:623
  153.9 2.4 %points_grad.3 = f32[2048,128]{1,0:T(8,128)} custom-call(f32[128,1024]{1,0:T(8,128)S(1)} %get-tuple-element.135.kept_ref, f32[2,1024]{1,0:T(2,128)S(1)} %get-tuple-element.136.sums_ref, bf16[144,1024]{1,0:T(8,128)(2,1)S(1)} %collective-permute-done.12.got_ref, bf16[128,2048]{1,0:T(8,128)(2,1)S(1)} %segment_rows.1.g0_ref.d_out_ref, ...), custom_call_target="tpu_custom_call", output_to_operand_aliasing={{}: (6, {})} | custom-call | flops 1048576 | bytes 3145728 | tf_op jit(solution)/shard_map/points_grad/pallas_call | solution.py:588
  156.4 0.1 convert_reduce_fusion
  156.4 0.6 slice.39
  157.1 0.6 copy_bitcast_fusion
  (41 shorter events, 0.1 us)
Async XLA Ops:
  0.6 12.4 %copy-start.23 = (s32[2048]{0:T(1024)S(1)}, s32[2048]{0:T(1024)}, u32[]{:S(2)}) copy-start(s32[2048]{0:T(1024)} %param.10) | copy-start | bytes 24580
  0.6 12.4 %copy-start.22 = (bf16[512,128]{1,0:T(8,128)(2,1)S(1)}, bf16[512,128]{1,0:T(8,128)(2,1)}, u32[]{:S(2)}) copy-start(bf16[512,128]{1,0:T(8,128)(2,1)} %param.12) | copy-start | bytes 393220
  0.7 12.5 %copy-start.21 = (bf16[512,3,128]{2,0,1:T(8,128)(2,1)S(1)}, bf16[512,3,128]{2,0,1:T(8,128)(2,1)}, u32[]{:S(2)}) copy-start(bf16[512,3,128]{2,0,1:T(8,128)(2,1)} %param.11) | copy-start | bytes 1179652
  5.8 21.7 %all-to-all-start.1 = ((bf16[8,256,128]{2,1,0:T(8,128)(2,1)}), bf16[8,256,128]{2,1,0:T(8,128)(2,1)S(1)}, u32[]{:S(2)}, u32[]{:S(2)}) async-start(bf16[8,256,128]{2,1,0:T(8,128)(2,1)} %bitcast.25), calls=%async_computation.1 | async-start | bytes 1048576 | tf_op jit(solution)/shard_map/all_to_all | solution.py:626
  27.5 44.3 %all-to-all-start = ((bf16[8,528,128]{2,1,0:T(8,128)(2,1)}), bf16[8,528,128]{2,1,0:T(8,128)(2,1)S(1)}, u32[]{:S(2)}, u32[]{:S(2)}) async-start(bf16[8,528,128]{2,1,0:T(8,128)(2,1)} %bucket_rows.1), calls=%async_computation | async-start | bytes 2162688 | tf_op jit(solution)/shard_map/all_to_all | solution.py:626
  33.1 7.7 %collective-permute-start.1 = (bf16[1024,128]{1,0:T(8,128)(2,1)S(1)}, bf16[1024,128]{1,0:T(8,128)(2,1)S(1)}, u32[]{:S(2)}, u32[]{:S(2)}) collective-permute-start(bf16[1024,128]{1,0:T(8,128)(2,1)S(1)} %permute_rows.5.x0_ref), channel_id=1, source_target_pairs={{0,2},{1,3},{2,0},{3,1},{4,6},{5,7},{6,4},{7,5},{8,10},{9,11},{10,... | collective-permute-start | bytes 786440 | tf_op jit(solution)/shard_map/ppermute | solution.py:623
  34.7 10.7 %collective-permute-start.2 = (bf16[1024,128]{1,0:T(8,128)(2,1)S(1)}, bf16[1024,128]{1,0:T(8,128)(2,1)S(1)}, u32[]{:S(2)}, u32[]{:S(2)}) collective-permute-start(bf16[1024,128]{1,0:T(8,128)(2,1)S(1)} %permute_rows.5.x0_ref), channel_id=1, source_target_pairs={{0,1},{1,0},{2,3},{3,2},{4,5},{5,4},{6,7},{7,6},{8,9},{9,8},{10,11... | collective-permute-start | bytes 786440 | tf_op jit(solution)/shard_map/ppermute | solution.py:623
  40.8 4.5 %copy-start.13 = (bf16[1024,128]{1,0:T(8,128)(2,1)}, bf16[1024,128]{1,0:T(8,128)(2,1)S(1)}, u32[]{:S(2)}) copy-start(bf16[1024,128]{1,0:T(8,128)(2,1)S(1)} %collective-permute-done.1.x1_ref) | copy-start | bytes 786436
  40.8 5.3 %collective-permute-start.3 = (bf16[1024,128]{1,0:T(8,128)(2,1)S(1)}, bf16[1024,128]{1,0:T(8,128)(2,1)S(1)}, u32[]{:S(2)}, u32[]{:S(2)}) collective-permute-start(bf16[1024,128]{1,0:T(8,128)(2,1)S(1)} %collective-permute-done.1.x1_ref), channel_id=1, source_target_pairs={{0,1},{1,0},{2,3},{3,2},{4,5},{5,4},{6,7},{7,6},{8,9},{9,8},{10,11... | collective-permute-start | bytes 786440 | tf_op jit(solution)/shard_map/ppermute | solution.py:623
  43.1 37.0 %collective-permute-start.5 = (bf16[1024,128]{1,0:T(8,128)(2,1)}, bf16[1024,128]{1,0:T(8,128)(2,1)}, u32[]{:S(2)}, u32[]{:S(2)}) collective-permute-start(bf16[1024,128]{1,0:T(8,128)(2,1)} %permute_rows.4.x0_ref), channel_id=1, source_target_pairs={{0,1},{1,0},{2,3},{3,2},{4,5},{5,4},{6,7},{7,6},{8,9},{9,8},{10,11... | collective-permute-start | bytes 786440 | tf_op jit(solution)/shard_map/ppermute | solution.py:623
  43.6 28.3 %collective-permute-start = (bf16[1024,128]{1,0:T(8,128)(2,1)}, bf16[1024,128]{1,0:T(8,128)(2,1)S(1)}, u32[]{:S(2)}, u32[]{:S(2)}) collective-permute-start(bf16[1024,128]{1,0:T(8,128)(2,1)} %permute_rows.4.x0_ref), channel_id=1, source_target_pairs={{0,2},{1,3},{2,0},{3,1},{4,6},{5,7},{6,4},{7,5},{8,10},{9,11},{10,... | collective-permute-start | bytes 786440 | tf_op jit(solution)/shard_map/ppermute | solution.py:623
  45.4 0.7 copy-start.15
  46.1 0.7 copy-start.17
  46.8 0.9 copy-start.14
  47.7 0.9 copy-start.16
  48.7 0.9 copy-start.18
  52.2 18.9 %copy-start.4 = (bf16[128,1024]{1,0:T(8,128)(2,1)}, bf16[128,1024]{1,0:T(8,128)(2,1)S(1)}, u32[]{:S(2)}) copy-start(bf16[128,1024]{1,0:T(8,128)(2,1)S(1)} %get-tuple-element.84.key_t_ref.key_ref) | copy-start | bytes 786436
  52.2 18.9 %copy-start.6 = (bf16[128,1024]{1,0:T(8,128)(2,1)}, bf16[128,1024]{1,0:T(8,128)(2,1)S(1)}, u32[]{:S(2)}) copy-start(bf16[128,1024]{1,0:T(8,128)(2,1)S(1)} %get-tuple-element.85.value_t_ref.value_ref) | copy-start | bytes 786436
  71.1 0.7 copy-start.8
  71.8 0.7 copy-start.11
  72.6 6.7 %copy-start.12 = (bf16[1024,128]{1,0:T(8,128)(2,1)S(1)}, bf16[1024,128]{1,0:T(8,128)(2,1)}, u32[]{:S(2)}) copy-start(bf16[1024,128]{1,0:T(8,128)(2,1)} %copy-done.11) | copy-start | bytes 786436
  79.3 1.6 %collective-permute-start.6 = (bf16[1024,128]{1,0:T(8,128)(2,1)S(1)}, bf16[1024,128]{1,0:T(8,128)(2,1)S(1)}, u32[]{:S(2)}, u32[]{:S(2)}) collective-permute-start(bf16[1024,128]{1,0:T(8,128)(2,1)S(1)} %copy-done.12), channel_id=1, source_target_pairs={{0,1},{1,0},{2,3},{3,2},{4,5},{5,4},{6,7},{7,6},{8,9},{9,8},{10,11... | collective-permute-start | bytes 786440 | tf_op jit(solution)/shard_map/ppermute | solution.py:623
  79.3 24.0 %collective-permute-start.4 = (bf16[128,2048]{1,0:T(8,128)(2,1)S(1)}, bf16[128,2048]{1,0:T(8,128)(2,1)S(1)}, u32[]{:S(2)}, u32[]{:S(2)}) collective-permute-start(bf16[128,2048]{1,0:T(8,128)(2,1)S(1)} %segment_rows.1.g0_ref.d_out_ref), channel_id=1, source_target_pairs={{0,2},{1,3},{2,0},{3,1},{4,6},{5,7},{6,4},{7,5},{8,10},{9,11},{10,... | collective-permute-start | bytes 1572872 | tf_op jit(solution)/shard_map/ppermute | solution.py:623
  79.9 23.6 %collective-permute-start.7 = (bf16[128,2048]{1,0:T(8,128)(2,1)S(1)}, bf16[128,2048]{1,0:T(8,128)(2,1)S(1)}, u32[]{:S(2)}, u32[]{:S(2)}) collective-permute-start(bf16[128,2048]{1,0:T(8,128)(2,1)S(1)} %segment_rows.1.g0_ref.d_out_ref), channel_id=1, source_target_pairs={{0,1},{1,0},{2,3},{3,2},{4,5},{5,4},{6,7},{7,6},{8,9},{9,8},{10,11... | collective-permute-start | bytes 1572872 | tf_op jit(solution)/shard_map/ppermute | solution.py:623
  84.3 20.9 %copy-start.7 = (bf16[128,1024]{1,0:T(8,128)(2,1)S(1)}, bf16[128,1024]{1,0:T(8,128)(2,1)}, u32[]{:S(2)}) copy-start(bf16[128,1024]{1,0:T(8,128)(2,1)} %copy-done.6) | copy-start | bytes 786436
  84.4 20.9 %copy-start.9 = (bf16[128,1024]{1,0:T(8,128)(2,1)S(1)}, bf16[128,1024]{1,0:T(8,128)(2,1)}, u32[]{:S(2)}) copy-start(bf16[128,1024]{1,0:T(8,128)(2,1)} %copy-done.8) | copy-start | bytes 786436
  84.4 20.9 %copy-start.19 = (bf16[8,256,1024]{2,1,0:T(8,128)(2,1)S(1)}, bf16[8,256,1024]{2,1,0:T(8,128)(2,1)}, u32[]{:S(2)}) copy-start(bf16[8,256,1024]{2,1,0:T(8,128)(2,1)} %get-tuple-element.104.covariance_ref) | copy-start | bytes 12582916
  103.4 1.9 %collective-permute-start.8 = (bf16[128,2048]{1,0:T(8,128)(2,1)S(1)}, bf16[128,2048]{1,0:T(8,128)(2,1)S(1)}, u32[]{:S(2)}, u32[]{:S(2)}) collective-permute-start(bf16[128,2048]{1,0:T(8,128)(2,1)S(1)} %collective-permute-done.4.g1_ref), channel_id=1, source_target_pairs={{0,1},{1,0},{2,3},{3,2},{4,5},{5,4},{6,7},{7,6},{8,9},{9,8},{10,11... | collective-permute-start | bytes 1572872 | tf_op jit(solution)/shard_map/ppermute | solution.py:623
  105.3 10.8 %copy-start.5 = (bf16[128,1024]{1,0:T(8,128)(2,1)S(1)}, bf16[128,1024]{1,0:T(8,128)(2,1)}, u32[]{:S(2)}) copy-start(bf16[128,1024]{1,0:T(8,128)(2,1)} %copy-done.4) | copy-start | bytes 786436
  105.3 15.6 %copy-start.20 = (bf16[8,256,1024]{2,1,0:T(8,128)(2,1)S(1)}, bf16[8,256,1024]{2,1,0:T(8,128)(2,1)}, u32[]{:S(2)}) copy-start(bf16[8,256,1024]{2,1,0:T(8,128)(2,1)} %get-tuple-element.120.covariance_ref) | copy-start | bytes 12582916
  117.1 2.0 %collective-permute-start.9 = (bf16[272,1024]{1,0:T(8,128)(2,1)S(1)}, bf16[272,1024]{1,0:T(8,128)(2,1)S(1)}, u32[]{:S(2)}, u32[]{:S(2)}) collective-permute-start(bf16[272,1024]{1,0:T(8,128)(2,1)S(1)} %get-tuple-element.115), channel_id=1, source_target_pairs={{0,1},{1,0},{2,3},{3,2},{4,5},{5,4},{6,7},{7,6},{8,9},{9,8},{10,11... | collective-permute-start | bytes 1671176 | tf_op jit(solution)/shard_map/ppermute | solution.py:623
  119.3 0.8 copy-start.2
  120.1 11.2 %collective-permute-start.10 = (bf16[144,1024]{1,0:T(8,128)(2,1)S(1)}, bf16[144,1024]{1,0:T(8,128)(2,1)S(1)}, u32[]{:S(2)}, u32[]{:S(2)}) collective-permute-start(bf16[144,1024]{1,0:T(8,128)(2,1)S(1)} %get-tuple-element.117), channel_id=1, source_target_pairs={{0,2},{1,3},{2,0},{3,1},{4,6},{5,7},{6,4},{7,5},{8,10},{9,11},{10,... | collective-permute-start | bytes 884744 | tf_op jit(solution)/shard_map/ppermute | solution.py:623
  132.3 0.8 copy-start
  133.1 2.6 %copy-start.10 = (bf16[272,1024]{1,0:T(8,128)(2,1)}, bf16[272,1024]{1,0:T(8,128)(2,1)S(1)}, u32[]{:S(2)}) copy-start(bf16[272,1024]{1,0:T(8,128)(2,1)S(1)} %get-tuple-element.134) | copy-start | bytes 1671172
  135.7 20.6 %all-to-all-start.2 = ((bf16[8,64,512]{2,1,0:T(8,128)(2,1)}), bf16[8,64,512]{2,1,0:T(8,128)(2,1)S(1)}, u32[]{:S(2)}, u32[]{:S(2)}) async-start(bf16[8,64,512]{2,1,0:T(8,128)(2,1)} %bitcast.12), calls=%async_computation.2 | async-start | bytes 1048576 | tf_op jit(solution)/shard_map/all_to_all | solution.py:626
  141.5 2.2 %collective-permute-start.11 = (bf16[272,1024]{1,0:T(8,128)(2,1)}, bf16[272,1024]{1,0:T(8,128)(2,1)S(1)}, u32[]{:S(2)}, u32[]{:S(2)}) collective-permute-start(bf16[272,1024]{1,0:T(8,128)(2,1)} %copy-done.10), channel_id=1, source_target_pairs={{0,1},{1,0},{2,3},{3,2},{4,5},{5,4},{6,7},{7,6},{8,9},{9,8},{10,11... | collective-permute-start | bytes 1671176 | tf_op jit(solution)/shard_map/ppermute | solution.py:623
  143.6 1.0 copy-start.1
  144.8 9.1 %collective-permute-start.12 = (bf16[144,1024]{1,0:T(8,128)(2,1)S(1)}, bf16[144,1024]{1,0:T(8,128)(2,1)S(1)}, u32[]{:S(2)}, u32[]{:S(2)}) collective-permute-start(bf16[144,1024]{1,0:T(8,128)(2,1)S(1)} %get-tuple-element.137), channel_id=1, source_target_pairs={{0,2},{1,3},{2,0},{3,1},{4,6},{5,7},{6,4},{7,5},{8,10},{9,11},{10,... | collective-permute-start | bytes 884744 | tf_op jit(solution)/shard_map/ppermute | solution.py:623
  146.1 1.0 copy-start.3

commit v4 on v3

--- a/solution.py
+++ b/solution.py
@@ -50,21 +50,31 @@
 
 def permute_body(column_ref, order_ref, block_ref, out_ref):
     step = pl.program_id(0)
-    source_rows = block_ref.shape[0]
+    half = block_ref.shape[0] // 2
     chunks = out_ref.shape[0] // LANES
     lane = lax.broadcasted_iota(i32, (LANES, LANES), 1)
-    block = block_ref[...]
+    sides = jnp.concatenate([block_ref[:half, :], block_ref[half:, :]], axis=1)
+    onehots, lows = [], []
     for j in range(chunks):
         wanted = order_ref[pl.ds(step * chunks + j, 1), :].astype(f32)
         wanted = jnp.broadcast_to(wanted, (LANES, LANES)).T.astype(i32)
-        onehot = jnp.concatenate(
-            [ones_where(wanted == lane + k * LANES) for k in range(source_rows // LANES)], axis=1
+        low = wanted < half
+        local_row = jnp.where(low, wanted, wanted - half)
+        onehots.append(
+            jnp.concatenate(
+                [ones_where(local_row == lane + k * LANES) for k in range(half // LANES)], axis=1
+            )
         )
-        out_ref[j * LANES : (j + 1) * LANES, :] = dot(onehot, block).astype(bf16)
-
-
-def permute_rows(rows, order, column, out, mib):
-    row_count = order.shape[0]
+        lows.append(low)
+    both = dot(jnp.concatenate(onehots, axis=0), sides)
+    for j in range(chunks):
+        rows = slice(j * LANES, (j + 1) * LANES)
+        out_ref[rows, :] = jnp.where(lows[j], both[rows, :LANES], both[rows, LANES:]).astype(bf16)
+
+
+def permute_rows(rows, order, column, part, parts, out, mib):
+    row_count = order.shape[0] // parts
+    groups = row_count // LANES
     step_rows = min(512, row_count)
     return pl.pallas_call(
         permute_body,
@@ -72,7 +82,7 @@
             num_scalar_prefetch=1,
             grid=(row_count // step_rows,),
             in_specs=[
-                pl.BlockSpec((row_count // LANES, LANES), lambda i, c: (0, 0)),
+                pl.BlockSpec((groups, LANES), lambda i, c: (part, 0)),
                 pl.BlockSpec((rows.shape[0], LANES), lambda i, c: (0, c[0])),
             ],
             out_specs=pl.BlockSpec((step_rows, LANES), lambda i, c: (i, 0)),
@@ -81,7 +91,7 @@
         compiler_params=params(mib),
         cost_estimate=cost(2 * row_count * row_count * LANES * 4, 3 * row_count * LANES * 2),
         name="permute_rows",
-    )(column, order.reshape(row_count // LANES, LANES), rows)
+    )(column, order.reshape(parts * groups, LANES), rows)
 
 
 def bucket_body(shards, capacity, column_ref, shard_ref, point_ref, grads_ref, out_ref, place_ref):
@@ -157,12 +167,21 @@
     step = pl.program_id(0)
     capacity = got_ref.shape[1] - INDEX_ROWS
     chunks = capacity // LANES
-    row_count = total_ref.shape[0]
+    half = total_ref.shape[0]
     digits = got_ref[0, capacity:, :].astype(f32)
-    index = (digits[:chunks] * float(INDEX_BASE) + digits[chunks : 2 * chunks]).astype(i32)
-    row = lax.broadcasted_iota(i32, (row_count, LANES), 0)
-    onehot = jnp.concatenate([ones_where(index[j : j + 1] == row) for j in range(chunks)], axis=1)
-    part = dot(onehot, got_ref[0, :capacity, :])
+    index = digits[:chunks] * float(INDEX_BASE) + digits[chunks : 2 * chunks]
+    position = index.astype(i32)
+    local_row = jnp.where(position < half, position, position - half)
+    row = lax.broadcasted_iota(i32, (half, LANES), 0)
+    onehot = jnp.concatenate([ones_where(local_row[j : j + 1] == row) for j in range(chunks)], axis=1)
+    sides = []
+    for j in range(chunks):
+        low = jnp.broadcast_to(index[j : j + 1], (LANES, LANES)).T < float(half)
+        rows = got_ref[0, j * LANES : (j + 1) * LANES, :].astype(f32)
+        sides.append(
+            jnp.concatenate([jnp.where(low, rows, 0.0), jnp.where(low, 0.0, rows)], axis=1).astype(bf16)
+        )
+    part = dot(onehot, jnp.concatenate(sides, axis=0))
 
     @pl.when(step == 0)
     def _():
@@ -174,7 +193,8 @@
 
     @pl.when(step == pl.num_programs(0) - 1)
     def _():
-        out_ref[...] = total_ref[...].T.astype(bf16)
+        out_ref[:, :half] = total_ref[:, :LANES].T.astype(bf16)
+        out_ref[:, half:] = total_ref[:, LANES:].T.astype(bf16)
 
 
 def segment_rows(got, row_count):
@@ -185,7 +205,7 @@
         in_specs=[pl.BlockSpec((1, message, LANES), lambda i: (i, 0, 0))],
         out_specs=pl.BlockSpec((LANES, row_count), lambda i: (0, 0)),
         out_shape=pltpu.VMEM((LANES, row_count), bf16),
-        scratch_shapes=[pltpu.VMEM((row_count, LANES), f32)],
+        scratch_shapes=[pltpu.VMEM((row_count // 2, 2 * LANES), f32)],
         compiler_params=params(16),
         cost_estimate=cost(
             8 * shards * message * row_count * LANES, 3 * shards * message * LANES * 2
@@ -218,12 +238,13 @@
     squares = [c * c for c in centered]
     var = jnp.sum(squares[0] + squares[1] + (squares[2] + squares[3]), axis=1, keepdims=True) / features
     inv = lax.rsqrt(var + epsilon)
-    normed_ref[...] = centered[0] * inv
-    inv_ref[...] = jnp.broadcast_to(inv, inv_ref.shape)
+    normed_ref[...] = (centered[0] * inv).T
+    inv_ref[...] = jnp.broadcast_to(inv, centered[0].shape).T[:8]
     for block, mask in zip(centered, BLOCK_MASKS):
         at = pl.multiple_of((me ^ mask) * LANES, LANES)
         hidden_ref[:, pl.ds(at, LANES)] = (block * inv).astype(bf16)
-    projected = dot(hidden_ref[...], weight_ref[...]).astype(bf16)
+    weight = jnp.concatenate([weight_ref[t] for t in range(3)], axis=1)
+    projected = dot(hidden_ref[...], weight).astype(bf16)
     key_ref[...] = projected[:, LANES : 2 * LANES]
     query = projected[:, :LANES].astype(f32).T * score_scale
     query_t_ref[...] = query.astype(bf16)
@@ -235,7 +256,7 @@
 def project(blocks, weight, column):
     row_count = blocks[0].shape[0]
     step_rows = 512
-    features = weight.shape[0]
+    features = weight.shape[1]
     width = pl.BlockSpec((step_rows, LANES), lambda i, c: (i, 0))
     tall = pl.BlockSpec((LANES, step_rows), lambda i, c: (0, i))
     normal = lambda t: pltpu.VMEM((row_count, LANES), t)
@@ -245,13 +266,17 @@
         grid_spec=pltpu.PrefetchScalarGridSpec(
             num_scalar_prefetch=1,
             grid=(row_count // step_rows,),
-            in_specs=[width] * 4 + [pl.BlockSpec(weight.shape, lambda i, c: (0, 0))],
-            out_specs=[pl.BlockSpec((step_rows, features), lambda i, c: (i, 0))]
-            + [width] * 3
+            in_specs=[width] * 4 + [pl.BlockSpec(weight.shape, lambda i, c: (0, 0, 0))],
+            out_specs=[
+                pl.BlockSpec((step_rows, features), lambda i, c: (i, 0)),
+                tall,
+                pl.BlockSpec((8, step_rows), lambda i, c: (0, i)),
+                width,
+            ]
             + [tall] * 4,
         ),
         out_shape=[pltpu.VMEM((row_count, features), bf16)]
-        + [pltpu.HBM((row_count, LANES), f32)] * 2
+        + [pltpu.HBM((LANES, row_count), f32), pltpu.HBM((8, row_count), f32)]
         + [normal(bf16)]
         + [turned] * 4,
         compiler_params=params(12),
@@ -357,7 +382,7 @@
     g1_ref,
     g2_ref,
     g3_ref,
-    weight_t_ref,
+    weight_ref,
     d_out_ref,
     d_query_ref,
     d_key_ref,
@@ -388,7 +413,7 @@
         for block, mask in zip((g0_ref, g1_ref, g2_ref, g3_ref), BLOCK_MASKS):
             start = pl.multiple_of((me ^ mask) * LANES, LANES)
             d_out_ref[pl.ds(start, LANES), :] = block[...]
-        d_attended_ref[...] = dot(weight_t_ref[...], d_out_ref[...]).astype(bf16)
+        d_attended_ref[...] = dot(weight_ref[...].T, d_out_ref[...]).astype(bf16)
 
     grads = d_attended_ref[pl.ds(at, HD), :].astype(f32)
     query = query_t_ref[pl.ds(at, HD), :].astype(f32)
@@ -414,8 +439,8 @@
     d_query_ref[pl.ds(at, HD), :] = (d_query * score_scale).astype(bf16)
 
 
-def attention_backward(patch, weights, inverse, covariance, query_t, value_t, attended, grads, weight_t, column):
-    features = weight_t.shape[1]
+def attention_backward(patch, weights, inverse, covariance, query_t, value_t, attended, grads, weight, column):
+    features = weight.shape[0]
     heads = LANES // HD
     tall = pl.BlockSpec((LANES, PATCH), lambda h, c: (0, 0))
     part = pl.BlockSpec((LANES, PATCH), lambda h, c: (0, patch))
@@ -438,7 +463,7 @@
                 part,
                 part,
                 part,
-                pl.BlockSpec(weight_t.shape, lambda h, c: (0, 0)),
+                pl.BlockSpec(weight.shape, lambda h, c: (0, 0)),
             ],
             out_specs=[pl.BlockSpec((features, PATCH), lambda h, c: (0, 0)), tall, tall, tall],
             scratch_shapes=[
@@ -453,7 +478,7 @@
         compiler_params=params(30),
         cost_estimate=cost(1100 * elements, 2 * elements),
         name="attention_backward",
-    )(column, weights, inverse, covariance, query_t, value_t, attended, *grads, weight_t)
+    )(column, weights, inverse, covariance, query_t, value_t, attended, *grads, weight)
 
 
 def whole(shape, dtype):
@@ -514,7 +539,8 @@
     plain = jnp.zeros((1, PATCH), f32)
     for j, mask in enumerate(BLOCK_MASKS):
         start = pl.multiple_of((me ^ mask) * LANES, LANES)
-        block = dot(weight_ref[pl.ds(start, LANES), :], d_projected).astype(bf16)
+        rows = [weight_ref[t, pl.ds(start, LANES), :] for t in range(3)]
+        block = dot(jnp.concatenate(rows, axis=1), d_projected).astype(bf16)
         plain += jnp.sum(block.astype(f32), axis=0, keepdims=True)
         to = mine_ref if j < 2 else other_ref
         to[(j % 2) * LANES : (j % 2 + 1) * LANES, :] = block
@@ -529,7 +555,7 @@
 
 
 def hidden_part(d_query, d_key, d_value, query, key, value, weight, column):
-    features = weight.shape[0]
+    features = weight.shape[1]
     return pl.pallas_call(
         partial_body,
         in_specs=[pl.BlockSpec(memory_space=pltpu.SMEM)] + [pl.BlockSpec(memory_space=pltpu.VMEM)] * 7,
@@ -572,9 +598,8 @@
     features = 4.0 * LANES
     means = (sums_ref[...] + join_sums(got_ref[LANES:, :])) / features
     d_hidden = kept_ref[...] + got_ref[:LANES, :].astype(f32) - means[0:1]
-    cross = jnp.broadcast_to(means[1:2], (LANES, PATCH)).T
-    inner = d_hidden.T - normed_ref[...] * cross
-    out_ref[...] = d_out_ref[...].astype(f32).T + inv_ref[...] * inner
+    inner = d_hidden - normed_ref[...] * means[1:2]
+    out_ref[...] = (d_out_ref[...].astype(f32) + inv_ref[0:1] * inner).T
 
 
 def points_grad(patch, patches, kept, sums, got, d_out, normed, inv_scale, before):
@@ -596,6 +621,26 @@
         cost_estimate=cost(8 * LANES * PATCH, 24 * LANES * PATCH),
         name="points_grad",
     )(*operands)
+
+
+def grad_sum_body(parts_ref, qkv_ref, out_ref):
+    total = parts_ref[0].astype(f32)
+    for j in range(1, parts_ref.shape[0]):
+        total += parts_ref[j].astype(f32)
+    for t in range(3):
+        qkv_ref[t] = total[:, t * LANES : (t + 1) * LANES]
+    out_ref[...] = total[:, 3 * LANES :]
+
+
+def grad_sum(parts):
+    shards, rows, width = parts.shape
+    return pl.pallas_call(
+        grad_sum_body,
+        out_shape=[whole((3, rows, LANES), f32), whole((rows, LANES), f32)],
+        compiler_params=params(8),
+        cost_estimate=cost(shards * rows * width, 4 * shards * rows * width),
+        name="grad_sum",
+    )(parts)
 
 
 def local(
@@ -616,8 +661,7 @@
     patches = local_rows // PATCH
     column = lax.axis_index("mp").astype(i32).reshape(1)
     zero = jnp.zeros((1,), i32)
-    weight = qkv_weight.reshape(features, 3 * LANES)
-    weight_t = out_weight.T
+    weight = qkv_weight.transpose(1, 0, 2)
 
     def swap(rows, mask):
         return lax.ppermute(rows, "mp", [(i, i ^ mask) for i in range(members)])
@@ -631,15 +675,15 @@
     def in_hbm(value):
         return pltpu.with_memory_space_constraint(value, pltpu.HBM)
 
-    arrived = exchange(permute_rows(scan_points, send_order, column, whole, 60))
+    arrived = exchange(permute_rows(scan_points, send_order, column, 0, 1, whole, 60))
     buckets = bucket_rows(voxel_grads, voxel_shard, voxel_point, column, shards, capacity)
     got = exchange(buckets.reshape(shards * (capacity + INDEX_ROWS), LANES))
-    (weight, weight_t), arrived = after((weight, weight_t), arrived)
     owns = [
-        permute_rows(arrived, arrive_order[p * PATCH : (p + 1) * PATCH], zero, pltpu.VMEM, 8)
+        permute_rows(arrived, arrive_order, zero, p, patches, pltpu.VMEM, 8)
         for p in range(patches)
     ]
     across = [swap(own, 2) for own in owns]
+    across[0], owns[1] = after(across[0], owns[1])
 
     def forward(p):
         columns = (owns[p], across[p], swap(owns[p], 1), swap(across[p], 1))
@@ -663,15 +707,22 @@
             weights, sent = after(weights, sent)
             received.append(swap(sent, 2))
         d_out, d_query, d_key, d_value = attention_backward(
-            p, weights, inverse, covariance, query_t, value_t, attended, grads, weight_t, column
+            p, weights, inverse, covariance, query_t, value_t, attended, grads, out_weight, column
         )
         if p > 0:
             received[p - 1], d_query = after(received[p - 1], d_query)
         grad_parts.append((d_query, d_key, d_value, attended, hidden, d_out))
+        if p == patches - 1:
+            weight_parts = weight_grads(grad_parts)
+            (d_query, d_key, d_value, query_t, key_t, value_t), weight_parts = after(
+                (d_query, d_key, d_value, query_t, key_t, value_t), weight_parts
+            )
+            d_query, d_key, d_value, query_t, key_t, value_t = map(
+                in_hbm, (d_query, d_key, d_value, query_t, key_t, value_t)
+            )
         mine, other, own_sums = hidden_part(d_query, d_key, d_value, query_t, key_t, value_t, weight, column)
-        if p == patches - 1:
-            grad_parts, other = after(grad_parts, other)
-        keep, pair_sums, sent = pair_sum(mine, own_sums, swap(other, 1))
+        partner = swap(other, 1)
+        keep, pair_sums, sent = pair_sum(mine, own_sums, partner)
         kept.append(keep)
         sums.append(pair_sums)
     received.append(swap(sent, 2))
@@ -681,11 +732,9 @@
         d_points = points_grad(
             p, patches, kept[p], sums[p], received[p], grads[0], normed, inv_scale, d_points
         )
-    parts = exchange(weight_grads(grad_parts)).reshape(shards, features // shards, 4 * LANES)
-    summed = jnp.sum(parts.astype(f32), axis=0)
-    grad_qkv = summed[:, : 3 * LANES].reshape(features // shards, 3, LANES)
-    grad_out = summed[:, 3 * LANES :]
-    return (d_points, grad_qkv, grad_out)
+    parts = exchange(weight_parts).reshape(shards, features // shards, 4 * LANES)
+    grad_qkv, grad_out = grad_sum(parts)
+    return (d_points, grad_qkv.transpose(1, 0, 2), grad_out)
 
 
 def solution(mesh):

time: 158 us -> 147 us (0.930)
  local copies, waits for them, and re-layouts: 11.2 us -> 3.42 us
  Pallas kernels: 103 us -> 98.6 us
    unnamed x51 -> x38, local copies, waits for them, and re-layouts: 10.3 us -> 3.42 us
    pallas_call x3, Pallas kernels: 9.02 us -> 5.91 us  [permute_rows(): pl.pallas_call(permute_body, grid_spec=pltpu.PrefetchScalarGridSpec(num_s...]
  transfers between devices with their start and end apart: 16 -> 16, of which waited for: 7 -> 6; matrix products, arithmetic and copies ran while one was open for 0% -> 0% of each run, Pallas kernels for 52% -> 54%
where the time goes in v4:
time: 147 us; the launch traced here: 146 us
  Pallas kernels  98.6 us (67%)
  starting transfers between devices  24.6 us (17%)
  waiting for transfers between devices  18.7 us (13%)
  local copies, waits for them, and re-layouts  3.42 us (2%)
    pallas_call x2, Pallas kernels, attention_forward(): pl.pallas_call(forward_body, grid=(heads,), in_specs=[pl.BlockSpec((PATCH...  37.9 us
    pallas_call x2, Pallas kernels, attention_backward(): pl.pallas_call(backward_body, grid_spec=pltpu.PrefetchScalarGridSpec(num_...  21.2 us
    all_to_all x3, starting transfers between devices, exchange(): return lax.all_to_all(rows, 'seq', split_axis=0, concat_axis=0, tiled=True)  16.6 us
    ppermute x13, waiting for transfers between devices, swap(): return lax.ppermute(rows, 'mp', [(i, i ^ mask) for i in range(members)])  16.3 us
    pallas_call x1, Pallas kernels, bucket_rows(): pl.pallas_call(functools.partial(bucket_body, shards, capacity), grid_spe...  12.1 us
    ppermute x13, starting transfers between devices, swap(): return lax.ppermute(rows, 'mp', [(i, i ^ mask) for i in range(members)])  8.06 us
    pallas_call x3, Pallas kernels, permute_rows(): pl.pallas_call(permute_body, grid_spec=pltpu.PrefetchScalarGridSpec(num_s...  5.91 us
    pallas_call x1, Pallas kernels, segment_rows(): pl.pallas_call(segment_body, grid=(shards,), in_specs=[pl.BlockSpec((1, m...  5.39 us
  transfers between devices with their start and end apart: 16, of which 6 were waited for; matrix products, arithmetic and copies ran while one was open for 0% of the time, Pallas kernels for 54%

profile of v4, /device:TPU:0, one launch (start us, length us, event | category | flops | bytes accessed | tf_op | source)
XLA Modules:
  0.0 146.2 jit_solution(1196965930606165653)
XLA Ops:
  0.6 3.9 %permute_rows.3 = bf16[2048,128]{1,0:T(8,128)(2,1)} custom-call(s32[1]{0:T(128)} %bitcast.column_ref, s32[16,128]{1,0:T(8,128)} %bitcast.22, bf16[2048,512]{1,0:T(8,128)(2,1)} %block_ref.1), custom_call_target="tpu_custom_call" | custom-call | flops 4294967296 | bytes 1572864 | tf_op jit(solution)/shard_map/permute_rows/pallas_call | solution.py:79
  4.5 7.3 %all-to-all-start.1 = ((bf16[8,256,128]{2,1,0:T(8,128)(2,1)}), bf16[8,256,128]{2,1,0:T(8,128)(2,1)S(1)}, u32[]{:S(2)}, u32[]{:S(2)}) async-start(bf16[8,256,128]{2,1,0:T(8,128)(2,1)} %bitcast.20), calls=%async_computation.1 | async-start | bytes 1048576 | tf_op jit(solution)/shard_map/all_to_all | solution.py:670
  11.8 12.1 %bucket_rows.1 = bf16[8,528,128]{2,1,0:T(8,128)(2,1)} custom-call(s32[1]{0:T(128)} %bitcast.column_ref, s32[16,128]{1,0:T(8,128)} %bitcast.23, s32[16,128]{1,0:T(8,128)} %bitcast.24, bf16[2048,512]{1,0:T(8,128)(2,1)} %grads_ref.1), custom_call_target="tpu_custom_call" | custom-call | flops 8589934592 | bytes 3145728 | tf_op jit(solution)/shard_map/bucket_rows/pallas_call | solution.py:144
  23.9 2.4 %all-to-all-done.1 = bf16[8,256,128]{2,1,0:T(8,128)(2,1)S(1)} async-done(((bf16[8,256,128]{2,1,0:T(8,128)(2,1)}), bf16[8,256,128]{2,1,0:T(8,128)(2,1)S(1)}, u32[]{:S(2)}, u32[]{:S(2)}) %all-to-all-start.1) | async-done | bytes 524320 | tf_op jit(solution)/shard_map/all_to_all | solution.py:670
  26.3 3.6 %all-to-all-start = ((bf16[8,528,128]{2,1,0:T(8,128)(2,1)}), bf16[8,528,128]{2,1,0:T(8,128)(2,1)S(1)}, u32[]{:S(2)}, u32[]{:S(2)}) async-start(bf16[8,528,128]{2,1,0:T(8,128)(2,1)} %bucket_rows.1), calls=%async_computation | async-start | bytes 2162688 | tf_op jit(solution)/shard_map/all_to_all | solution.py:670
  29.9 0.0 copy-done.16
  29.9 1.0 permute_rows.5.x0_ref
  30.9 1.6 %collective-permute-start.1 = (bf16[1024,128]{1,0:T(8,128)(2,1)S(1)}, bf16[1024,128]{1,0:T(8,128)(2,1)S(1)}, u32[]{:S(2)}, u32[]{:S(2)}) collective-permute-start(bf16[1024,128]{1,0:T(8,128)(2,1)S(1)} %permute_rows.5.x0_ref), channel_id=1, source_target_pairs={{0,2},{1,3},{2,0},{3,1},{4,6},{5,7},{6,4},{7,5},{8,10},{9,11},{10,... | collective-permute-start | bytes 786440 | tf_op jit(solution)/shard_map/ppermute | solution.py:667
  32.5 0.0 collective-permute-start.2
  32.5 1.0 permute_rows.4.x0_ref
  33.5 5.4 %collective-permute-done.1.x1_ref = bf16[1024,128]{1,0:T(8,128)(2,1)S(1)} collective-permute-done((bf16[1024,128]{1,0:T(8,128)(2,1)S(1)}, bf16[1024,128]{1,0:T(8,128)(2,1)S(1)}, u32[]{:S(2)}, u32[]{:S(2)}) %collective-permute-start.1) | collective-permute-done | bytes 262176 | tf_op jit(solution)/shard_map/ppermute | solution.py:667
  39.0 0.0 collective-permute-start.3
  39.0 1.5 %collective-permute-start = (bf16[1024,128]{1,0:T(8,128)(2,1)S(1)}, bf16[1024,128]{1,0:T(8,128)(2,1)S(1)}, u32[]{:S(2)}, u32[]{:S(2)}) collective-permute-start(bf16[1024,128]{1,0:T(8,128)(2,1)S(1)} %permute_rows.4.x0_ref), channel_id=1, source_target_pairs={{0,2},{1,3},{2,0},{3,1},{4,6},{5,7},{6,4},{7,5},{8,10},{9,11},{10,... | collective-permute-start | bytes 786440 | tf_op jit(solution)/shard_map/ppermute | solution.py:667
  40.5 0.2 collective-permute-start.5
  40.7 0.0 collective-permute-done.2.x2_ref
  40.7 0.0 collective-permute-done.3.x3_ref
  40.7 0.0 copy-done
  40.7 2.5 %project.2 = (bf16[1024,512]{1,0:T(8,128)(2,1)S(1)}, f32[128,1024]{1,0:T(8,128)}, f32[8,1024]{1,0:T(8,128)}, bf16[1024,128]{1,0:T(8,128)(2,1)S(1)}, bf16[128,102...) custom-call(s32[1]{0:T(128)} %bitcast.column_ref, ...), custom_call_target="tpu_custom_call" | custom-call | flops 805306368 | bytes 5242880 | tf_op jit(solution)/shard_map/project/pallas_call | solution.py:264
  43.3 1.0 copy-done.1
  44.2 18.9 %attention_forward.2 = (bf16[8,1024,1024]{2,1,0:T(8,128)(2,1)}, bf16[128,1024]{1,0:T(8,128)(2,1)S(1)}, f32[8,1,1024]{2,1,0:T(1,128)S(1)}, bf16[8,256,1024]{2,1,0:T(8,128)(2,1)}) custom-call(bf16[1024,128]{1,0:T(8,128)(2,1)S(1)} %get-tuple-element.76.key_ref, bf16[128,1024]{1,0:T(8,128)(2,1)S(1)} %get-tuple-element.77.base2_t_ref, ...), custom_call_target="tpu_custom_call" | custom-call | flops 13421772800 | bytes 16777216 | tf_op jit(solution)/shard_map/attention_forward/pallas_call | solution.py:350
  63.1 0.0 copy-done.9
  63.1 0.7 copy-done.11
  63.9 0.0 collective-permute-done.x1_ref
  63.9 0.0 all-to-all-done
  63.9 5.4 %segment_rows.1.g0_ref.d_out_ref = bf16[128,2048]{1,0:T(8,128)(2,1)S(1)} custom-call(bf16[8,528,128]{2,1,0:T(8,128)(2,1)S(1)} %all-to-all-done), custom_call_target="tpu_custom_call" | custom-call | flops 8858370048 | bytes 3244032 | tf_op jit(solution)/shard_map/segment_rows/pallas_call | solution.py:202
  69.3 0.3 collective-permute-start.6
  69.6 1.1 collective-permute-start.4
  70.8 0.1 collective-permute-start.7
  70.8 0.0 collective-permute-done.5.x2_ref
  70.8 0.7 copy-done.13
  71.6 0.0 collective-permute-done.6.x3_ref
  71.6 0.9 copy-done.14
  72.5 2.5 %project.3 = (bf16[1024,512]{1,0:T(8,128)(2,1)S(1)}, f32[128,1024]{1,0:T(8,128)}, f32[8,1024]{1,0:T(8,128)}, bf16[1024,128]{1,0:T(8,128)(2,1)S(1)}, bf16[128,102...) custom-call(s32[1]{0:T(128)} %bitcast.column_ref, ...), custom_call_target="tpu_custom_call" | custom-call | flops 805306368 | bytes 5242880 | tf_op jit(solution)/shard_map/project/pallas_call | solution.py:264
  75.0 0.0 copy-start.10
  75.0 0.0 copy-start.15
  75.1 19.0 %attention_forward.3 = (bf16[8,1024,1024]{2,1,0:T(8,128)(2,1)}, bf16[128,1024]{1,0:T(8,128)(2,1)S(1)}, f32[8,1,1024]{2,1,0:T(1,128)S(1)}, bf16[8,256,1024]{2,1,0:T(8,128)(2,1)}) custom-call(bf16[1024,128]{1,0:T(8,128)(2,1)S(1)} %get-tuple-element.88.key_ref, bf16[128,1024]{1,0:T(8,128)(2,1)S(1)} %get-tuple-element.89.base2_t_ref, ...), custom_call_target="tpu_custom_call" | custom-call | flops 13421772800 | bytes 16777216 | tf_op jit(solution)/shard_map/attention_forward/pallas_call | solution.py:350
  94.0 0.0 collective-permute-done.4.g1_ref
  94.0 0.4 collective-permute-start.8
  94.5 0.0 collective-permute-done.7.g2_ref
  94.5 1.5 %collective-permute-done.8.g3_ref = bf16[128,2048]{1,0:T(8,128)(2,1)S(1)} collective-permute-done((bf16[128,2048]{1,0:T(8,128)(2,1)S(1)}, bf16[128,2048]{1,0:T(8,128)(2,1)S(1)}, u32[]{:S(2)}, u32[]{:S(2)}) %collective-permute-start.8) | collective-permute-done | bytes 524320 | tf_op jit(solution)/shard_map/ppermute | solution.py:667
  96.0 0.0 copy-done.10
  96.0 0.0 copy-start.18
  96.0 10.7 %attention_backward.2 = (bf16[512,1024]{1,0:T(8,128)(2,1)S(1)}, bf16[128,1024]{1,0:T(8,128)(2,1)S(1)}, bf16[128,1024]{1,0:T(8,128)(2,1)S(1)}, bf16[128,1024]{1,0:T(8,128)(2,1)S(1)}) custom-call(s32[1]{0:T(128)} %bitcast.column_ref, bf16[8,1024,1024]{2,1,0:T(8,128)(2,1)} %get-tuple-element.97.exp_ref, f32[8,1,1024]{2,1,0:T(1,128)S(1)} %get-tuple-element.98.inverse_ref, ...), custom_call_target="tpu_custom_call" | custom-call | flops 9227468800 | bytes 16777216 | tf_op jit(solution)/shard_map/attention_backward/pallas_call | solution.py:450
  106.8 1.0 hidden_part.2
  107.8 0.5 collective-permute-start.9
  108.3 1.6 %collective-permute-done.9.got_ref = bf16[272,1024]{1,0:T(8,128)(2,1)S(1)} collective-permute-done((bf16[272,1024]{1,0:T(8,128)(2,1)S(1)}, bf16[272,1024]{1,0:T(8,128)(2,1)S(1)}, u32[]{:S(2)}, u32[]{:S(2)}) %collective-permute-start.9) | collective-permute-done | bytes 557088 | tf_op jit(solution)/shard_map/ppermute | solution.py:667
  109.9 0.1 pair_sum.2
  110.0 1.0 collective-permute-start.10
  111.0 10.5 %attention_backward.3 = (bf16[512,1024]{1,0:T(8,128)(2,1)S(1)}, bf16[128,1024]{1,0:T(8,128)(2,1)S(1)}, bf16[128,1024]{1,0:T(8,128)(2,1)S(1)}, bf16[128,1024]{1,0:T(8,128)(2,1)S(1)}) custom-call(s32[1]{0:T(128)} %bitcast.column_ref, bf16[8,1024,1024]{2,1,0:T(8,128)(2,1)} %get-tuple-element.112.exp_ref, f32[8,1,1024]{2,1,0:T(1,128)S(1)} %get-tuple-element.113.inverse_ref, ...), custom_call_target="tpu_custom_call" | custom-call | flops 9227468800 | bytes 16777216 | tf_op jit(solution)/shard_map/attention_backward/pallas_call | solution.py:450
  121.5 0.0 collective-permute-done.10.got_ref
  121.5 0.0 copy-done.2
  121.5 2.5 %weight_grads.1 = bf16[512,512]{1,0:T(8,128)(2,1)} custom-call(bf16[128,1024]{1,0:T(8,128)(2,1)S(1)} %get-tuple-element.104.d_query_ref.refs_0_, bf16[128,1024]{1,0:T(8,128)(2,1)S(1)} %get-tuple-element.105.d_key_ref.refs_1_, bf16[128,1024]{1,0:T(8,128)(2,1)S(1)} %get-tuple-element.106.d_value_ref.refs_2_, bf16[128,1024]{1,0:T(8,128)(2,1)S(1)} %copy-done.12, ...), custom_call_target="tpu_custom_call" | custom-call | flops 1073741824 | bytes 6291456 | tf_op jit(solution)/shard_map/weight_grads/pallas_call | solution.py:503
  124.0 5.7 %all-to-all-start.2 = ((bf16[8,64,512]{2,1,0:T(8,128)(2,1)}), bf16[8,64,512]{2,1,0:T(8,128)(2,1)S(1)}, u32[]{:S(2)}, u32[]{:S(2)}) async-start(bf16[8,64,512]{2,1,0:T(8,128)(2,1)} %bitcast.10), calls=%async_computation.2 | async-start | bytes 1048576 | tf_op jit(solution)/shard_map/all_to_all | solution.py:670
  129.7 0.0 copy-done.3
  129.8 2.4 %hidden_part.3 = (bf16[256,1024]{1,0:T(8,128)(2,1)S(1)}, bf16[272,1024]{1,0:T(8,128)(2,1)S(1)}, f32[2,1024]{1,0:T(2,128)S(1)}) custom-call(s32[1]{0:T(128)} %bitcast.column_ref, bf16[128,1024]{1,0:T(8,128)(2,1)} %copy-done.3, bf16[128,1024]{1,0:T(8,128)(2,1)} %copy-done.4, bf16[128,1024]{1,0:T(8,128)(2,1)} %copy-done.5, bf16[128,1024]{1,0:T(8,128)(2,1)} %copy-done.6, ...), custom_call_target="tpu_custom_call" | custom-call | flops 402653184 | bytes 2097152 | tf_op jit(solution)/shard_map/hidden_part/pallas_call | solution.py:559
  132.1 0.1 collective-permute-start.11
  132.2 1.9 %collective-permute-done.11.got_ref = bf16[272,1024]{1,0:T(8,128)(2,1)S(1)} collective-permute-done((bf16[272,1024]{1,0:T(8,128)(2,1)S(1)}, bf16[272,1024]{1,0:T(8,128)(2,1)S(1)}, u32[]{:S(2)}, u32[]{:S(2)}) %collective-permute-start.11) | collective-permute-done | bytes 557088 | tf_op jit(solution)/shard_map/ppermute | solution.py:667
  134.2 0.1 pair_sum.3
  134.3 1.2 collective-permute-start.12
  135.5 2.1 %points_grad.2.rest_0_ = f32[2048,128]{1,0:T(8,128)} custom-call(f32[128,1024]{1,0:T(8,128)S(1)} %get-tuple-element.139.kept_ref, f32[2,1024]{1,0:T(2,128)S(1)} %get-tuple-element.140.sums_ref, bf16[144,1024]{1,0:T(8,128)(2,1)S(1)} %collective-permute-done.10.got_ref, bf16[128,2048]{1,0:T(8,128)(2,1)S(1)} %segment_rows.1.g0_ref.d_out_ref, ...), custom_call_target="tpu_custom_call" | custom-call | flops 1048576 | bytes 3145728 | tf_op jit(solution)/shard_map/points_grad/pallas_call | solution.py:613
  137.6 5.8 %collective-permute-done.12.got_ref = bf16[144,1024]{1,0:T(8,128)(2,1)S(1)} collective-permute-done((bf16[144,1024]{1,0:T(8,128)(2,1)S(1)}, bf16[144,1024]{1,0:T(8,128)(2,1)S(1)}, u32[]{:S(2)}, u32[]{:S(2)}) %collective-permute-start.12) | collective-permute-done | bytes 294944 | tf_op jit(solution)/shard_map/ppermute | solution.py:667
  143.4 2.1 %points_grad.3 = f32[2048,128]{1,0:T(8,128)} custom-call(f32[128,1024]{1,0:T(8,128)S(1)} %get-tuple-element.134.kept_ref, f32[2,1024]{1,0:T(2,128)S(1)} %get-tuple-element.135.sums_ref, bf16[144,1024]{1,0:T(8,128)(2,1)S(1)} %collective-permute-done.12.got_ref, bf16[128,2048]{1,0:T(8,128)(2,1)S(1)} %segment_rows.1.g0_ref.d_out_ref, ...), custom_call_target="tpu_custom_call", output_to_operand_aliasing={{}: (6, {})} | custom-call | flops 1048576 | bytes 3145728 | tf_op jit(solution)/shard_map/points_grad/pallas_call | solution.py:613
  145.5 0.0 all-to-all-done.2.parts_ref
  145.5 0.7 grad_sum.1
  (25 shorter events, 0.0 us)
Async XLA Ops:
  4.5 21.7 %all-to-all-start.1 = ((bf16[8,256,128]{2,1,0:T(8,128)(2,1)}), bf16[8,256,128]{2,1,0:T(8,128)(2,1)S(1)}, u32[]{:S(2)}, u32[]{:S(2)}) async-start(bf16[8,256,128]{2,1,0:T(8,128)(2,1)} %bitcast.20), calls=%async_computation.1 | async-start | bytes 1048576 | tf_op jit(solution)/shard_map/all_to_all | solution.py:670
  11.8 18.1 %copy-start.16 = (s32[2048]{0:T(1024)S(1)}, s32[2048]{0:T(1024)}, u32[]{:S(2)}) copy-start(s32[2048]{0:T(1024)} %param.10) | copy-start | bytes 24580
  26.3 37.6 %all-to-all-start = ((bf16[8,528,128]{2,1,0:T(8,128)(2,1)}), bf16[8,528,128]{2,1,0:T(8,128)(2,1)S(1)}, u32[]{:S(2)}, u32[]{:S(2)}) async-start(bf16[8,528,128]{2,1,0:T(8,128)(2,1)} %bucket_rows.1), calls=%async_computation | async-start | bytes 2162688 | tf_op jit(solution)/shard_map/all_to_all | solution.py:670
  29.9 10.8 %copy-start = (bf16[512,3,128]{2,0,1:T(8,128)(2,1)S(1)}, bf16[512,3,128]{2,0,1:T(8,128)(2,1)}, u32[]{:S(2)}) copy-start(bf16[512,3,128]{2,0,1:T(8,128)(2,1)} %param.11) | copy-start | bytes 1179652
  30.9 8.0 %collective-permute-start.1 = (bf16[1024,128]{1,0:T(8,128)(2,1)S(1)}, bf16[1024,128]{1,0:T(8,128)(2,1)S(1)}, u32[]{:S(2)}, u32[]{:S(2)}) collective-permute-start(bf16[1024,128]{1,0:T(8,128)(2,1)S(1)} %permute_rows.5.x0_ref), channel_id=1, source_target_pairs={{0,2},{1,3},{2,0},{3,1},{4,6},{5,7},{6,4},{7,5},{8,10},{9,11},{10,... | collective-permute-start | bytes 786440 | tf_op jit(solution)/shard_map/ppermute | solution.py:667
  32.5 8.2 %collective-permute-start.2 = (bf16[1024,128]{1,0:T(8,128)(2,1)S(1)}, bf16[1024,128]{1,0:T(8,128)(2,1)S(1)}, u32[]{:S(2)}, u32[]{:S(2)}) collective-permute-start(bf16[1024,128]{1,0:T(8,128)(2,1)S(1)} %permute_rows.5.x0_ref), channel_id=1, source_target_pairs={{0,1},{1,0},{2,3},{3,2},{4,5},{5,4},{6,7},{7,6},{8,9},{9,8},{10,11... | collective-permute-start | bytes 786440 | tf_op jit(solution)/shard_map/ppermute | solution.py:667
  39.0 1.8 %collective-permute-start.3 = (bf16[1024,128]{1,0:T(8,128)(2,1)S(1)}, bf16[1024,128]{1,0:T(8,128)(2,1)S(1)}, u32[]{:S(2)}, u32[]{:S(2)}) collective-permute-start(bf16[1024,128]{1,0:T(8,128)(2,1)S(1)} %collective-permute-done.1.x1_ref), channel_id=1, source_target_pairs={{0,1},{1,0},{2,3},{3,2},{4,5},{5,4},{6,7},{7,6},{8,9},{9,8},{10,11... | collective-permute-start | bytes 786440 | tf_op jit(solution)/shard_map/ppermute | solution.py:667
  39.0 24.9 %collective-permute-start = (bf16[1024,128]{1,0:T(8,128)(2,1)S(1)}, bf16[1024,128]{1,0:T(8,128)(2,1)S(1)}, u32[]{:S(2)}, u32[]{:S(2)}) collective-permute-start(bf16[1024,128]{1,0:T(8,128)(2,1)S(1)} %permute_rows.4.x0_ref), channel_id=1, source_target_pairs={{0,2},{1,3},{2,0},{3,1},{4,6},{5,7},{6,4},{7,5},{8,10},{9,11},{10,... | collective-permute-start | bytes 786440 | tf_op jit(solution)/shard_map/ppermute | solution.py:667
  40.5 30.4 %collective-permute-start.5 = (bf16[1024,128]{1,0:T(8,128)(2,1)S(1)}, bf16[1024,128]{1,0:T(8,128)(2,1)S(1)}, u32[]{:S(2)}, u32[]{:S(2)}) collective-permute-start(bf16[1024,128]{1,0:T(8,128)(2,1)S(1)} %permute_rows.4.x0_ref), channel_id=1, source_target_pairs={{0,1},{1,0},{2,3},{3,2},{4,5},{5,4},{6,7},{7,6},{8,9},{9,8},{10,11... | collective-permute-start | bytes 786440 | tf_op jit(solution)/shard_map/ppermute | solution.py:667
  43.3 1.0 copy-start.1
  44.2 18.9 %copy-start.9 = (bf16[128,1024]{1,0:T(8,128)(2,1)}, bf16[128,1024]{1,0:T(8,128)(2,1)S(1)}, u32[]{:S(2)}) copy-start(bf16[128,1024]{1,0:T(8,128)(2,1)S(1)} %get-tuple-element.79.value_t_ref.value_ref) | copy-start | bytes 786436
  63.1 0.7 copy-start.11
  69.3 2.3 %collective-permute-start.6 = (bf16[1024,128]{1,0:T(8,128)(2,1)S(1)}, bf16[1024,128]{1,0:T(8,128)(2,1)S(1)}, u32[]{:S(2)}, u32[]{:S(2)}) collective-permute-start(bf16[1024,128]{1,0:T(8,128)(2,1)S(1)} %collective-permute-done.x1_ref), channel_id=1, source_target_pairs={{0,1},{1,0},{2,3},{3,2},{4,5},{5,4},{6,7},{7,6},{8,9},{9,8},{10,11... | collective-permute-start | bytes 786440 | tf_op jit(solution)/shard_map/ppermute | solution.py:667
  69.6 24.4 %collective-permute-start.4 = (bf16[128,2048]{1,0:T(8,128)(2,1)S(1)}, bf16[128,2048]{1,0:T(8,128)(2,1)S(1)}, u32[]{:S(2)}, u32[]{:S(2)}) collective-permute-start(bf16[128,2048]{1,0:T(8,128)(2,1)S(1)} %segment_rows.1.g0_ref.d_out_ref), channel_id=1, source_target_pairs={{0,2},{1,3},{2,0},{3,1},{4,6},{5,7},{6,4},{7,5},{8,10},{9,11},{10,... | collective-permute-start | bytes 1572872 | tf_op jit(solution)/shard_map/ppermute | solution.py:667
  70.8 23.7 %collective-permute-start.7 = (bf16[128,2048]{1,0:T(8,128)(2,1)S(1)}, bf16[128,2048]{1,0:T(8,128)(2,1)S(1)}, u32[]{:S(2)}, u32[]{:S(2)}) collective-permute-start(bf16[128,2048]{1,0:T(8,128)(2,1)S(1)} %segment_rows.1.g0_ref.d_out_ref), channel_id=1, source_target_pairs={{0,1},{1,0},{2,3},{3,2},{4,5},{5,4},{6,7},{7,6},{8,9},{9,8},{10,11... | collective-permute-start | bytes 1572872 | tf_op jit(solution)/shard_map/ppermute | solution.py:667
  70.8 0.7 copy-start.13
  71.6 1.0 copy-start.14
  75.0 19.0 %copy-start.7 = (bf16[128,1024]{1,0:T(8,128)(2,1)}, bf16[128,1024]{1,0:T(8,128)(2,1)S(1)}, u32[]{:S(2)}) copy-start(bf16[128,1024]{1,0:T(8,128)(2,1)S(1)} %get-tuple-element.129.key_t_ref.key_ref) | copy-start | bytes 786436
  75.0 35.9 %copy-start.6 = (bf16[128,1024]{1,0:T(8,128)(2,1)}, bf16[128,1024]{1,0:T(8,128)(2,1)S(1)}, u32[]{:S(2)}) copy-start(bf16[128,1024]{1,0:T(8,128)(2,1)S(1)} %get-tuple-element.128.query_t_ref.query_ref) | copy-start | bytes 786436
  75.0 35.9 %copy-start.8 = (bf16[128,1024]{1,0:T(8,128)(2,1)}, bf16[128,1024]{1,0:T(8,128)(2,1)S(1)}, u32[]{:S(2)}) copy-start(bf16[128,1024]{1,0:T(8,128)(2,1)S(1)} %get-tuple-element.130.value_t_ref.value_ref) | copy-start | bytes 786436
  75.0 21.0 %copy-start.10 = (bf16[128,1024]{1,0:T(8,128)(2,1)S(1)}, bf16[128,1024]{1,0:T(8,128)(2,1)}, u32[]{:S(2)}) copy-start(bf16[128,1024]{1,0:T(8,128)(2,1)} %copy-done.9) | copy-start | bytes 786436
  75.0 21.0 %copy-start.12 = (bf16[128,1024]{1,0:T(8,128)(2,1)S(1)}, bf16[128,1024]{1,0:T(8,128)(2,1)}, u32[]{:S(2)}) copy-start(bf16[128,1024]{1,0:T(8,128)(2,1)} %copy-done.11) | copy-start | bytes 786436
  75.0 21.0 %copy-start.15 = (bf16[512,128]{1,0:T(8,128)(2,1)S(1)}, bf16[512,128]{1,0:T(8,128)(2,1)}, u32[]{:S(2)}) copy-start(bf16[512,128]{1,0:T(8,128)(2,1)} %weight_ref.3) | copy-start | bytes 393220
  75.0 21.0 %copy-start.17 = (bf16[8,256,1024]{2,1,0:T(8,128)(2,1)S(1)}, bf16[8,256,1024]{2,1,0:T(8,128)(2,1)}, u32[]{:S(2)}) copy-start(bf16[8,256,1024]{2,1,0:T(8,128)(2,1)} %get-tuple-element.99.covariance_ref) | copy-start | bytes 12582916
  94.0 2.0 %collective-permute-start.8 = (bf16[128,2048]{1,0:T(8,128)(2,1)S(1)}, bf16[128,2048]{1,0:T(8,128)(2,1)S(1)}, u32[]{:S(2)}, u32[]{:S(2)}) collective-permute-start(bf16[128,2048]{1,0:T(8,128)(2,1)S(1)} %collective-permute-done.4.g1_ref), channel_id=1, source_target_pairs={{0,1},{1,0},{2,3},{3,2},{4,5},{5,4},{6,7},{7,6},{8,9},{9,8},{10,11... | collective-permute-start | bytes 1572872 | tf_op jit(solution)/shard_map/ppermute | solution.py:667
  96.0 14.9 %copy-start.18 = (bf16[8,256,1024]{2,1,0:T(8,128)(2,1)S(1)}, bf16[8,256,1024]{2,1,0:T(8,128)(2,1)}, u32[]{:S(2)}) copy-start(bf16[8,256,1024]{2,1,0:T(8,128)(2,1)} %get-tuple-element.114.covariance_ref) | copy-start | bytes 12582916
  107.8 2.0 %collective-permute-start.9 = (bf16[272,1024]{1,0:T(8,128)(2,1)S(1)}, bf16[272,1024]{1,0:T(8,128)(2,1)S(1)}, u32[]{:S(2)}, u32[]{:S(2)}) collective-permute-start(bf16[272,1024]{1,0:T(8,128)(2,1)S(1)} %get-tuple-element.109), channel_id=1, source_target_pairs={{0,1},{1,0},{2,3},{3,2},{4,5},{5,4},{6,7},{7,6},{8,9},{9,8},{10,11... | collective-permute-start | bytes 1671176 | tf_op jit(solution)/shard_map/ppermute | solution.py:667
  110.0 11.5 %collective-permute-start.10 = (bf16[144,1024]{1,0:T(8,128)(2,1)S(1)}, bf16[144,1024]{1,0:T(8,128)(2,1)S(1)}, u32[]{:S(2)}, u32[]{:S(2)}) collective-permute-start(bf16[144,1024]{1,0:T(8,128)(2,1)S(1)} %get-tuple-element.111), channel_id=1, source_target_pairs={{0,2},{1,3},{2,0},{3,1},{4,6},{5,7},{6,4},{7,5},{8,10},{9,11},{10,... | collective-permute-start | bytes 884744 | tf_op jit(solution)/shard_map/ppermute | solution.py:667
  111.0 10.6 %copy-start.2 = (bf16[1024,512]{1,0:T(8,128)(2,1)S(1)}, bf16[1024,512]{1,0:T(8,128)(2,1)}, u32[]{:S(2)}) copy-start(bf16[1024,512]{1,0:T(8,128)(2,1)} %copy-done.1) | copy-start | bytes 3145732
  121.5 8.3 %copy-start.3 = (bf16[128,1024]{1,0:T(8,128)(2,1)}, bf16[128,1024]{1,0:T(8,128)(2,1)S(1)}, u32[]{:S(2)}) copy-start(bf16[128,1024]{1,0:T(8,128)(2,1)S(1)} %get-tuple-element.125.refs_6_.d_query_ref) | copy-start | bytes 786436
  121.5 8.3 %copy-start.4 = (bf16[128,1024]{1,0:T(8,128)(2,1)}, bf16[128,1024]{1,0:T(8,128)(2,1)S(1)}, u32[]{:S(2)}) copy-start(bf16[128,1024]{1,0:T(8,128)(2,1)S(1)} %get-tuple-element.126.refs_7_.d_key_ref) | copy-start | bytes 786436
  121.5 8.3 %copy-start.5 = (bf16[128,1024]{1,0:T(8,128)(2,1)}, bf16[128,1024]{1,0:T(8,128)(2,1)S(1)}, u32[]{:S(2)}) copy-start(bf16[128,1024]{1,0:T(8,128)(2,1)S(1)} %get-tuple-element.127.refs_8_.d_value_ref) | copy-start | bytes 786436
  124.0 21.5 %all-to-all-start.2 = ((bf16[8,64,512]{2,1,0:T(8,128)(2,1)}), bf16[8,64,512]{2,1,0:T(8,128)(2,1)S(1)}, u32[]{:S(2)}, u32[]{:S(2)}) async-start(bf16[8,64,512]{2,1,0:T(8,128)(2,1)} %bitcast.10), calls=%async_computation.2 | async-start | bytes 1048576 | tf_op jit(solution)/shard_map/all_to_all | solution.py:670
  132.1 2.0 %collective-permute-start.11 = (bf16[272,1024]{1,0:T(8,128)(2,1)S(1)}, bf16[272,1024]{1,0:T(8,128)(2,1)S(1)}, u32[]{:S(2)}, u32[]{:S(2)}) collective-permute-start(bf16[272,1024]{1,0:T(8,128)(2,1)S(1)} %get-tuple-element.133), channel_id=1, source_target_pairs={{0,1},{1,0},{2,3},{3,2},{4,5},{5,4},{6,7},{7,6},{8,9},{9,8},{10,11... | collective-permute-start | bytes 1671176 | tf_op jit(solution)/shard_map/ppermute | solution.py:667
  134.3 9.1 %collective-permute-start.12 = (bf16[144,1024]{1,0:T(8,128)(2,1)S(1)}, bf16[144,1024]{1,0:T(8,128)(2,1)S(1)}, u32[]{:S(2)}, u32[]{:S(2)}) collective-permute-start(bf16[144,1024]{1,0:T(8,128)(2,1)S(1)} %get-tuple-element.136), channel_id=1, source_target_pairs={{0,2},{1,3},{2,0},{3,1},{4,6},{5,7},{6,4},{7,5},{8,10},{9,11},{10,... | collective-permute-start | bytes 884744 | tf_op jit(solution)/shard_map/ppermute | solution.py:667

commit v5 on v4

--- a/solution.py
+++ b/solution.py
@@ -14,6 +14,8 @@
 INDEX_BASE = 64
 BLOCK_MASKS = (0, 2, 1, 3)
 SAFE_SCORE = 60.0
+SEGMENT_SHARDS = 4
+BUCKET_SHARDS = 2
 
 score_scale = 0.25
 epsilon = 1e-05
@@ -75,7 +77,7 @@
 def permute_rows(rows, order, column, part, parts, out, mib):
     row_count = order.shape[0] // parts
     groups = row_count // LANES
-    step_rows = min(512, row_count)
+    step_rows = min(1024, row_count)
     return pl.pallas_call(
         permute_body,
         grid_spec=pltpu.PrefetchScalarGridSpec(
@@ -120,38 +122,47 @@
             places = jnp.where(targets == t, place, places)
         place_ref[...] = places.astype(i32)
 
-    slot = lax.broadcasted_iota(i32, (capacity, LANES), 0) + step * capacity
-    onehot = jnp.concatenate(
-        [ones_where(place_ref[j : j + 1, :] == slot) for j in range(groups)], axis=1
-    )
-    out_ref[0, :capacity, :] = dot(onehot, grads_ref[...]).astype(bf16)
     points = jnp.concatenate([point_ref[j : j + 1, :] for j in range(groups)], axis=1)
     high = points // INDEX_BASE
     low = points - high * INDEX_BASE
     digits = jnp.concatenate(
         [high.astype(f32), low.astype(f32), jnp.zeros((INDEX_ROWS - 2, row_count), f32)], axis=0
     )
+    group = out_ref.shape[0]
+    chunks = capacity // LANES
+    slot = lax.broadcasted_iota(i32, (group * capacity, LANES), 0) + step * (group * capacity)
+    onehot = jnp.concatenate(
+        [ones_where(place_ref[j : j + 1, :] == slot) for j in range(groups)], axis=1
+    )
+    filled = dot(onehot, grads_ref[...]).astype(bf16)
     sent = dot_rows(digits.astype(bf16), onehot)
-    chunks = capacity // LANES
-    rows = [sent[d : d + 1, j * LANES : (j + 1) * LANES] for d in range(2) for j in range(chunks)]
-    rows.append(jnp.zeros((INDEX_ROWS - 2 * chunks, LANES), f32))
-    out_ref[0, capacity:, :] = jnp.concatenate(rows, axis=0).astype(bf16)
+    for shard in range(group):
+        start = shard * capacity
+        out_ref[shard, :capacity, :] = filled[start : start + capacity]
+        rows = [
+            sent[d : d + 1, start + j * LANES : start + (j + 1) * LANES]
+            for d in range(2)
+            for j in range(chunks)
+        ]
+        rows.append(jnp.zeros((INDEX_ROWS - 2 * chunks, LANES), f32))
+        out_ref[shard, capacity:, :] = jnp.concatenate(rows, axis=0).astype(bf16)
 
 
 def bucket_rows(grads, targets, points, column, shards, capacity):
     row_count = grads.shape[0]
     groups = row_count // LANES
+    group = BUCKET_SHARDS if shards % BUCKET_SHARDS == 0 else 1
     return pl.pallas_call(
         functools.partial(bucket_body, shards, capacity),
         grid_spec=pltpu.PrefetchScalarGridSpec(
             num_scalar_prefetch=1,
-            grid=(shards,),
+            grid=(shards // group,),
             in_specs=[
                 pl.BlockSpec((groups, LANES), lambda i, c: (0, 0)),
                 pl.BlockSpec((groups, LANES), lambda i, c: (0, 0)),
                 pl.BlockSpec((row_count, LANES), lambda i, c: (0, c[0])),
             ],
-            out_specs=pl.BlockSpec((1, capacity + INDEX_ROWS, LANES), lambda i, c: (i, 0, 0)),
+            out_specs=pl.BlockSpec((group, capacity + INDEX_ROWS, LANES), lambda i, c: (i, 0, 0)),
             scratch_shapes=[pltpu.VMEM((groups, LANES), i32)],
         ),
         out_shape=jax.ShapeDtypeStruct((shards, capacity + INDEX_ROWS, LANES), bf16),
@@ -168,20 +179,20 @@
     capacity = got_ref.shape[1] - INDEX_ROWS
     chunks = capacity // LANES
     half = total_ref.shape[0]
-    digits = got_ref[0, capacity:, :].astype(f32)
-    index = digits[:chunks] * float(INDEX_BASE) + digits[chunks : 2 * chunks]
-    position = index.astype(i32)
-    local_row = jnp.where(position < half, position, position - half)
     row = lax.broadcasted_iota(i32, (half, LANES), 0)
-    onehot = jnp.concatenate([ones_where(local_row[j : j + 1] == row) for j in range(chunks)], axis=1)
-    sides = []
-    for j in range(chunks):
-        low = jnp.broadcast_to(index[j : j + 1], (LANES, LANES)).T < float(half)
-        rows = got_ref[0, j * LANES : (j + 1) * LANES, :].astype(f32)
-        sides.append(
-            jnp.concatenate([jnp.where(low, rows, 0.0), jnp.where(low, 0.0, rows)], axis=1).astype(bf16)
-        )
-    part = dot(onehot, jnp.concatenate(sides, axis=0))
+    onehots, sides = [], []
+    for shard in range(got_ref.shape[0]):
+        digits = got_ref[shard, capacity:, :].astype(f32)
+        index = digits[:chunks] * float(INDEX_BASE) + digits[chunks : 2 * chunks]
+        position = index.astype(i32)
+        local_row = jnp.where(position < half, position, position - half)
+        for j in range(chunks):
+            onehots.append(ones_where(local_row[j : j + 1] == row))
+            low = jnp.broadcast_to(index[j : j + 1], (LANES, LANES)).T < float(half)
+            rows = got_ref[shard, j * LANES : (j + 1) * LANES, :].astype(f32)
+            both = [jnp.where(low, rows, 0.0), jnp.where(low, 0.0, rows)]
+            sides.append(jnp.concatenate(both, axis=1).astype(bf16))
+    part = dot(jnp.concatenate(onehots, axis=1), jnp.concatenate(sides, axis=0))
 
     @pl.when(step == 0)
     def _():
@@ -199,14 +210,15 @@
 
 def segment_rows(got, row_count):
     shards, message, _ = got.shape
+    group = SEGMENT_SHARDS if shards % SEGMENT_SHARDS == 0 else 1
     return pl.pallas_call(
         segment_body,
-        grid=(shards,),
-        in_specs=[pl.BlockSpec((1, message, LANES), lambda i: (i, 0, 0))],
+        grid=(shards // group,),
+        in_specs=[pl.BlockSpec((group, message, LANES), lambda i: (i, 0, 0))],
         out_specs=pl.BlockSpec((LANES, row_count), lambda i: (0, 0)),
         out_shape=pltpu.VMEM((LANES, row_count), bf16),
         scratch_shapes=[pltpu.VMEM((row_count // 2, 2 * LANES), f32)],
-        compiler_params=params(16),
+        compiler_params=params(24),
         cost_estimate=cost(
             8 * shards * message * row_count * LANES, 3 * shards * message * LANES * 2
         ),
@@ -253,7 +265,7 @@
     value_t_ref[...] = projected[:, 2 * LANES :].astype(f32).T.astype(bf16)
 
 
-def project(blocks, weight, column):
+def project(blocks, weight, column, space):
     row_count = blocks[0].shape[0]
     step_rows = 512
     features = weight.shape[1]
@@ -275,7 +287,7 @@
             ]
             + [tall] * 4,
         ),
-        out_shape=[pltpu.VMEM((row_count, features), bf16)]
+        out_shape=[space((row_count, features), bf16)]
         + [pltpu.HBM((LANES, row_count), f32), pltpu.HBM((8, row_count), f32)]
         + [normal(bf16)]
         + [turned] * 4,
@@ -342,7 +354,7 @@
         attend(True)
 
 
-def attention_forward(keys, base2_t, key_t, value_t):
+def attention_forward(keys, base2_t, key_t, value_t, space):
     heads = LANES // HD
     tall = pl.BlockSpec((LANES, PATCH), lambda h: (0, 0))
     per_head = lambda h: (h, 0, 0)
@@ -358,13 +370,13 @@
             pl.BlockSpec((1, HD * HD, PATCH), per_head),
         ],
         out_shape=[
-            pltpu.HBM((heads, PATCH, PATCH), bf16),
-            pltpu.VMEM((LANES, PATCH), bf16),
+            space((heads, PATCH, PATCH), bf16),
+            space((LANES, PATCH), bf16),
             pltpu.VMEM((heads, 1, PATCH), f32),
-            pltpu.HBM((heads, HD * HD, PATCH), bf16),
+            space((heads, HD * HD, PATCH), bf16),
         ],
         scratch_shapes=[pltpu.SMEM((1,), i32)],
-        compiler_params=params(28),
+        compiler_params=params(16),
         cost_estimate=cost(1600 * elements, 2 * elements, elements),
         name="attention_forward",
     )(keys, base2_t, key_t, value_t)
@@ -388,15 +400,13 @@
     d_key_ref,
     d_value_ref,
     d_attended_ref,
-    exp_all_ref,
-    covariance_all_ref,
-    exp_sems,
-    covariance_sems,
+    *early,
 ):
     head = pl.program_id(0)
     at = pl.multiple_of(head * HD, HD)
 
     def copies(h):
+        exp_all_ref, covariance_all_ref, exp_sems, covariance_sems = early
         return (
             pltpu.make_async_copy(exp_ref.at[h], exp_all_ref.at[h], exp_sems.at[h]),
             pltpu.make_async_copy(
@@ -406,7 +416,7 @@
 
     @pl.when(head == 0)
     def _():
-        for h in range(LANES // HD):
+        for h in range(LANES // HD if early else 0):
             for copy in copies(h):
                 copy.start()
         me = column_ref[0]
@@ -425,23 +435,34 @@
     scaled = grads * inverse
     delta = jnp.sum(scaled * offset, axis=0, keepdims=True)
     features = [scaled[j : j + 1] * query for j in range(HD)] + [delta * query, scaled]
-    for copy in copies(head):
-        copy.wait()
-    sums = dot_rows(jnp.concatenate([f.astype(bf16) for f in features], axis=0), exp_all_ref[head])
+    if early:
+        for copy in copies(head):
+            copy.wait()
+        weights, covariance = early[0].at[head], early[1].at[head]
+    else:
+        weights, covariance = exp_ref.at[0], covariance_ref.at[0]
+    sums = dot_rows(jnp.concatenate([f.astype(bf16) for f in features], axis=0), weights[...])
     d_value_ref[pl.ds(at, HD), :] = sums[(HD + 1) * HD :].astype(bf16)
     d_key = centered[0:1] * sums[:HD]
-    d_query = grads[0:1] * covariance_all_ref[head, :HD, :].astype(f32)
+    d_query = grads[0:1] * covariance[:HD, :].astype(f32)
     for j in range(1, HD):
         rows = slice(j * HD, (j + 1) * HD)
         d_key += centered[j : j + 1] * sums[rows]
-        d_query += grads[j : j + 1] * covariance_all_ref[head, rows, :].astype(f32)
+        d_query += grads[j : j + 1] * covariance[rows, :].astype(f32)
     d_key_ref[pl.ds(at, HD), :] = (d_key - sums[HD * HD : (HD + 1) * HD]).astype(bf16)
     d_query_ref[pl.ds(at, HD), :] = (d_query * score_scale).astype(bf16)
 
 
-def attention_backward(patch, weights, inverse, covariance, query_t, value_t, attended, grads, weight, column):
+def attention_backward(patch, resident, weights, inverse, covariance, query_t, value_t, attended, grads, weight, column):
     features = weight.shape[0]
     heads = LANES // HD
+    in_hbm = pl.BlockSpec(memory_space=pltpu.HBM)
+    early = [
+        pltpu.VMEM((heads, PATCH, PATCH), bf16),
+        pltpu.VMEM((heads, HD * HD, PATCH), bf16),
+        pltpu.SemaphoreType.DMA((heads,)),
+        pltpu.SemaphoreType.DMA((heads,)),
+    ]
     tall = pl.BlockSpec((LANES, PATCH), lambda h, c: (0, 0))
     part = pl.BlockSpec((LANES, PATCH), lambda h, c: (0, patch))
     per_head = lambda h, c: (h, 0, 0)
@@ -453,9 +474,9 @@
             num_scalar_prefetch=1,
             grid=(heads,),
             in_specs=[
-                pl.BlockSpec(memory_space=pltpu.HBM),
+                pl.BlockSpec((1, PATCH, PATCH), per_head) if resident else in_hbm,
                 pl.BlockSpec((1, 1, PATCH), per_head),
-                pl.BlockSpec(memory_space=pltpu.HBM),
+                pl.BlockSpec((1, HD * HD, PATCH), per_head) if resident else in_hbm,
                 tall,
                 tall,
                 tall,
@@ -466,16 +487,10 @@
                 pl.BlockSpec(weight.shape, lambda h, c: (0, 0)),
             ],
             out_specs=[pl.BlockSpec((features, PATCH), lambda h, c: (0, 0)), tall, tall, tall],
-            scratch_shapes=[
-                pltpu.VMEM((LANES, PATCH), bf16),
-                pltpu.VMEM((heads, PATCH, PATCH), bf16),
-                pltpu.VMEM((heads, HD * HD, PATCH), bf16),
-                pltpu.SemaphoreType.DMA((heads,)),
-                pltpu.SemaphoreType.DMA((heads,)),
-            ],
+            scratch_shapes=[pltpu.VMEM((LANES, PATCH), bf16)] + ([] if resident else early),
         ),
         out_shape=[pltpu.VMEM((features, PATCH), bf16), turned, turned, turned],
-        compiler_params=params(30),
+        compiler_params=params(14 if resident else 30),
         cost_estimate=cost(1100 * elements, 2 * elements),
         name="attention_backward",
     )(column, weights, inverse, covariance, query_t, value_t, attended, *grads, weight)
@@ -486,27 +501,29 @@
 
 
 def weight_grad_body(*refs):
-    *ins, out_ref = refs
-    patches = [ins[:6], ins[6:]]
-    for t in range(3):
-        total = dot(patches[0][t][...], patches[0][4][...]) + dot(patches[1][t][...], patches[1][4][...])
-        out_ref[:, t * LANES : (t + 1) * LANES] = total.T.astype(bf16)
-    total = dot_rows(patches[0][3][...], patches[0][5][...]) + dot_rows(
-        patches[1][3][...], patches[1][5][...]
-    )
-    out_ref[:, 3 * LANES :] = total.T.astype(bf16)
-
-
-def weight_grads(patches):
-    features = patches[0][4].shape[1]
+    d_query_ref, d_key_ref, d_value_ref, attended_ref, hidden_ref, d_out_ref, *before, out_ref = refs
+    hidden = hidden_ref[...]
+    parts = [dot(ref[...], hidden) for ref in (d_query_ref, d_key_ref, d_value_ref)]
+    parts.append(dot_rows(attended_ref[...], d_out_ref[...]))
+    for t, part in enumerate(parts):
+        columns = slice(t * LANES, (t + 1) * LANES)
+        if before:
+            out_ref[:, columns] = (before[0][columns, :] + part).T.astype(bf16)
+        else:
+            out_ref[columns, :] = part
+
+
+def weight_grads(*operands):
+    features = operands[4].shape[1]
     work = 2 * PATCH * features * LANES
+    last = len(operands) > 6
     return pl.pallas_call(
         weight_grad_body,
-        out_shape=whole((features, 4 * LANES), bf16),
+        out_shape=whole((features, 4 * LANES), bf16) if last else pltpu.VMEM((4 * LANES, features), f32),
         compiler_params=params(12),
-        cost_estimate=cost(8 * work, 12 * PATCH * features),
+        cost_estimate=cost(4 * work, 12 * PATCH * features),
         name="weight_grads",
-    )(*patches[0], *patches[1])
+    )(*operands)
 
 
 def split_sums(sums):
@@ -679,7 +696,7 @@
     buckets = bucket_rows(voxel_grads, voxel_shard, voxel_point, column, shards, capacity)
     got = exchange(buckets.reshape(shards * (capacity + INDEX_ROWS), LANES))
     owns = [
-        permute_rows(arrived, arrive_order, zero, p, patches, pltpu.VMEM, 8)
+        permute_rows(arrived, arrive_order, zero, p, patches, pltpu.VMEM, 12)
         for p in range(patches)
     ]
     across = [swap(own, 2) for own in owns]
@@ -687,8 +704,9 @@
 
     def forward(p):
         columns = (owns[p], across[p], swap(owns[p], 1), swap(across[p], 1))
-        projected = project(columns, weight, column)
-        return projected, attention_forward(projected[3], projected[4], *projected[6:])
+        space = pltpu.VMEM if p == patches - 1 else pltpu.HBM
+        projected = project(columns, weight, column, space)
+        return projected, attention_forward(projected[3], projected[4], *projected[6:], space)
 
     projected0, forward0 = forward(0)
     (got, across[1]), forward0 = after((got, across[1]), forward0)
@@ -700,35 +718,37 @@
     grads = (summed_rows, summed_across, swap(summed_rows, 1), swap(summed_across, 1))
     forwards = [(projected0, forward0), (projected1, forward1)]
 
-    kept, sums, received, grad_parts = [], [], [], []
-    for p in range(patches):
+    kept, sums, received = {}, {}, {}
+    for p in reversed(range(patches)):
         (hidden, _, _, _, _, query_t, key_t, value_t), (weights, attended, inverse, covariance) = forwards[p]
-        if p > 0:
+        if p == 0:
             weights, sent = after(weights, sent)
-            received.append(swap(sent, 2))
+            received[1] = swap(sent, 2)
+            weights, covariance = in_hbm(weights), in_hbm(covariance)
         d_out, d_query, d_key, d_value = attention_backward(
-            p, weights, inverse, covariance, query_t, value_t, attended, grads, out_weight, column
+            p, p == patches - 1, weights, inverse, covariance, query_t, value_t, attended, grads,
+            out_weight, column,
         )
-        if p > 0:
-            received[p - 1], d_query = after(received[p - 1], d_query)
-        grad_parts.append((d_query, d_key, d_value, attended, hidden, d_out))
-        if p == patches - 1:
-            weight_parts = weight_grads(grad_parts)
-            (d_query, d_key, d_value, query_t, key_t, value_t), weight_parts = after(
-                (d_query, d_key, d_value, query_t, key_t, value_t), weight_parts
-            )
-            d_query, d_key, d_value, query_t, key_t, value_t = map(
-                in_hbm, (d_query, d_key, d_value, query_t, key_t, value_t)
-            )
+        if p == 0:
+            received[1], d_query = after(received[1], d_query)
+        grad_operands = (d_query, d_key, d_value, attended, hidden, d_out)
+        if p == 0:
+            weight_parts = weight_grads(*grad_operands, first_parts)
+            operands = (d_query, d_key, d_value, query_t, key_t, value_t)
+            operands, weight_parts = after(operands, weight_parts)
+            d_query, d_key, d_value, query_t, key_t, value_t = map(in_hbm, operands)
         mine, other, own_sums = hidden_part(d_query, d_key, d_value, query_t, key_t, value_t, weight, column)
         partner = swap(other, 1)
-        keep, pair_sums, sent = pair_sum(mine, own_sums, partner)
-        kept.append(keep)
-        sums.append(pair_sums)
-    received.append(swap(sent, 2))
+        if p > 0:
+            first_parts = weight_grads(*grad_operands)
+            partner, first_parts = after(partner, first_parts)
+        kept[p], sums[p], sent = pair_sum(mine, own_sums, partner)
+    received[0] = swap(sent, 2)
     d_points = None
-    for p in range(patches):
-        normed, inv_scale = map(in_hbm, forwards[p][0][1:3])
+    for p in reversed(range(patches)):
+        normed, inv_scale = forwards[p][0][1:3]
+        if p > 0:
+            normed, inv_scale = in_hbm(normed), in_hbm(inv_scale)
         d_points = points_grad(
             p, patches, kept[p], sums[p], received[p], grads[0], normed, inv_scale, d_points
         )

time: 147 us -> 136 us (0.925)
  Pallas kernels: 98.6 us -> 90.4 us
  local copies, waits for them, and re-layouts: 3.42 us -> 1.03 us
    unnamed x38 -> x34, local copies, waits for them, and re-layouts: 3.42 us -> 1.03 us
    pallas_call x2, Pallas kernels: 21.2 us -> 19 us  [attention_backward(): pl.pallas_call(backward_body, grid_spec=pltpu.PrefetchScalarGridSpec(num_...]
    pallas_call x1, Pallas kernels: 5.39 us -> 3.19 us  [segment_rows(): pl.pallas_call(segment_body, grid=(shards // group,), in_specs=[pl.BlockS...]
  transfers between devices with their start and end apart: 16 -> 16, of which waited for: 6 -> 6; matrix products, arithmetic and copies ran while one was open for 0% -> 0% of each run, Pallas kernels for 54% -> 56%
where the time goes in v5:
time: 136 us; the launch traced here: 135 us
  Pallas kernels  90.4 us (66%)
  starting transfers between devices  24.8 us (18%)
  waiting for transfers between devices  18 us (13%)
    pallas_call x2, Pallas kernels, attention_forward(): pl.pallas_call(forward_body, grid=(heads,), in_specs=[pl.BlockSpec((PATCH...  36.5 us
    pallas_call x2, Pallas kernels, attention_backward(): pl.pallas_call(backward_body, grid_spec=pltpu.PrefetchScalarGridSpec(num_...  19 us
    all_to_all x3, starting transfers between devices, exchange(): return lax.all_to_all(rows, 'seq', split_axis=0, concat_axis=0, tiled=True)  16.8 us
    ppermute x13, waiting for transfers between devices, swap(): return lax.ppermute(rows, 'mp', [(i, i ^ mask) for i in range(members)])  15 us
    pallas_call x1, Pallas kernels, bucket_rows(): pl.pallas_call(functools.partial(bucket_body, shards, capacity), grid_spe...  11.5 us
    ppermute x13, starting transfers between devices, swap(): return lax.ppermute(rows, 'mp', [(i, i ^ mask) for i in range(members)])  8.02 us
    pallas_call x2, Pallas kernels, project(): pl.pallas_call(project_body, grid_spec=pltpu.PrefetchScalarGridSpec(num_s...  5.18 us
    pallas_call x3, Pallas kernels, permute_rows(): pl.pallas_call(permute_body, grid_spec=pltpu.PrefetchScalarGridSpec(num_s...  4.86 us
  transfers between devices with their start and end apart: 16, of which 6 were waited for; matrix products, arithmetic and copies ran while one was open for 0% of the time, Pallas kernels for 56%

profile of v5, /device:TPU:0, one launch (start us, length us, event | category | flops | bytes accessed | tf_op | source)
XLA Modules:
  0.0 135.1 jit_solution(3775043832849622641)
XLA Ops:
  0.6 3.3 %permute_rows.3 = bf16[2048,128]{1,0:T(8,128)(2,1)} custom-call(s32[1]{0:T(128)} %bitcast.column_ref, s32[16,128]{1,0:T(8,128)} %bitcast.22, bf16[2048,512]{1,0:T(8,128)(2,1)} %block_ref.1), custom_call_target="tpu_custom_call" | custom-call | flops 4294967296 | bytes 1572864 | tf_op jit(solution)/shard_map/permute_rows/pallas_call | solution.py:81
  4.0 7.2 %all-to-all-start.1 = ((bf16[8,256,128]{2,1,0:T(8,128)(2,1)}), bf16[8,256,128]{2,1,0:T(8,128)(2,1)S(1)}, u32[]{:S(2)}, u32[]{:S(2)}) async-start(bf16[8,256,128]{2,1,0:T(8,128)(2,1)} %bitcast.20), calls=%async_computation.1 | async-start | bytes 1048576 | tf_op jit(solution)/shard_map/all_to_all | solution.py:687
  11.2 11.5 %bucket_rows.1 = bf16[8,528,128]{2,1,0:T(8,128)(2,1)} custom-call(s32[1]{0:T(128)} %bitcast.column_ref, s32[16,128]{1,0:T(8,128)} %bitcast.23, s32[16,128]{1,0:T(8,128)} %bitcast.24, bf16[2048,512]{1,0:T(8,128)(2,1)} %grads_ref.1), custom_call_target="tpu_custom_call" | custom-call | flops 8589934592 | bytes 3145728 | tf_op jit(solution)/shard_map/bucket_rows/pallas_call | solution.py:155
  22.7 3.0 %all-to-all-done.1 = bf16[8,256,128]{2,1,0:T(8,128)(2,1)S(1)} async-done(((bf16[8,256,128]{2,1,0:T(8,128)(2,1)}), bf16[8,256,128]{2,1,0:T(8,128)(2,1)S(1)}, u32[]{:S(2)}, u32[]{:S(2)}) %all-to-all-start.1) | async-done | bytes 524320 | tf_op jit(solution)/shard_map/all_to_all | solution.py:687
  25.7 3.7 %all-to-all-start = ((bf16[8,528,128]{2,1,0:T(8,128)(2,1)}), bf16[8,528,128]{2,1,0:T(8,128)(2,1)S(1)}, u32[]{:S(2)}, u32[]{:S(2)}) async-start(bf16[8,528,128]{2,1,0:T(8,128)(2,1)} %bucket_rows.1), calls=%async_computation | async-start | bytes 2162688 | tf_op jit(solution)/shard_map/all_to_all | solution.py:687
  29.5 0.0 copy-start
  29.5 0.0 copy-done.14
  29.5 0.8 permute_rows.5.x0_ref
  30.2 1.6 %collective-permute-start.1 = (bf16[1024,128]{1,0:T(8,128)(2,1)S(1)}, bf16[1024,128]{1,0:T(8,128)(2,1)S(1)}, u32[]{:S(2)}, u32[]{:S(2)}) collective-permute-start(bf16[1024,128]{1,0:T(8,128)(2,1)S(1)} %permute_rows.5.x0_ref), channel_id=1, source_target_pairs={{0,2},{1,3},{2,0},{3,1},{4,6},{5,7},{6,4},{7,5},{8,10},{9,11},{10,... | collective-permute-start | bytes 786440 | tf_op jit(solution)/shard_map/ppermute | solution.py:684
  31.8 0.0 collective-permute-start.2
  31.8 0.8 permute_rows.4.x0_ref
  32.6 5.5 %collective-permute-done.1.x1_ref = bf16[1024,128]{1,0:T(8,128)(2,1)S(1)} collective-permute-done((bf16[1024,128]{1,0:T(8,128)(2,1)S(1)}, bf16[1024,128]{1,0:T(8,128)(2,1)S(1)}, u32[]{:S(2)}, u32[]{:S(2)}) %collective-permute-start.1) | collective-permute-done | bytes 262176 | tf_op jit(solution)/shard_map/ppermute | solution.py:684
  38.1 0.0 collective-permute-start.3
  38.2 1.5 %collective-permute-start = (bf16[1024,128]{1,0:T(8,128)(2,1)S(1)}, bf16[1024,128]{1,0:T(8,128)(2,1)S(1)}, u32[]{:S(2)}, u32[]{:S(2)}) collective-permute-start(bf16[1024,128]{1,0:T(8,128)(2,1)S(1)} %permute_rows.4.x0_ref), channel_id=1, source_target_pairs={{0,2},{1,3},{2,0},{3,1},{4,6},{5,7},{6,4},{7,5},{8,10},{9,11},{10,... | collective-permute-start | bytes 786440 | tf_op jit(solution)/shard_map/ppermute | solution.py:684
  39.7 0.2 collective-permute-start.5
  39.9 0.0 collective-permute-done.2.x2_ref
  39.9 0.0 collective-permute-done.3.x3_ref
  39.9 0.0 copy-done
  39.9 2.7 %project.2 = (bf16[1024,512]{1,0:T(8,128)(2,1)}, f32[128,1024]{1,0:T(8,128)}, f32[8,1024]{1,0:T(8,128)}, bf16[1024,128]{1,0:T(8,128)(2,1)S(1)}, bf16[128,1024]{1...) custom-call(s32[1]{0:T(128)} %bitcast.column_ref, ...), custom_call_target="tpu_custom_call" | custom-call | flops 805306368 | bytes 5242880 | tf_op jit(solution)/shard_map/project/pallas_call | solution.py:276
  42.6 19.1 %attention_forward.2 = (bf16[8,1024,1024]{2,1,0:T(8,128)(2,1)}, bf16[128,1024]{1,0:T(8,128)(2,1)}, f32[8,1,1024]{2,1,0:T(1,128)S(1)}, bf16[8,256,1024]{2,1,0:T(8,128)(2,1)}) custom-call(bf16[1024,128]{1,0:T(8,128)(2,1)S(1)} %get-tuple-element.78.key_ref, bf16[128,1024]{1,0:T(8,128)(2,1)S(1)} %get-tuple-element.79.base2_t_ref, ...), custom_call_target="tpu_custom_call" | custom-call | flops 13421772800 | bytes 16777216 | tf_op jit(solution)/shard_map/attention_forward/pallas_call | solution.py:362
  61.7 0.0 copy-done.9
  61.7 0.0 collective-permute-done.x1_ref
  61.7 0.0 all-to-all-done
  61.8 3.2 %segment_rows.1.g0_ref.d_out_ref = bf16[128,2048]{1,0:T(8,128)(2,1)S(1)} custom-call(bf16[8,528,128]{2,1,0:T(8,128)(2,1)S(1)} %all-to-all-done), custom_call_target="tpu_custom_call" | custom-call | flops 8858370048 | bytes 3244032 | tf_op jit(solution)/shard_map/segment_rows/pallas_call | solution.py:214
  64.9 0.0 copy-done.15
  65.0 0.3 collective-permute-start.6
  65.3 1.1 collective-permute-start.4
  66.4 0.2 collective-permute-start.7
  66.5 0.0 collective-permute-done.5.x2_ref
  66.5 0.0 collective-permute-done.6.x3_ref
  66.6 2.5 %project.3 = (bf16[1024,512]{1,0:T(8,128)(2,1)S(1)}, f32[128,1024]{1,0:T(8,128)}, f32[8,1024]{1,0:T(8,128)}, bf16[1024,128]{1,0:T(8,128)(2,1)S(1)}, bf16[128,102...) custom-call(s32[1]{0:T(128)} %bitcast.column_ref, ...), custom_call_target="tpu_custom_call" | custom-call | flops 805306368 | bytes 5242880 | tf_op jit(solution)/shard_map/project/pallas_call | solution.py:276
  69.1 17.4 %attention_forward.3 = (bf16[8,1024,1024]{2,1,0:T(8,128)(2,1)S(1)}, bf16[128,1024]{1,0:T(8,128)(2,1)S(1)}, f32[8,1,1024]{2,1,0:T(1,128)S(1)}, bf16[8,256,1024]{2,1,0:T(8,128)(2,1)S(1)}) custom-call(bf16[1024,128]{1,0:T(8,128)(2,1)S(1)} %get-tuple-element.91.key_ref, bf16[128,1024]{1,0:T(8,128)(2,1)S(1)} %get-tuple-element.92.base2_t_ref, ...), custom_call_target="tpu_custom_call" | custom-call | flops 13421772800 | bytes 16777216 | tf_op jit(solution)/shard_map/attention_forward/pallas_call | solution.py:362
  86.4 0.0 collective-permute-done.4.g1_ref
  86.4 0.4 collective-permute-start.8
  86.9 0.0 collective-permute-done.7.g2_ref
  86.9 1.6 %collective-permute-done.8.g3_ref = bf16[128,2048]{1,0:T(8,128)(2,1)S(1)} collective-permute-done((bf16[128,2048]{1,0:T(8,128)(2,1)S(1)}, bf16[128,2048]{1,0:T(8,128)(2,1)S(1)}, u32[]{:S(2)}, u32[]{:S(2)}) %collective-permute-start.8) | collective-permute-done | bytes 524320 | tf_op jit(solution)/shard_map/ppermute | solution.py:684
  88.4 8.2 %attention_backward.2 = (bf16[512,1024]{1,0:T(8,128)(2,1)S(1)}, bf16[128,1024]{1,0:T(8,128)(2,1)S(1)}, bf16[128,1024]{1,0:T(8,128)(2,1)S(1)}, bf16[128,1024]{1,0:T(8,128)(2,1)S(1)}) custom-call(s32[1]{0:T(128)} %bitcast.column_ref, bf16[8,1024,1024]{2,1,0:T(8,128)(2,1)S(1)} %get-tuple-element.99.exp_ref, f32[8,1,1024]{2,1,0:T(1,128)S(1)} %get-tuple-element.100.inverse_ref, ...), custom_call_target="tpu_custom_call" | custom-call | flops 9227468800 | bytes 16777216 | tf_op jit(solution)/shard_map/attention_backward/pallas_call | solution.py:471
  96.6 0.0 copy-start.16
  96.6 1.0 hidden_part.2
  97.6 0.4 collective-permute-start.9
  98.1 0.9 weight_grads.2.refs_6_
  99.0 0.7 collective-permute-done.9.got_ref
  99.7 0.1 pair_sum.2
  99.8 1.3 collective-permute-start.10
  101.1 0.0 copy-done.16
  101.1 0.0 copy-start.4
  101.2 10.8 %attention_backward.3 = (bf16[512,1024]{1,0:T(8,128)(2,1)S(1)}, bf16[128,1024]{1,0:T(8,128)(2,1)S(1)}, bf16[128,1024]{1,0:T(8,128)(2,1)S(1)}, bf16[128,1024]{1,0:T(8,128)(2,1)S(1)}) custom-call(s32[1]{0:T(128)} %bitcast.column_ref, bf16[8,1024,1024]{2,1,0:T(8,128)(2,1)} %get-tuple-element.117.exp_ref, f32[8,1,1024]{2,1,0:T(1,128)S(1)} %copy-done.16, ...), custom_call_target="tpu_custom_call" | custom-call | flops 9227468800 | bytes 16777216 | tf_op jit(solution)/shard_map/attention_backward/pallas_call | solution.py:471
  112.0 0.0 collective-permute-done.10.got_ref
  112.0 0.0 copy-start.6
  112.0 0.0 copy-done.4
  112.1 1.8 %weight_grads.3 = bf16[512,512]{1,0:T(8,128)(2,1)} custom-call(bf16[128,1024]{1,0:T(8,128)(2,1)S(1)} %get-tuple-element.129.refs_0_.d_query_ref, bf16[128,1024]{1,0:T(8,128)(2,1)S(1)} %get-tuple-element.130.refs_1_.d_key_ref, bf16[128,1024]{1,0:T(8,128)(2,1)S(1)} %get-tuple-element.131.refs_2_.d_value_ref, bf16[128,1024]{1,0:T(8,128)(2,1)S(1)} %copy-done.11, ...), custom_call_target="tpu_custom_call" | custom-call | flops 536870912 | bytes 6291456 | tf_op jit(solution)/shard_map/weight_grads/pallas_call | solution.py:520
  113.9 5.8 %all-to-all-start.2 = ((bf16[8,64,512]{2,1,0:T(8,128)(2,1)}), bf16[8,64,512]{2,1,0:T(8,128)(2,1)S(1)}, u32[]{:S(2)}, u32[]{:S(2)}) async-start(bf16[8,64,512]{2,1,0:T(8,128)(2,1)} %bitcast.10), calls=%async_computation.2 | async-start | bytes 1048576 | tf_op jit(solution)/shard_map/all_to_all | solution.py:687
  119.8 2.4 %hidden_part.3 = (bf16[256,1024]{1,0:T(8,128)(2,1)S(1)}, bf16[272,1024]{1,0:T(8,128)(2,1)S(1)}, f32[2,1024]{1,0:T(2,128)S(1)}) custom-call(s32[1]{0:T(128)} %bitcast.column_ref, bf16[128,1024]{1,0:T(8,128)(2,1)} %copy-done.1, bf16[128,1024]{1,0:T(8,128)(2,1)} %copy-done.2, bf16[128,1024]{1,0:T(8,128)(2,1)} %copy-done.3, bf16[128,1024]{1,0:T(8,128)(2,1)} %copy-done.8, ...), custom_call_target="tpu_custom_call" | custom-call | flops 402653184 | bytes 2097152 | tf_op jit(solution)/shard_map/hidden_part/pallas_call | solution.py:576
  122.1 0.1 collective-permute-start.11
  122.2 1.9 %collective-permute-done.11.got_ref = bf16[272,1024]{1,0:T(8,128)(2,1)S(1)} collective-permute-done((bf16[272,1024]{1,0:T(8,128)(2,1)S(1)}, bf16[272,1024]{1,0:T(8,128)(2,1)S(1)}, u32[]{:S(2)}, u32[]{:S(2)}) %collective-permute-start.11) | collective-permute-done | bytes 557088 | tf_op jit(solution)/shard_map/ppermute | solution.py:684
  124.2 0.1 pair_sum.3
  124.3 0.9 collective-permute-start.12
  125.2 1.0 copy-done.7
  126.1 2.1 %points_grad.2.rest_0_ = f32[2048,128]{1,0:T(8,128)} custom-call(f32[128,1024]{1,0:T(8,128)S(1)} %get-tuple-element.143.kept_ref, f32[2,1024]{1,0:T(2,128)S(1)} %get-tuple-element.144.sums_ref, bf16[144,1024]{1,0:T(8,128)(2,1)S(1)} %copy-done.7, bf16[128,2048]{1,0:T(8,128)(2,1)S(1)} %segment_rows.1.g0_ref.d_out_ref, ...), custom_call_target="tpu_custom_call" | custom-call | flops 1048576 | bytes 3145728 | tf_op jit(solution)/shard_map/points_grad/pallas_call | solution.py:630
  128.2 5.2 %collective-permute-done.12.got_ref = bf16[144,1024]{1,0:T(8,128)(2,1)S(1)} collective-permute-done((bf16[144,1024]{1,0:T(8,128)(2,1)S(1)}, bf16[144,1024]{1,0:T(8,128)(2,1)S(1)}, u32[]{:S(2)}, u32[]{:S(2)}) %collective-permute-start.12) | collective-permute-done | bytes 294944 | tf_op jit(solution)/shard_map/ppermute | solution.py:684
  133.4 0.0 copy-done.12
  133.4 1.0 points_grad.3
  134.4 0.0 all-to-all-done.2.parts_ref
  134.4 0.7 grad_sum.1
  (22 shorter events, 0.0 us)
Async XLA Ops:
  4.0 21.7 %all-to-all-start.1 = ((bf16[8,256,128]{2,1,0:T(8,128)(2,1)}), bf16[8,256,128]{2,1,0:T(8,128)(2,1)S(1)}, u32[]{:S(2)}, u32[]{:S(2)}) async-start(bf16[8,256,128]{2,1,0:T(8,128)(2,1)} %bitcast.20), calls=%async_computation.1 | async-start | bytes 1048576 | tf_op jit(solution)/shard_map/all_to_all | solution.py:687
  11.2 18.3 %copy-start.14 = (s32[2048]{0:T(1024)S(1)}, s32[2048]{0:T(1024)}, u32[]{:S(2)}) copy-start(s32[2048]{0:T(1024)} %param.10) | copy-start | bytes 24580
  25.7 36.0 %all-to-all-start = ((bf16[8,528,128]{2,1,0:T(8,128)(2,1)}), bf16[8,528,128]{2,1,0:T(8,128)(2,1)S(1)}, u32[]{:S(2)}, u32[]{:S(2)}) async-start(bf16[8,528,128]{2,1,0:T(8,128)(2,1)} %bucket_rows.1), calls=%async_computation | async-start | bytes 2162688 | tf_op jit(solution)/shard_map/all_to_all | solution.py:687
  29.5 10.4 %copy-start = (bf16[512,3,128]{2,0,1:T(8,128)(2,1)S(1)}, bf16[512,3,128]{2,0,1:T(8,128)(2,1)}, u32[]{:S(2)}) copy-start(bf16[512,3,128]{2,0,1:T(8,128)(2,1)} %param.11) | copy-start | bytes 1179652
  30.2 7.9 %collective-permute-start.1 = (bf16[1024,128]{1,0:T(8,128)(2,1)S(1)}, bf16[1024,128]{1,0:T(8,128)(2,1)S(1)}, u32[]{:S(2)}, u32[]{:S(2)}) collective-permute-start(bf16[1024,128]{1,0:T(8,128)(2,1)S(1)} %permute_rows.5.x0_ref), channel_id=1, source_target_pairs={{0,2},{1,3},{2,0},{3,1},{4,6},{5,7},{6,4},{7,5},{8,10},{9,11},{10,... | collective-permute-start | bytes 786440 | tf_op jit(solution)/shard_map/ppermute | solution.py:684
  31.8 8.1 %collective-permute-start.2 = (bf16[1024,128]{1,0:T(8,128)(2,1)S(1)}, bf16[1024,128]{1,0:T(8,128)(2,1)S(1)}, u32[]{:S(2)}, u32[]{:S(2)}) collective-permute-start(bf16[1024,128]{1,0:T(8,128)(2,1)S(1)} %permute_rows.5.x0_ref), channel_id=1, source_target_pairs={{0,1},{1,0},{2,3},{3,2},{4,5},{5,4},{6,7},{7,6},{8,9},{9,8},{10,11... | collective-permute-start | bytes 786440 | tf_op jit(solution)/shard_map/ppermute | solution.py:684
  38.1 1.8 %collective-permute-start.3 = (bf16[1024,128]{1,0:T(8,128)(2,1)S(1)}, bf16[1024,128]{1,0:T(8,128)(2,1)S(1)}, u32[]{:S(2)}, u32[]{:S(2)}) collective-permute-start(bf16[1024,128]{1,0:T(8,128)(2,1)S(1)} %collective-permute-done.1.x1_ref), channel_id=1, source_target_pairs={{0,1},{1,0},{2,3},{3,2},{4,5},{5,4},{6,7},{7,6},{8,9},{9,8},{10,11... | collective-permute-start | bytes 786440 | tf_op jit(solution)/shard_map/ppermute | solution.py:684
  38.2 23.6 %collective-permute-start = (bf16[1024,128]{1,0:T(8,128)(2,1)S(1)}, bf16[1024,128]{1,0:T(8,128)(2,1)S(1)}, u32[]{:S(2)}, u32[]{:S(2)}) collective-permute-start(bf16[1024,128]{1,0:T(8,128)(2,1)S(1)} %permute_rows.4.x0_ref), channel_id=1, source_target_pairs={{0,2},{1,3},{2,0},{3,1},{4,6},{5,7},{6,4},{7,5},{8,10},{9,11},{10,... | collective-permute-start | bytes 786440 | tf_op jit(solution)/shard_map/ppermute | solution.py:684
  39.7 26.9 %collective-permute-start.5 = (bf16[1024,128]{1,0:T(8,128)(2,1)S(1)}, bf16[1024,128]{1,0:T(8,128)(2,1)S(1)}, u32[]{:S(2)}, u32[]{:S(2)}) collective-permute-start(bf16[1024,128]{1,0:T(8,128)(2,1)S(1)} %permute_rows.4.x0_ref), channel_id=1, source_target_pairs={{0,1},{1,0},{2,3},{3,2},{4,5},{5,4},{6,7},{7,6},{8,9},{9,8},{10,11... | collective-permute-start | bytes 786440 | tf_op jit(solution)/shard_map/ppermute | solution.py:684
  42.6 19.1 %copy-start.9 = (bf16[128,1024]{1,0:T(8,128)(2,1)}, bf16[128,1024]{1,0:T(8,128)(2,1)S(1)}, u32[]{:S(2)}) copy-start(bf16[128,1024]{1,0:T(8,128)(2,1)S(1)} %get-tuple-element.133.key_t_ref.key_ref) | copy-start | bytes 786436
  42.6 58.5 %copy-start.8 = (bf16[128,1024]{1,0:T(8,128)(2,1)}, bf16[128,1024]{1,0:T(8,128)(2,1)S(1)}, u32[]{:S(2)}) copy-start(bf16[128,1024]{1,0:T(8,128)(2,1)S(1)} %get-tuple-element.132.query_t_ref.query_ref) | copy-start | bytes 786436
  42.6 58.5 %copy-start.10 = (bf16[128,1024]{1,0:T(8,128)(2,1)}, bf16[128,1024]{1,0:T(8,128)(2,1)S(1)}, u32[]{:S(2)}) copy-start(bf16[128,1024]{1,0:T(8,128)(2,1)S(1)} %get-tuple-element.134.value_t_ref.value_ref) | copy-start | bytes 786436
  61.7 3.2 %copy-start.15 = (f32[8,1,1024]{2,1,0:T(1,128)}, f32[8,1,1024]{2,1,0:T(1,128)S(1)}, u32[]{:S(2)}) copy-start(f32[8,1,1024]{2,1,0:T(1,128)S(1)} %get-tuple-element.118.inverse_ref) | copy-start | bytes 98308
  65.0 1.6 %collective-permute-start.6 = (bf16[1024,128]{1,0:T(8,128)(2,1)S(1)}, bf16[1024,128]{1,0:T(8,128)(2,1)S(1)}, u32[]{:S(2)}, u32[]{:S(2)}) collective-permute-start(bf16[1024,128]{1,0:T(8,128)(2,1)S(1)} %collective-permute-done.x1_ref), channel_id=1, source_target_pairs={{0,1},{1,0},{2,3},{3,2},{4,5},{5,4},{6,7},{7,6},{8,9},{9,8},{10,11... | collective-permute-start | bytes 786440 | tf_op jit(solution)/shard_map/ppermute | solution.py:684
  65.3 21.1 %collective-permute-start.4 = (bf16[128,2048]{1,0:T(8,128)(2,1)S(1)}, bf16[128,2048]{1,0:T(8,128)(2,1)S(1)}, u32[]{:S(2)}, u32[]{:S(2)}) collective-permute-start(bf16[128,2048]{1,0:T(8,128)(2,1)S(1)} %segment_rows.1.g0_ref.d_out_ref), channel_id=1, source_target_pairs={{0,2},{1,3},{2,0},{3,1},{4,6},{5,7},{6,4},{7,5},{8,10},{9,11},{10,... | collective-permute-start | bytes 1572872 | tf_op jit(solution)/shard_map/ppermute | solution.py:684
  66.4 20.5 %collective-permute-start.7 = (bf16[128,2048]{1,0:T(8,128)(2,1)S(1)}, bf16[128,2048]{1,0:T(8,128)(2,1)S(1)}, u32[]{:S(2)}, u32[]{:S(2)}) collective-permute-start(bf16[128,2048]{1,0:T(8,128)(2,1)S(1)} %segment_rows.1.g0_ref.d_out_ref), channel_id=1, source_target_pairs={{0,1},{1,0},{2,3},{3,2},{4,5},{5,4},{6,7},{7,6},{8,9},{9,8},{10,11... | collective-permute-start | bytes 1572872 | tf_op jit(solution)/shard_map/ppermute | solution.py:684
  69.1 19.4 %copy-start.13 = (bf16[512,128]{1,0:T(8,128)(2,1)S(1)}, bf16[512,128]{1,0:T(8,128)(2,1)}, u32[]{:S(2)}) copy-start(bf16[512,128]{1,0:T(8,128)(2,1)} %weight_ref.3) | copy-start | bytes 393220
  86.4 2.0 %collective-permute-start.8 = (bf16[128,2048]{1,0:T(8,128)(2,1)S(1)}, bf16[128,2048]{1,0:T(8,128)(2,1)S(1)}, u32[]{:S(2)}, u32[]{:S(2)}) collective-permute-start(bf16[128,2048]{1,0:T(8,128)(2,1)S(1)} %collective-permute-done.4.g1_ref), channel_id=1, source_target_pairs={{0,1},{1,0},{2,3},{3,2},{4,5},{5,4},{6,7},{7,6},{8,9},{9,8},{10,11... | collective-permute-start | bytes 1572872 | tf_op jit(solution)/shard_map/ppermute | solution.py:684
  96.6 4.5 %copy-start.11 = (bf16[128,1024]{1,0:T(8,128)(2,1)S(1)}, bf16[128,1024]{1,0:T(8,128)(2,1)}, u32[]{:S(2)}) copy-start(bf16[128,1024]{1,0:T(8,128)(2,1)} %get-tuple-element.121.attended_ref.refs_3_) | copy-start | bytes 786436
  96.6 4.5 %copy-start.16 = (f32[8,1,1024]{2,1,0:T(1,128)S(1)}, f32[8,1,1024]{2,1,0:T(1,128)}, u32[]{:S(2)}) copy-start(f32[8,1,1024]{2,1,0:T(1,128)} %copy-done.15) | copy-start | bytes 98308
  97.6 2.0 %collective-permute-start.9 = (bf16[272,1024]{1,0:T(8,128)(2,1)S(1)}, bf16[272,1024]{1,0:T(8,128)(2,1)S(1)}, u32[]{:S(2)}, u32[]{:S(2)}) collective-permute-start(bf16[272,1024]{1,0:T(8,128)(2,1)S(1)} %get-tuple-element.111), channel_id=1, source_target_pairs={{0,1},{1,0},{2,3},{3,2},{4,5},{5,4},{6,7},{7,6},{8,9},{9,8},{10,11... | collective-permute-start | bytes 1671176 | tf_op jit(solution)/shard_map/ppermute | solution.py:684
  99.8 12.2 %collective-permute-start.10 = (bf16[144,1024]{1,0:T(8,128)(2,1)S(1)}, bf16[144,1024]{1,0:T(8,128)(2,1)S(1)}, u32[]{:S(2)}, u32[]{:S(2)}) collective-permute-start(bf16[144,1024]{1,0:T(8,128)(2,1)S(1)} %get-tuple-element.116), channel_id=1, source_target_pairs={{0,2},{1,3},{2,0},{3,1},{4,6},{5,7},{6,4},{7,5},{8,10},{9,11},{10,... | collective-permute-start | bytes 884744 | tf_op jit(solution)/shard_map/ppermute | solution.py:684
  101.1 10.9 %copy-start.4 = (bf16[1024,512]{1,0:T(8,128)(2,1)S(1)}, bf16[1024,512]{1,0:T(8,128)(2,1)}, u32[]{:S(2)}) copy-start(bf16[1024,512]{1,0:T(8,128)(2,1)} %get-tuple-element.126.refs_4_) | copy-start | bytes 3145732
  112.0 7.7 %copy-start.1 = (bf16[128,1024]{1,0:T(8,128)(2,1)}, bf16[128,1024]{1,0:T(8,128)(2,1)S(1)}, u32[]{:S(2)}) copy-start(bf16[128,1024]{1,0:T(8,128)(2,1)S(1)} %get-tuple-element.129.refs_0_.d_query_ref) | copy-start | bytes 786436
  112.0 7.7 %copy-start.2 = (bf16[128,1024]{1,0:T(8,128)(2,1)}, bf16[128,1024]{1,0:T(8,128)(2,1)S(1)}, u32[]{:S(2)}) copy-start(bf16[128,1024]{1,0:T(8,128)(2,1)S(1)} %get-tuple-element.130.refs_1_.d_key_ref) | copy-start | bytes 786436
  112.0 7.7 %copy-start.3 = (bf16[128,1024]{1,0:T(8,128)(2,1)}, bf16[128,1024]{1,0:T(8,128)(2,1)S(1)}, u32[]{:S(2)}) copy-start(bf16[128,1024]{1,0:T(8,128)(2,1)S(1)} %get-tuple-element.131.refs_2_.d_value_ref) | copy-start | bytes 786436
  112.0 1.9 %copy-start.6 = (bf16[144,1024]{1,0:T(8,128)(2,1)}, bf16[144,1024]{1,0:T(8,128)(2,1)S(1)}, u32[]{:S(2)}) copy-start(bf16[144,1024]{1,0:T(8,128)(2,1)S(1)} %collective-permute-done.10.got_ref) | copy-start | bytes 884740
  113.9 19.5 %copy-start.5 = (f32[128,1024]{1,0:T(8,128)S(1)}, f32[128,1024]{1,0:T(8,128)}, u32[]{:S(2)}) copy-start(f32[128,1024]{1,0:T(8,128)} %get-tuple-element.141.normed_ref) | copy-start | bytes 1572868
  113.9 19.5 %copy-start.12 = (f32[8,1024]{1,0:T(8,128)S(1)}, f32[8,1024]{1,0:T(8,128)}, u32[]{:S(2)}) copy-start(f32[8,1024]{1,0:T(8,128)} %get-tuple-element.142.inv_ref) | copy-start | bytes 98308
  113.9 20.5 %all-to-all-start.2 = ((bf16[8,64,512]{2,1,0:T(8,128)(2,1)}), bf16[8,64,512]{2,1,0:T(8,128)(2,1)S(1)}, u32[]{:S(2)}, u32[]{:S(2)}) async-start(bf16[8,64,512]{2,1,0:T(8,128)(2,1)} %bitcast.10), calls=%async_computation.2 | async-start | bytes 1048576 | tf_op jit(solution)/shard_map/all_to_all | solution.py:687
  122.1 2.0 %collective-permute-start.11 = (bf16[272,1024]{1,0:T(8,128)(2,1)S(1)}, bf16[272,1024]{1,0:T(8,128)(2,1)S(1)}, u32[]{:S(2)}, u32[]{:S(2)}) collective-permute-start(bf16[272,1024]{1,0:T(8,128)(2,1)S(1)} %get-tuple-element.137), channel_id=1, source_target_pairs={{0,1},{1,0},{2,3},{3,2},{4,5},{5,4},{6,7},{7,6},{8,9},{9,8},{10,11... | collective-permute-start | bytes 1671176 | tf_op jit(solution)/shard_map/ppermute | solution.py:684
  124.3 9.1 %collective-permute-start.12 = (bf16[144,1024]{1,0:T(8,128)(2,1)S(1)}, bf16[144,1024]{1,0:T(8,128)(2,1)S(1)}, u32[]{:S(2)}, u32[]{:S(2)}) collective-permute-start(bf16[144,1024]{1,0:T(8,128)(2,1)S(1)} %get-tuple-element.140), channel_id=1, source_target_pairs={{0,2},{1,3},{2,0},{3,1},{4,6},{5,7},{6,4},{7,5},{8,10},{9,11},{10,... | collective-permute-start | bytes 884744 | tf_op jit(solution)/shard_map/ppermute | solution.py:684
  125.2 1.0 copy-start.7

commit v6 on v5

--- a/solution.py
+++ b/solution.py
@@ -14,7 +14,8 @@
 INDEX_BASE = 64
 BLOCK_MASKS = (0, 2, 1, 3)
 SAFE_SCORE = 60.0
-SEGMENT_SHARDS = 4
+STAGED_HEADS = 1
+SEGMENT_SHARDS = 8
 BUCKET_SHARDS = 2
 
 score_scale = 0.25
@@ -218,7 +219,7 @@
         out_specs=pl.BlockSpec((LANES, row_count), lambda i: (0, 0)),
         out_shape=pltpu.VMEM((LANES, row_count), bf16),
         scratch_shapes=[pltpu.VMEM((row_count // 2, 2 * LANES), f32)],
-        compiler_params=params(24),
+        compiler_params=params(40),
         cost_estimate=cost(
             8 * shards * message * row_count * LANES, 3 * shards * message * LANES * 2
         ),
@@ -267,7 +268,7 @@
 
 def project(blocks, weight, column, space):
     row_count = blocks[0].shape[0]
-    step_rows = 512
+    step_rows = row_count
     features = weight.shape[1]
     width = pl.BlockSpec((step_rows, LANES), lambda i, c: (i, 0))
     tall = pl.BlockSpec((LANES, step_rows), lambda i, c: (0, i))
@@ -382,118 +383,160 @@
     )(keys, base2_t, key_t, value_t)
 
 
-def backward_body(
-    column_ref,
-    exp_ref,
-    inverse_ref,
-    covariance_ref,
-    query_t_ref,
-    value_t_ref,
-    attended_ref,
-    g0_ref,
-    g1_ref,
-    g2_ref,
-    g3_ref,
-    weight_ref,
-    d_out_ref,
-    d_query_ref,
-    d_key_ref,
-    d_value_ref,
-    d_attended_ref,
-    *early,
-):
+def backward_body(first, *refs):
+    (
+        column_ref,
+        exp_ref,
+        inverse_ref,
+        query_t_ref,
+        value_t_ref,
+        attended_ref,
+        g0_ref,
+        g1_ref,
+        g2_ref,
+        g3_ref,
+        weight_ref,
+        covariance_ref,
+        *refs,
+    ) = refs
+    if first:
+        later_exp_ref, *refs = refs
+    else:
+        rest_ref, *refs = refs
+    d_out_ref, d_query_ref, d_key_ref, d_value_ref, *refs = refs
+    if first:
+        staged_ref, d_attended_ref, staged_sem = refs
+        staged = pltpu.make_async_copy(
+            later_exp_ref.at[pl.ds(0, STAGED_HEADS)], staged_ref, staged_sem
+        )
+    else:
+        d_attended_ref, exp_all_ref, exp_sems, covariance_all_ref, covariance_sems = refs
     head = pl.program_id(0)
     at = pl.multiple_of(head * HD, HD)
 
-    def copies(h):
-        exp_all_ref, covariance_all_ref, exp_sems, covariance_sems = early
-        return (
-            pltpu.make_async_copy(exp_ref.at[h], exp_all_ref.at[h], exp_sems.at[h]),
-            pltpu.make_async_copy(
-                covariance_ref.at[h], covariance_all_ref.at[h], covariance_sems.at[h]
-            ),
+    def exp_copy(h):
+        return pltpu.make_async_copy(
+            rest_ref.at[h + STAGED_HEADS], exp_all_ref.at[h], exp_sems.at[h]
+        )
+
+    def covariance_copy(h):
+        return pltpu.make_async_copy(
+            covariance_ref.at[h], covariance_all_ref.at[h], covariance_sems.at[h]
         )
 
     @pl.when(head == 0)
     def _():
-        for h in range(LANES // HD if early else 0):
-            for copy in copies(h):
-                copy.start()
+        if first:
+            staged.start()
+        else:
+            for h in range(LANES // HD):
+                if h >= STAGED_HEADS:
+                    exp_copy(h - STAGED_HEADS).start()
+                covariance_copy(h).start()
         me = column_ref[0]
         for block, mask in zip((g0_ref, g1_ref, g2_ref, g3_ref), BLOCK_MASKS):
             start = pl.multiple_of((me ^ mask) * LANES, LANES)
             d_out_ref[pl.ds(start, LANES), :] = block[...]
         d_attended_ref[...] = dot(weight_ref[...].T, d_out_ref[...]).astype(bf16)
 
-    grads = d_attended_ref[pl.ds(at, HD), :].astype(f32)
-    query = query_t_ref[pl.ds(at, HD), :].astype(f32)
-    values = value_t_ref[pl.ds(at, HD), :].astype(f32)
-    inverse = inverse_ref[0]
-    middle = jnp.mean(values, axis=1, keepdims=True)
-    centered = values - middle
-    offset = attended_ref[pl.ds(at, HD), :].astype(f32) - middle
-    scaled = grads * inverse
-    delta = jnp.sum(scaled * offset, axis=0, keepdims=True)
-    features = [scaled[j : j + 1] * query for j in range(HD)] + [delta * query, scaled]
-    if early:
-        for copy in copies(head):
-            copy.wait()
-        weights, covariance = early[0].at[head], early[1].at[head]
+    def one_head(weights):
+        grads = d_attended_ref[pl.ds(at, HD), :].astype(f32)
+        query = query_t_ref[pl.ds(at, HD), :].astype(f32)
+        values = value_t_ref[pl.ds(at, HD), :].astype(f32)
+        inverse = inverse_ref[0]
+        middle = jnp.mean(values, axis=1, keepdims=True)
+        centered = values - middle
+        offset = attended_ref[pl.ds(at, HD), :].astype(f32) - middle
+        scaled = grads * inverse
+        delta = jnp.sum(scaled * offset, axis=0, keepdims=True)
+        features = [scaled[j : j + 1] * query for j in range(HD)] + [delta * query, scaled]
+        sums = dot_rows(jnp.concatenate([f.astype(bf16) for f in features], axis=0), weights())
+        d_value_ref[pl.ds(at, HD), :] = sums[(HD + 1) * HD :].astype(bf16)
+        if first:
+            covariance = covariance_ref.at[0]
+        else:
+            covariance_copy(head).wait()
+            covariance = covariance_all_ref.at[head]
+        d_key = centered[0:1] * sums[:HD]
+        d_query = grads[0:1] * covariance[:HD, :].astype(f32)
+        for j in range(1, HD):
+            rows = slice(j * HD, (j + 1) * HD)
+            d_key += centered[j : j + 1] * sums[rows]
+            d_query += grads[j : j + 1] * covariance[rows, :].astype(f32)
+        d_key_ref[pl.ds(at, HD), :] = (d_key - sums[HD * HD : (HD + 1) * HD]).astype(bf16)
+        d_query_ref[pl.ds(at, HD), :] = (d_query * score_scale).astype(bf16)
+
+    if first:
+        one_head(lambda: exp_ref[0])
+
+        @pl.when(head == pl.num_programs(0) - 1)
+        def _():
+            staged.wait()
+
     else:
-        weights, covariance = exp_ref.at[0], covariance_ref.at[0]
-    sums = dot_rows(jnp.concatenate([f.astype(bf16) for f in features], axis=0), weights[...])
-    d_value_ref[pl.ds(at, HD), :] = sums[(HD + 1) * HD :].astype(bf16)
-    d_key = centered[0:1] * sums[:HD]
-    d_query = grads[0:1] * covariance[:HD, :].astype(f32)
-    for j in range(1, HD):
-        rows = slice(j * HD, (j + 1) * HD)
-        d_key += centered[j : j + 1] * sums[rows]
-        d_query += grads[j : j + 1] * covariance[rows, :].astype(f32)
-    d_key_ref[pl.ds(at, HD), :] = (d_key - sums[HD * HD : (HD + 1) * HD]).astype(bf16)
-    d_query_ref[pl.ds(at, HD), :] = (d_query * score_scale).astype(bf16)
-
-
-def attention_backward(patch, resident, weights, inverse, covariance, query_t, value_t, attended, grads, weight, column):
+
+        @pl.when(head < STAGED_HEADS)
+        def _():
+            one_head(lambda: exp_ref[0])
+
+        @pl.when(head >= STAGED_HEADS)
+        def _():
+            exp_copy(head - STAGED_HEADS).wait()
+            one_head(lambda: exp_all_ref[head - STAGED_HEADS])
+
+
+def attention_backward(
+    patch, first, weights, other, inverse, covariance, query_t, value_t, attended, grads, weight, column
+):
     features = weight.shape[0]
     heads = LANES // HD
-    in_hbm = pl.BlockSpec(memory_space=pltpu.HBM)
-    early = [
-        pltpu.VMEM((heads, PATCH, PATCH), bf16),
-        pltpu.VMEM((heads, HD * HD, PATCH), bf16),
-        pltpu.SemaphoreType.DMA((heads,)),
-        pltpu.SemaphoreType.DMA((heads,)),
-    ]
     tall = pl.BlockSpec((LANES, PATCH), lambda h, c: (0, 0))
     part = pl.BlockSpec((LANES, PATCH), lambda h, c: (0, patch))
     per_head = lambda h, c: (h, 0, 0)
+    kept_head = lambda h, c: (jnp.minimum(h, weights.shape[0] - 1), 0, 0)
+    hbm = pl.BlockSpec(memory_space=pltpu.HBM)
     elements = heads * PATCH * PATCH
     turned = pltpu.VMEM((LANES, PATCH), bf16)
-    return pl.pallas_call(
-        backward_body,
+    in_specs = [
+        pl.BlockSpec((1, PATCH, PATCH), kept_head),
+        pl.BlockSpec((1, 1, PATCH), per_head),
+        tall,
+        tall,
+        tall,
+        part,
+        part,
+        part,
+        part,
+        pl.BlockSpec(weight.shape, lambda h, c: (0, 0)),
+        pl.BlockSpec((1, HD * HD, PATCH), per_head) if first else hbm,
+        hbm,
+    ]
+    operands = [weights, inverse, query_t, value_t, attended, *grads, weight, covariance, other]
+    out_specs = [pl.BlockSpec((features, PATCH), lambda h, c: (0, 0)), tall, tall, tall]
+    out_shape = [pltpu.VMEM((features, PATCH), bf16), turned, turned, turned]
+    scratch = [pltpu.VMEM((LANES, PATCH), bf16)]
+    if first:
+        out_specs.append(pl.BlockSpec(memory_space=pl.ANY))
+        out_shape.append(pltpu.VMEM((STAGED_HEADS, PATCH, PATCH), bf16))
+        scratch.append(pltpu.SemaphoreType.DMA(()))
+    else:
+        rest = heads - STAGED_HEADS
+        scratch += [pltpu.VMEM((rest, PATCH, PATCH), bf16), pltpu.SemaphoreType.DMA((rest,))]
+        scratch += [pltpu.VMEM((heads, HD * HD, PATCH), bf16), pltpu.SemaphoreType.DMA((heads,))]
+    return pl.pallas_call(
+        functools.partial(backward_body, first),
         grid_spec=pltpu.PrefetchScalarGridSpec(
             num_scalar_prefetch=1,
             grid=(heads,),
-            in_specs=[
-                pl.BlockSpec((1, PATCH, PATCH), per_head) if resident else in_hbm,
-                pl.BlockSpec((1, 1, PATCH), per_head),
-                pl.BlockSpec((1, HD * HD, PATCH), per_head) if resident else in_hbm,
-                tall,
-                tall,
-                tall,
-                part,
-                part,
-                part,
-                part,
-                pl.BlockSpec(weight.shape, lambda h, c: (0, 0)),
-            ],
-            out_specs=[pl.BlockSpec((features, PATCH), lambda h, c: (0, 0)), tall, tall, tall],
-            scratch_shapes=[pltpu.VMEM((LANES, PATCH), bf16)] + ([] if resident else early),
+            in_specs=in_specs,
+            out_specs=out_specs,
+            scratch_shapes=scratch,
         ),
-        out_shape=[pltpu.VMEM((features, PATCH), bf16), turned, turned, turned],
-        compiler_params=params(14 if resident else 30),
+        out_shape=out_shape,
+        compiler_params=params(9 if first else 27),
         cost_estimate=cost(1100 * elements, 2 * elements),
         name="attention_backward",
-    )(column, weights, inverse, covariance, query_t, value_t, attended, *grads, weight)
+    )(column, *operands)
 
 
 def whole(shape, dtype):
@@ -502,15 +545,15 @@
 
 def weight_grad_body(*refs):
     d_query_ref, d_key_ref, d_value_ref, attended_ref, hidden_ref, d_out_ref, *before, out_ref = refs
-    hidden = hidden_ref[...]
-    parts = [dot(ref[...], hidden) for ref in (d_query_ref, d_key_ref, d_value_ref)]
-    parts.append(dot_rows(attended_ref[...], d_out_ref[...]))
-    for t, part in enumerate(parts):
-        columns = slice(t * LANES, (t + 1) * LANES)
-        if before:
-            out_ref[:, columns] = (before[0][columns, :] + part).T.astype(bf16)
-        else:
-            out_ref[columns, :] = part
+    d_projected = jnp.concatenate([d_query_ref[...], d_key_ref[...], d_value_ref[...]], axis=0)
+    projections = dot(d_projected, hidden_ref[...])
+    output = dot_rows(attended_ref[...], d_out_ref[...])
+    if before:
+        out_ref[:, : 3 * LANES] = (before[0][: 3 * LANES, :] + projections).T.astype(bf16)
+        out_ref[:, 3 * LANES :] = (before[0][3 * LANES :, :] + output).T.astype(bf16)
+    else:
+        out_ref[: 3 * LANES, :] = projections
+        out_ref[3 * LANES :, :] = output
 
 
 def weight_grads(*operands):
@@ -724,10 +767,11 @@
         if p == 0:
             weights, sent = after(weights, sent)
             received[1] = swap(sent, 2)
-            weights, covariance = in_hbm(weights), in_hbm(covariance)
-        d_out, d_query, d_key, d_value = attention_backward(
-            p, p == patches - 1, weights, inverse, covariance, query_t, value_t, attended, grads,
-            out_weight, column,
+            other_exp, covariance, weights = in_hbm(weights), in_hbm(covariance), staged[0]
+        else:
+            other_exp = in_hbm(forwards[0][1][0])
+        d_out, d_query, d_key, d_value, *staged = attention_backward(
+            p, p > 0, weights, other_exp, inverse, covariance, query_t, value_t, attended, grads, out_weight, column
         )
         if p == 0:
             received[1], d_query = after(received[1], d_query)

time: 136 us -> 133 us (0.978)
  Pallas kernels: 90.4 us -> 88.3 us
  transfers between devices with their start and end apart: 16 -> 16, of which waited for: 6 -> 6; matrix products, arithmetic and copies ran while one was open for 0% -> 0% of each run, Pallas kernels for 56% -> 55%
where the time goes in v6:
time: 133 us
  Pallas kernels  88.3 us (66%)
  starting transfers between devices  24.8 us (19%)
  waiting for transfers between devices  19 us (14%)
    pallas_call x2, Pallas kernels, attention_forward(): pl.pallas_call(forward_body, grid=(heads,), in_specs=[pl.BlockSpec((PATCH...  36.5 us
    pallas_call x2, Pallas kernels, attention_backward(): pl.pallas_call(functools.partial(backward_body, first), grid_spec=pltpu.P...  18 us
    all_to_all x3, starting transfers between devices, exchange(): return lax.all_to_all(rows, 'seq', split_axis=0, concat_axis=0, tiled=True)  16.7 us
    ppermute x13, waiting for transfers between devices, swap(): return lax.ppermute(rows, 'mp', [(i, i ^ mask) for i in range(members)])  16 us
    pallas_call x1, Pallas kernels, bucket_rows(): pl.pallas_call(functools.partial(bucket_body, shards, capacity), grid_spe...  11.5 us
    ppermute x13, starting transfers between devices, swap(): return lax.ppermute(rows, 'mp', [(i, i ^ mask) for i in range(members)])  8.07 us
    pallas_call x3, Pallas kernels, permute_rows(): pl.pallas_call(permute_body, grid_spec=pltpu.PrefetchScalarGridSpec(num_s...  4.87 us
    pallas_call x2, Pallas kernels, project(): pl.pallas_call(project_body, grid_spec=pltpu.PrefetchScalarGridSpec(num_s...  4.79 us
  transfers between devices with their start and end apart: 16, of which 6 were waited for; matrix products, arithmetic and copies ran while one was open for 0% of the time, Pallas kernels for 55%

profile of v6, /device:TPU:0, one launch (start us, length us, event | category | flops | bytes accessed | tf_op | source)
XLA Modules:
  0.0 133.0 jit_solution(5816446930277623436)
XLA Ops:
  0.6 3.3 %permute_rows.3 = bf16[2048,128]{1,0:T(8,128)(2,1)} custom-call(s32[1]{0:T(128)} %bitcast.column_ref.refs_0_, s32[16,128]{1,0:T(8,128)} %bitcast.22, bf16[2048,512]{1,0:T(8,128)(2,1)} %block_ref.1), custom_call_target="tpu_custom_call" | custom-call | flops 4294967296 | bytes 1572864 | tf_op jit(solution)/shard_map/permute_rows/pallas_call | solution.py:82
  4.0 7.3 %all-to-all-start.1 = ((bf16[8,256,128]{2,1,0:T(8,128)(2,1)}), bf16[8,256,128]{2,1,0:T(8,128)(2,1)S(1)}, u32[]{:S(2)}, u32[]{:S(2)}) async-start(bf16[8,256,128]{2,1,0:T(8,128)(2,1)} %bitcast.20), calls=%async_computation.1 | async-start | bytes 1048576 | tf_op jit(solution)/shard_map/all_to_all | solution.py:730
  11.2 11.5 %bucket_rows.1 = bf16[8,528,128]{2,1,0:T(8,128)(2,1)} custom-call(s32[1]{0:T(128)} %bitcast.column_ref.refs_0_, s32[16,128]{1,0:T(8,128)} %bitcast.23, s32[16,128]{1,0:T(8,128)} %bitcast.24, bf16[2048,512]{1,0:T(8,128)(2,1)} %grads_ref.1), custom_call_target="tpu_custom_call" | custom-call | flops 8589934592 | bytes 3145728 | tf_op jit(solution)/shard_map/bucket_rows/pallas_call | solution.py:156
  22.7 3.0 %all-to-all-done.1 = bf16[8,256,128]{2,1,0:T(8,128)(2,1)S(1)} async-done(((bf16[8,256,128]{2,1,0:T(8,128)(2,1)}), bf16[8,256,128]{2,1,0:T(8,128)(2,1)S(1)}, u32[]{:S(2)}, u32[]{:S(2)}) %all-to-all-start.1) | async-done | bytes 524320 | tf_op jit(solution)/shard_map/all_to_all | solution.py:730
  25.7 3.7 %all-to-all-start = ((bf16[8,528,128]{2,1,0:T(8,128)(2,1)}), bf16[8,528,128]{2,1,0:T(8,128)(2,1)S(1)}, u32[]{:S(2)}, u32[]{:S(2)}) async-start(bf16[8,528,128]{2,1,0:T(8,128)(2,1)} %bucket_rows.1), calls=%async_computation | async-start | bytes 2162688 | tf_op jit(solution)/shard_map/all_to_all | solution.py:730
  29.5 0.0 copy-done.13
  29.5 0.8 permute_rows.5.x0_ref
  30.2 0.0 copy-start
  30.3 1.6 %collective-permute-start.1 = (bf16[1024,128]{1,0:T(8,128)(2,1)S(1)}, bf16[1024,128]{1,0:T(8,128)(2,1)S(1)}, u32[]{:S(2)}, u32[]{:S(2)}) collective-permute-start(bf16[1024,128]{1,0:T(8,128)(2,1)S(1)} %permute_rows.5.x0_ref), channel_id=1, source_target_pairs={{0,2},{1,3},{2,0},{3,1},{4,6},{5,7},{6,4},{7,5},{8,10},{9,11},{10,... | collective-permute-start | bytes 786440 | tf_op jit(solution)/shard_map/ppermute | solution.py:727
  31.8 0.0 collective-permute-start.2
  31.8 0.8 permute_rows.4.x0_ref
  32.6 5.5 %collective-permute-done.1.x1_ref = bf16[1024,128]{1,0:T(8,128)(2,1)S(1)} collective-permute-done((bf16[1024,128]{1,0:T(8,128)(2,1)S(1)}, bf16[1024,128]{1,0:T(8,128)(2,1)S(1)}, u32[]{:S(2)}, u32[]{:S(2)}) %collective-permute-start.1) | collective-permute-done | bytes 262176 | tf_op jit(solution)/shard_map/ppermute | solution.py:727
  38.1 0.0 collective-permute-start.3
  38.1 1.5 %collective-permute-start = (bf16[1024,128]{1,0:T(8,128)(2,1)S(1)}, bf16[1024,128]{1,0:T(8,128)(2,1)S(1)}, u32[]{:S(2)}, u32[]{:S(2)}) collective-permute-start(bf16[1024,128]{1,0:T(8,128)(2,1)S(1)} %permute_rows.4.x0_ref), channel_id=1, source_target_pairs={{0,2},{1,3},{2,0},{3,1},{4,6},{5,7},{6,4},{7,5},{8,10},{9,11},{10,... | collective-permute-start | bytes 786440 | tf_op jit(solution)/shard_map/ppermute | solution.py:727
  39.7 0.2 collective-permute-start.5
  39.9 0.0 collective-permute-done.2.x2_ref
  39.9 0.0 collective-permute-done.3.x3_ref
  39.9 0.0 copy-done
  39.9 2.5 %project.2 = (bf16[1024,512]{1,0:T(8,128)(2,1)}, f32[128,1024]{1,0:T(8,128)}, f32[8,1024]{1,0:T(8,128)}, bf16[1024,128]{1,0:T(8,128)(2,1)S(1)}, bf16[128,1024]{1...) custom-call(s32[1]{0:T(128)} %bitcast.column_ref.refs_0_, ...), custom_call_target="tpu_custom_call" | custom-call | flops 805306368 | bytes 5242880 | tf_op jit(solution)/shard_map/project/pallas_call | solution.py:277
  42.4 19.1 %attention_forward.2 = (bf16[8,1024,1024]{2,1,0:T(8,128)(2,1)}, bf16[128,1024]{1,0:T(8,128)(2,1)}, f32[8,1,1024]{2,1,0:T(1,128)S(1)}, bf16[8,256,1024]{2,1,0:T(8,128)(2,1)}) custom-call(bf16[1024,128]{1,0:T(8,128)(2,1)S(1)} %get-tuple-element.79.key_ref, bf16[128,1024]{1,0:T(8,128)(2,1)S(1)} %get-tuple-element.80.base2_t_ref, ...), custom_call_target="tpu_custom_call" | custom-call | flops 13421772800 | bytes 16777216 | tf_op jit(solution)/shard_map/attention_forward/pallas_call | solution.py:363
  61.5 0.0 copy-done.7
  61.5 0.0 copy-done.8
  61.5 0.0 collective-permute-done.x1_ref
  61.5 0.0 all-to-all-done
  61.5 2.6 %segment_rows.1.refs_6_.d_out_ref = bf16[128,2048]{1,0:T(8,128)(2,1)S(1)} custom-call(bf16[8,528,128]{2,1,0:T(8,128)(2,1)S(1)} %all-to-all-done), custom_call_target="tpu_custom_call" | custom-call | flops 8858370048 | bytes 3244032 | tf_op jit(solution)/shard_map/segment_rows/pallas_call | solution.py:215
  64.2 0.3 collective-permute-start.6
  64.5 1.2 collective-permute-start.4
  65.7 0.1 collective-permute-start.7
  65.8 0.0 collective-permute-done.5.x2_ref
  65.8 0.0 collective-permute-done.6.x3_ref
  65.8 2.3 %project.3 = (bf16[1024,512]{1,0:T(8,128)(2,1)S(1)}, f32[128,1024]{1,0:T(8,128)}, f32[8,1024]{1,0:T(8,128)}, bf16[1024,128]{1,0:T(8,128)(2,1)S(1)}, bf16[128,102...) custom-call(s32[1]{0:T(128)} %bitcast.column_ref.refs_0_, ...), custom_call_target="tpu_custom_call" | custom-call | flops 805306368 | bytes 5242880 | tf_op jit(solution)/shard_map/project/pallas_call | solution.py:277
  68.0 17.4 %attention_forward.3 = (bf16[8,1024,1024]{2,1,0:T(8,128)(2,1)S(1)}, bf16[128,1024]{1,0:T(8,128)(2,1)S(1)}, f32[8,1,1024]{2,1,0:T(1,128)S(1)}, bf16[8,256,1024]{2,1,0:T(8,128)(2,1)S(1)}) custom-call(bf16[1024,128]{1,0:T(8,128)(2,1)S(1)} %get-tuple-element.92.key_ref, bf16[128,1024]{1,0:T(8,128)(2,1)S(1)} %get-tuple-element.93.base2_t_ref, ...), custom_call_target="tpu_custom_call" | custom-call | flops 13421772800 | bytes 16777216 | tf_op jit(solution)/shard_map/attention_forward/pallas_call | solution.py:363
  85.4 0.0 collective-permute-done.4.refs_7_
  85.4 0.5 collective-permute-start.8
  85.9 0.0 collective-permute-done.7.refs_8_
  85.9 1.5 %collective-permute-done.8.refs_9_ = bf16[128,2048]{1,0:T(8,128)(2,1)S(1)} collective-permute-done((bf16[128,2048]{1,0:T(8,128)(2,1)S(1)}, bf16[128,2048]{1,0:T(8,128)(2,1)S(1)}, u32[]{:S(2)}, u32[]{:S(2)}) %collective-permute-start.8) | collective-permute-done | bytes 524320 | tf_op jit(solution)/shard_map/ppermute | solution.py:727
  87.5 0.0 copy-done.11
  87.5 8.2 %attention_backward.2 = (bf16[512,1024]{1,0:T(8,128)(2,1)S(1)}, bf16[128,1024]{1,0:T(8,128)(2,1)S(1)}, bf16[128,1024]{1,0:T(8,128)(2,1)S(1)}, bf16[128,1024]{1,0:T(8,128)(2,1)S(1)}, bf16[1,1024,1024]{2,1,0:T(8,128)(2,1)S(1)}) custom-call(s32[1]{0:T(128)} %bitcast.column_ref.refs_0_, bf16[8,1024,1024]{2,1,0:T(8,128)(2,1)S(1)} %get-tuple-element.100.refs_1_, ...), custom_call_target="tpu_custom_call" | custom-call | flops 9227468800 | bytes 16777216 | tf_op jit(solution)/shard_map/attention_backward/pallas_call | solution.py:526
  95.7 1.0 hidden_part.2
  96.7 0.4 collective-permute-start.9
  97.1 0.8 weight_grads.2.refs_6_
  98.0 0.7 collective-permute-done.9.got_ref
  98.7 0.1 pair_sum.2
  98.8 1.3 collective-permute-start.10
  100.1 0.0 copy-done.6
  100.1 0.0 copy-done.9
  100.2 0.0 copy-done.10
  100.2 9.9 %attention_backward.3 = (bf16[512,1024]{1,0:T(8,128)(2,1)S(1)}, bf16[128,1024]{1,0:T(8,128)(2,1)S(1)}, bf16[128,1024]{1,0:T(8,128)(2,1)S(1)}, bf16[128,1024]{1,0:T(8,128)(2,1)S(1)}) custom-call(s32[1]{0:T(128)} %bitcast.column_ref.refs_0_, bf16[1,1024,1024]{2,1,0:T(8,128)(2,1)S(1)} %get-tuple-element.118.refs_1_, ...), custom_call_target="tpu_custom_call" | custom-call | flops 9227468800 | bytes 16777216 | tf_op jit(solution)/shard_map/attention_backward/pallas_call | solution.py:526
  110.1 0.0 collective-permute-done.10.got_ref
  110.1 1.8 %weight_grads.3 = bf16[512,512]{1,0:T(8,128)(2,1)} custom-call(bf16[128,1024]{1,0:T(8,128)(2,1)S(1)} %get-tuple-element.131.refs_0_.d_query_ref, bf16[128,1024]{1,0:T(8,128)(2,1)S(1)} %get-tuple-element.132.refs_1_.d_key_ref, bf16[128,1024]{1,0:T(8,128)(2,1)S(1)} %get-tuple-element.133.refs_2_.d_value_ref, bf16[128,1024]{1,0:T(8,128)(2,1)S(1)} %copy-done.10, ...), custom_call_target="tpu_custom_call" | custom-call | flops 536870912 | bytes 6291456 | tf_op jit(solution)/shard_map/weight_grads/pallas_call | solution.py:563
  111.8 5.7 %all-to-all-start.2 = ((bf16[8,64,512]{2,1,0:T(8,128)(2,1)}), bf16[8,64,512]{2,1,0:T(8,128)(2,1)S(1)}, u32[]{:S(2)}, u32[]{:S(2)}) async-start(bf16[8,64,512]{2,1,0:T(8,128)(2,1)} %bitcast.10), calls=%async_computation.2 | async-start | bytes 1048576 | tf_op jit(solution)/shard_map/all_to_all | solution.py:730
  117.6 2.4 %hidden_part.3 = (bf16[256,1024]{1,0:T(8,128)(2,1)S(1)}, bf16[272,1024]{1,0:T(8,128)(2,1)S(1)}, f32[2,1024]{1,0:T(2,128)S(1)}) custom-call(s32[1]{0:T(128)} %bitcast.column_ref.refs_0_, bf16[128,1024]{1,0:T(8,128)(2,1)} %copy-done.1, bf16[128,1024]{1,0:T(8,128)(2,1)} %copy-done.2, bf16[128,1024]{1,0:T(8,128)(2,1)} %copy-done.3, bf16[128,1024]{1,0:T(8,128)(2,1)} %copy-done.6, ...), custom_call_target="tpu_custom_call" | custom-call | flops 402653184 | bytes 2097152 | tf_op jit(solution)/shard_map/hidden_part/pallas_call | solution.py:619
  119.9 0.0 copy-start.5
  119.9 0.0 copy-start.12
  120.0 0.1 collective-permute-start.11
  120.0 1.9 %collective-permute-done.11.got_ref = bf16[272,1024]{1,0:T(8,128)(2,1)S(1)} collective-permute-done((bf16[272,1024]{1,0:T(8,128)(2,1)S(1)}, bf16[272,1024]{1,0:T(8,128)(2,1)S(1)}, u32[]{:S(2)}, u32[]{:S(2)}) %collective-permute-start.11) | collective-permute-done | bytes 557088 | tf_op jit(solution)/shard_map/ppermute | solution.py:727
  122.0 0.1 pair_sum.3
  122.1 0.9 collective-permute-start.12
  123.0 2.1 %points_grad.2.rest_0_ = f32[2048,128]{1,0:T(8,128)} custom-call(f32[128,1024]{1,0:T(8,128)S(1)} %get-tuple-element.145.kept_ref, f32[2,1024]{1,0:T(2,128)S(1)} %get-tuple-element.146.sums_ref, bf16[144,1024]{1,0:T(8,128)(2,1)S(1)} %collective-permute-done.10.got_ref, bf16[128,2048]{1,0:T(8,128)(2,1)S(1)} %segment_rows.1.refs_6_.d_out_ref, ...), custom_call_target="tpu_custom_call" | custom-call | flops 1048576 | bytes 3145728 | tf_op jit(solution)/shard_map/points_grad/pallas_call | solution.py:673
  125.1 6.2 %collective-permute-done.12.got_ref = bf16[144,1024]{1,0:T(8,128)(2,1)S(1)} collective-permute-done((bf16[144,1024]{1,0:T(8,128)(2,1)S(1)}, bf16[144,1024]{1,0:T(8,128)(2,1)S(1)}, u32[]{:S(2)}, u32[]{:S(2)}) %collective-permute-start.12) | collective-permute-done | bytes 294944 | tf_op jit(solution)/shard_map/ppermute | solution.py:727
  131.2 0.0 copy-done.5
  131.2 1.0 points_grad.3
  132.3 0.0 all-to-all-done.2.parts_ref
  132.3 0.7 grad_sum.1
  (16 shorter events, 0.0 us)
Async XLA Ops:
  4.0 21.7 %all-to-all-start.1 = ((bf16[8,256,128]{2,1,0:T(8,128)(2,1)}), bf16[8,256,128]{2,1,0:T(8,128)(2,1)S(1)}, u32[]{:S(2)}, u32[]{:S(2)}) async-start(bf16[8,256,128]{2,1,0:T(8,128)(2,1)} %bitcast.20), calls=%async_computation.1 | async-start | bytes 1048576 | tf_op jit(solution)/shard_map/all_to_all | solution.py:730
  22.7 6.8 %copy-start.13 = (s32[2048]{0:T(1024)S(1)}, s32[2048]{0:T(1024)}, u32[]{:S(2)}) copy-start(s32[2048]{0:T(1024)} %param.10) | copy-start | bytes 24580
  25.7 35.8 %all-to-all-start = ((bf16[8,528,128]{2,1,0:T(8,128)(2,1)}), bf16[8,528,128]{2,1,0:T(8,128)(2,1)S(1)}, u32[]{:S(2)}, u32[]{:S(2)}) async-start(bf16[8,528,128]{2,1,0:T(8,128)(2,1)} %bucket_rows.1), calls=%async_computation | async-start | bytes 2162688 | tf_op jit(solution)/shard_map/all_to_all | solution.py:730
  30.2 9.7 %copy-start = (bf16[512,3,128]{2,0,1:T(8,128)(2,1)S(1)}, bf16[512,3,128]{2,0,1:T(8,128)(2,1)}, u32[]{:S(2)}) copy-start(bf16[512,3,128]{2,0,1:T(8,128)(2,1)} %param.11) | copy-start | bytes 1179652
  30.3 7.9 %collective-permute-start.1 = (bf16[1024,128]{1,0:T(8,128)(2,1)S(1)}, bf16[1024,128]{1,0:T(8,128)(2,1)S(1)}, u32[]{:S(2)}, u32[]{:S(2)}) collective-permute-start(bf16[1024,128]{1,0:T(8,128)(2,1)S(1)} %permute_rows.5.x0_ref), channel_id=1, source_target_pairs={{0,2},{1,3},{2,0},{3,1},{4,6},{5,7},{6,4},{7,5},{8,10},{9,11},{10,... | collective-permute-start | bytes 786440 | tf_op jit(solution)/shard_map/ppermute | solution.py:727
  31.8 8.1 %collective-permute-start.2 = (bf16[1024,128]{1,0:T(8,128)(2,1)S(1)}, bf16[1024,128]{1,0:T(8,128)(2,1)S(1)}, u32[]{:S(2)}, u32[]{:S(2)}) collective-permute-start(bf16[1024,128]{1,0:T(8,128)(2,1)S(1)} %permute_rows.5.x0_ref), channel_id=1, source_target_pairs={{0,1},{1,0},{2,3},{3,2},{4,5},{5,4},{6,7},{7,6},{8,9},{9,8},{10,11... | collective-permute-start | bytes 786440 | tf_op jit(solution)/shard_map/ppermute | solution.py:727
  38.1 1.8 %collective-permute-start.3 = (bf16[1024,128]{1,0:T(8,128)(2,1)S(1)}, bf16[1024,128]{1,0:T(8,128)(2,1)S(1)}, u32[]{:S(2)}, u32[]{:S(2)}) collective-permute-start(bf16[1024,128]{1,0:T(8,128)(2,1)S(1)} %collective-permute-done.1.x1_ref), channel_id=1, source_target_pairs={{0,1},{1,0},{2,3},{3,2},{4,5},{5,4},{6,7},{7,6},{8,9},{9,8},{10,11... | collective-permute-start | bytes 786440 | tf_op jit(solution)/shard_map/ppermute | solution.py:727
  38.1 23.4 %collective-permute-start = (bf16[1024,128]{1,0:T(8,128)(2,1)S(1)}, bf16[1024,128]{1,0:T(8,128)(2,1)S(1)}, u32[]{:S(2)}, u32[]{:S(2)}) collective-permute-start(bf16[1024,128]{1,0:T(8,128)(2,1)S(1)} %permute_rows.4.x0_ref), channel_id=1, source_target_pairs={{0,2},{1,3},{2,0},{3,1},{4,6},{5,7},{6,4},{7,5},{8,10},{9,11},{10,... | collective-permute-start | bytes 786440 | tf_op jit(solution)/shard_map/ppermute | solution.py:727
  39.7 26.1 %collective-permute-start.5 = (bf16[1024,128]{1,0:T(8,128)(2,1)S(1)}, bf16[1024,128]{1,0:T(8,128)(2,1)S(1)}, u32[]{:S(2)}, u32[]{:S(2)}) collective-permute-start(bf16[1024,128]{1,0:T(8,128)(2,1)S(1)} %permute_rows.4.x0_ref), channel_id=1, source_target_pairs={{0,1},{1,0},{2,3},{3,2},{4,5},{5,4},{6,7},{7,6},{8,9},{9,8},{10,11... | collective-permute-start | bytes 786440 | tf_op jit(solution)/shard_map/ppermute | solution.py:727
  42.4 19.1 %copy-start.7 = (bf16[128,1024]{1,0:T(8,128)(2,1)}, bf16[128,1024]{1,0:T(8,128)(2,1)S(1)}, u32[]{:S(2)}) copy-start(bf16[128,1024]{1,0:T(8,128)(2,1)S(1)} %get-tuple-element.135.key_t_ref.key_ref) | copy-start | bytes 786436
  42.4 19.1 %copy-start.8 = (bf16[128,1024]{1,0:T(8,128)(2,1)}, bf16[128,1024]{1,0:T(8,128)(2,1)S(1)}, u32[]{:S(2)}) copy-start(bf16[128,1024]{1,0:T(8,128)(2,1)S(1)} %get-tuple-element.136.value_t_ref.refs_4_.value_ref) | copy-start | bytes 786436
  42.4 57.7 %copy-start.6 = (bf16[128,1024]{1,0:T(8,128)(2,1)}, bf16[128,1024]{1,0:T(8,128)(2,1)S(1)}, u32[]{:S(2)}) copy-start(bf16[128,1024]{1,0:T(8,128)(2,1)S(1)} %get-tuple-element.134.refs_3_.query_ref) | copy-start | bytes 786436
  64.2 1.6 %collective-permute-start.6 = (bf16[1024,128]{1,0:T(8,128)(2,1)S(1)}, bf16[1024,128]{1,0:T(8,128)(2,1)S(1)}, u32[]{:S(2)}, u32[]{:S(2)}) collective-permute-start(bf16[1024,128]{1,0:T(8,128)(2,1)S(1)} %collective-permute-done.x1_ref), channel_id=1, source_target_pairs={{0,1},{1,0},{2,3},{3,2},{4,5},{5,4},{6,7},{7,6},{8,9},{9,8},{10,11... | collective-permute-start | bytes 786440 | tf_op jit(solution)/shard_map/ppermute | solution.py:727
  64.5 20.9 %collective-permute-start.4 = (bf16[128,2048]{1,0:T(8,128)(2,1)S(1)}, bf16[128,2048]{1,0:T(8,128)(2,1)S(1)}, u32[]{:S(2)}, u32[]{:S(2)}) collective-permute-start(bf16[128,2048]{1,0:T(8,128)(2,1)S(1)} %segment_rows.1.refs_6_.d_out_ref), channel_id=1, source_target_pairs={{0,2},{1,3},{2,0},{3,1},{4,6},{5,7},{6,4},{7,5},{8,10},{9,11},{10,... | collective-permute-start | bytes 1572872 | tf_op jit(solution)/shard_map/ppermute | solution.py:727
  65.7 20.3 %collective-permute-start.7 = (bf16[128,2048]{1,0:T(8,128)(2,1)S(1)}, bf16[128,2048]{1,0:T(8,128)(2,1)S(1)}, u32[]{:S(2)}, u32[]{:S(2)}) collective-permute-start(bf16[128,2048]{1,0:T(8,128)(2,1)S(1)} %segment_rows.1.refs_6_.d_out_ref), channel_id=1, source_target_pairs={{0,1},{1,0},{2,3},{3,2},{4,5},{5,4},{6,7},{7,6},{8,9},{9,8},{10,11... | collective-permute-start | bytes 1572872 | tf_op jit(solution)/shard_map/ppermute | solution.py:727
  68.0 19.4 %copy-start.11 = (bf16[512,128]{1,0:T(8,128)(2,1)S(1)}, bf16[512,128]{1,0:T(8,128)(2,1)}, u32[]{:S(2)}) copy-start(bf16[512,128]{1,0:T(8,128)(2,1)} %refs_10_.3) | copy-start | bytes 393220
  85.4 2.0 %collective-permute-start.8 = (bf16[128,2048]{1,0:T(8,128)(2,1)S(1)}, bf16[128,2048]{1,0:T(8,128)(2,1)S(1)}, u32[]{:S(2)}, u32[]{:S(2)}) collective-permute-start(bf16[128,2048]{1,0:T(8,128)(2,1)S(1)} %collective-permute-done.4.refs_7_), channel_id=1, source_target_pairs={{0,1},{1,0},{2,3},{3,2},{4,5},{5,4},{6,7},{7,6},{8,9},{9,8},{10,11... | collective-permute-start | bytes 1572872 | tf_op jit(solution)/shard_map/ppermute | solution.py:727
  96.7 2.0 %collective-permute-start.9 = (bf16[272,1024]{1,0:T(8,128)(2,1)S(1)}, bf16[272,1024]{1,0:T(8,128)(2,1)S(1)}, u32[]{:S(2)}, u32[]{:S(2)}) collective-permute-start(bf16[272,1024]{1,0:T(8,128)(2,1)S(1)} %get-tuple-element.112), channel_id=1, source_target_pairs={{0,1},{1,0},{2,3},{3,2},{4,5},{5,4},{6,7},{7,6},{8,9},{9,8},{10,11... | collective-permute-start | bytes 1671176 | tf_op jit(solution)/shard_map/ppermute | solution.py:727
  97.1 3.0 %copy-start.9 = (bf16[128,1024]{1,0:T(8,128)(2,1)S(1)}, bf16[128,1024]{1,0:T(8,128)(2,1)}, u32[]{:S(2)}) copy-start(bf16[128,1024]{1,0:T(8,128)(2,1)} %copy-done.8) | copy-start | bytes 786436
  97.1 3.0 %copy-start.10 = (bf16[128,1024]{1,0:T(8,128)(2,1)S(1)}, bf16[128,1024]{1,0:T(8,128)(2,1)}, u32[]{:S(2)}) copy-start(bf16[128,1024]{1,0:T(8,128)(2,1)} %get-tuple-element.121.refs_5_.refs_3_) | copy-start | bytes 786436
  98.8 11.2 %collective-permute-start.10 = (bf16[144,1024]{1,0:T(8,128)(2,1)S(1)}, bf16[144,1024]{1,0:T(8,128)(2,1)S(1)}, u32[]{:S(2)}, u32[]{:S(2)}) collective-permute-start(bf16[144,1024]{1,0:T(8,128)(2,1)S(1)} %get-tuple-element.117), channel_id=1, source_target_pairs={{0,2},{1,3},{2,0},{3,1},{4,6},{5,7},{6,4},{7,5},{8,10},{9,11},{10,... | collective-permute-start | bytes 884744 | tf_op jit(solution)/shard_map/ppermute | solution.py:727
  100.2 9.9 %copy-start.4 = (bf16[1024,512]{1,0:T(8,128)(2,1)S(1)}, bf16[1024,512]{1,0:T(8,128)(2,1)}, u32[]{:S(2)}) copy-start(bf16[1024,512]{1,0:T(8,128)(2,1)} %get-tuple-element.128.refs_4_) | copy-start | bytes 3145732
  110.0 1.8 %copy-start.1 = (bf16[128,1024]{1,0:T(8,128)(2,1)}, bf16[128,1024]{1,0:T(8,128)(2,1)S(1)}, u32[]{:S(2)}) copy-start(bf16[128,1024]{1,0:T(8,128)(2,1)S(1)} %get-tuple-element.131.refs_0_.d_query_ref) | copy-start | bytes 786436
  110.0 1.8 %copy-start.2 = (bf16[128,1024]{1,0:T(8,128)(2,1)}, bf16[128,1024]{1,0:T(8,128)(2,1)S(1)}, u32[]{:S(2)}) copy-start(bf16[128,1024]{1,0:T(8,128)(2,1)S(1)} %get-tuple-element.132.refs_1_.d_key_ref) | copy-start | bytes 786436
  110.0 1.8 %copy-start.3 = (bf16[128,1024]{1,0:T(8,128)(2,1)}, bf16[128,1024]{1,0:T(8,128)(2,1)S(1)}, u32[]{:S(2)}) copy-start(bf16[128,1024]{1,0:T(8,128)(2,1)S(1)} %get-tuple-element.133.refs_2_.d_value_ref) | copy-start | bytes 786436
  111.8 20.4 %all-to-all-start.2 = ((bf16[8,64,512]{2,1,0:T(8,128)(2,1)}), bf16[8,64,512]{2,1,0:T(8,128)(2,1)S(1)}, u32[]{:S(2)}, u32[]{:S(2)}) async-start(bf16[8,64,512]{2,1,0:T(8,128)(2,1)} %bitcast.10), calls=%async_computation.2 | async-start | bytes 1048576 | tf_op jit(solution)/shard_map/all_to_all | solution.py:730
  119.9 11.3 %copy-start.5 = (f32[128,1024]{1,0:T(8,128)S(1)}, f32[128,1024]{1,0:T(8,128)}, u32[]{:S(2)}) copy-start(f32[128,1024]{1,0:T(8,128)} %get-tuple-element.143.normed_ref) | copy-start | bytes 1572868
  119.9 11.3 %copy-start.12 = (f32[8,1024]{1,0:T(8,128)S(1)}, f32[8,1024]{1,0:T(8,128)}, u32[]{:S(2)}) copy-start(f32[8,1024]{1,0:T(8,128)} %get-tuple-element.144.inv_ref) | copy-start | bytes 98308
  120.0 2.0 %collective-permute-start.11 = (bf16[272,1024]{1,0:T(8,128)(2,1)S(1)}, bf16[272,1024]{1,0:T(8,128)(2,1)S(1)}, u32[]{:S(2)}, u32[]{:S(2)}) collective-permute-start(bf16[272,1024]{1,0:T(8,128)(2,1)S(1)} %get-tuple-element.139), channel_id=1, source_target_pairs={{0,1},{1,0},{2,3},{3,2},{4,5},{5,4},{6,7},{7,6},{8,9},{9,8},{10,11... | collective-permute-start | bytes 1671176 | tf_op jit(solution)/shard_map/ppermute | solution.py:727
  122.1 9.1 %collective-permute-start.12 = (bf16[144,1024]{1,0:T(8,128)(2,1)S(1)}, bf16[144,1024]{1,0:T(8,128)(2,1)S(1)}, u32[]{:S(2)}, u32[]{:S(2)}) collective-permute-start(bf16[144,1024]{1,0:T(8,128)(2,1)S(1)} %get-tuple-element.142), channel_id=1, source_target_pairs={{0,2},{1,3},{2,0},{3,1},{4,6},{5,7},{6,4},{7,5},{8,10},{9,11},{10,... | collective-permute-start | bytes 884744 | tf_op jit(solution)/shard_map/ppermute | solution.py:727

commit v7 on v6

--- a/solution.py
+++ b/solution.py
@@ -92,7 +92,7 @@
         ),
         out_shape=out((row_count, LANES), bf16),
         compiler_params=params(mib),
-        cost_estimate=cost(2 * row_count * row_count * LANES * 4, 3 * row_count * LANES * 2),
+        cost_estimate=cost(2 * row_count * LANES, row_count),
         name="permute_rows",
     )(column, order.reshape(parts * groups, LANES), rows)
 
@@ -266,14 +266,14 @@
     value_t_ref[...] = projected[:, 2 * LANES :].astype(f32).T.astype(bf16)
 
 
-def project(blocks, weight, column, space):
+def project(blocks, weight, column, hidden_space, space):
     row_count = blocks[0].shape[0]
     step_rows = row_count
     features = weight.shape[1]
     width = pl.BlockSpec((step_rows, LANES), lambda i, c: (i, 0))
     tall = pl.BlockSpec((LANES, step_rows), lambda i, c: (0, i))
-    normal = lambda t: pltpu.VMEM((row_count, LANES), t)
-    turned = pltpu.VMEM((LANES, row_count), bf16)
+    normal = lambda t: space((row_count, LANES), t)
+    turned = space((LANES, row_count), bf16)
     return pl.pallas_call(
         project_body,
         grid_spec=pltpu.PrefetchScalarGridSpec(
@@ -288,7 +288,7 @@
             ]
             + [tall] * 4,
         ),
-        out_shape=[space((row_count, features), bf16)]
+        out_shape=[hidden_space((row_count, features), bf16)]
         + [pltpu.HBM((LANES, row_count), f32), pltpu.HBM((8, row_count), f32)]
         + [normal(bf16)]
         + [turned] * 4,
@@ -378,7 +378,7 @@
         ],
         scratch_shapes=[pltpu.SMEM((1,), i32)],
         compiler_params=params(16),
-        cost_estimate=cost(1600 * elements, 2 * elements, elements),
+        cost_estimate=cost(1360 * elements, 2 * elements, elements),
         name="attention_forward",
     )(keys, base2_t, key_t, value_t)
 
@@ -737,26 +737,32 @@
 
     arrived = exchange(permute_rows(scan_points, send_order, column, 0, 1, whole, 60))
     buckets = bucket_rows(voxel_grads, voxel_shard, voxel_point, column, shards, capacity)
-    got = exchange(buckets.reshape(shards * (capacity + INDEX_ROWS), LANES))
     owns = [
         permute_rows(arrived, arrive_order, zero, p, patches, pltpu.VMEM, 12)
         for p in range(patches)
     ]
+    buckets, owns[0] = after(buckets, owns[0])
+    got = exchange(buckets.reshape(shards * (capacity + INDEX_ROWS), LANES))
     across = [swap(own, 2) for own in owns]
     across[0], owns[1] = after(across[0], owns[1])
 
-    def forward(p):
+    def project_patch(p):
         columns = (owns[p], across[p], swap(owns[p], 1), swap(across[p], 1))
+        return project(columns, weight, column, pltpu.HBM, pltpu.VMEM if p == 0 else pltpu.HBM)
+
+    def forward(p, projected):
         space = pltpu.VMEM if p == patches - 1 else pltpu.HBM
-        projected = project(columns, weight, column, space)
-        return projected, attention_forward(projected[3], projected[4], *projected[6:], space)
-
-    projected0, forward0 = forward(0)
-    (got, across[1]), forward0 = after((got, across[1]), forward0)
+        return attention_forward(projected[3], projected[4], *projected[6:], space)
+
+    projected0 = project_patch(0)
+    forward0 = forward(0, projected0)
+    across[1], forward0 = after(across[1], forward0)
+    projected1 = project_patch(1)
+    got, projected1 = after(got, projected1)
     summed_rows = segment_rows(got.reshape(shards, capacity + INDEX_ROWS, LANES), local_rows)
     summed_across = swap(summed_rows, 2)
-    across[1], summed_rows = after(across[1], summed_rows)
-    projected1, forward1 = forward(1)
+    projected1, summed_rows = after(projected1, summed_rows)
+    forward1 = forward(1, projected1)
     summed_across, forward1 = after(summed_across, forward1)
     grads = (summed_rows, summed_across, swap(summed_rows, 1), swap(summed_across, 1))
     forwards = [(projected0, forward0), (projected1, forward1)]

time: 133 us -> 131 us (0.985)
  waiting for transfers between devices: 19 us -> 15.1 us
  local copies, waits for them, and re-layouts: 0.06 us -> 1.74 us
    ppermute x13, waiting for transfers between devices: 16 us -> 12 us  [swap(): return lax.ppermute(rows, 'mp', [(i, i ^ mask) for i in range(members)])]
    unnamed x28 -> x44, local copies, waits for them, and re-layouts: 0.06 us -> 1.74 us
  transfers between devices with their start and end apart: 16 -> 16, of which waited for: 6 -> 7; matrix products, arithmetic and copies ran while one was open for 0% -> 0% of each run, Pallas kernels for 55% -> 54%
where the time goes in v7:
time: 131 us
  Pallas kernels  88.9 us (68%)
  starting transfers between devices  24.2 us (18%)
  waiting for transfers between devices  15.1 us (12%)
  local copies, waits for them, and re-layouts  1.74 us (1%)
    pallas_call x2, Pallas kernels, attention_forward(): pl.pallas_call(forward_body, grid=(heads,), in_specs=[pl.BlockSpec((PATCH...  36.8 us
    pallas_call x2, Pallas kernels, attention_backward(): pl.pallas_call(functools.partial(backward_body, first), grid_spec=pltpu.P...  18 us
    all_to_all x3, starting transfers between devices, exchange(): return lax.all_to_all(rows, 'seq', split_axis=0, concat_axis=0, tiled=True)  16.1 us
    ppermute x13, waiting for transfers between devices, swap(): return lax.ppermute(rows, 'mp', [(i, i ^ mask) for i in range(members)])  12 us
    pallas_call x1, Pallas kernels, bucket_rows(): pl.pallas_call(functools.partial(bucket_body, shards, capacity), grid_spe...  11.5 us
    ppermute x13, starting transfers between devices, swap(): return lax.ppermute(rows, 'mp', [(i, i ^ mask) for i in range(members)])  8.08 us
    pallas_call x2, Pallas kernels, project(): pl.pallas_call(project_body, grid_spec=pltpu.PrefetchScalarGridSpec(num_s...  5.11 us
    pallas_call x3, Pallas kernels, permute_rows(): pl.pallas_call(permute_body, grid_spec=pltpu.PrefetchScalarGridSpec(num_s...  4.86 us
  transfers between devices with their start and end apart: 16, of which 7 were waited for; matrix products, arithmetic and copies ran while one was open for 0% of the time, Pallas kernels for 54%

profile of v7, /device:TPU:0, one launch (start us, length us, event | category | flops | bytes accessed | tf_op | source)
XLA Modules:
  0.0 130.8 jit_solution(1270330366297608096)
XLA Ops:
  0.6 3.3 %permute_rows.3 = bf16[2048,128]{1,0:T(8,128)(2,1)} custom-call(s32[1]{0:T(128)} %bitcast.column_ref.refs_0_, s32[16,128]{1,0:T(8,128)} %bitcast.21, bf16[2048,512]{1,0:T(8,128)(2,1)} %block_ref.1), custom_call_target="tpu_custom_call" | custom-call | flops 524288 | bytes 2048 | tf_op jit(solution)/shard_map/permute_rows/pallas_call | solution.py:82
  4.0 7.3 %all-to-all-start = ((bf16[8,256,128]{2,1,0:T(8,128)(2,1)}), bf16[8,256,128]{2,1,0:T(8,128)(2,1)S(1)}, u32[]{:S(2)}, u32[]{:S(2)}) async-start(bf16[8,256,128]{2,1,0:T(8,128)(2,1)} %bitcast.20), calls=%async_computation | async-start | bytes 1048576 | tf_op jit(solution)/shard_map/all_to_all | solution.py:730
  11.2 11.5 %bucket_rows.1 = bf16[8,528,128]{2,1,0:T(8,128)(2,1)} custom-call(s32[1]{0:T(128)} %bitcast.column_ref.refs_0_, s32[16,128]{1,0:T(8,128)} %bitcast.23, s32[16,128]{1,0:T(8,128)} %bitcast.24, bf16[2048,512]{1,0:T(8,128)(2,1)} %grads_ref.1), custom_call_target="tpu_custom_call" | custom-call | flops 8589934592 | bytes 3145728 | tf_op jit(solution)/shard_map/bucket_rows/pallas_call | solution.py:156
  22.7 3.0 %all-to-all-done = bf16[8,256,128]{2,1,0:T(8,128)(2,1)S(1)} async-done(((bf16[8,256,128]{2,1,0:T(8,128)(2,1)}), bf16[8,256,128]{2,1,0:T(8,128)(2,1)S(1)}, u32[]{:S(2)}, u32[]{:S(2)}) %all-to-all-start) | async-done | bytes 524320 | tf_op jit(solution)/shard_map/all_to_all | solution.py:730
  25.7 0.8 permute_rows.5.x0_ref
  26.5 1.6 %collective-permute-start.1 = (bf16[1024,128]{1,0:T(8,128)(2,1)S(1)}, bf16[1024,128]{1,0:T(8,128)(2,1)S(1)}, u32[]{:S(2)}, u32[]{:S(2)}) collective-permute-start(bf16[1024,128]{1,0:T(8,128)(2,1)S(1)} %permute_rows.5.x0_ref), channel_id=1, source_target_pairs={{0,2},{1,3},{2,0},{3,1},{4,6},{5,7},{6,4},{7,5},{8,10},{9,11},{10,... | collective-permute-start | bytes 786440 | tf_op jit(solution)/shard_map/ppermute | solution.py:727
  28.1 3.7 %all-to-all-start.1 = ((bf16[8,528,128]{2,1,0:T(8,128)(2,1)}), bf16[8,528,128]{2,1,0:T(8,128)(2,1)S(1)}, u32[]{:S(2)}, u32[]{:S(2)}) async-start(bf16[8,528,128]{2,1,0:T(8,128)(2,1)} %bucket_rows.1), calls=%async_computation.1 | async-start | bytes 2162688 | tf_op jit(solution)/shard_map/all_to_all | solution.py:730
  31.8 0.8 permute_rows.4.x0_ref
  32.6 0.1 collective-permute-start.2
  32.7 0.6 collective-permute-done.1.x1_ref
  33.3 0.0 collective-permute-start.3
  33.3 0.7 copy-done.18
  34.0 1.5 %collective-permute-start = (bf16[1024,128]{1,0:T(8,128)(2,1)S(1)}, bf16[1024,128]{1,0:T(8,128)(2,1)S(1)}, u32[]{:S(2)}, u32[]{:S(2)}) collective-permute-start(bf16[1024,128]{1,0:T(8,128)(2,1)S(1)} %permute_rows.4.x0_ref), channel_id=1, source_target_pairs={{0,2},{1,3},{2,0},{3,1},{4,6},{5,7},{6,4},{7,5},{8,10},{9,11},{10,... | collective-permute-start | bytes 786440 | tf_op jit(solution)/shard_map/ppermute | solution.py:727
  35.5 0.2 collective-permute-start.4
  35.7 0.0 collective-permute-done.2.x2_ref
  35.7 0.0 collective-permute-done.3.x3_ref
  35.7 0.0 copy-start.19
  35.7 0.9 copy-done.19
  36.7 2.5 %project.2 = (bf16[1024,512]{1,0:T(8,128)(2,1)}, f32[128,1024]{1,0:T(8,128)}, f32[8,1024]{1,0:T(8,128)}, bf16[1024,128]{1,0:T(8,128)(2,1)S(1)}, bf16[128,1024]{1...) custom-call(s32[1]{0:T(128)} %bitcast.column_ref.refs_0_, ...), custom_call_target="tpu_custom_call" | custom-call | flops 805306368 | bytes 5242880 | tf_op jit(solution)/shard_map/project/pallas_call | solution.py:277
  39.2 19.1 %attention_forward.2 = (bf16[8,1024,1024]{2,1,0:T(8,128)(2,1)}, bf16[128,1024]{1,0:T(8,128)(2,1)}, f32[8,1,1024]{2,1,0:T(1,128)S(1)}, bf16[8,256,1024]{2,1,0:T(8,128)(2,1)}) custom-call(bf16[1024,128]{1,0:T(8,128)(2,1)S(1)} %get-tuple-element.97.key_ref, bf16[128,1024]{1,0:T(8,128)(2,1)S(1)} %get-tuple-element.98.base2_t_ref, ...), custom_call_target="tpu_custom_call" | custom-call | flops 11408506880 | bytes 16777216 | tf_op jit(solution)/shard_map/attention_forward/pallas_call | solution.py:363
  58.4 0.0 collective-permute-done.x1_ref
  58.4 0.3 collective-permute-start.5
  58.7 0.0 collective-permute-done.4.x2_ref
  58.7 1.2 collective-permute-done.5.x3_ref
  60.0 2.6 %project.3 = (bf16[1024,512]{1,0:T(8,128)(2,1)}, f32[128,1024]{1,0:T(8,128)}, f32[8,1024]{1,0:T(8,128)}, bf16[1024,128]{1,0:T(8,128)(2,1)}, bf16[128,1024]{1,0:T...) custom-call(s32[1]{0:T(128)} %bitcast.column_ref.refs_0_, ...), custom_call_target="tpu_custom_call" | custom-call | flops 805306368 | bytes 5242880 | tf_op jit(solution)/shard_map/project/pallas_call | solution.py:277
  62.6 0.0 all-to-all-done.1
  62.6 2.6 %segment_rows.1.refs_6_.d_out_ref = bf16[128,2048]{1,0:T(8,128)(2,1)S(1)} custom-call(bf16[8,528,128]{2,1,0:T(8,128)(2,1)S(1)} %all-to-all-done.1), custom_call_target="tpu_custom_call" | custom-call | flops 8858370048 | bytes 3244032 | tf_op jit(solution)/shard_map/segment_rows/pallas_call | solution.py:215
  65.2 0.0 copy-start.15
  65.2 0.6 collective-permute-start.6
  65.9 0.0 collective-permute-start.7
  65.9 0.0 copy-done.14
  65.9 0.0 copy-done.20
  65.9 0.0 copy-done.21
  65.9 17.6 %attention_forward.3 = (bf16[8,1024,1024]{2,1,0:T(8,128)(2,1)S(1)}, bf16[128,1024]{1,0:T(8,128)(2,1)S(1)}, f32[8,1,1024]{2,1,0:T(1,128)S(1)}, bf16[8,256,1024]{2,1,0:T(8,128)(2,1)S(1)}) custom-call(bf16[1024,128]{1,0:T(8,128)(2,1)S(1)} %copy-done.20, bf16[128,1024]{1,0:T(8,128)(2,1)S(1)} %copy-done.21, bf16[128,1024]{1,0:T(8,128)(2,1)S(1)} %copy-done.14, ...), custom_call_target="tpu_custom_call" | custom-call | flops 11408506880 | bytes 16777216 | tf_op jit(solution)/shard_map/attention_forward/pallas_call | solution.py:363
  83.5 0.0 collective-permute-done.6.refs_7_
  83.5 0.6 collective-permute-start.8
  84.1 0.0 collective-permute-done.7.refs_8_
  84.1 1.5 %collective-permute-done.8.refs_9_ = bf16[128,2048]{1,0:T(8,128)(2,1)S(1)} collective-permute-done((bf16[128,2048]{1,0:T(8,128)(2,1)S(1)}, bf16[128,2048]{1,0:T(8,128)(2,1)S(1)}, u32[]{:S(2)}, u32[]{:S(2)}) %collective-permute-start.8) | collective-permute-done | bytes 524320 | tf_op jit(solution)/shard_map/ppermute | solution.py:727
  85.6 8.2 %attention_backward.2 = (bf16[512,1024]{1,0:T(8,128)(2,1)S(1)}, bf16[128,1024]{1,0:T(8,128)(2,1)S(1)}, bf16[128,1024]{1,0:T(8,128)(2,1)S(1)}, bf16[128,1024]{1,0:T(8,128)(2,1)S(1)}, bf16[1,1024,1024]{2,1,0:T(8,128)(2,1)S(1)}) custom-call(s32[1]{0:T(128)} %bitcast.column_ref.refs_0_, bf16[8,1024,1024]{2,1,0:T(8,128)(2,1)S(1)} %get-tuple-element.134.refs_1_, ...), custom_call_target="tpu_custom_call" | custom-call | flops 9227468800 | bytes 16777216 | tf_op jit(solution)/shard_map/attention_backward/pallas_call | solution.py:526
  93.8 0.0 copy-start.7
  93.8 1.0 hidden_part.2
  94.9 0.4 collective-permute-start.9
  95.3 0.8 weight_grads.2.refs_6_
  96.1 0.7 collective-permute-done.9.got_ref
  96.9 0.1 pair_sum.2
  97.0 1.5 %collective-permute-start.10 = (bf16[144,1024]{1,0:T(8,128)(2,1)S(1)}, bf16[144,1024]{1,0:T(8,128)(2,1)S(1)}, u32[]{:S(2)}, u32[]{:S(2)}) collective-permute-start(bf16[144,1024]{1,0:T(8,128)(2,1)S(1)} %get-tuple-element.151), channel_id=1, source_target_pairs={{0,2},{1,3},{2,0},{3,1},{4,6},{5,7},{6,4},{7,5},{8,10},{9,11},{10,... | collective-permute-start | bytes 884744 | tf_op jit(solution)/shard_map/ppermute | solution.py:727
  98.6 0.0 copy-done.12
  98.6 9.9 %attention_backward.3 = (bf16[512,1024]{1,0:T(8,128)(2,1)S(1)}, bf16[128,1024]{1,0:T(8,128)(2,1)S(1)}, bf16[128,1024]{1,0:T(8,128)(2,1)S(1)}, bf16[128,1024]{1,0:T(8,128)(2,1)S(1)}) custom-call(s32[1]{0:T(128)} %bitcast.column_ref.refs_0_, bf16[1,1024,1024]{2,1,0:T(8,128)(2,1)S(1)} %get-tuple-element.152.refs_1_, ...), custom_call_target="tpu_custom_call" | custom-call | flops 9227468800 | bytes 16777216 | tf_op jit(solution)/shard_map/attention_backward/pallas_call | solution.py:526
  108.4 0.0 copy-start.3
  108.4 0.0 copy-start.4
  108.5 0.0 collective-permute-done.10.got_ref
  108.5 1.7 %weight_grads.3 = bf16[512,512]{1,0:T(8,128)(2,1)} custom-call(bf16[128,1024]{1,0:T(8,128)(2,1)S(1)} %get-tuple-element.165.refs_0_.d_query_ref, bf16[128,1024]{1,0:T(8,128)(2,1)S(1)} %get-tuple-element.166.refs_1_.d_key_ref, bf16[128,1024]{1,0:T(8,128)(2,1)S(1)} %get-tuple-element.167.refs_2_.d_value_ref, bf16[128,1024]{1,0:T(8,128)(2,1)S(1)} %copy-done.13, ...), custom_call_target="tpu_custom_call" | custom-call | flops 536870912 | bytes 6291456 | tf_op jit(solution)/shard_map/weight_grads/pallas_call | solution.py:563
  110.2 5.2 %all-to-all-start.2 = ((bf16[8,64,512]{2,1,0:T(8,128)(2,1)}), bf16[8,64,512]{2,1,0:T(8,128)(2,1)S(1)}, u32[]{:S(2)}, u32[]{:S(2)}) async-start(bf16[8,64,512]{2,1,0:T(8,128)(2,1)} %bitcast.10), calls=%async_computation.2 | async-start | bytes 1048576 | tf_op jit(solution)/shard_map/all_to_all | solution.py:730
  115.4 2.4 %hidden_part.3 = (bf16[256,1024]{1,0:T(8,128)(2,1)S(1)}, bf16[272,1024]{1,0:T(8,128)(2,1)S(1)}, f32[2,1024]{1,0:T(2,128)S(1)}) custom-call(s32[1]{0:T(128)} %bitcast.column_ref.refs_0_, bf16[128,1024]{1,0:T(8,128)(2,1)} %copy-done.3, bf16[128,1024]{1,0:T(8,128)(2,1)} %copy-done.4, bf16[128,1024]{1,0:T(8,128)(2,1)} %copy-done.5, bf16[128,1024]{1,0:T(8,128)(2,1)} %copy-done.9, ...), custom_call_target="tpu_custom_call" | custom-call | flops 402653184 | bytes 2097152 | tf_op jit(solution)/shard_map/hidden_part/pallas_call | solution.py:619
  117.8 0.0 copy-start.16
  117.8 0.1 collective-permute-start.11
  117.9 1.9 %collective-permute-done.11.got_ref = bf16[272,1024]{1,0:T(8,128)(2,1)S(1)} collective-permute-done((bf16[272,1024]{1,0:T(8,128)(2,1)S(1)}, bf16[272,1024]{1,0:T(8,128)(2,1)S(1)}, u32[]{:S(2)}, u32[]{:S(2)}) %collective-permute-start.11) | collective-permute-done | bytes 557088 | tf_op jit(solution)/shard_map/ppermute | solution.py:727
  119.8 0.1 pair_sum.3
  119.9 1.1 collective-permute-start.12
  121.0 2.1 %points_grad.2.rest_0_ = f32[2048,128]{1,0:T(8,128)} custom-call(f32[128,1024]{1,0:T(8,128)S(1)} %get-tuple-element.179.kept_ref, f32[2,1024]{1,0:T(2,128)S(1)} %get-tuple-element.180.sums_ref, bf16[144,1024]{1,0:T(8,128)(2,1)S(1)} %collective-permute-done.10.got_ref, bf16[128,2048]{1,0:T(8,128)(2,1)S(1)} %segment_rows.1.refs_6_.d_out_ref, ...), custom_call_target="tpu_custom_call" | custom-call | flops 1048576 | bytes 3145728 | tf_op jit(solution)/shard_map/points_grad/pallas_call | solution.py:673
  123.1 5.9 %collective-permute-done.12.got_ref = bf16[144,1024]{1,0:T(8,128)(2,1)S(1)} collective-permute-done((bf16[144,1024]{1,0:T(8,128)(2,1)S(1)}, bf16[144,1024]{1,0:T(8,128)(2,1)S(1)}, u32[]{:S(2)}, u32[]{:S(2)}) %collective-permute-start.12) | collective-permute-done | bytes 294944 | tf_op jit(solution)/shard_map/ppermute | solution.py:727
  129.1 1.0 points_grad.3
  130.1 0.0 all-to-all-done.2.parts_ref
  130.1 0.7 grad_sum.1
  (32 shorter events, 0.1 us)
Async XLA Ops:
  4.0 21.7 %all-to-all-start = ((bf16[8,256,128]{2,1,0:T(8,128)(2,1)}), bf16[8,256,128]{2,1,0:T(8,128)(2,1)S(1)}, u32[]{:S(2)}, u32[]{:S(2)}) async-start(bf16[8,256,128]{2,1,0:T(8,128)(2,1)} %bitcast.20), calls=%async_computation | async-start | bytes 1048576 | tf_op jit(solution)/shard_map/all_to_all | solution.py:730
  11.2 14.5 %copy-start.17 = (s32[2048]{0:T(1024)S(1)}, s32[2048]{0:T(1024)}, u32[]{:S(2)}) copy-start(s32[2048]{0:T(1024)} %param.10) | copy-start | bytes 24580
  22.7 13.0 %copy-start = (bf16[512,3,128]{2,0,1:T(8,128)(2,1)S(1)}, bf16[512,3,128]{2,0,1:T(8,128)(2,1)}, u32[]{:S(2)}) copy-start(bf16[512,3,128]{2,0,1:T(8,128)(2,1)} %param.11) | copy-start | bytes 1179652
  26.5 6.8 %collective-permute-start.1 = (bf16[1024,128]{1,0:T(8,128)(2,1)S(1)}, bf16[1024,128]{1,0:T(8,128)(2,1)S(1)}, u32[]{:S(2)}, u32[]{:S(2)}) collective-permute-start(bf16[1024,128]{1,0:T(8,128)(2,1)S(1)} %permute_rows.5.x0_ref), channel_id=1, source_target_pairs={{0,2},{1,3},{2,0},{3,1},{4,6},{5,7},{6,4},{7,5},{8,10},{9,11},{10,... | collective-permute-start | bytes 786440 | tf_op jit(solution)/shard_map/ppermute | solution.py:727
  28.1 34.5 %all-to-all-start.1 = ((bf16[8,528,128]{2,1,0:T(8,128)(2,1)}), bf16[8,528,128]{2,1,0:T(8,128)(2,1)S(1)}, u32[]{:S(2)}, u32[]{:S(2)}) async-start(bf16[8,528,128]{2,1,0:T(8,128)(2,1)} %bucket_rows.1), calls=%async_computation.1 | async-start | bytes 2162688 | tf_op jit(solution)/shard_map/all_to_all | solution.py:730
  32.6 3.1 %collective-permute-start.2 = (bf16[1024,128]{1,0:T(8,128)(2,1)S(1)}, bf16[1024,128]{1,0:T(8,128)(2,1)S(1)}, u32[]{:S(2)}, u32[]{:S(2)}) collective-permute-start(bf16[1024,128]{1,0:T(8,128)(2,1)S(1)} %permute_rows.5.x0_ref), channel_id=1, source_target_pairs={{0,1},{1,0},{2,3},{3,2},{4,5},{5,4},{6,7},{7,6},{8,9},{9,8},{10,11... | collective-permute-start | bytes 786440 | tf_op jit(solution)/shard_map/ppermute | solution.py:727
  33.3 2.5 %collective-permute-start.3 = (bf16[1024,128]{1,0:T(8,128)(2,1)S(1)}, bf16[1024,128]{1,0:T(8,128)(2,1)S(1)}, u32[]{:S(2)}, u32[]{:S(2)}) collective-permute-start(bf16[1024,128]{1,0:T(8,128)(2,1)S(1)} %collective-permute-done.1.x1_ref), channel_id=1, source_target_pairs={{0,1},{1,0},{2,3},{3,2},{4,5},{5,4},{6,7},{7,6},{8,9},{9,8},{10,11... | collective-permute-start | bytes 786440 | tf_op jit(solution)/shard_map/ppermute | solution.py:727
  33.3 0.7 copy-start.18
  34.0 24.4 %collective-permute-start = (bf16[1024,128]{1,0:T(8,128)(2,1)S(1)}, bf16[1024,128]{1,0:T(8,128)(2,1)S(1)}, u32[]{:S(2)}, u32[]{:S(2)}) collective-permute-start(bf16[1024,128]{1,0:T(8,128)(2,1)S(1)} %permute_rows.4.x0_ref), channel_id=1, source_target_pairs={{0,2},{1,3},{2,0},{3,1},{4,6},{5,7},{6,4},{7,5},{8,10},{9,11},{10,... | collective-permute-start | bytes 786440 | tf_op jit(solution)/shard_map/ppermute | solution.py:727
  35.5 23.2 %collective-permute-start.4 = (bf16[1024,128]{1,0:T(8,128)(2,1)S(1)}, bf16[1024,128]{1,0:T(8,128)(2,1)S(1)}, u32[]{:S(2)}, u32[]{:S(2)}) collective-permute-start(bf16[1024,128]{1,0:T(8,128)(2,1)S(1)} %permute_rows.4.x0_ref), channel_id=1, source_target_pairs={{0,1},{1,0},{2,3},{3,2},{4,5},{5,4},{6,7},{7,6},{8,9},{9,8},{10,11... | collective-permute-start | bytes 786440 | tf_op jit(solution)/shard_map/ppermute | solution.py:727
  35.7 1.0 copy-start.19
  39.2 19.2 %copy-start.10 = (bf16[128,1024]{1,0:T(8,128)(2,1)}, bf16[128,1024]{1,0:T(8,128)(2,1)S(1)}, u32[]{:S(2)}) copy-start(bf16[128,1024]{1,0:T(8,128)(2,1)S(1)} %get-tuple-element.169.key_t_ref.key_ref) | copy-start | bytes 786436
  39.2 19.2 %copy-start.11 = (bf16[128,1024]{1,0:T(8,128)(2,1)}, bf16[128,1024]{1,0:T(8,128)(2,1)S(1)}, u32[]{:S(2)}) copy-start(bf16[128,1024]{1,0:T(8,128)(2,1)S(1)} %get-tuple-element.170.value_t_ref.refs_4_.value_ref) | copy-start | bytes 786436
  39.2 59.4 %copy-start.9 = (bf16[128,1024]{1,0:T(8,128)(2,1)}, bf16[128,1024]{1,0:T(8,128)(2,1)S(1)}, u32[]{:S(2)}) copy-start(bf16[128,1024]{1,0:T(8,128)(2,1)S(1)} %get-tuple-element.168.refs_3_.query_ref) | copy-start | bytes 786436
  58.4 1.6 %collective-permute-start.5 = (bf16[1024,128]{1,0:T(8,128)(2,1)S(1)}, bf16[1024,128]{1,0:T(8,128)(2,1)S(1)}, u32[]{:S(2)}, u32[]{:S(2)}) collective-permute-start(bf16[1024,128]{1,0:T(8,128)(2,1)S(1)} %collective-permute-done.x1_ref), channel_id=1, source_target_pairs={{0,1},{1,0},{2,3},{3,2},{4,5},{5,4},{6,7},{7,6},{8,9},{9,8},{10,11... | collective-permute-start | bytes 786440 | tf_op jit(solution)/shard_map/ppermute | solution.py:727
  62.6 3.3 %copy-start.2 = (bf16[128,1024]{1,0:T(8,128)(2,1)S(1)}, bf16[128,1024]{1,0:T(8,128)(2,1)}, u32[]{:S(2)}) copy-start(bf16[128,1024]{1,0:T(8,128)(2,1)} %get-tuple-element.129.value_t_ref.refs_4_.value_ref) | copy-start | bytes 786436
  62.6 3.3 %copy-start.14 = (bf16[128,1024]{1,0:T(8,128)(2,1)S(1)}, bf16[128,1024]{1,0:T(8,128)(2,1)}, u32[]{:S(2)}) copy-start(bf16[128,1024]{1,0:T(8,128)(2,1)} %get-tuple-element.128.key_t_ref.key_ref) | copy-start | bytes 786436
  62.6 3.3 %copy-start.20 = (bf16[1024,128]{1,0:T(8,128)(2,1)S(1)}, bf16[1024,128]{1,0:T(8,128)(2,1)}, u32[]{:S(2)}) copy-start(bf16[1024,128]{1,0:T(8,128)(2,1)} %get-tuple-element.126.key_ref) | copy-start | bytes 786436
  62.6 3.3 %copy-start.21 = (bf16[128,1024]{1,0:T(8,128)(2,1)S(1)}, bf16[128,1024]{1,0:T(8,128)(2,1)}, u32[]{:S(2)}) copy-start(bf16[128,1024]{1,0:T(8,128)(2,1)} %get-tuple-element.127.base2_t_ref) | copy-start | bytes 786436
  65.2 20.4 %copy-start.1 = (bf16[128,1024]{1,0:T(8,128)(2,1)S(1)}, bf16[128,1024]{1,0:T(8,128)(2,1)}, u32[]{:S(2)}) copy-start(bf16[128,1024]{1,0:T(8,128)(2,1)} %get-tuple-element.136.refs_3_.query_ref) | copy-start | bytes 786436
  65.2 20.4 %copy-start.15 = (bf16[512,128]{1,0:T(8,128)(2,1)S(1)}, bf16[512,128]{1,0:T(8,128)(2,1)}, u32[]{:S(2)}) copy-start(bf16[512,128]{1,0:T(8,128)(2,1)} %refs_10_.3) | copy-start | bytes 393220
  65.2 18.3 %collective-permute-start.6 = (bf16[128,2048]{1,0:T(8,128)(2,1)S(1)}, bf16[128,2048]{1,0:T(8,128)(2,1)S(1)}, u32[]{:S(2)}, u32[]{:S(2)}) collective-permute-start(bf16[128,2048]{1,0:T(8,128)(2,1)S(1)} %segment_rows.1.refs_6_.d_out_ref), channel_id=1, source_target_pairs={{0,2},{1,3},{2,0},{3,1},{4,6},{5,7},{6,4},{7,5},{8,10},{9,11},{10,... | collective-permute-start | bytes 1572872 | tf_op jit(solution)/shard_map/ppermute | solution.py:727
  65.9 18.2 %collective-permute-start.7 = (bf16[128,2048]{1,0:T(8,128)(2,1)S(1)}, bf16[128,2048]{1,0:T(8,128)(2,1)S(1)}, u32[]{:S(2)}, u32[]{:S(2)}) collective-permute-start(bf16[128,2048]{1,0:T(8,128)(2,1)S(1)} %segment_rows.1.refs_6_.d_out_ref), channel_id=1, source_target_pairs={{0,1},{1,0},{2,3},{3,2},{4,5},{5,4},{6,7},{7,6},{8,9},{9,8},{10,11... | collective-permute-start | bytes 1572872 | tf_op jit(solution)/shard_map/ppermute | solution.py:727
  83.5 2.1 %collective-permute-start.8 = (bf16[128,2048]{1,0:T(8,128)(2,1)S(1)}, bf16[128,2048]{1,0:T(8,128)(2,1)S(1)}, u32[]{:S(2)}, u32[]{:S(2)}) collective-permute-start(bf16[128,2048]{1,0:T(8,128)(2,1)S(1)} %collective-permute-done.6.refs_7_), channel_id=1, source_target_pairs={{0,1},{1,0},{2,3},{3,2},{4,5},{5,4},{6,7},{7,6},{8,9},{9,8},{10,11... | collective-permute-start | bytes 1572872 | tf_op jit(solution)/shard_map/ppermute | solution.py:727
  93.8 1.5 %copy-start.7 = (bf16[1024,512]{1,0:T(8,128)(2,1)S(1)}, bf16[1024,512]{1,0:T(8,128)(2,1)}, u32[]{:S(2)}) copy-start(bf16[1024,512]{1,0:T(8,128)(2,1)} %get-tuple-element.147.refs_4_) | copy-start | bytes 3145732
  94.9 2.0 %collective-permute-start.9 = (bf16[272,1024]{1,0:T(8,128)(2,1)S(1)}, bf16[272,1024]{1,0:T(8,128)(2,1)S(1)}, u32[]{:S(2)}, u32[]{:S(2)}) collective-permute-start(bf16[272,1024]{1,0:T(8,128)(2,1)S(1)} %get-tuple-element.146), channel_id=1, source_target_pairs={{0,1},{1,0},{2,3},{3,2},{4,5},{5,4},{6,7},{7,6},{8,9},{9,8},{10,11... | collective-permute-start | bytes 1671176 | tf_op jit(solution)/shard_map/ppermute | solution.py:727
  95.3 3.3 %copy-start.12 = (bf16[128,1024]{1,0:T(8,128)(2,1)S(1)}, bf16[128,1024]{1,0:T(8,128)(2,1)}, u32[]{:S(2)}) copy-start(bf16[128,1024]{1,0:T(8,128)(2,1)} %copy-done.11) | copy-start | bytes 786436
  95.3 3.3 %copy-start.13 = (bf16[128,1024]{1,0:T(8,128)(2,1)S(1)}, bf16[128,1024]{1,0:T(8,128)(2,1)}, u32[]{:S(2)}) copy-start(bf16[128,1024]{1,0:T(8,128)(2,1)} %get-tuple-element.155.refs_5_.refs_3_) | copy-start | bytes 786436
  97.0 11.5 %collective-permute-start.10 = (bf16[144,1024]{1,0:T(8,128)(2,1)S(1)}, bf16[144,1024]{1,0:T(8,128)(2,1)S(1)}, u32[]{:S(2)}, u32[]{:S(2)}) collective-permute-start(bf16[144,1024]{1,0:T(8,128)(2,1)S(1)} %get-tuple-element.151), channel_id=1, source_target_pairs={{0,2},{1,3},{2,0},{3,1},{4,6},{5,7},{6,4},{7,5},{8,10},{9,11},{10,... | collective-permute-start | bytes 884744 | tf_op jit(solution)/shard_map/ppermute | solution.py:727
  98.6 9.9 %copy-start.6 = (bf16[1024,512]{1,0:T(8,128)(2,1)S(1)}, bf16[1024,512]{1,0:T(8,128)(2,1)}, u32[]{:S(2)}) copy-start(bf16[1024,512]{1,0:T(8,128)(2,1)} %get-tuple-element.162.refs_4_) | copy-start | bytes 3145732
  108.4 1.8 %copy-start.3 = (bf16[128,1024]{1,0:T(8,128)(2,1)}, bf16[128,1024]{1,0:T(8,128)(2,1)S(1)}, u32[]{:S(2)}) copy-start(bf16[128,1024]{1,0:T(8,128)(2,1)S(1)} %get-tuple-element.165.refs_0_.d_query_ref) | copy-start | bytes 786436
  108.4 1.8 %copy-start.4 = (bf16[128,1024]{1,0:T(8,128)(2,1)}, bf16[128,1024]{1,0:T(8,128)(2,1)S(1)}, u32[]{:S(2)}) copy-start(bf16[128,1024]{1,0:T(8,128)(2,1)S(1)} %get-tuple-element.166.refs_1_.d_key_ref) | copy-start | bytes 786436
  108.5 1.8 %copy-start.5 = (bf16[128,1024]{1,0:T(8,128)(2,1)}, bf16[128,1024]{1,0:T(8,128)(2,1)S(1)}, u32[]{:S(2)}) copy-start(bf16[128,1024]{1,0:T(8,128)(2,1)S(1)} %get-tuple-element.167.refs_2_.d_value_ref) | copy-start | bytes 786436
  110.2 19.9 %all-to-all-start.2 = ((bf16[8,64,512]{2,1,0:T(8,128)(2,1)}), bf16[8,64,512]{2,1,0:T(8,128)(2,1)S(1)}, u32[]{:S(2)}, u32[]{:S(2)}) async-start(bf16[8,64,512]{2,1,0:T(8,128)(2,1)} %bitcast.10), calls=%async_computation.2 | async-start | bytes 1048576 | tf_op jit(solution)/shard_map/all_to_all | solution.py:730
  117.7 11.3 %copy-start.8 = (f32[128,1024]{1,0:T(8,128)S(1)}, f32[128,1024]{1,0:T(8,128)}, u32[]{:S(2)}) copy-start(f32[128,1024]{1,0:T(8,128)} %get-tuple-element.177.normed_ref) | copy-start | bytes 1572868
  117.8 11.3 %copy-start.16 = (f32[8,1024]{1,0:T(8,128)S(1)}, f32[8,1024]{1,0:T(8,128)}, u32[]{:S(2)}) copy-start(f32[8,1024]{1,0:T(8,128)} %get-tuple-element.178.inv_ref) | copy-start | bytes 98308
  117.8 2.0 %collective-permute-start.11 = (bf16[272,1024]{1,0:T(8,128)(2,1)S(1)}, bf16[272,1024]{1,0:T(8,128)(2,1)S(1)}, u32[]{:S(2)}, u32[]{:S(2)}) collective-permute-start(bf16[272,1024]{1,0:T(8,128)(2,1)S(1)} %get-tuple-element.173), channel_id=1, source_target_pairs={{0,1},{1,0},{2,3},{3,2},{4,5},{5,4},{6,7},{7,6},{8,9},{9,8},{10,11... | collective-permute-start | bytes 1671176 | tf_op jit(solution)/shard_map/ppermute | solution.py:727
  119.9 9.1 %collective-permute-start.12 = (bf16[144,1024]{1,0:T(8,128)(2,1)S(1)}, bf16[144,1024]{1,0:T(8,128)(2,1)S(1)}, u32[]{:S(2)}, u32[]{:S(2)}) collective-permute-start(bf16[144,1024]{1,0:T(8,128)(2,1)S(1)} %get-tuple-element.176), channel_id=1, source_target_pairs={{0,2},{1,3},{2,0},{3,1},{4,6},{5,7},{6,4},{7,5},{8,10},{9,11},{10,... | collective-permute-start | bytes 884744 | tf_op jit(solution)/shard_map/ppermute | solution.py:727

commit v8 on v7

--- a/solution.py
+++ b/solution.py
@@ -301,6 +301,7 @@
 def forward_body(
     key_ref,
     base2_t_ref,
+    query_t_ref,
     key_t_ref,
     value_t_ref,
     exp_ref,
@@ -323,10 +324,10 @@
 
     def attend(shifted):
         in_head = lax.broadcasted_iota(i32, (LANES, 1), 0) // HD == head
-        query = jnp.where(in_head, base2_t_ref[...], jnp.zeros((), bf16))
-        scores = dot(key_ref[...], query)
+        query_ref = query_t_ref if shifted else base2_t_ref
+        scores = dot(key_ref[...], jnp.where(in_head, query_ref[...], jnp.zeros((), bf16)))
         if shifted:
-            scores = scores - jnp.max(scores, axis=0, keepdims=True)
+            scores = (scores - jnp.max(scores, axis=0, keepdims=True)) * log2_e
         weights = jnp.exp2(scores).astype(bf16)
         exp_ref[0] = weights
         keys = key_t_ref[pl.ds(at, HD), :].astype(f32)
@@ -355,7 +356,7 @@
         attend(True)
 
 
-def attention_forward(keys, base2_t, key_t, value_t, space):
+def attention_forward(keys, base2_t, query_t, key_t, value_t, space):
     heads = LANES // HD
     tall = pl.BlockSpec((LANES, PATCH), lambda h: (0, 0))
     per_head = lambda h: (h, 0, 0)
@@ -363,7 +364,7 @@
     return pl.pallas_call(
         forward_body,
         grid=(heads,),
-        in_specs=[pl.BlockSpec((PATCH, LANES), lambda h: (0, 0)), tall, tall, tall],
+        in_specs=[pl.BlockSpec((PATCH, LANES), lambda h: (0, 0))] + [tall] * 4,
         out_specs=[
             pl.BlockSpec((1, PATCH, PATCH), per_head),
             tall,
@@ -380,7 +381,7 @@
         compiler_params=params(16),
         cost_estimate=cost(1360 * elements, 2 * elements, elements),
         name="attention_forward",
-    )(keys, base2_t, key_t, value_t)
+    )(keys, base2_t, query_t, key_t, value_t)
 
 
 def backward_body(first, *refs):
@@ -752,7 +753,7 @@
 
     def forward(p, projected):
         space = pltpu.VMEM if p == patches - 1 else pltpu.HBM
-        return attention_forward(projected[3], projected[4], *projected[6:], space)
+        return attention_forward(*projected[3:], space)
 
     projected0 = project_patch(0)
     forward0 = forward(0, projected0)

time: 131 us -> 133 us (1.015)
  Pallas kernels: 88.9 us -> 92.1 us
  local copies, waits for them, and re-layouts: 1.74 us -> 0.09 us
    pallas_call x2, Pallas kernels: 36.8 us -> 39.9 us  [attention_forward(): pl.pallas_call(forward_body, grid=(heads,), in_specs=[pl.BlockSpec((PATCH...]
    unnamed x44 -> x40, local copies, waits for them, and re-layouts: 1.74 us -> 0.09 us
  transfers between devices with their start and end apart: 16 -> 16, of which waited for: 7 -> 8; matrix products, arithmetic and copies ran while one was open for 0% -> 0% of each run, Pallas kernels for 54% -> 56%
where the time goes in v8:
time: 133 us
  Pallas kernels  92.1 us (69%)
  starting transfers between devices  24.5 us (18%)
  waiting for transfers between devices  15.1 us (11%)
    pallas_call x2, Pallas kernels, attention_forward(): pl.pallas_call(forward_body, grid=(heads,), in_specs=[pl.BlockSpec((PATCH...  39.9 us
    pallas_call x2, Pallas kernels, attention_backward(): pl.pallas_call(functools.partial(backward_body, first), grid_spec=pltpu.P...  18 us
    all_to_all x3, starting transfers between devices, exchange(): return lax.all_to_all(rows, 'seq', split_axis=0, concat_axis=0, tiled=True)  16.4 us
    ppermute x13, waiting for transfers between devices, swap(): return lax.ppermute(rows, 'mp', [(i, i ^ mask) for i in range(members)])  12 us
    pallas_call x1, Pallas kernels, bucket_rows(): pl.pallas_call(functools.partial(bucket_body, shards, capacity), grid_spe...  11.5 us
    ppermute x13, starting transfers between devices, swap(): return lax.ppermute(rows, 'mp', [(i, i ^ mask) for i in range(members)])  8.05 us
    pallas_call x2, Pallas kernels, project(): pl.pallas_call(project_body, grid_spec=pltpu.PrefetchScalarGridSpec(num_s...  5.13 us
    pallas_call x3, Pallas kernels, permute_rows(): pl.pallas_call(permute_body, grid_spec=pltpu.PrefetchScalarGridSpec(num_s...  4.86 us
  transfers between devices with their start and end apart: 16, of which 8 were waited for; matrix products, arithmetic and copies ran while one was open for 0% of the time, Pallas kernels for 56%

profile of v8, /device:TPU:0, one launch (start us, length us, event | category | flops | bytes accessed | tf_op | source)
XLA Modules:
  0.0 132.6 jit_solution(11636784730539738262)
XLA Ops:
  0.6 3.3 %permute_rows.3 = bf16[2048,128]{1,0:T(8,128)(2,1)} custom-call(s32[1]{0:T(128)} %bitcast.column_ref.refs_0_, s32[16,128]{1,0:T(8,128)} %bitcast.21, bf16[2048,512]{1,0:T(8,128)(2,1)} %block_ref.1), custom_call_target="tpu_custom_call" | custom-call | flops 524288 | bytes 2048 | tf_op jit(solution)/shard_map/permute_rows/pallas_call | solution.py:82
  4.0 7.3 %all-to-all-start = ((bf16[8,256,128]{2,1,0:T(8,128)(2,1)}), bf16[8,256,128]{2,1,0:T(8,128)(2,1)S(1)}, u32[]{:S(2)}, u32[]{:S(2)}) async-start(bf16[8,256,128]{2,1,0:T(8,128)(2,1)} %bitcast.20), calls=%async_computation | async-start | bytes 1048576 | tf_op jit(solution)/shard_map/all_to_all | solution.py:731
  11.2 11.5 %bucket_rows.1 = bf16[8,528,128]{2,1,0:T(8,128)(2,1)} custom-call(s32[1]{0:T(128)} %bitcast.column_ref.refs_0_, s32[16,128]{1,0:T(8,128)} %bitcast.23, s32[16,128]{1,0:T(8,128)} %bitcast.24, bf16[2048,512]{1,0:T(8,128)(2,1)} %grads_ref.1), custom_call_target="tpu_custom_call" | custom-call | flops 8589934592 | bytes 3145728 | tf_op jit(solution)/shard_map/bucket_rows/pallas_call | solution.py:156
  22.7 3.0 %all-to-all-done = bf16[8,256,128]{2,1,0:T(8,128)(2,1)S(1)} async-done(((bf16[8,256,128]{2,1,0:T(8,128)(2,1)}), bf16[8,256,128]{2,1,0:T(8,128)(2,1)S(1)}, u32[]{:S(2)}, u32[]{:S(2)}) %all-to-all-start) | async-done | bytes 524320 | tf_op jit(solution)/shard_map/all_to_all | solution.py:731
  25.7 0.0 copy-done.17
  25.7 0.8 permute_rows.5.x0_ref
  26.5 1.6 %collective-permute-start.1 = (bf16[1024,128]{1,0:T(8,128)(2,1)S(1)}, bf16[1024,128]{1,0:T(8,128)(2,1)S(1)}, u32[]{:S(2)}, u32[]{:S(2)}) collective-permute-start(bf16[1024,128]{1,0:T(8,128)(2,1)S(1)} %permute_rows.5.x0_ref), channel_id=1, source_target_pairs={{0,2},{1,3},{2,0},{3,1},{4,6},{5,7},{6,4},{7,5},{8,10},{9,11},{10,... | collective-permute-start | bytes 786440 | tf_op jit(solution)/shard_map/ppermute | solution.py:728
  28.1 3.7 %all-to-all-start.1 = ((bf16[8,528,128]{2,1,0:T(8,128)(2,1)}), bf16[8,528,128]{2,1,0:T(8,128)(2,1)S(1)}, u32[]{:S(2)}, u32[]{:S(2)}) async-start(bf16[8,528,128]{2,1,0:T(8,128)(2,1)} %bucket_rows.1), calls=%async_computation.1 | async-start | bytes 2162688 | tf_op jit(solution)/shard_map/all_to_all | solution.py:731
  31.8 0.8 permute_rows.4.x0_ref
  32.6 0.1 collective-permute-start.2
  32.7 0.6 collective-permute-done.1.x1_ref
  33.3 0.0 collective-permute-start.3
  33.3 1.5 %collective-permute-start = (bf16[1024,128]{1,0:T(8,128)(2,1)S(1)}, bf16[1024,128]{1,0:T(8,128)(2,1)S(1)}, u32[]{:S(2)}, u32[]{:S(2)}) collective-permute-start(bf16[1024,128]{1,0:T(8,128)(2,1)S(1)} %permute_rows.4.x0_ref), channel_id=1, source_target_pairs={{0,2},{1,3},{2,0},{3,1},{4,6},{5,7},{6,4},{7,5},{8,10},{9,11},{10,... | collective-permute-start | bytes 786440 | tf_op jit(solution)/shard_map/ppermute | solution.py:728
  34.8 0.2 collective-permute-start.4
  35.0 0.0 collective-permute-done.2.x2_ref
  35.0 0.0 collective-permute-done.3.x3_ref
  35.0 2.5 %project.2 = (bf16[1024,512]{1,0:T(8,128)(2,1)}, f32[128,1024]{1,0:T(8,128)}, f32[8,1024]{1,0:T(8,128)}, bf16[1024,128]{1,0:T(8,128)(2,1)S(1)}, bf16[128,1024]{1...) custom-call(s32[1]{0:T(128)} %bitcast.column_ref.refs_0_, ...), custom_call_target="tpu_custom_call" | custom-call | flops 805306368 | bytes 5242880 | tf_op jit(solution)/shard_map/project/pallas_call | solution.py:277
  37.6 20.7 %attention_forward.2 = (bf16[8,1024,1024]{2,1,0:T(8,128)(2,1)}, bf16[128,1024]{1,0:T(8,128)(2,1)}, f32[8,1,1024]{2,1,0:T(1,128)S(1)}, bf16[8,256,1024]{2,1,0:T(8,128)(2,1)}) custom-call(bf16[1024,128]{1,0:T(8,128)(2,1)S(1)} %get-tuple-element.97.key_ref, bf16[128,1024]{1,0:T(8,128)(2,1)S(1)} %get-tuple-element.98.base2_t_ref, ...), custom_call_target="tpu_custom_call" | custom-call | flops 11408506880 | bytes 16777216 | tf_op jit(solution)/shard_map/attention_forward/pallas_call | solution.py:364
  58.2 0.0 copy-done.10
  58.2 0.0 collective-permute-done.x1_ref
  58.2 0.3 collective-permute-start.5
  58.6 0.0 collective-permute-done.4.x2_ref
  58.6 1.2 collective-permute-done.5.x3_ref
  59.8 2.6 %project.3 = (bf16[1024,512]{1,0:T(8,128)(2,1)}, f32[128,1024]{1,0:T(8,128)}, f32[8,1024]{1,0:T(8,128)}, bf16[1024,128]{1,0:T(8,128)(2,1)}, bf16[128,1024]{1,0:T...) custom-call(s32[1]{0:T(128)} %bitcast.column_ref.refs_0_, ...), custom_call_target="tpu_custom_call" | custom-call | flops 805306368 | bytes 5242880 | tf_op jit(solution)/shard_map/project/pallas_call | solution.py:277
  62.4 0.0 all-to-all-done.1
  62.5 2.6 %segment_rows.1.refs_6_.d_out_ref = bf16[128,2048]{1,0:T(8,128)(2,1)S(1)} custom-call(bf16[8,528,128]{2,1,0:T(8,128)(2,1)S(1)} %all-to-all-done.1), custom_call_target="tpu_custom_call" | custom-call | flops 8858370048 | bytes 3244032 | tf_op jit(solution)/shard_map/segment_rows/pallas_call | solution.py:215
  65.1 0.0 copy-start.15
  65.1 1.3 collective-permute-start.6
  66.4 0.0 collective-permute-start.7
  66.5 0.0 copy-done.14
  66.5 0.0 copy-done.18
  66.5 0.0 copy-done.19
  66.5 19.3 %attention_forward.3 = (bf16[8,1024,1024]{2,1,0:T(8,128)(2,1)S(1)}, bf16[128,1024]{1,0:T(8,128)(2,1)S(1)}, f32[8,1,1024]{2,1,0:T(1,128)S(1)}, bf16[8,256,1024]{2,1,0:T(8,128)(2,1)S(1)}) custom-call(bf16[1024,128]{1,0:T(8,128)(2,1)S(1)} %copy-done.18, bf16[128,1024]{1,0:T(8,128)(2,1)S(1)} %copy-done.19, bf16[128,1024]{1,0:T(8,128)(2,1)S(1)} %copy-done.1, ...), custom_call_target="tpu_custom_call" | custom-call | flops 11408506880 | bytes 16777216 | tf_op jit(solution)/shard_map/attention_forward/pallas_call | solution.py:364
  85.8 0.0 collective-permute-done.6.refs_7_
  85.8 0.6 collective-permute-start.8
  86.3 0.0 collective-permute-done.7.refs_8_
  86.3 1.5 %collective-permute-done.8.refs_9_ = bf16[128,2048]{1,0:T(8,128)(2,1)S(1)} collective-permute-done((bf16[128,2048]{1,0:T(8,128)(2,1)S(1)}, bf16[128,2048]{1,0:T(8,128)(2,1)S(1)}, u32[]{:S(2)}, u32[]{:S(2)}) %collective-permute-start.8) | collective-permute-done | bytes 524320 | tf_op jit(solution)/shard_map/ppermute | solution.py:728
  87.9 8.2 %attention_backward.2 = (bf16[512,1024]{1,0:T(8,128)(2,1)S(1)}, bf16[128,1024]{1,0:T(8,128)(2,1)S(1)}, bf16[128,1024]{1,0:T(8,128)(2,1)S(1)}, bf16[128,1024]{1,0:T(8,128)(2,1)S(1)}, bf16[1,1024,1024]{2,1,0:T(8,128)(2,1)S(1)}) custom-call(s32[1]{0:T(128)} %bitcast.column_ref.refs_0_, bf16[8,1024,1024]{2,1,0:T(8,128)(2,1)S(1)} %get-tuple-element.136.refs_1_, ...), custom_call_target="tpu_custom_call" | custom-call | flops 9227468800 | bytes 16777216 | tf_op jit(solution)/shard_map/attention_backward/pallas_call | solution.py:527
  96.0 0.0 copy-start.7
  96.1 1.0 hidden_part.2
  97.1 0.4 collective-permute-start.9
  97.5 0.8 weight_grads.2.refs_6_
  98.4 0.7 collective-permute-done.9.got_ref
  99.1 0.1 pair_sum.2
  99.2 0.8 collective-permute-start.10
  100.1 0.0 copy-done.9
  100.1 9.9 %attention_backward.3 = (bf16[512,1024]{1,0:T(8,128)(2,1)S(1)}, bf16[128,1024]{1,0:T(8,128)(2,1)S(1)}, bf16[128,1024]{1,0:T(8,128)(2,1)S(1)}, bf16[128,1024]{1,0:T(8,128)(2,1)S(1)}) custom-call(s32[1]{0:T(128)} %bitcast.column_ref.refs_0_, bf16[1,1024,1024]{2,1,0:T(8,128)(2,1)S(1)} %get-tuple-element.153.refs_1_, ...), custom_call_target="tpu_custom_call" | custom-call | flops 9227468800 | bytes 16777216 | tf_op jit(solution)/shard_map/attention_backward/pallas_call | solution.py:527
  110.0 0.0 copy-start.3
  110.0 0.0 collective-permute-done.10.got_ref
  110.0 1.7 %weight_grads.3 = bf16[512,512]{1,0:T(8,128)(2,1)} custom-call(bf16[128,1024]{1,0:T(8,128)(2,1)S(1)} %get-tuple-element.165.refs_0_.d_query_ref, bf16[128,1024]{1,0:T(8,128)(2,1)S(1)} %get-tuple-element.166.refs_1_.d_key_ref, bf16[128,1024]{1,0:T(8,128)(2,1)S(1)} %get-tuple-element.167.refs_2_.d_value_ref, bf16[128,1024]{1,0:T(8,128)(2,1)S(1)} %copy-done.13, ...), custom_call_target="tpu_custom_call" | custom-call | flops 536870912 | bytes 6291456 | tf_op jit(solution)/shard_map/weight_grads/pallas_call | solution.py:564
  111.8 0.0 copy-done.4
  111.8 5.4 %all-to-all-start.2 = ((bf16[8,64,512]{2,1,0:T(8,128)(2,1)}), bf16[8,64,512]{2,1,0:T(8,128)(2,1)S(1)}, u32[]{:S(2)}, u32[]{:S(2)}) async-start(bf16[8,64,512]{2,1,0:T(8,128)(2,1)} %bitcast.10), calls=%async_computation.2 | async-start | bytes 1048576 | tf_op jit(solution)/shard_map/all_to_all | solution.py:731
  117.2 2.4 %hidden_part.3 = (bf16[256,1024]{1,0:T(8,128)(2,1)S(1)}, bf16[272,1024]{1,0:T(8,128)(2,1)S(1)}, f32[2,1024]{1,0:T(2,128)S(1)}) custom-call(s32[1]{0:T(128)} %bitcast.column_ref.refs_0_, bf16[128,1024]{1,0:T(8,128)(2,1)} %copy-done.3, bf16[128,1024]{1,0:T(8,128)(2,1)} %copy-done.4, bf16[128,1024]{1,0:T(8,128)(2,1)} %copy-done.5, bf16[128,1024]{1,0:T(8,128)(2,1)} %copy-done.9, ...), custom_call_target="tpu_custom_call" | custom-call | flops 402653184 | bytes 2097152 | tf_op jit(solution)/shard_map/hidden_part/pallas_call | solution.py:620
  119.5 0.0 copy-start.8
  119.6 0.0 copy-start.16
  119.6 0.1 collective-permute-start.11
  119.6 1.9 %collective-permute-done.11.got_ref = bf16[272,1024]{1,0:T(8,128)(2,1)S(1)} collective-permute-done((bf16[272,1024]{1,0:T(8,128)(2,1)S(1)}, bf16[272,1024]{1,0:T(8,128)(2,1)S(1)}, u32[]{:S(2)}, u32[]{:S(2)}) %collective-permute-start.11) | collective-permute-done | bytes 557088 | tf_op jit(solution)/shard_map/ppermute | solution.py:728
  121.6 0.1 pair_sum.3
  121.7 1.1 collective-permute-start.12
  122.8 2.1 %points_grad.2.rest_0_ = f32[2048,128]{1,0:T(8,128)} custom-call(f32[128,1024]{1,0:T(8,128)S(1)} %get-tuple-element.179.kept_ref, f32[2,1024]{1,0:T(2,128)S(1)} %get-tuple-element.180.sums_ref, bf16[144,1024]{1,0:T(8,128)(2,1)S(1)} %collective-permute-done.10.got_ref, bf16[128,2048]{1,0:T(8,128)(2,1)S(1)} %segment_rows.1.refs_6_.d_out_ref, ...), custom_call_target="tpu_custom_call" | custom-call | flops 1048576 | bytes 3145728 | tf_op jit(solution)/shard_map/points_grad/pallas_call | solution.py:674
  124.9 6.0 %collective-permute-done.12.got_ref = bf16[144,1024]{1,0:T(8,128)(2,1)S(1)} collective-permute-done((bf16[144,1024]{1,0:T(8,128)(2,1)S(1)}, bf16[144,1024]{1,0:T(8,128)(2,1)S(1)}, u32[]{:S(2)}, u32[]{:S(2)}) %collective-permute-start.12) | collective-permute-done | bytes 294944 | tf_op jit(solution)/shard_map/ppermute | solution.py:728
  130.8 1.0 points_grad.3
  131.9 0.1 all-to-all-done.2.parts_ref
  131.9 0.7 grad_sum.1
  (28 shorter events, 0.1 us)
Async XLA Ops:
  4.0 21.7 %all-to-all-start = ((bf16[8,256,128]{2,1,0:T(8,128)(2,1)}), bf16[8,256,128]{2,1,0:T(8,128)(2,1)S(1)}, u32[]{:S(2)}, u32[]{:S(2)}) async-start(bf16[8,256,128]{2,1,0:T(8,128)(2,1)} %bitcast.20), calls=%async_computation | async-start | bytes 1048576 | tf_op jit(solution)/shard_map/all_to_all | solution.py:731
  11.2 14.5 %copy-start.17 = (s32[2048]{0:T(1024)S(1)}, s32[2048]{0:T(1024)}, u32[]{:S(2)}) copy-start(s32[2048]{0:T(1024)} %param.10) | copy-start | bytes 24580
  22.7 12.3 %copy-start = (bf16[512,3,128]{2,0,1:T(8,128)(2,1)S(1)}, bf16[512,3,128]{2,0,1:T(8,128)(2,1)}, u32[]{:S(2)}) copy-start(bf16[512,3,128]{2,0,1:T(8,128)(2,1)} %param.11) | copy-start | bytes 1179652
  26.5 6.8 %collective-permute-start.1 = (bf16[1024,128]{1,0:T(8,128)(2,1)S(1)}, bf16[1024,128]{1,0:T(8,128)(2,1)S(1)}, u32[]{:S(2)}, u32[]{:S(2)}) collective-permute-start(bf16[1024,128]{1,0:T(8,128)(2,1)S(1)} %permute_rows.5.x0_ref), channel_id=1, source_target_pairs={{0,2},{1,3},{2,0},{3,1},{4,6},{5,7},{6,4},{7,5},{8,10},{9,11},{10,... | collective-permute-start | bytes 786440 | tf_op jit(solution)/shard_map/ppermute | solution.py:728
  28.1 34.4 %all-to-all-start.1 = ((bf16[8,528,128]{2,1,0:T(8,128)(2,1)}), bf16[8,528,128]{2,1,0:T(8,128)(2,1)S(1)}, u32[]{:S(2)}, u32[]{:S(2)}) async-start(bf16[8,528,128]{2,1,0:T(8,128)(2,1)} %bucket_rows.1), calls=%async_computation.1 | async-start | bytes 2162688 | tf_op jit(solution)/shard_map/all_to_all | solution.py:731
  32.6 2.4 %collective-permute-start.2 = (bf16[1024,128]{1,0:T(8,128)(2,1)S(1)}, bf16[1024,128]{1,0:T(8,128)(2,1)S(1)}, u32[]{:S(2)}, u32[]{:S(2)}) collective-permute-start(bf16[1024,128]{1,0:T(8,128)(2,1)S(1)} %permute_rows.5.x0_ref), channel_id=1, source_target_pairs={{0,1},{1,0},{2,3},{3,2},{4,5},{5,4},{6,7},{7,6},{8,9},{9,8},{10,11... | collective-permute-start | bytes 786440 | tf_op jit(solution)/shard_map/ppermute | solution.py:728
  33.3 1.8 %collective-permute-start.3 = (bf16[1024,128]{1,0:T(8,128)(2,1)S(1)}, bf16[1024,128]{1,0:T(8,128)(2,1)S(1)}, u32[]{:S(2)}, u32[]{:S(2)}) collective-permute-start(bf16[1024,128]{1,0:T(8,128)(2,1)S(1)} %collective-permute-done.1.x1_ref), channel_id=1, source_target_pairs={{0,1},{1,0},{2,3},{3,2},{4,5},{5,4},{6,7},{7,6},{8,9},{9,8},{10,11... | collective-permute-start | bytes 786440 | tf_op jit(solution)/shard_map/ppermute | solution.py:728
  33.3 25.0 %collective-permute-start = (bf16[1024,128]{1,0:T(8,128)(2,1)S(1)}, bf16[1024,128]{1,0:T(8,128)(2,1)S(1)}, u32[]{:S(2)}, u32[]{:S(2)}) collective-permute-start(bf16[1024,128]{1,0:T(8,128)(2,1)S(1)} %permute_rows.4.x0_ref), channel_id=1, source_target_pairs={{0,2},{1,3},{2,0},{3,1},{4,6},{5,7},{6,4},{7,5},{8,10},{9,11},{10,... | collective-permute-start | bytes 786440 | tf_op jit(solution)/shard_map/ppermute | solution.py:728
  34.8 23.8 %collective-permute-start.4 = (bf16[1024,128]{1,0:T(8,128)(2,1)S(1)}, bf16[1024,128]{1,0:T(8,128)(2,1)S(1)}, u32[]{:S(2)}, u32[]{:S(2)}) collective-permute-start(bf16[1024,128]{1,0:T(8,128)(2,1)S(1)} %permute_rows.4.x0_ref), channel_id=1, source_target_pairs={{0,1},{1,0},{2,3},{3,2},{4,5},{5,4},{6,7},{7,6},{8,9},{9,8},{10,11... | collective-permute-start | bytes 786440 | tf_op jit(solution)/shard_map/ppermute | solution.py:728
  37.5 20.7 %copy-start.10 = (bf16[128,1024]{1,0:T(8,128)(2,1)}, bf16[128,1024]{1,0:T(8,128)(2,1)S(1)}, u32[]{:S(2)}) copy-start(bf16[128,1024]{1,0:T(8,128)(2,1)S(1)} %get-tuple-element.169.key_t_ref.key_ref) | copy-start | bytes 786436
  37.6 20.7 %copy-start.11 = (bf16[128,1024]{1,0:T(8,128)(2,1)}, bf16[128,1024]{1,0:T(8,128)(2,1)S(1)}, u32[]{:S(2)}) copy-start(bf16[128,1024]{1,0:T(8,128)(2,1)S(1)} %get-tuple-element.170.value_t_ref.refs_4_.value_ref) | copy-start | bytes 786436
  37.6 62.5 %copy-start.9 = (bf16[128,1024]{1,0:T(8,128)(2,1)}, bf16[128,1024]{1,0:T(8,128)(2,1)S(1)}, u32[]{:S(2)}) copy-start(bf16[128,1024]{1,0:T(8,128)(2,1)S(1)} %get-tuple-element.168.query_t_ref.refs_3_.query_ref) | copy-start | bytes 786436
  58.2 1.6 %collective-permute-start.5 = (bf16[1024,128]{1,0:T(8,128)(2,1)S(1)}, bf16[1024,128]{1,0:T(8,128)(2,1)S(1)}, u32[]{:S(2)}, u32[]{:S(2)}) collective-permute-start(bf16[1024,128]{1,0:T(8,128)(2,1)S(1)} %collective-permute-done.x1_ref), channel_id=1, source_target_pairs={{0,1},{1,0},{2,3},{3,2},{4,5},{5,4},{6,7},{7,6},{8,9},{9,8},{10,11... | collective-permute-start | bytes 786440 | tf_op jit(solution)/shard_map/ppermute | solution.py:728
  62.4 4.0 %copy-start.1 = (bf16[128,1024]{1,0:T(8,128)(2,1)S(1)}, bf16[128,1024]{1,0:T(8,128)(2,1)}, u32[]{:S(2)}) copy-start(bf16[128,1024]{1,0:T(8,128)(2,1)} %get-tuple-element.129.query_t_ref.refs_3_.query_ref) | copy-start | bytes 786436
  62.4 4.0 %copy-start.2 = (bf16[128,1024]{1,0:T(8,128)(2,1)S(1)}, bf16[128,1024]{1,0:T(8,128)(2,1)}, u32[]{:S(2)}) copy-start(bf16[128,1024]{1,0:T(8,128)(2,1)} %get-tuple-element.131.value_t_ref.refs_4_.value_ref) | copy-start | bytes 786436
  62.5 4.0 %copy-start.14 = (bf16[128,1024]{1,0:T(8,128)(2,1)S(1)}, bf16[128,1024]{1,0:T(8,128)(2,1)}, u32[]{:S(2)}) copy-start(bf16[128,1024]{1,0:T(8,128)(2,1)} %get-tuple-element.130.key_t_ref.key_ref) | copy-start | bytes 786436
  62.5 4.0 %copy-start.18 = (bf16[1024,128]{1,0:T(8,128)(2,1)S(1)}, bf16[1024,128]{1,0:T(8,128)(2,1)}, u32[]{:S(2)}) copy-start(bf16[1024,128]{1,0:T(8,128)(2,1)} %get-tuple-element.127.key_ref) | copy-start | bytes 786436
  62.5 4.0 %copy-start.19 = (bf16[128,1024]{1,0:T(8,128)(2,1)S(1)}, bf16[128,1024]{1,0:T(8,128)(2,1)}, u32[]{:S(2)}) copy-start(bf16[128,1024]{1,0:T(8,128)(2,1)} %get-tuple-element.128.base2_t_ref) | copy-start | bytes 786436
  65.1 22.7 %copy-start.15 = (bf16[512,128]{1,0:T(8,128)(2,1)S(1)}, bf16[512,128]{1,0:T(8,128)(2,1)}, u32[]{:S(2)}) copy-start(bf16[512,128]{1,0:T(8,128)(2,1)} %refs_10_.3) | copy-start | bytes 393220
  65.1 20.6 %collective-permute-start.6 = (bf16[128,2048]{1,0:T(8,128)(2,1)S(1)}, bf16[128,2048]{1,0:T(8,128)(2,1)S(1)}, u32[]{:S(2)}, u32[]{:S(2)}) collective-permute-start(bf16[128,2048]{1,0:T(8,128)(2,1)S(1)} %segment_rows.1.refs_6_.d_out_ref), channel_id=1, source_target_pairs={{0,2},{1,3},{2,0},{3,1},{4,6},{5,7},{6,4},{7,5},{8,10},{9,11},{10,... | collective-permute-start | bytes 1572872 | tf_op jit(solution)/shard_map/ppermute | solution.py:728
  66.4 19.9 %collective-permute-start.7 = (bf16[128,2048]{1,0:T(8,128)(2,1)S(1)}, bf16[128,2048]{1,0:T(8,128)(2,1)S(1)}, u32[]{:S(2)}, u32[]{:S(2)}) collective-permute-start(bf16[128,2048]{1,0:T(8,128)(2,1)S(1)} %segment_rows.1.refs_6_.d_out_ref), channel_id=1, source_target_pairs={{0,1},{1,0},{2,3},{3,2},{4,5},{5,4},{6,7},{7,6},{8,9},{9,8},{10,11... | collective-permute-start | bytes 1572872 | tf_op jit(solution)/shard_map/ppermute | solution.py:728
  85.8 2.1 %collective-permute-start.8 = (bf16[128,2048]{1,0:T(8,128)(2,1)S(1)}, bf16[128,2048]{1,0:T(8,128)(2,1)S(1)}, u32[]{:S(2)}, u32[]{:S(2)}) collective-permute-start(bf16[128,2048]{1,0:T(8,128)(2,1)S(1)} %collective-permute-done.6.refs_7_), channel_id=1, source_target_pairs={{0,1},{1,0},{2,3},{3,2},{4,5},{5,4},{6,7},{7,6},{8,9},{9,8},{10,11... | collective-permute-start | bytes 1572872 | tf_op jit(solution)/shard_map/ppermute | solution.py:728
  96.0 1.5 %copy-start.7 = (bf16[1024,512]{1,0:T(8,128)(2,1)S(1)}, bf16[1024,512]{1,0:T(8,128)(2,1)}, u32[]{:S(2)}) copy-start(bf16[1024,512]{1,0:T(8,128)(2,1)} %get-tuple-element.148.refs_4_) | copy-start | bytes 3145732
  97.1 2.0 %collective-permute-start.9 = (bf16[272,1024]{1,0:T(8,128)(2,1)S(1)}, bf16[272,1024]{1,0:T(8,128)(2,1)S(1)}, u32[]{:S(2)}, u32[]{:S(2)}) collective-permute-start(bf16[272,1024]{1,0:T(8,128)(2,1)S(1)} %get-tuple-element.147), channel_id=1, source_target_pairs={{0,1},{1,0},{2,3},{3,2},{4,5},{5,4},{6,7},{7,6},{8,9},{9,8},{10,11... | collective-permute-start | bytes 1671176 | tf_op jit(solution)/shard_map/ppermute | solution.py:728
  97.5 2.6 %copy-start.12 = (bf16[128,1024]{1,0:T(8,128)(2,1)S(1)}, bf16[128,1024]{1,0:T(8,128)(2,1)}, u32[]{:S(2)}) copy-start(bf16[128,1024]{1,0:T(8,128)(2,1)} %copy-done.11) | copy-start | bytes 786436
  97.5 2.6 %copy-start.13 = (bf16[128,1024]{1,0:T(8,128)(2,1)S(1)}, bf16[128,1024]{1,0:T(8,128)(2,1)}, u32[]{:S(2)}) copy-start(bf16[128,1024]{1,0:T(8,128)(2,1)} %get-tuple-element.155.refs_5_.refs_3_) | copy-start | bytes 786436
  99.2 10.8 %collective-permute-start.10 = (bf16[144,1024]{1,0:T(8,128)(2,1)S(1)}, bf16[144,1024]{1,0:T(8,128)(2,1)S(1)}, u32[]{:S(2)}, u32[]{:S(2)}) collective-permute-start(bf16[144,1024]{1,0:T(8,128)(2,1)S(1)} %get-tuple-element.152), channel_id=1, source_target_pairs={{0,2},{1,3},{2,0},{3,1},{4,6},{5,7},{6,4},{7,5},{8,10},{9,11},{10,... | collective-permute-start | bytes 884744 | tf_op jit(solution)/shard_map/ppermute | solution.py:728
  100.1 9.9 %copy-start.6 = (bf16[1024,512]{1,0:T(8,128)(2,1)S(1)}, bf16[1024,512]{1,0:T(8,128)(2,1)}, u32[]{:S(2)}) copy-start(bf16[1024,512]{1,0:T(8,128)(2,1)} %get-tuple-element.162.refs_4_) | copy-start | bytes 3145732
  110.0 1.8 %copy-start.3 = (bf16[128,1024]{1,0:T(8,128)(2,1)}, bf16[128,1024]{1,0:T(8,128)(2,1)S(1)}, u32[]{:S(2)}) copy-start(bf16[128,1024]{1,0:T(8,128)(2,1)S(1)} %get-tuple-element.165.refs_0_.d_query_ref) | copy-start | bytes 786436
  110.0 1.8 %copy-start.4 = (bf16[128,1024]{1,0:T(8,128)(2,1)}, bf16[128,1024]{1,0:T(8,128)(2,1)S(1)}, u32[]{:S(2)}) copy-start(bf16[128,1024]{1,0:T(8,128)(2,1)S(1)} %get-tuple-element.166.refs_1_.d_key_ref) | copy-start | bytes 786436
  110.0 1.8 %copy-start.5 = (bf16[128,1024]{1,0:T(8,128)(2,1)}, bf16[128,1024]{1,0:T(8,128)(2,1)S(1)}, u32[]{:S(2)}) copy-start(bf16[128,1024]{1,0:T(8,128)(2,1)S(1)} %get-tuple-element.167.refs_2_.d_value_ref) | copy-start | bytes 786436
  111.8 20.2 %all-to-all-start.2 = ((bf16[8,64,512]{2,1,0:T(8,128)(2,1)}), bf16[8,64,512]{2,1,0:T(8,128)(2,1)S(1)}, u32[]{:S(2)}, u32[]{:S(2)}) async-start(bf16[8,64,512]{2,1,0:T(8,128)(2,1)} %bitcast.10), calls=%async_computation.2 | async-start | bytes 1048576 | tf_op jit(solution)/shard_map/all_to_all | solution.py:731
  119.5 11.3 %copy-start.8 = (f32[128,1024]{1,0:T(8,128)S(1)}, f32[128,1024]{1,0:T(8,128)}, u32[]{:S(2)}) copy-start(f32[128,1024]{1,0:T(8,128)} %get-tuple-element.177.normed_ref) | copy-start | bytes 1572868
  119.6 11.3 %copy-start.16 = (f32[8,1024]{1,0:T(8,128)S(1)}, f32[8,1024]{1,0:T(8,128)}, u32[]{:S(2)}) copy-start(f32[8,1024]{1,0:T(8,128)} %get-tuple-element.178.inv_ref) | copy-start | bytes 98308
  119.6 2.0 %collective-permute-start.11 = (bf16[272,1024]{1,0:T(8,128)(2,1)S(1)}, bf16[272,1024]{1,0:T(8,128)(2,1)S(1)}, u32[]{:S(2)}, u32[]{:S(2)}) collective-permute-start(bf16[272,1024]{1,0:T(8,128)(2,1)S(1)} %get-tuple-element.173), channel_id=1, source_target_pairs={{0,1},{1,0},{2,3},{3,2},{4,5},{5,4},{6,7},{7,6},{8,9},{9,8},{10,11... | collective-permute-start | bytes 1671176 | tf_op jit(solution)/shard_map/ppermute | solution.py:728
  121.7 9.1 %collective-permute-start.12 = (bf16[144,1024]{1,0:T(8,128)(2,1)S(1)}, bf16[144,1024]{1,0:T(8,128)(2,1)S(1)}, u32[]{:S(2)}, u32[]{:S(2)}) collective-permute-start(bf16[144,1024]{1,0:T(8,128)(2,1)S(1)} %get-tuple-element.176), channel_id=1, source_target_pairs={{0,2},{1,3},{2,0},{3,1},{4,6},{5,7},{6,4},{7,5},{8,10},{9,11},{10,... | collective-permute-start | bytes 884744 | tf_op jit(solution)/shard_map/ppermute | solution.py:728

commit v9 on v8

--- a/solution.py
+++ b/solution.py
@@ -14,6 +14,7 @@
 INDEX_BASE = 64
 BLOCK_MASKS = (0, 2, 1, 3)
 SAFE_SCORE = 60.0
+QUERY_BLOCK = 256
 STAGED_HEADS = 1
 SEGMENT_SHARDS = 8
 BUCKET_SHARDS = 2
@@ -78,7 +79,7 @@
 def permute_rows(rows, order, column, part, parts, out, mib):
     row_count = order.shape[0] // parts
     groups = row_count // LANES
-    step_rows = min(1024, row_count)
+    step_rows = min(2048, row_count)
     return pl.pallas_call(
         permute_body,
         grid_spec=pltpu.PrefetchScalarGridSpec(
@@ -325,27 +326,39 @@
     def attend(shifted):
         in_head = lax.broadcasted_iota(i32, (LANES, 1), 0) // HD == head
         query_ref = query_t_ref if shifted else base2_t_ref
-        scores = dot(key_ref[...], jnp.where(in_head, query_ref[...], jnp.zeros((), bf16)))
-        if shifted:
-            scores = (scores - jnp.max(scores, axis=0, keepdims=True)) * log2_e
-        weights = jnp.exp2(scores).astype(bf16)
-        exp_ref[0] = weights
         keys = key_t_ref[pl.ds(at, HD), :].astype(f32)
         values = value_t_ref[pl.ds(at, HD), :].astype(f32)
         middle = jnp.mean(values, axis=1, keepdims=True)
         centered = values - middle
         features = [centered[j : j + 1] * keys for j in range(HD)]
         features += [keys, values, jnp.ones((HD, PATCH), f32)]
-        sums = dot(jnp.concatenate([f.astype(bf16) for f in features], axis=0), weights)
-        inverse = 1.0 / sums[(HD + 2) * HD : (HD + 2) * HD + 1]
-        inverse_ref[0] = inverse
-        mean_key = sums[HD * HD : (HD + 1) * HD] * inverse
-        mean_value = sums[(HD + 1) * HD : (HD + 2) * HD] * inverse
-        attended_ref[pl.ds(at, HD), :] = mean_value.astype(bf16)
-        offset = mean_value - middle
-        for j in range(HD):
-            crossed = sums[j * HD : (j + 1) * HD] * inverse - offset[j : j + 1] * mean_key
-            covariance_ref[0, j * HD : (j + 1) * HD, :] = crossed.astype(bf16)
+        features = jnp.concatenate([f.astype(bf16) for f in features], axis=0)
+
+        def finish(weights, columns):
+            sums = dot(features, weights)
+            inverse = 1.0 / sums[(HD + 2) * HD : (HD + 2) * HD + 1]
+            inverse_ref[0, :, columns] = inverse
+            mean_key = sums[HD * HD : (HD + 1) * HD] * inverse
+            mean_value = sums[(HD + 1) * HD : (HD + 2) * HD] * inverse
+            attended_ref[pl.ds(at, HD), columns] = mean_value.astype(bf16)
+            offset = mean_value - middle
+            for j in range(HD):
+                crossed = sums[j * HD : (j + 1) * HD] * inverse - offset[j : j + 1] * mean_key
+                covariance_ref[0, j * HD : (j + 1) * HD, columns] = crossed.astype(bf16)
+
+        before = None
+        for start in range(0, PATCH, QUERY_BLOCK):
+            columns = slice(start, start + QUERY_BLOCK)
+            query = jnp.where(in_head, query_ref[:, columns], jnp.zeros((), bf16))
+            scores = dot(key_ref[...], query)
+            if shifted:
+                scores = (scores - jnp.max(scores, axis=0, keepdims=True)) * log2_e
+            weights = jnp.exp2(scores).astype(bf16)
+            exp_ref[0, :, columns] = weights
+            if before is not None:
+                finish(*before)
+            before = (weights, columns)
+        finish(*before)
 
     @pl.when(safe_ref[0] == 1)
     def _():

time: 133 us -> 134 us (level)
  no operation moved by 1% of the time
where the time goes in v9:
time: 134 us; the launch traced here: 133 us
  Pallas kernels  92.8 us (69%)
  starting transfers between devices  24.5 us (18%)
  waiting for transfers between devices  15.1 us (11%)
    pallas_call x2, Pallas kernels, attention_forward(): pl.pallas_call(forward_body, grid=(heads,), in_specs=[pl.BlockSpec((PATCH...  40.8 us
    pallas_call x2, Pallas kernels, attention_backward(): pl.pallas_call(functools.partial(backward_body, first), grid_spec=pltpu.P...  18 us
    all_to_all x3, starting transfers between devices, exchange(): return lax.all_to_all(rows, 'seq', split_axis=0, concat_axis=0, tiled=True)  16.4 us
    ppermute x13, waiting for transfers between devices, swap(): return lax.ppermute(rows, 'mp', [(i, i ^ mask) for i in range(members)])  12.1 us
    pallas_call x1, Pallas kernels, bucket_rows(): pl.pallas_call(functools.partial(bucket_body, shards, capacity), grid_spe...  11.5 us
    ppermute x13, starting transfers between devices, swap(): return lax.ppermute(rows, 'mp', [(i, i ^ mask) for i in range(members)])  8.04 us
    pallas_call x2, Pallas kernels, project(): pl.pallas_call(project_body, grid_spec=pltpu.PrefetchScalarGridSpec(num_s...  5.12 us
    pallas_call x3, Pallas kernels, permute_rows(): pl.pallas_call(permute_body, grid_spec=pltpu.PrefetchScalarGridSpec(num_s...  4.68 us
  transfers between devices with their start and end apart: 16, of which 8 were waited for; matrix products, arithmetic and copies ran while one was open for 0% of the time, Pallas kernels for 56%

profile of v9, /device:TPU:0, one launch (start us, length us, event | category | flops | bytes accessed | tf_op | source)
XLA Modules:
  0.0 133.3 jit_solution(15004484623968091978)
XLA Ops:
  0.6 3.2 %permute_rows.3 = bf16[2048,128]{1,0:T(8,128)(2,1)} custom-call(s32[1]{0:T(128)} %bitcast.column_ref.refs_0_, s32[16,128]{1,0:T(8,128)} %bitcast.21, bf16[2048,512]{1,0:T(8,128)(2,1)} %block_ref.1), custom_call_target="tpu_custom_call" | custom-call | flops 524288 | bytes 2048 | tf_op jit(solution)/shard_map/permute_rows/pallas_call | solution.py:83
  3.8 7.3 %all-to-all-start = ((bf16[8,256,128]{2,1,0:T(8,128)(2,1)}), bf16[8,256,128]{2,1,0:T(8,128)(2,1)S(1)}, u32[]{:S(2)}, u32[]{:S(2)}) async-start(bf16[8,256,128]{2,1,0:T(8,128)(2,1)} %bitcast.20), calls=%async_computation | async-start | bytes 1048576 | tf_op jit(solution)/shard_map/all_to_all | solution.py:744
  11.1 11.5 %bucket_rows.1 = bf16[8,528,128]{2,1,0:T(8,128)(2,1)} custom-call(s32[1]{0:T(128)} %bitcast.column_ref.refs_0_, s32[16,128]{1,0:T(8,128)} %bitcast.23, s32[16,128]{1,0:T(8,128)} %bitcast.24, bf16[2048,512]{1,0:T(8,128)(2,1)} %grads_ref.1), custom_call_target="tpu_custom_call" | custom-call | flops 8589934592 | bytes 3145728 | tf_op jit(solution)/shard_map/bucket_rows/pallas_call | solution.py:157
  22.5 3.0 %all-to-all-done = bf16[8,256,128]{2,1,0:T(8,128)(2,1)S(1)} async-done(((bf16[8,256,128]{2,1,0:T(8,128)(2,1)}), bf16[8,256,128]{2,1,0:T(8,128)(2,1)S(1)}, u32[]{:S(2)}, u32[]{:S(2)}) %all-to-all-start) | async-done | bytes 524320 | tf_op jit(solution)/shard_map/all_to_all | solution.py:744
  25.5 0.8 permute_rows.5.x0_ref
  26.3 1.6 %collective-permute-start.1 = (bf16[1024,128]{1,0:T(8,128)(2,1)S(1)}, bf16[1024,128]{1,0:T(8,128)(2,1)S(1)}, u32[]{:S(2)}, u32[]{:S(2)}) collective-permute-start(bf16[1024,128]{1,0:T(8,128)(2,1)S(1)} %permute_rows.5.x0_ref), channel_id=1, source_target_pairs={{0,2},{1,3},{2,0},{3,1},{4,6},{5,7},{6,4},{7,5},{8,10},{9,11},{10,... | collective-permute-start | bytes 786440 | tf_op jit(solution)/shard_map/ppermute | solution.py:741
  27.9 3.7 %all-to-all-start.1 = ((bf16[8,528,128]{2,1,0:T(8,128)(2,1)}), bf16[8,528,128]{2,1,0:T(8,128)(2,1)S(1)}, u32[]{:S(2)}, u32[]{:S(2)}) async-start(bf16[8,528,128]{2,1,0:T(8,128)(2,1)} %bucket_rows.1), calls=%async_computation.1 | async-start | bytes 2162688 | tf_op jit(solution)/shard_map/all_to_all | solution.py:744
  31.6 0.8 permute_rows.4.x0_ref
  32.4 0.1 collective-permute-start.2
  32.5 0.6 collective-permute-done.1.x1_ref
  33.1 0.0 collective-permute-start.3
  33.1 1.5 %collective-permute-start = (bf16[1024,128]{1,0:T(8,128)(2,1)S(1)}, bf16[1024,128]{1,0:T(8,128)(2,1)S(1)}, u32[]{:S(2)}, u32[]{:S(2)}) collective-permute-start(bf16[1024,128]{1,0:T(8,128)(2,1)S(1)} %permute_rows.4.x0_ref), channel_id=1, source_target_pairs={{0,2},{1,3},{2,0},{3,1},{4,6},{5,7},{6,4},{7,5},{8,10},{9,11},{10,... | collective-permute-start | bytes 786440 | tf_op jit(solution)/shard_map/ppermute | solution.py:741
  34.6 0.2 collective-permute-start.4
  34.8 0.0 collective-permute-done.2.x2_ref
  34.8 0.0 collective-permute-done.3.x3_ref
  34.8 0.0 copy-done
  34.8 2.5 %project.2 = (bf16[1024,512]{1,0:T(8,128)(2,1)}, f32[128,1024]{1,0:T(8,128)}, f32[8,1024]{1,0:T(8,128)}, bf16[1024,128]{1,0:T(8,128)(2,1)S(1)}, bf16[128,1024]{1...) custom-call(s32[1]{0:T(128)} %bitcast.column_ref.refs_0_, ...), custom_call_target="tpu_custom_call" | custom-call | flops 805306368 | bytes 5242880 | tf_op jit(solution)/shard_map/project/pallas_call | solution.py:278
  37.4 21.1 %attention_forward.2 = (bf16[8,1024,1024]{2,1,0:T(8,128)(2,1)}, bf16[128,1024]{1,0:T(8,128)(2,1)}, f32[8,1,1024]{2,1,0:T(1,128)S(1)}, bf16[8,256,1024]{2,1,0:T(8,128)(2,1)}) custom-call(bf16[1024,128]{1,0:T(8,128)(2,1)S(1)} %get-tuple-element.97.key_ref, bf16[128,1024]{1,0:T(8,128)(2,1)S(1)} %get-tuple-element.98.base2_t_ref, ...), custom_call_target="tpu_custom_call" | custom-call | flops 11408506880 | bytes 16777216 | tf_op jit(solution)/shard_map/attention_forward/pallas_call | solution.py:377
  58.5 0.0 copy-done.11
  58.5 0.0 collective-permute-done.x1_ref
  58.5 0.3 collective-permute-start.5
  58.9 0.0 collective-permute-done.4.x2_ref
  58.9 1.2 collective-permute-done.5.x3_ref
  60.1 2.6 %project.3 = (bf16[1024,512]{1,0:T(8,128)(2,1)}, f32[128,1024]{1,0:T(8,128)}, f32[8,1024]{1,0:T(8,128)}, bf16[1024,128]{1,0:T(8,128)(2,1)}, bf16[128,1024]{1,0:T...) custom-call(s32[1]{0:T(128)} %bitcast.column_ref.refs_0_, ...), custom_call_target="tpu_custom_call" | custom-call | flops 805306368 | bytes 5242880 | tf_op jit(solution)/shard_map/project/pallas_call | solution.py:278
  62.7 0.0 all-to-all-done.1
  62.8 2.6 %segment_rows.1.refs_6_.d_out_ref = bf16[128,2048]{1,0:T(8,128)(2,1)S(1)} custom-call(bf16[8,528,128]{2,1,0:T(8,128)(2,1)S(1)} %all-to-all-done.1), custom_call_target="tpu_custom_call" | custom-call | flops 8858370048 | bytes 3244032 | tf_op jit(solution)/shard_map/segment_rows/pallas_call | solution.py:216
  65.4 0.0 copy-start.15
  65.4 1.3 collective-permute-start.6
  66.7 0.0 collective-permute-start.7
  66.7 0.0 copy-done.14
  66.8 0.0 copy-done.18
  66.8 0.0 copy-done.19
  66.8 19.7 %attention_forward.3 = (bf16[8,1024,1024]{2,1,0:T(8,128)(2,1)S(1)}, bf16[128,1024]{1,0:T(8,128)(2,1)S(1)}, f32[8,1,1024]{2,1,0:T(1,128)S(1)}, bf16[8,256,1024]{2,1,0:T(8,128)(2,1)S(1)}) custom-call(bf16[1024,128]{1,0:T(8,128)(2,1)S(1)} %copy-done.18, bf16[128,1024]{1,0:T(8,128)(2,1)S(1)} %copy-done.19, bf16[128,1024]{1,0:T(8,128)(2,1)S(1)} %copy-done.1, ...), custom_call_target="tpu_custom_call" | custom-call | flops 11408506880 | bytes 16777216 | tf_op jit(solution)/shard_map/attention_forward/pallas_call | solution.py:377
  86.4 0.0 collective-permute-done.6.refs_7_
  86.4 0.6 collective-permute-start.8
  87.0 0.0 collective-permute-done.7.refs_8_
  87.0 1.5 %collective-permute-done.8.refs_9_ = bf16[128,2048]{1,0:T(8,128)(2,1)S(1)} collective-permute-done((bf16[128,2048]{1,0:T(8,128)(2,1)S(1)}, bf16[128,2048]{1,0:T(8,128)(2,1)S(1)}, u32[]{:S(2)}, u32[]{:S(2)}) %collective-permute-start.8) | collective-permute-done | bytes 524320 | tf_op jit(solution)/shard_map/ppermute | solution.py:741
  88.5 8.2 %attention_backward.2 = (bf16[512,1024]{1,0:T(8,128)(2,1)S(1)}, bf16[128,1024]{1,0:T(8,128)(2,1)S(1)}, bf16[128,1024]{1,0:T(8,128)(2,1)S(1)}, bf16[128,1024]{1,0:T(8,128)(2,1)S(1)}, bf16[1,1024,1024]{2,1,0:T(8,128)(2,1)S(1)}) custom-call(s32[1]{0:T(128)} %bitcast.column_ref.refs_0_, bf16[8,1024,1024]{2,1,0:T(8,128)(2,1)S(1)} %get-tuple-element.136.refs_1_, ...), custom_call_target="tpu_custom_call" | custom-call | flops 9227468800 | bytes 16777216 | tf_op jit(solution)/shard_map/attention_backward/pallas_call | solution.py:540
  96.7 0.0 copy-start.7
  96.8 1.0 hidden_part.2
  97.8 0.4 collective-permute-start.9
  98.2 0.8 weight_grads.2.refs_6_
  99.1 0.7 collective-permute-done.9.got_ref
  99.8 0.1 pair_sum.2
  99.9 0.8 collective-permute-start.10
  100.8 0.0 copy-done.12
  100.8 9.9 %attention_backward.3 = (bf16[512,1024]{1,0:T(8,128)(2,1)S(1)}, bf16[128,1024]{1,0:T(8,128)(2,1)S(1)}, bf16[128,1024]{1,0:T(8,128)(2,1)S(1)}, bf16[128,1024]{1,0:T(8,128)(2,1)S(1)}) custom-call(s32[1]{0:T(128)} %bitcast.column_ref.refs_0_, bf16[1,1024,1024]{2,1,0:T(8,128)(2,1)S(1)} %get-tuple-element.153.refs_1_, ...), custom_call_target="tpu_custom_call" | custom-call | flops 9227468800 | bytes 16777216 | tf_op jit(solution)/shard_map/attention_backward/pallas_call | solution.py:540
  110.7 0.0 copy-start.3
  110.7 0.0 collective-permute-done.10.got_ref
  110.7 0.0 copy-done.6
  110.7 1.7 %weight_grads.3 = bf16[512,512]{1,0:T(8,128)(2,1)} custom-call(bf16[128,1024]{1,0:T(8,128)(2,1)S(1)} %get-tuple-element.165.refs_0_.d_query_ref, bf16[128,1024]{1,0:T(8,128)(2,1)S(1)} %get-tuple-element.166.refs_1_.d_key_ref, bf16[128,1024]{1,0:T(8,128)(2,1)S(1)} %get-tuple-element.167.refs_2_.d_value_ref, bf16[128,1024]{1,0:T(8,128)(2,1)S(1)} %copy-done.13, ...), custom_call_target="tpu_custom_call" | custom-call | flops 536870912 | bytes 6291456 | tf_op jit(solution)/shard_map/weight_grads/pallas_call | solution.py:577
  112.5 0.0 copy-done.5
  112.5 5.5 %all-to-all-start.2 = ((bf16[8,64,512]{2,1,0:T(8,128)(2,1)}), bf16[8,64,512]{2,1,0:T(8,128)(2,1)S(1)}, u32[]{:S(2)}, u32[]{:S(2)}) async-start(bf16[8,64,512]{2,1,0:T(8,128)(2,1)} %bitcast.10), calls=%async_computation.2 | async-start | bytes 1048576 | tf_op jit(solution)/shard_map/all_to_all | solution.py:744
  117.9 2.4 %hidden_part.3 = (bf16[256,1024]{1,0:T(8,128)(2,1)S(1)}, bf16[272,1024]{1,0:T(8,128)(2,1)S(1)}, f32[2,1024]{1,0:T(2,128)S(1)}) custom-call(s32[1]{0:T(128)} %bitcast.column_ref.refs_0_, bf16[128,1024]{1,0:T(8,128)(2,1)} %copy-done.3, bf16[128,1024]{1,0:T(8,128)(2,1)} %copy-done.4, bf16[128,1024]{1,0:T(8,128)(2,1)} %copy-done.5, bf16[128,1024]{1,0:T(8,128)(2,1)} %copy-done.9, ...), custom_call_target="tpu_custom_call" | custom-call | flops 402653184 | bytes 2097152 | tf_op jit(solution)/shard_map/hidden_part/pallas_call | solution.py:633
  120.3 0.0 copy-start.16
  120.3 0.1 collective-permute-start.11
  120.4 1.9 %collective-permute-done.11.got_ref = bf16[272,1024]{1,0:T(8,128)(2,1)S(1)} collective-permute-done((bf16[272,1024]{1,0:T(8,128)(2,1)S(1)}, bf16[272,1024]{1,0:T(8,128)(2,1)S(1)}, u32[]{:S(2)}, u32[]{:S(2)}) %collective-permute-start.11) | collective-permute-done | bytes 557088 | tf_op jit(solution)/shard_map/ppermute | solution.py:741
  122.3 0.1 pair_sum.3
  122.5 1.0 collective-permute-start.12
  123.5 2.1 %points_grad.2.rest_0_ = f32[2048,128]{1,0:T(8,128)} custom-call(f32[128,1024]{1,0:T(8,128)S(1)} %get-tuple-element.179.kept_ref, f32[2,1024]{1,0:T(2,128)S(1)} %get-tuple-element.180.sums_ref, bf16[144,1024]{1,0:T(8,128)(2,1)S(1)} %collective-permute-done.10.got_ref, bf16[128,2048]{1,0:T(8,128)(2,1)S(1)} %segment_rows.1.refs_6_.d_out_ref, ...), custom_call_target="tpu_custom_call" | custom-call | flops 1048576 | bytes 3145728 | tf_op jit(solution)/shard_map/points_grad/pallas_call | solution.py:687
  125.6 6.0 %collective-permute-done.12.got_ref = bf16[144,1024]{1,0:T(8,128)(2,1)S(1)} collective-permute-done((bf16[144,1024]{1,0:T(8,128)(2,1)S(1)}, bf16[144,1024]{1,0:T(8,128)(2,1)S(1)}, u32[]{:S(2)}, u32[]{:S(2)}) %collective-permute-start.12) | collective-permute-done | bytes 294944 | tf_op jit(solution)/shard_map/ppermute | solution.py:741
  131.6 1.0 points_grad.3
  132.6 0.1 all-to-all-done.2.parts_ref
  132.6 0.7 grad_sum.1
  (28 shorter events, 0.1 us)
Async XLA Ops:
  3.8 21.7 %all-to-all-start = ((bf16[8,256,128]{2,1,0:T(8,128)(2,1)}), bf16[8,256,128]{2,1,0:T(8,128)(2,1)S(1)}, u32[]{:S(2)}, u32[]{:S(2)}) async-start(bf16[8,256,128]{2,1,0:T(8,128)(2,1)} %bitcast.20), calls=%async_computation | async-start | bytes 1048576 | tf_op jit(solution)/shard_map/all_to_all | solution.py:744
  11.1 14.5 %copy-start.17 = (s32[2048]{0:T(1024)S(1)}, s32[2048]{0:T(1024)}, u32[]{:S(2)}) copy-start(s32[2048]{0:T(1024)} %param.10) | copy-start | bytes 24580
  22.5 12.3 %copy-start = (bf16[512,3,128]{2,0,1:T(8,128)(2,1)S(1)}, bf16[512,3,128]{2,0,1:T(8,128)(2,1)}, u32[]{:S(2)}) copy-start(bf16[512,3,128]{2,0,1:T(8,128)(2,1)} %param.11) | copy-start | bytes 1179652
  26.3 6.8 %collective-permute-start.1 = (bf16[1024,128]{1,0:T(8,128)(2,1)S(1)}, bf16[1024,128]{1,0:T(8,128)(2,1)S(1)}, u32[]{:S(2)}, u32[]{:S(2)}) collective-permute-start(bf16[1024,128]{1,0:T(8,128)(2,1)S(1)} %permute_rows.5.x0_ref), channel_id=1, source_target_pairs={{0,2},{1,3},{2,0},{3,1},{4,6},{5,7},{6,4},{7,5},{8,10},{9,11},{10,... | collective-permute-start | bytes 786440 | tf_op jit(solution)/shard_map/ppermute | solution.py:741
  27.9 34.8 %all-to-all-start.1 = ((bf16[8,528,128]{2,1,0:T(8,128)(2,1)}), bf16[8,528,128]{2,1,0:T(8,128)(2,1)S(1)}, u32[]{:S(2)}, u32[]{:S(2)}) async-start(bf16[8,528,128]{2,1,0:T(8,128)(2,1)} %bucket_rows.1), calls=%async_computation.1 | async-start | bytes 2162688 | tf_op jit(solution)/shard_map/all_to_all | solution.py:744
  32.4 2.4 %collective-permute-start.2 = (bf16[1024,128]{1,0:T(8,128)(2,1)S(1)}, bf16[1024,128]{1,0:T(8,128)(2,1)S(1)}, u32[]{:S(2)}, u32[]{:S(2)}) collective-permute-start(bf16[1024,128]{1,0:T(8,128)(2,1)S(1)} %permute_rows.5.x0_ref), channel_id=1, source_target_pairs={{0,1},{1,0},{2,3},{3,2},{4,5},{5,4},{6,7},{7,6},{8,9},{9,8},{10,11... | collective-permute-start | bytes 786440 | tf_op jit(solution)/shard_map/ppermute | solution.py:741
  33.1 1.8 %collective-permute-start.3 = (bf16[1024,128]{1,0:T(8,128)(2,1)S(1)}, bf16[1024,128]{1,0:T(8,128)(2,1)S(1)}, u32[]{:S(2)}, u32[]{:S(2)}) collective-permute-start(bf16[1024,128]{1,0:T(8,128)(2,1)S(1)} %collective-permute-done.1.x1_ref), channel_id=1, source_target_pairs={{0,1},{1,0},{2,3},{3,2},{4,5},{5,4},{6,7},{7,6},{8,9},{9,8},{10,11... | collective-permute-start | bytes 786440 | tf_op jit(solution)/shard_map/ppermute | solution.py:741
  33.1 25.4 %collective-permute-start = (bf16[1024,128]{1,0:T(8,128)(2,1)S(1)}, bf16[1024,128]{1,0:T(8,128)(2,1)S(1)}, u32[]{:S(2)}, u32[]{:S(2)}) collective-permute-start(bf16[1024,128]{1,0:T(8,128)(2,1)S(1)} %permute_rows.4.x0_ref), channel_id=1, source_target_pairs={{0,2},{1,3},{2,0},{3,1},{4,6},{5,7},{6,4},{7,5},{8,10},{9,11},{10,... | collective-permute-start | bytes 786440 | tf_op jit(solution)/shard_map/ppermute | solution.py:741
  34.6 24.3 %collective-permute-start.4 = (bf16[1024,128]{1,0:T(8,128)(2,1)S(1)}, bf16[1024,128]{1,0:T(8,128)(2,1)S(1)}, u32[]{:S(2)}, u32[]{:S(2)}) collective-permute-start(bf16[1024,128]{1,0:T(8,128)(2,1)S(1)} %permute_rows.4.x0_ref), channel_id=1, source_target_pairs={{0,1},{1,0},{2,3},{3,2},{4,5},{5,4},{6,7},{7,6},{8,9},{9,8},{10,11... | collective-permute-start | bytes 786440 | tf_op jit(solution)/shard_map/ppermute | solution.py:741
  37.4 21.1 %copy-start.10 = (bf16[128,1024]{1,0:T(8,128)(2,1)}, bf16[128,1024]{1,0:T(8,128)(2,1)S(1)}, u32[]{:S(2)}) copy-start(bf16[128,1024]{1,0:T(8,128)(2,1)S(1)} %get-tuple-element.169.key_t_ref.key_ref) | copy-start | bytes 786436
  37.4 21.1 %copy-start.11 = (bf16[128,1024]{1,0:T(8,128)(2,1)}, bf16[128,1024]{1,0:T(8,128)(2,1)S(1)}, u32[]{:S(2)}) copy-start(bf16[128,1024]{1,0:T(8,128)(2,1)S(1)} %get-tuple-element.170.value_t_ref.refs_4_.value_ref) | copy-start | bytes 786436
  37.4 63.4 %copy-start.9 = (bf16[128,1024]{1,0:T(8,128)(2,1)}, bf16[128,1024]{1,0:T(8,128)(2,1)S(1)}, u32[]{:S(2)}) copy-start(bf16[128,1024]{1,0:T(8,128)(2,1)S(1)} %get-tuple-element.168.query_t_ref.refs_3_.query_ref) | copy-start | bytes 786436
  58.5 1.6 %collective-permute-start.5 = (bf16[1024,128]{1,0:T(8,128)(2,1)S(1)}, bf16[1024,128]{1,0:T(8,128)(2,1)S(1)}, u32[]{:S(2)}, u32[]{:S(2)}) collective-permute-start(bf16[1024,128]{1,0:T(8,128)(2,1)S(1)} %collective-permute-done.x1_ref), channel_id=1, source_target_pairs={{0,1},{1,0},{2,3},{3,2},{4,5},{5,4},{6,7},{7,6},{8,9},{9,8},{10,11... | collective-permute-start | bytes 786440 | tf_op jit(solution)/shard_map/ppermute | solution.py:741
  62.7 4.0 %copy-start.1 = (bf16[128,1024]{1,0:T(8,128)(2,1)S(1)}, bf16[128,1024]{1,0:T(8,128)(2,1)}, u32[]{:S(2)}) copy-start(bf16[128,1024]{1,0:T(8,128)(2,1)} %get-tuple-element.129.query_t_ref.refs_3_.query_ref) | copy-start | bytes 786436
  62.7 4.0 %copy-start.2 = (bf16[128,1024]{1,0:T(8,128)(2,1)S(1)}, bf16[128,1024]{1,0:T(8,128)(2,1)}, u32[]{:S(2)}) copy-start(bf16[128,1024]{1,0:T(8,128)(2,1)} %get-tuple-element.131.value_t_ref.refs_4_.value_ref) | copy-start | bytes 786436
  62.7 4.0 %copy-start.14 = (bf16[128,1024]{1,0:T(8,128)(2,1)S(1)}, bf16[128,1024]{1,0:T(8,128)(2,1)}, u32[]{:S(2)}) copy-start(bf16[128,1024]{1,0:T(8,128)(2,1)} %get-tuple-element.130.key_t_ref.key_ref) | copy-start | bytes 786436
  62.8 4.0 %copy-start.18 = (bf16[1024,128]{1,0:T(8,128)(2,1)S(1)}, bf16[1024,128]{1,0:T(8,128)(2,1)}, u32[]{:S(2)}) copy-start(bf16[1024,128]{1,0:T(8,128)(2,1)} %get-tuple-element.127.key_ref) | copy-start | bytes 786436
  62.8 4.0 %copy-start.19 = (bf16[128,1024]{1,0:T(8,128)(2,1)S(1)}, bf16[128,1024]{1,0:T(8,128)(2,1)}, u32[]{:S(2)}) copy-start(bf16[128,1024]{1,0:T(8,128)(2,1)} %get-tuple-element.128.base2_t_ref) | copy-start | bytes 786436
  65.4 23.2 %copy-start.15 = (bf16[512,128]{1,0:T(8,128)(2,1)S(1)}, bf16[512,128]{1,0:T(8,128)(2,1)}, u32[]{:S(2)}) copy-start(bf16[512,128]{1,0:T(8,128)(2,1)} %refs_10_.3) | copy-start | bytes 393220
  65.4 21.0 %collective-permute-start.6 = (bf16[128,2048]{1,0:T(8,128)(2,1)S(1)}, bf16[128,2048]{1,0:T(8,128)(2,1)S(1)}, u32[]{:S(2)}, u32[]{:S(2)}) collective-permute-start(bf16[128,2048]{1,0:T(8,128)(2,1)S(1)} %segment_rows.1.refs_6_.d_out_ref), channel_id=1, source_target_pairs={{0,2},{1,3},{2,0},{3,1},{4,6},{5,7},{6,4},{7,5},{8,10},{9,11},{10,... | collective-permute-start | bytes 1572872 | tf_op jit(solution)/shard_map/ppermute | solution.py:741
  66.7 20.3 %collective-permute-start.7 = (bf16[128,2048]{1,0:T(8,128)(2,1)S(1)}, bf16[128,2048]{1,0:T(8,128)(2,1)S(1)}, u32[]{:S(2)}, u32[]{:S(2)}) collective-permute-start(bf16[128,2048]{1,0:T(8,128)(2,1)S(1)} %segment_rows.1.refs_6_.d_out_ref), channel_id=1, source_target_pairs={{0,1},{1,0},{2,3},{3,2},{4,5},{5,4},{6,7},{7,6},{8,9},{9,8},{10,11... | collective-permute-start | bytes 1572872 | tf_op jit(solution)/shard_map/ppermute | solution.py:741
  86.4 2.1 %collective-permute-start.8 = (bf16[128,2048]{1,0:T(8,128)(2,1)S(1)}, bf16[128,2048]{1,0:T(8,128)(2,1)S(1)}, u32[]{:S(2)}, u32[]{:S(2)}) collective-permute-start(bf16[128,2048]{1,0:T(8,128)(2,1)S(1)} %collective-permute-done.6.refs_7_), channel_id=1, source_target_pairs={{0,1},{1,0},{2,3},{3,2},{4,5},{5,4},{6,7},{7,6},{8,9},{9,8},{10,11... | collective-permute-start | bytes 1572872 | tf_op jit(solution)/shard_map/ppermute | solution.py:741
  96.7 1.5 %copy-start.7 = (bf16[1024,512]{1,0:T(8,128)(2,1)S(1)}, bf16[1024,512]{1,0:T(8,128)(2,1)}, u32[]{:S(2)}) copy-start(bf16[1024,512]{1,0:T(8,128)(2,1)} %get-tuple-element.148.refs_4_) | copy-start | bytes 3145732
  97.8 2.0 %collective-permute-start.9 = (bf16[272,1024]{1,0:T(8,128)(2,1)S(1)}, bf16[272,1024]{1,0:T(8,128)(2,1)S(1)}, u32[]{:S(2)}, u32[]{:S(2)}) collective-permute-start(bf16[272,1024]{1,0:T(8,128)(2,1)S(1)} %get-tuple-element.147), channel_id=1, source_target_pairs={{0,1},{1,0},{2,3},{3,2},{4,5},{5,4},{6,7},{7,6},{8,9},{9,8},{10,11... | collective-permute-start | bytes 1671176 | tf_op jit(solution)/shard_map/ppermute | solution.py:741
  98.2 2.6 %copy-start.12 = (bf16[128,1024]{1,0:T(8,128)(2,1)S(1)}, bf16[128,1024]{1,0:T(8,128)(2,1)}, u32[]{:S(2)}) copy-start(bf16[128,1024]{1,0:T(8,128)(2,1)} %copy-done.11) | copy-start | bytes 786436
  98.2 2.6 %copy-start.13 = (bf16[128,1024]{1,0:T(8,128)(2,1)S(1)}, bf16[128,1024]{1,0:T(8,128)(2,1)}, u32[]{:S(2)}) copy-start(bf16[128,1024]{1,0:T(8,128)(2,1)} %get-tuple-element.155.refs_5_.refs_3_) | copy-start | bytes 786436
  99.9 10.8 %collective-permute-start.10 = (bf16[144,1024]{1,0:T(8,128)(2,1)S(1)}, bf16[144,1024]{1,0:T(8,128)(2,1)S(1)}, u32[]{:S(2)}, u32[]{:S(2)}) collective-permute-start(bf16[144,1024]{1,0:T(8,128)(2,1)S(1)} %get-tuple-element.152), channel_id=1, source_target_pairs={{0,2},{1,3},{2,0},{3,1},{4,6},{5,7},{6,4},{7,5},{8,10},{9,11},{10,... | collective-permute-start | bytes 884744 | tf_op jit(solution)/shard_map/ppermute | solution.py:741
  100.8 9.9 %copy-start.6 = (bf16[1024,512]{1,0:T(8,128)(2,1)S(1)}, bf16[1024,512]{1,0:T(8,128)(2,1)}, u32[]{:S(2)}) copy-start(bf16[1024,512]{1,0:T(8,128)(2,1)} %get-tuple-element.162.refs_4_) | copy-start | bytes 3145732
  110.7 1.8 %copy-start.3 = (bf16[128,1024]{1,0:T(8,128)(2,1)}, bf16[128,1024]{1,0:T(8,128)(2,1)S(1)}, u32[]{:S(2)}) copy-start(bf16[128,1024]{1,0:T(8,128)(2,1)S(1)} %get-tuple-element.165.refs_0_.d_query_ref) | copy-start | bytes 786436
  110.7 1.8 %copy-start.4 = (bf16[128,1024]{1,0:T(8,128)(2,1)}, bf16[128,1024]{1,0:T(8,128)(2,1)S(1)}, u32[]{:S(2)}) copy-start(bf16[128,1024]{1,0:T(8,128)(2,1)S(1)} %get-tuple-element.166.refs_1_.d_key_ref) | copy-start | bytes 786436
  110.7 1.8 %copy-start.5 = (bf16[128,1024]{1,0:T(8,128)(2,1)}, bf16[128,1024]{1,0:T(8,128)(2,1)S(1)}, u32[]{:S(2)}) copy-start(bf16[128,1024]{1,0:T(8,128)(2,1)S(1)} %get-tuple-element.167.refs_2_.d_value_ref) | copy-start | bytes 786436
  112.5 20.2 %all-to-all-start.2 = ((bf16[8,64,512]{2,1,0:T(8,128)(2,1)}), bf16[8,64,512]{2,1,0:T(8,128)(2,1)S(1)}, u32[]{:S(2)}, u32[]{:S(2)}) async-start(bf16[8,64,512]{2,1,0:T(8,128)(2,1)} %bitcast.10), calls=%async_computation.2 | async-start | bytes 1048576 | tf_op jit(solution)/shard_map/all_to_all | solution.py:744
  120.3 11.3 %copy-start.8 = (f32[128,1024]{1,0:T(8,128)S(1)}, f32[128,1024]{1,0:T(8,128)}, u32[]{:S(2)}) copy-start(f32[128,1024]{1,0:T(8,128)} %get-tuple-element.177.normed_ref) | copy-start | bytes 1572868
  120.3 11.3 %copy-start.16 = (f32[8,1024]{1,0:T(8,128)S(1)}, f32[8,1024]{1,0:T(8,128)}, u32[]{:S(2)}) copy-start(f32[8,1024]{1,0:T(8,128)} %get-tuple-element.178.inv_ref) | copy-start | bytes 98308
  120.3 2.0 %collective-permute-start.11 = (bf16[272,1024]{1,0:T(8,128)(2,1)S(1)}, bf16[272,1024]{1,0:T(8,128)(2,1)S(1)}, u32[]{:S(2)}, u32[]{:S(2)}) collective-permute-start(bf16[272,1024]{1,0:T(8,128)(2,1)S(1)} %get-tuple-element.173), channel_id=1, source_target_pairs={{0,1},{1,0},{2,3},{3,2},{4,5},{5,4},{6,7},{7,6},{8,9},{9,8},{10,11... | collective-permute-start | bytes 1671176 | tf_op jit(solution)/shard_map/ppermute | solution.py:741
  122.5 9.1 %collective-permute-start.12 = (bf16[144,1024]{1,0:T(8,128)(2,1)S(1)}, bf16[144,1024]{1,0:T(8,128)(2,1)S(1)}, u32[]{:S(2)}, u32[]{:S(2)}) collective-permute-start(bf16[144,1024]{1,0:T(8,128)(2,1)S(1)} %get-tuple-element.176), channel_id=1, source_target_pairs={{0,2},{1,3},{2,0},{3,1},{4,6},{5,7},{6,4},{7,5},{8,10},{9,11},{10,... | collective-permute-start | bytes 884744 | tf_op jit(solution)/shard_map/ppermute | solution.py:741

commit v10 on v9

--- a/solution.py
+++ b/solution.py
@@ -17,7 +17,7 @@
 QUERY_BLOCK = 256
 STAGED_HEADS = 1
 SEGMENT_SHARDS = 8
-BUCKET_SHARDS = 2
+BUCKET_SHARDS = 4
 
 score_scale = 0.25
 epsilon = 1e-05

time: 134 us -> 134 us (level)
  no operation moved by 1% of the time
where the time goes in v10:
time: 134 us; the launch traced here: 133 us
  Pallas kernels  92.6 us (69%)
  starting transfers between devices  24.5 us (18%)
  waiting for transfers between devices  15.3 us (11%)
    pallas_call x2, Pallas kernels, attention_forward(): pl.pallas_call(forward_body, grid=(heads,), in_specs=[pl.BlockSpec((PATCH...  40.8 us
    pallas_call x2, Pallas kernels, attention_backward(): pl.pallas_call(functools.partial(backward_body, first), grid_spec=pltpu.P...  18 us
    all_to_all x3, starting transfers between devices, exchange(): return lax.all_to_all(rows, 'seq', split_axis=0, concat_axis=0, tiled=True)  16.4 us
    ppermute x13, waiting for transfers between devices, swap(): return lax.ppermute(rows, 'mp', [(i, i ^ mask) for i in range(members)])  12.1 us
    pallas_call x1, Pallas kernels, bucket_rows(): pl.pallas_call(functools.partial(bucket_body, shards, capacity), grid_spe...  11.3 us
    ppermute x13, starting transfers between devices, swap(): return lax.ppermute(rows, 'mp', [(i, i ^ mask) for i in range(members)])  8.04 us
    pallas_call x2, Pallas kernels, project(): pl.pallas_call(project_body, grid_spec=pltpu.PrefetchScalarGridSpec(num_s...  5.12 us
    pallas_call x3, Pallas kernels, permute_rows(): pl.pallas_call(permute_body, grid_spec=pltpu.PrefetchScalarGridSpec(num_s...  4.68 us
  transfers between devices with their start and end apart: 16, of which 8 were waited for; matrix products, arithmetic and copies ran while one was open for 0% of the time, Pallas kernels for 56%

profile of v10, /device:TPU:0, one launch (start us, length us, event | category | flops | bytes accessed | tf_op | source)
XLA Modules:
  0.0 133.3 jit_solution(6630751491069957783)
XLA Ops:
  0.6 3.2 %permute_rows.3 = bf16[2048,128]{1,0:T(8,128)(2,1)} custom-call(s32[1]{0:T(128)} %bitcast.column_ref.refs_0_, s32[16,128]{1,0:T(8,128)} %bitcast.21, bf16[2048,512]{1,0:T(8,128)(2,1)} %block_ref.1), custom_call_target="tpu_custom_call" | custom-call | flops 524288 | bytes 2048 | tf_op jit(solution)/shard_map/permute_rows/pallas_call | solution.py:83
  3.8 7.3 %all-to-all-start = ((bf16[8,256,128]{2,1,0:T(8,128)(2,1)}), bf16[8,256,128]{2,1,0:T(8,128)(2,1)S(1)}, u32[]{:S(2)}, u32[]{:S(2)}) async-start(bf16[8,256,128]{2,1,0:T(8,128)(2,1)} %bitcast.20), calls=%async_computation | async-start | bytes 1048576 | tf_op jit(solution)/shard_map/all_to_all | solution.py:744
  11.1 11.3 %bucket_rows.1 = bf16[8,528,128]{2,1,0:T(8,128)(2,1)} custom-call(s32[1]{0:T(128)} %bitcast.column_ref.refs_0_, s32[16,128]{1,0:T(8,128)} %bitcast.23, s32[16,128]{1,0:T(8,128)} %bitcast.24, bf16[2048,512]{1,0:T(8,128)(2,1)} %grads_ref.1), custom_call_target="tpu_custom_call" | custom-call | flops 8589934592 | bytes 3145728 | tf_op jit(solution)/shard_map/bucket_rows/pallas_call | solution.py:157
  22.4 3.1 %all-to-all-done = bf16[8,256,128]{2,1,0:T(8,128)(2,1)S(1)} async-done(((bf16[8,256,128]{2,1,0:T(8,128)(2,1)}), bf16[8,256,128]{2,1,0:T(8,128)(2,1)S(1)}, u32[]{:S(2)}, u32[]{:S(2)}) %all-to-all-start) | async-done | bytes 524320 | tf_op jit(solution)/shard_map/all_to_all | solution.py:744
  25.5 0.8 permute_rows.5.x0_ref
  26.3 1.6 %collective-permute-start.1 = (bf16[1024,128]{1,0:T(8,128)(2,1)S(1)}, bf16[1024,128]{1,0:T(8,128)(2,1)S(1)}, u32[]{:S(2)}, u32[]{:S(2)}) collective-permute-start(bf16[1024,128]{1,0:T(8,128)(2,1)S(1)} %permute_rows.5.x0_ref), channel_id=1, source_target_pairs={{0,2},{1,3},{2,0},{3,1},{4,6},{5,7},{6,4},{7,5},{8,10},{9,11},{10,... | collective-permute-start | bytes 786440 | tf_op jit(solution)/shard_map/ppermute | solution.py:741
  27.9 3.7 %all-to-all-start.1 = ((bf16[8,528,128]{2,1,0:T(8,128)(2,1)}), bf16[8,528,128]{2,1,0:T(8,128)(2,1)S(1)}, u32[]{:S(2)}, u32[]{:S(2)}) async-start(bf16[8,528,128]{2,1,0:T(8,128)(2,1)} %bucket_rows.1), calls=%async_computation.1 | async-start | bytes 2162688 | tf_op jit(solution)/shard_map/all_to_all | solution.py:744
  31.6 0.8 permute_rows.4.x0_ref
  32.4 0.1 collective-permute-start.2
  32.5 0.6 collective-permute-done.1.x1_ref
  33.1 0.0 collective-permute-start.3
  33.1 1.5 %collective-permute-start = (bf16[1024,128]{1,0:T(8,128)(2,1)S(1)}, bf16[1024,128]{1,0:T(8,128)(2,1)S(1)}, u32[]{:S(2)}, u32[]{:S(2)}) collective-permute-start(bf16[1024,128]{1,0:T(8,128)(2,1)S(1)} %permute_rows.4.x0_ref), channel_id=1, source_target_pairs={{0,2},{1,3},{2,0},{3,1},{4,6},{5,7},{6,4},{7,5},{8,10},{9,11},{10,... | collective-permute-start | bytes 786440 | tf_op jit(solution)/shard_map/ppermute | solution.py:741
  34.6 0.2 collective-permute-start.4
  34.8 0.0 collective-permute-done.2.x2_ref
  34.8 0.0 collective-permute-done.3.x3_ref
  34.8 0.0 copy-done
  34.8 2.5 %project.2 = (bf16[1024,512]{1,0:T(8,128)(2,1)}, f32[128,1024]{1,0:T(8,128)}, f32[8,1024]{1,0:T(8,128)}, bf16[1024,128]{1,0:T(8,128)(2,1)S(1)}, bf16[128,1024]{1...) custom-call(s32[1]{0:T(128)} %bitcast.column_ref.refs_0_, ...), custom_call_target="tpu_custom_call" | custom-call | flops 805306368 | bytes 5242880 | tf_op jit(solution)/shard_map/project/pallas_call | solution.py:278
  37.4 21.1 %attention_forward.2 = (bf16[8,1024,1024]{2,1,0:T(8,128)(2,1)}, bf16[128,1024]{1,0:T(8,128)(2,1)}, f32[8,1,1024]{2,1,0:T(1,128)S(1)}, bf16[8,256,1024]{2,1,0:T(8,128)(2,1)}) custom-call(bf16[1024,128]{1,0:T(8,128)(2,1)S(1)} %get-tuple-element.97.key_ref, bf16[128,1024]{1,0:T(8,128)(2,1)S(1)} %get-tuple-element.98.base2_t_ref, ...), custom_call_target="tpu_custom_call" | custom-call | flops 11408506880 | bytes 16777216 | tf_op jit(solution)/shard_map/attention_forward/pallas_call | solution.py:377
  58.5 0.0 copy-done.11
  58.5 0.0 collective-permute-done.x1_ref
  58.5 0.3 collective-permute-start.5
  58.9 0.0 collective-permute-done.4.x2_ref
  58.9 1.2 collective-permute-done.5.x3_ref
  60.1 2.6 %project.3 = (bf16[1024,512]{1,0:T(8,128)(2,1)}, f32[128,1024]{1,0:T(8,128)}, f32[8,1024]{1,0:T(8,128)}, bf16[1024,128]{1,0:T(8,128)(2,1)}, bf16[128,1024]{1,0:T...) custom-call(s32[1]{0:T(128)} %bitcast.column_ref.refs_0_, ...), custom_call_target="tpu_custom_call" | custom-call | flops 805306368 | bytes 5242880 | tf_op jit(solution)/shard_map/project/pallas_call | solution.py:278
  62.7 0.0 all-to-all-done.1
  62.8 2.6 %segment_rows.1.refs_6_.d_out_ref = bf16[128,2048]{1,0:T(8,128)(2,1)S(1)} custom-call(bf16[8,528,128]{2,1,0:T(8,128)(2,1)S(1)} %all-to-all-done.1), custom_call_target="tpu_custom_call" | custom-call | flops 8858370048 | bytes 3244032 | tf_op jit(solution)/shard_map/segment_rows/pallas_call | solution.py:216
  65.4 0.0 copy-start.15
  65.4 1.3 collective-permute-start.6
  66.7 0.0 collective-permute-start.7
  66.7 0.0 copy-done.14
  66.8 0.0 copy-done.18
  66.8 0.0 copy-done.19
  66.8 19.7 %attention_forward.3 = (bf16[8,1024,1024]{2,1,0:T(8,128)(2,1)S(1)}, bf16[128,1024]{1,0:T(8,128)(2,1)S(1)}, f32[8,1,1024]{2,1,0:T(1,128)S(1)}, bf16[8,256,1024]{2,1,0:T(8,128)(2,1)S(1)}) custom-call(bf16[1024,128]{1,0:T(8,128)(2,1)S(1)} %copy-done.18, bf16[128,1024]{1,0:T(8,128)(2,1)S(1)} %copy-done.19, bf16[128,1024]{1,0:T(8,128)(2,1)S(1)} %copy-done.1, ...), custom_call_target="tpu_custom_call" | custom-call | flops 11408506880 | bytes 16777216 | tf_op jit(solution)/shard_map/attention_forward/pallas_call | solution.py:377
  86.4 0.0 collective-permute-done.6.refs_7_
  86.4 0.6 collective-permute-start.8
  87.0 0.0 collective-permute-done.7.refs_8_
  87.0 1.5 %collective-permute-done.8.refs_9_ = bf16[128,2048]{1,0:T(8,128)(2,1)S(1)} collective-permute-done((bf16[128,2048]{1,0:T(8,128)(2,1)S(1)}, bf16[128,2048]{1,0:T(8,128)(2,1)S(1)}, u32[]{:S(2)}, u32[]{:S(2)}) %collective-permute-start.8) | collective-permute-done | bytes 524320 | tf_op jit(solution)/shard_map/ppermute | solution.py:741
  88.5 8.2 %attention_backward.2 = (bf16[512,1024]{1,0:T(8,128)(2,1)S(1)}, bf16[128,1024]{1,0:T(8,128)(2,1)S(1)}, bf16[128,1024]{1,0:T(8,128)(2,1)S(1)}, bf16[128,1024]{1,0:T(8,128)(2,1)S(1)}, bf16[1,1024,1024]{2,1,0:T(8,128)(2,1)S(1)}) custom-call(s32[1]{0:T(128)} %bitcast.column_ref.refs_0_, bf16[8,1024,1024]{2,1,0:T(8,128)(2,1)S(1)} %get-tuple-element.136.refs_1_, ...), custom_call_target="tpu_custom_call" | custom-call | flops 9227468800 | bytes 16777216 | tf_op jit(solution)/shard_map/attention_backward/pallas_call | solution.py:540
  96.7 0.0 copy-start.7
  96.8 1.0 hidden_part.2
  97.8 0.4 collective-permute-start.9
  98.2 0.8 weight_grads.2.refs_6_
  99.1 0.7 collective-permute-done.9.got_ref
  99.8 0.1 pair_sum.2
  99.9 0.8 collective-permute-start.10
  100.8 0.0 copy-done.12
  100.8 9.9 %attention_backward.3 = (bf16[512,1024]{1,0:T(8,128)(2,1)S(1)}, bf16[128,1024]{1,0:T(8,128)(2,1)S(1)}, bf16[128,1024]{1,0:T(8,128)(2,1)S(1)}, bf16[128,1024]{1,0:T(8,128)(2,1)S(1)}) custom-call(s32[1]{0:T(128)} %bitcast.column_ref.refs_0_, bf16[1,1024,1024]{2,1,0:T(8,128)(2,1)S(1)} %get-tuple-element.153.refs_1_, ...), custom_call_target="tpu_custom_call" | custom-call | flops 9227468800 | bytes 16777216 | tf_op jit(solution)/shard_map/attention_backward/pallas_call | solution.py:540
  110.7 0.0 copy-start.3
  110.7 0.0 collective-permute-done.10.got_ref
  110.7 0.0 copy-done.6
  110.7 1.7 %weight_grads.3 = bf16[512,512]{1,0:T(8,128)(2,1)} custom-call(bf16[128,1024]{1,0:T(8,128)(2,1)S(1)} %get-tuple-element.165.refs_0_.d_query_ref, bf16[128,1024]{1,0:T(8,128)(2,1)S(1)} %get-tuple-element.166.refs_1_.d_key_ref, bf16[128,1024]{1,0:T(8,128)(2,1)S(1)} %get-tuple-element.167.refs_2_.d_value_ref, bf16[128,1024]{1,0:T(8,128)(2,1)S(1)} %copy-done.13, ...), custom_call_target="tpu_custom_call" | custom-call | flops 536870912 | bytes 6291456 | tf_op jit(solution)/shard_map/weight_grads/pallas_call | solution.py:577
  112.5 0.0 copy-done.5
  112.5 5.5 %all-to-all-start.2 = ((bf16[8,64,512]{2,1,0:T(8,128)(2,1)}), bf16[8,64,512]{2,1,0:T(8,128)(2,1)S(1)}, u32[]{:S(2)}, u32[]{:S(2)}) async-start(bf16[8,64,512]{2,1,0:T(8,128)(2,1)} %bitcast.10), calls=%async_computation.2 | async-start | bytes 1048576 | tf_op jit(solution)/shard_map/all_to_all | solution.py:744
  117.9 2.4 %hidden_part.3 = (bf16[256,1024]{1,0:T(8,128)(2,1)S(1)}, bf16[272,1024]{1,0:T(8,128)(2,1)S(1)}, f32[2,1024]{1,0:T(2,128)S(1)}) custom-call(s32[1]{0:T(128)} %bitcast.column_ref.refs_0_, bf16[128,1024]{1,0:T(8,128)(2,1)} %copy-done.3, bf16[128,1024]{1,0:T(8,128)(2,1)} %copy-done.4, bf16[128,1024]{1,0:T(8,128)(2,1)} %copy-done.5, bf16[128,1024]{1,0:T(8,128)(2,1)} %copy-done.9, ...), custom_call_target="tpu_custom_call" | custom-call | flops 402653184 | bytes 2097152 | tf_op jit(solution)/shard_map/hidden_part/pallas_call | solution.py:633
  120.3 0.0 copy-start.16
  120.3 0.1 collective-permute-start.11
  120.4 1.9 %collective-permute-done.11.got_ref = bf16[272,1024]{1,0:T(8,128)(2,1)S(1)} collective-permute-done((bf16[272,1024]{1,0:T(8,128)(2,1)S(1)}, bf16[272,1024]{1,0:T(8,128)(2,1)S(1)}, u32[]{:S(2)}, u32[]{:S(2)}) %collective-permute-start.11) | collective-permute-done | bytes 557088 | tf_op jit(solution)/shard_map/ppermute | solution.py:741
  122.3 0.1 pair_sum.3
  122.5 1.0 collective-permute-start.12
  123.5 2.1 %points_grad.2.rest_0_ = f32[2048,128]{1,0:T(8,128)} custom-call(f32[128,1024]{1,0:T(8,128)S(1)} %get-tuple-element.179.kept_ref, f32[2,1024]{1,0:T(2,128)S(1)} %get-tuple-element.180.sums_ref, bf16[144,1024]{1,0:T(8,128)(2,1)S(1)} %collective-permute-done.10.got_ref, bf16[128,2048]{1,0:T(8,128)(2,1)S(1)} %segment_rows.1.refs_6_.d_out_ref, ...), custom_call_target="tpu_custom_call" | custom-call | flops 1048576 | bytes 3145728 | tf_op jit(solution)/shard_map/points_grad/pallas_call | solution.py:687
  125.6 6.0 %collective-permute-done.12.got_ref = bf16[144,1024]{1,0:T(8,128)(2,1)S(1)} collective-permute-done((bf16[144,1024]{1,0:T(8,128)(2,1)S(1)}, bf16[144,1024]{1,0:T(8,128)(2,1)S(1)}, u32[]{:S(2)}, u32[]{:S(2)}) %collective-permute-start.12) | collective-permute-done | bytes 294944 | tf_op jit(solution)/shard_map/ppermute | solution.py:741
  131.6 1.0 points_grad.3
  132.6 0.1 all-to-all-done.2.parts_ref
  132.6 0.7 grad_sum.1
  (28 shorter events, 0.1 us)
Async XLA Ops:
  3.8 21.7 %all-to-all-start = ((bf16[8,256,128]{2,1,0:T(8,128)(2,1)}), bf16[8,256,128]{2,1,0:T(8,128)(2,1)S(1)}, u32[]{:S(2)}, u32[]{:S(2)}) async-start(bf16[8,256,128]{2,1,0:T(8,128)(2,1)} %bitcast.20), calls=%async_computation | async-start | bytes 1048576 | tf_op jit(solution)/shard_map/all_to_all | solution.py:744
  11.1 14.5 %copy-start.17 = (s32[2048]{0:T(1024)S(1)}, s32[2048]{0:T(1024)}, u32[]{:S(2)}) copy-start(s32[2048]{0:T(1024)} %param.10) | copy-start | bytes 24580
  22.4 12.4 %copy-start = (bf16[512,3,128]{2,0,1:T(8,128)(2,1)S(1)}, bf16[512,3,128]{2,0,1:T(8,128)(2,1)}, u32[]{:S(2)}) copy-start(bf16[512,3,128]{2,0,1:T(8,128)(2,1)} %param.11) | copy-start | bytes 1179652
  26.3 6.8 %collective-permute-start.1 = (bf16[1024,128]{1,0:T(8,128)(2,1)S(1)}, bf16[1024,128]{1,0:T(8,128)(2,1)S(1)}, u32[]{:S(2)}, u32[]{:S(2)}) collective-permute-start(bf16[1024,128]{1,0:T(8,128)(2,1)S(1)} %permute_rows.5.x0_ref), channel_id=1, source_target_pairs={{0,2},{1,3},{2,0},{3,1},{4,6},{5,7},{6,4},{7,5},{8,10},{9,11},{10,... | collective-permute-start | bytes 786440 | tf_op jit(solution)/shard_map/ppermute | solution.py:741
  27.9 34.8 %all-to-all-start.1 = ((bf16[8,528,128]{2,1,0:T(8,128)(2,1)}), bf16[8,528,128]{2,1,0:T(8,128)(2,1)S(1)}, u32[]{:S(2)}, u32[]{:S(2)}) async-start(bf16[8,528,128]{2,1,0:T(8,128)(2,1)} %bucket_rows.1), calls=%async_computation.1 | async-start | bytes 2162688 | tf_op jit(solution)/shard_map/all_to_all | solution.py:744
  32.4 2.4 %collective-permute-start.2 = (bf16[1024,128]{1,0:T(8,128)(2,1)S(1)}, bf16[1024,128]{1,0:T(8,128)(2,1)S(1)}, u32[]{:S(2)}, u32[]{:S(2)}) collective-permute-start(bf16[1024,128]{1,0:T(8,128)(2,1)S(1)} %permute_rows.5.x0_ref), channel_id=1, source_target_pairs={{0,1},{1,0},{2,3},{3,2},{4,5},{5,4},{6,7},{7,6},{8,9},{9,8},{10,11... | collective-permute-start | bytes 786440 | tf_op jit(solution)/shard_map/ppermute | solution.py:741
  33.1 1.8 %collective-permute-start.3 = (bf16[1024,128]{1,0:T(8,128)(2,1)S(1)}, bf16[1024,128]{1,0:T(8,128)(2,1)S(1)}, u32[]{:S(2)}, u32[]{:S(2)}) collective-permute-start(bf16[1024,128]{1,0:T(8,128)(2,1)S(1)} %collective-permute-done.1.x1_ref), channel_id=1, source_target_pairs={{0,1},{1,0},{2,3},{3,2},{4,5},{5,4},{6,7},{7,6},{8,9},{9,8},{10,11... | collective-permute-start | bytes 786440 | tf_op jit(solution)/shard_map/ppermute | solution.py:741
  33.1 25.4 %collective-permute-start = (bf16[1024,128]{1,0:T(8,128)(2,1)S(1)}, bf16[1024,128]{1,0:T(8,128)(2,1)S(1)}, u32[]{:S(2)}, u32[]{:S(2)}) collective-permute-start(bf16[1024,128]{1,0:T(8,128)(2,1)S(1)} %permute_rows.4.x0_ref), channel_id=1, source_target_pairs={{0,2},{1,3},{2,0},{3,1},{4,6},{5,7},{6,4},{7,5},{8,10},{9,11},{10,... | collective-permute-start | bytes 786440 | tf_op jit(solution)/shard_map/ppermute | solution.py:741
  34.6 24.3 %collective-permute-start.4 = (bf16[1024,128]{1,0:T(8,128)(2,1)S(1)}, bf16[1024,128]{1,0:T(8,128)(2,1)S(1)}, u32[]{:S(2)}, u32[]{:S(2)}) collective-permute-start(bf16[1024,128]{1,0:T(8,128)(2,1)S(1)} %permute_rows.4.x0_ref), channel_id=1, source_target_pairs={{0,1},{1,0},{2,3},{3,2},{4,5},{5,4},{6,7},{7,6},{8,9},{9,8},{10,11... | collective-permute-start | bytes 786440 | tf_op jit(solution)/shard_map/ppermute | solution.py:741
  37.4 21.1 %copy-start.10 = (bf16[128,1024]{1,0:T(8,128)(2,1)}, bf16[128,1024]{1,0:T(8,128)(2,1)S(1)}, u32[]{:S(2)}) copy-start(bf16[128,1024]{1,0:T(8,128)(2,1)S(1)} %get-tuple-element.169.key_t_ref.key_ref) | copy-start | bytes 786436
  37.4 21.1 %copy-start.11 = (bf16[128,1024]{1,0:T(8,128)(2,1)}, bf16[128,1024]{1,0:T(8,128)(2,1)S(1)}, u32[]{:S(2)}) copy-start(bf16[128,1024]{1,0:T(8,128)(2,1)S(1)} %get-tuple-element.170.value_t_ref.refs_4_.value_ref) | copy-start | bytes 786436
  37.4 63.4 %copy-start.9 = (bf16[128,1024]{1,0:T(8,128)(2,1)}, bf16[128,1024]{1,0:T(8,128)(2,1)S(1)}, u32[]{:S(2)}) copy-start(bf16[128,1024]{1,0:T(8,128)(2,1)S(1)} %get-tuple-element.168.query_t_ref.refs_3_.query_ref) | copy-start | bytes 786436
  58.5 1.6 %collective-permute-start.5 = (bf16[1024,128]{1,0:T(8,128)(2,1)S(1)}, bf16[1024,128]{1,0:T(8,128)(2,1)S(1)}, u32[]{:S(2)}, u32[]{:S(2)}) collective-permute-start(bf16[1024,128]{1,0:T(8,128)(2,1)S(1)} %collective-permute-done.x1_ref), channel_id=1, source_target_pairs={{0,1},{1,0},{2,3},{3,2},{4,5},{5,4},{6,7},{7,6},{8,9},{9,8},{10,11... | collective-permute-start | bytes 786440 | tf_op jit(solution)/shard_map/ppermute | solution.py:741
  62.7 4.0 %copy-start.1 = (bf16[128,1024]{1,0:T(8,128)(2,1)S(1)}, bf16[128,1024]{1,0:T(8,128)(2,1)}, u32[]{:S(2)}) copy-start(bf16[128,1024]{1,0:T(8,128)(2,1)} %get-tuple-element.129.query_t_ref.refs_3_.query_ref) | copy-start | bytes 786436
  62.7 4.0 %copy-start.2 = (bf16[128,1024]{1,0:T(8,128)(2,1)S(1)}, bf16[128,1024]{1,0:T(8,128)(2,1)}, u32[]{:S(2)}) copy-start(bf16[128,1024]{1,0:T(8,128)(2,1)} %get-tuple-element.131.value_t_ref.refs_4_.value_ref) | copy-start | bytes 786436
  62.7 4.0 %copy-start.14 = (bf16[128,1024]{1,0:T(8,128)(2,1)S(1)}, bf16[128,1024]{1,0:T(8,128)(2,1)}, u32[]{:S(2)}) copy-start(bf16[128,1024]{1,0:T(8,128)(2,1)} %get-tuple-element.130.key_t_ref.key_ref) | copy-start | bytes 786436
  62.8 4.0 %copy-start.18 = (bf16[1024,128]{1,0:T(8,128)(2,1)S(1)}, bf16[1024,128]{1,0:T(8,128)(2,1)}, u32[]{:S(2)}) copy-start(bf16[1024,128]{1,0:T(8,128)(2,1)} %get-tuple-element.127.key_ref) | copy-start | bytes 786436
  62.8 4.0 %copy-start.19 = (bf16[128,1024]{1,0:T(8,128)(2,1)S(1)}, bf16[128,1024]{1,0:T(8,128)(2,1)}, u32[]{:S(2)}) copy-start(bf16[128,1024]{1,0:T(8,128)(2,1)} %get-tuple-element.128.base2_t_ref) | copy-start | bytes 786436
  65.4 23.2 %copy-start.15 = (bf16[512,128]{1,0:T(8,128)(2,1)S(1)}, bf16[512,128]{1,0:T(8,128)(2,1)}, u32[]{:S(2)}) copy-start(bf16[512,128]{1,0:T(8,128)(2,1)} %refs_10_.3) | copy-start | bytes 393220
  65.4 21.0 %collective-permute-start.6 = (bf16[128,2048]{1,0:T(8,128)(2,1)S(1)}, bf16[128,2048]{1,0:T(8,128)(2,1)S(1)}, u32[]{:S(2)}, u32[]{:S(2)}) collective-permute-start(bf16[128,2048]{1,0:T(8,128)(2,1)S(1)} %segment_rows.1.refs_6_.d_out_ref), channel_id=1, source_target_pairs={{0,2},{1,3},{2,0},{3,1},{4,6},{5,7},{6,4},{7,5},{8,10},{9,11},{10,... | collective-permute-start | bytes 1572872 | tf_op jit(solution)/shard_map/ppermute | solution.py:741
  66.7 20.3 %collective-permute-start.7 = (bf16[128,2048]{1,0:T(8,128)(2,1)S(1)}, bf16[128,2048]{1,0:T(8,128)(2,1)S(1)}, u32[]{:S(2)}, u32[]{:S(2)}) collective-permute-start(bf16[128,2048]{1,0:T(8,128)(2,1)S(1)} %segment_rows.1.refs_6_.d_out_ref), channel_id=1, source_target_pairs={{0,1},{1,0},{2,3},{3,2},{4,5},{5,4},{6,7},{7,6},{8,9},{9,8},{10,11... | collective-permute-start | bytes 1572872 | tf_op jit(solution)/shard_map/ppermute | solution.py:741
  86.4 2.1 %collective-permute-start.8 = (bf16[128,2048]{1,0:T(8,128)(2,1)S(1)}, bf16[128,2048]{1,0:T(8,128)(2,1)S(1)}, u32[]{:S(2)}, u32[]{:S(2)}) collective-permute-start(bf16[128,2048]{1,0:T(8,128)(2,1)S(1)} %collective-permute-done.6.refs_7_), channel_id=1, source_target_pairs={{0,1},{1,0},{2,3},{3,2},{4,5},{5,4},{6,7},{7,6},{8,9},{9,8},{10,11... | collective-permute-start | bytes 1572872 | tf_op jit(solution)/shard_map/ppermute | solution.py:741
  96.7 1.5 %copy-start.7 = (bf16[1024,512]{1,0:T(8,128)(2,1)S(1)}, bf16[1024,512]{1,0:T(8,128)(2,1)}, u32[]{:S(2)}) copy-start(bf16[1024,512]{1,0:T(8,128)(2,1)} %get-tuple-element.148.refs_4_) | copy-start | bytes 3145732
  97.8 2.0 %collective-permute-start.9 = (bf16[272,1024]{1,0:T(8,128)(2,1)S(1)}, bf16[272,1024]{1,0:T(8,128)(2,1)S(1)}, u32[]{:S(2)}, u32[]{:S(2)}) collective-permute-start(bf16[272,1024]{1,0:T(8,128)(2,1)S(1)} %get-tuple-element.147), channel_id=1, source_target_pairs={{0,1},{1,0},{2,3},{3,2},{4,5},{5,4},{6,7},{7,6},{8,9},{9,8},{10,11... | collective-permute-start | bytes 1671176 | tf_op jit(solution)/shard_map/ppermute | solution.py:741
  98.2 2.6 %copy-start.12 = (bf16[128,1024]{1,0:T(8,128)(2,1)S(1)}, bf16[128,1024]{1,0:T(8,128)(2,1)}, u32[]{:S(2)}) copy-start(bf16[128,1024]{1,0:T(8,128)(2,1)} %copy-done.11) | copy-start | bytes 786436
  98.2 2.6 %copy-start.13 = (bf16[128,1024]{1,0:T(8,128)(2,1)S(1)}, bf16[128,1024]{1,0:T(8,128)(2,1)}, u32[]{:S(2)}) copy-start(bf16[128,1024]{1,0:T(8,128)(2,1)} %get-tuple-element.155.refs_5_.refs_3_) | copy-start | bytes 786436
  99.9 10.8 %collective-permute-start.10 = (bf16[144,1024]{1,0:T(8,128)(2,1)S(1)}, bf16[144,1024]{1,0:T(8,128)(2,1)S(1)}, u32[]{:S(2)}, u32[]{:S(2)}) collective-permute-start(bf16[144,1024]{1,0:T(8,128)(2,1)S(1)} %get-tuple-element.152), channel_id=1, source_target_pairs={{0,2},{1,3},{2,0},{3,1},{4,6},{5,7},{6,4},{7,5},{8,10},{9,11},{10,... | collective-permute-start | bytes 884744 | tf_op jit(solution)/shard_map/ppermute | solution.py:741
  100.8 9.9 %copy-start.6 = (bf16[1024,512]{1,0:T(8,128)(2,1)S(1)}, bf16[1024,512]{1,0:T(8,128)(2,1)}, u32[]{:S(2)}) copy-start(bf16[1024,512]{1,0:T(8,128)(2,1)} %get-tuple-element.162.refs_4_) | copy-start | bytes 3145732
  110.7 1.8 %copy-start.3 = (bf16[128,1024]{1,0:T(8,128)(2,1)}, bf16[128,1024]{1,0:T(8,128)(2,1)S(1)}, u32[]{:S(2)}) copy-start(bf16[128,1024]{1,0:T(8,128)(2,1)S(1)} %get-tuple-element.165.refs_0_.d_query_ref) | copy-start | bytes 786436
  110.7 1.8 %copy-start.4 = (bf16[128,1024]{1,0:T(8,128)(2,1)}, bf16[128,1024]{1,0:T(8,128)(2,1)S(1)}, u32[]{:S(2)}) copy-start(bf16[128,1024]{1,0:T(8,128)(2,1)S(1)} %get-tuple-element.166.refs_1_.d_key_ref) | copy-start | bytes 786436
  110.7 1.8 %copy-start.5 = (bf16[128,1024]{1,0:T(8,128)(2,1)}, bf16[128,1024]{1,0:T(8,128)(2,1)S(1)}, u32[]{:S(2)}) copy-start(bf16[128,1024]{1,0:T(8,128)(2,1)S(1)} %get-tuple-element.167.refs_2_.d_value_ref) | copy-start | bytes 786436
  112.5 20.2 %all-to-all-start.2 = ((bf16[8,64,512]{2,1,0:T(8,128)(2,1)}), bf16[8,64,512]{2,1,0:T(8,128)(2,1)S(1)}, u32[]{:S(2)}, u32[]{:S(2)}) async-start(bf16[8,64,512]{2,1,0:T(8,128)(2,1)} %bitcast.10), calls=%async_computation.2 | async-start | bytes 1048576 | tf_op jit(solution)/shard_map/all_to_all | solution.py:744
  120.3 11.3 %copy-start.8 = (f32[128,1024]{1,0:T(8,128)S(1)}, f32[128,1024]{1,0:T(8,128)}, u32[]{:S(2)}) copy-start(f32[128,1024]{1,0:T(8,128)} %get-tuple-element.177.normed_ref) | copy-start | bytes 1572868
  120.3 11.3 %copy-start.16 = (f32[8,1024]{1,0:T(8,128)S(1)}, f32[8,1024]{1,0:T(8,128)}, u32[]{:S(2)}) copy-start(f32[8,1024]{1,0:T(8,128)} %get-tuple-element.178.inv_ref) | copy-start | bytes 98308
  120.3 2.0 %collective-permute-start.11 = (bf16[272,1024]{1,0:T(8,128)(2,1)S(1)}, bf16[272,1024]{1,0:T(8,128)(2,1)S(1)}, u32[]{:S(2)}, u32[]{:S(2)}) collective-permute-start(bf16[272,1024]{1,0:T(8,128)(2,1)S(1)} %get-tuple-element.173), channel_id=1, source_target_pairs={{0,1},{1,0},{2,3},{3,2},{4,5},{5,4},{6,7},{7,6},{8,9},{9,8},{10,11... | collective-permute-start | bytes 1671176 | tf_op jit(solution)/shard_map/ppermute | solution.py:741
  122.5 9.1 %collective-permute-start.12 = (bf16[144,1024]{1,0:T(8,128)(2,1)S(1)}, bf16[144,1024]{1,0:T(8,128)(2,1)S(1)}, u32[]{:S(2)}, u32[]{:S(2)}) collective-permute-start(bf16[144,1024]{1,0:T(8,128)(2,1)S(1)} %get-tuple-element.176), channel_id=1, source_target_pairs={{0,2},{1,3},{2,0},{3,1},{4,6},{5,7},{6,4},{7,5},{8,10},{9,11},{10,... | collective-permute-start | bytes 884744 | tf_op jit(solution)/shard_map/ppermute | solution.py:741
